TPU v7x, 32 devices: a whole 2x2x4 slice. The times are simulated.
32 devices in a mesh: expert: 16 (over z, y, x), tensor: 2 (over core).
Axes of the slice: x: 2, y: 2, z: 4, core: 2. Of those that a mesh axis runs over, the one named last changes fastest.
Arguments:
- first_half: bfloat16 [2048, 2048], P('expert', 'tensor'), may hold values from -6 to 6
- second_half: bfloat16 [2048, 2048], P('expert', 'tensor'), may hold values from -1.5 to 1.5
- first_grad: bfloat16 [2048, 2048], P('expert', 'tensor'), may hold values from -1.5 to 1.5
- second_grad: bfloat16 [2048, 2048], P('expert', 'tensor'), may hold values from -6 to 6
- expert_ids: int32 [2048, 6], P('expert'), may hold values from 0 to 15, as said below
- gate_weights: bfloat16 [2048, 6], P('expert'), may hold values from 0.049804688 to 0.5
- expert_in: bfloat16 [16, 2, 1408, 2048], P('expert', None, 'tensor'), may hold values from -0.125 to 0.125
- expert_out: bfloat16 [16, 1408, 2048], P('expert', 'tensor'), may hold values from -0.15625 to 0.15625
Outputs:
- restored: bfloat16 [2048, 2048], P('expert', 'tensor')
- carried_grad: bfloat16 [2048, 2048], P('expert', 'tensor')
- gate_grad: float32 [2048, 6], P('expert')
- grad_in: bfloat16 [16, 2, 1408, 2048], P('expert', None, 'tensor')
- grad_out: bfloat16 [16, 1408, 2048], P('expert', 'tensor')
Inputs may be any that keep to these rules, and one draw needn't show every extreme that they name: `expert_ids`: each token names 6 different experts. In the rows of one index of expert (128 tokens) each expert is named by at least 40 and at most 56 tokens, and one expert is named by exactly 56 tokens of every index of expert.
All inputs are finite; a program needn't handle non-finite values.
Results may differ from a plain program's by a relative error of at most 0.02.
Values may be sent and summed in bfloat16 or wider, within the bound.
No kernel may reach another device: no remote copies, remote signals or barrier semaphores. Data moves between devices by JAX's collectives and lax.ppermute only.
A program may use at most 128 MiB of HBM per device.

v0:
```python
import jax
import jax.numpy as jnp
from jax import lax
from jax.sharding import PartitionSpec as P


def expert_work(slot_rows, slot_cots, slot_gates, weights_in, weights_out):
    pre = jnp.einsum("erd,ekhd->ekrh", slot_rows, weights_in, preferred_element_type=jnp.float32)
    gate_pre = pre[:, 0]
    up_pre = pre[:, 1]
    sigma = jax.nn.sigmoid(gate_pre)
    active = gate_pre * sigma
    hidden = (active * up_pre).astype(jnp.bfloat16)
    part_out = jnp.einsum("erh,ehd->erd", hidden, weights_out, preferred_element_type=jnp.float32)
    gate_piece = jnp.sum(slot_cots.astype(jnp.float32) * part_out, axis=2)
    scaled = (slot_gates[:, :, None].astype(jnp.float32) * slot_cots.astype(jnp.float32)).astype(
        jnp.bfloat16
    )
    hidden_grad = jnp.einsum(
        "erd,ehd->erh", scaled, weights_out, preferred_element_type=jnp.float32
    )
    gate_pre_grad = (hidden_grad * up_pre * sigma * (1.0 + gate_pre * (1.0 - sigma))).astype(
        jnp.bfloat16
    )
    up_grad = (hidden_grad * active).astype(jnp.bfloat16)
    input_piece = jnp.einsum(
        "erh,ehd->erd", gate_pre_grad, weights_in[:, 0], preferred_element_type=jnp.float32
    ) + jnp.einsum("erh,ehd->erd", up_grad, weights_in[:, 1], preferred_element_type=jnp.float32)
    grad_gate = jnp.einsum(
        "erh,erd->ehd", gate_pre_grad, slot_rows, preferred_element_type=jnp.float32
    ).astype(jnp.bfloat16)
    grad_up = jnp.einsum(
        "erh,erd->ehd", up_grad, slot_rows, preferred_element_type=jnp.float32
    ).astype(jnp.bfloat16)
    grad_in = jnp.stack([grad_gate, grad_up], axis=1)
    grad_out = jnp.einsum(
        "erh,erd->ehd", hidden, scaled, preferred_element_type=jnp.float32
    ).astype(jnp.bfloat16)
    return (part_out, input_piece, gate_piece, grad_in, grad_out)


def body(
    first_half,
    second_half,
    first_grad,
    second_grad,
    expert_ids,
    gate_weights,
    expert_in,
    expert_out,
):
    tokens_here = expert_ids.shape[0]
    picks = expert_ids.shape[1]
    groups = lax.axis_size("expert")
    local_count = expert_in.shape[0]
    experts_all = groups * local_count
    capacity = tokens_here * picks * 7 // (6 * experts_all)
    routes = expert_ids.reshape(-1)
    onehot = (routes[:, None] == jnp.arange(experts_all, dtype=jnp.int32)[None, :]).astype(
        jnp.int32
    )
    before = jnp.cumsum(onehot, axis=0) - onehot
    slot_index = jnp.sum(before * onehot, axis=1)
    destination = routes * capacity + slot_index
    route_token = jnp.arange(tokens_here * picks, dtype=jnp.int32) // picks
    slot_token = (
        jnp.full((experts_all * capacity,), tokens_here, jnp.int32).at[destination].set(route_token)
    )
    slot_gate = (
        jnp.zeros((experts_all * capacity,), jnp.bfloat16)
        .at[destination]
        .set(gate_weights.reshape(-1))
    )
    slot_gate = slot_gate.reshape(experts_all, capacity)

    def to_slots(values):
        padded = jnp.concatenate([values, jnp.zeros((1, values.shape[1]), values.dtype)], axis=0)
        return padded[slot_token].reshape(experts_all, capacity, values.shape[1])

    def to_local(values):
        shaped = values.reshape((groups, local_count) + values.shape[1:])
        shaped = jnp.moveaxis(shaped, 1, 0)
        return shaped.reshape((local_count, groups * capacity) + values.shape[2:])

    def to_sources(values):
        shaped = values.reshape((local_count, groups, capacity) + values.shape[2:])
        shaped = jnp.moveaxis(shaped, 0, 1)
        return shaped.reshape((experts_all, capacity) + values.shape[2:])

    whole_first, whole_cots = (
        lax.all_gather(first_half, "tensor", axis=1, tiled=True),
        lax.all_gather(second_grad, "tensor", axis=1, tiled=True),
    )
    recv_rows, recv_cots, recv_gates = (
        lax.all_to_all(to_slots(whole_first), "expert", split_axis=0, concat_axis=0, tiled=True),
        lax.all_to_all(to_slots(whole_cots), "expert", split_axis=0, concat_axis=0, tiled=True),
        lax.all_to_all(slot_gate, "expert", split_axis=0, concat_axis=0, tiled=True),
    )
    results = expert_work(
        to_local(recv_rows), to_local(recv_cots), to_local(recv_gates), expert_in, expert_out
    )
    grad_in = results[3]
    grad_out = results[4]
    gate_all = to_sources(results[2]).astype(jnp.bfloat16)
    weights_f = gate_weights.astype(jnp.float32)
    out_all = to_sources(results[0].astype(jnp.bfloat16))
    input_all = to_sources(results[1].astype(jnp.bfloat16))
    back_out, back_input, back_gate = (
        lax.all_to_all(out_all, "expert", split_axis=0, concat_axis=0, tiled=True),
        lax.all_to_all(input_all, "expert", split_axis=0, concat_axis=0, tiled=True),
        lax.all_to_all(gate_all, "expert", split_axis=0, concat_axis=0, tiled=True),
    )
    width = back_out.shape[2]
    picked_out = back_out.reshape(-1, width)[destination].reshape(tokens_here, picks, width)
    picked_input = back_input.reshape(-1, width)[destination].reshape(tokens_here, picks, width)
    mixed = jnp.sum(weights_f[:, :, None] * picked_out.astype(jnp.float32), axis=1)
    summed_input = jnp.sum(picked_input.astype(jnp.float32), axis=1)
    branch_cols, input_cols = (
        lax.psum_scatter(
            mixed.astype(jnp.bfloat16), "tensor", scatter_dimension=1, tiled=True
        ).astype(jnp.float32),
        lax.psum_scatter(
            summed_input.astype(jnp.bfloat16), "tensor", scatter_dimension=1, tiled=True
        ).astype(jnp.float32),
    )
    gate_back = back_gate.astype(jnp.float32)
    gate_parts = gate_back.reshape(-1)[destination].reshape(tokens_here, picks)
    gate_grad = lax.psum(gate_parts, "tensor")
    restored = (second_half.astype(jnp.float32) - branch_cols).astype(jnp.bfloat16)
    carried_grad = (first_grad.astype(jnp.float32) + input_cols).astype(jnp.bfloat16)
    return (restored, carried_grad, gate_grad, grad_in, grad_out)


def solution(mesh):
    in_specs = (
        P("expert", "tensor"),
        P("expert", "tensor"),
        P("expert", "tensor"),
        P("expert", "tensor"),
        P("expert", None),
        P("expert", None),
        P("expert", None, "tensor", None),
        P("expert", "tensor", None),
    )
    out_specs = (
        P("expert", "tensor"),
        P("expert", "tensor"),
        P("expert", None),
        P("expert", None, "tensor", None),
        P("expert", "tensor", None),
    )
    return jax.shard_map(body, mesh=mesh, in_specs=in_specs, out_specs=out_specs, check_vma=False)
```

profile of v0, /device:TPU:0, one launch (start us, length us, event | category | flops | bytes accessed | tf_op | source)
XLA Modules:
  0.0 445.9 jit_solution(11520407222823611700)
XLA Ops:
  7.2 0.8 broadcast_multiply_fusion
  8.0 0.8 copy.23
  9.4 1.7 reduce-window.6
  11.1 0.3 slice_reduce_fusion
  11.5 3.4 scatter_custom_fusion
  14.9 2.5 all_gather.6
  17.5 5.0 %gather_fusion = bf16[896,2048]{1,0:T(8,128)(2,1)} fusion(bf16[129,2048]{1,0:T(8,128)(2,1)S(1)} %concatenate.6, s32[1024]{0:T(1024)S(1)} %pad_clamp_fusion.1), kind=kCustom, calls=%fused_computation | custom fusion | bytes 7343616 | tf_op jit(solution)/shard_map/gather | solution.py:78
  22.4 8.4 %all-to-all-start = ((bf16[16,56,2048]{2,1,0:T(8,128)(2,1)}), bf16[16,56,2048]{2,1,0:T(8,128)(2,1)}, u32[]{:S(2)}, u32[]{:S(2)}) async-start(bf16[16,56,2048]{2,1,0:T(8,128)(2,1)} %bitcast.120), calls=%async_computation | async-start | bytes 7340032 | tf_op jit(solution)/shard_map/all_to_all | solution.py:95
  30.8 2.2 all_gather.7
  33.1 5.0 %gather_fusion.2 = bf16[896,2048]{1,0:T(8,128)(2,1)} fusion(bf16[129,2048]{1,0:T(8,128)(2,1)S(1)} %concatenate.7, s32[1024]{0:T(1024)S(1)} %pad_clamp_fusion.1), kind=kCustom, calls=%fused_computation.2 | custom fusion | bytes 7343616 | tf_op jit(solution)/shard_map/gather | solution.py:78
  38.1 63.5 %all-to-all-done = bf16[16,56,2048]{2,1,0:T(8,128)(2,1)} async-done(((bf16[16,56,2048]{2,1,0:T(8,128)(2,1)}), bf16[16,56,2048]{2,1,0:T(8,128)(2,1)}, u32[]{:S(2)}, u32[]{:S(2)}) %all-to-all-start) | async-done | bytes 3670048 | tf_op jit(solution)/shard_map/all_to_all | solution.py:95
  101.6 18.2 %all-to-all-start.3 = ((bf16[16,56,2048]{2,1,0:T(8,128)(2,1)}), bf16[16,56,2048]{2,1,0:T(8,128)(2,1)}, u32[]{:S(2)}, u32[]{:S(2)}) async-start(bf16[16,56,2048]{2,1,0:T(8,128)(2,1)} %bitcast.119), calls=%async_computation.4 | async-start | bytes 7340032 | tf_op jit(solution)/shard_map/all_to_all | solution.py:96
  120.1 9.1 %scatter_custom_fusion.1 = bf16[896]{0:T(1024)(128)(2,1)S(1)} fusion(s32[768]{0:T(1024)S(1)} %fusion.37, bf16[768]{0:T(1024)(128)(2,1)S(1)} %reshape.337, bf16[]{:T(256)} %constant.11.clone.1), kind=kCustom, calls=%fused_computation.76 | custom fusion | bytes 1794 | tf_op jit(solution)/shard_map/scatter | solution.py:72
  129.3 0.7 all_to_all.29
  130.0 9.3 %fusion.25 = f32[1,2,896,704]{2,3,1,0:T(8,128)S(1)} fusion(bf16[896,2048,1]{1,0,2:T(8,128)(2,1)} %bitcast.3, bf16[1,2,704,2048]{3,2,1,0:T(8,128)(2,1)} %param.14), kind=kOutput, calls=%fused_computation.45 | convolution fusion | flops 5167382528 | bytes 14483456 | tf_op jit(solution)/shard_map/erd,ekhd->ekrh/dot_general | solution.py:8
  139.3 2.3 copy-done.2
  141.6 1.7 multiply_convert_fusion.1
  143.3 46.2 %all-to-all-done.3 = bf16[16,56,2048]{2,1,0:T(8,128)(2,1)} async-done(((bf16[16,56,2048]{2,1,0:T(8,128)(2,1)}), bf16[16,56,2048]{2,1,0:T(8,128)(2,1)}, u32[]{:S(2)}, u32[]{:S(2)}) %all-to-all-start.3) | async-done | bytes 3670048 | tf_op jit(solution)/shard_map/all_to_all | solution.py:96
  189.5 16.7 %all-to-all-start.2 = ((bf16[16,1,56]{2,1,0:T(2,128)(2,1)}), bf16[16,1,56]{2,1,0:T(2,128)(2,1)S(1)}, u32[]{:S(2)}, u32[]{:S(2)}) async-start(bf16[16,1,56]{2,1,0:T(2,128)(2,1)} %all_to_all.29), calls=%async_computation.3 | async-start | bytes 16384 | tf_op jit(solution)/shard_map/all_to_all | solution.py:97
  206.2 6.6 %fusion = (bf16[896]{0:T(1024)(128)(2,1)S(1)}, bf16[896,2048]{1,0:T(8,128)(2,1)}) fusion(bf16[16,56,2048]{2,1,0:T(8,128)(2,1)} %all-to-all-done.3, bf16[1,704,2048]{2,1,0:T(8,128)(2,1)S(1)} %copy-done, bf16[1,1,896,704]{2,3,1,0:T(8,128)(2,1)} %multiply_convert_fusion.1), kind=kOutput, calls=%fused_computation.9 | convolution fusion | flops 2591030272 | bytes 11486976 | tf_op jit(solution)/shard_map/erh,ehd->erd/dot_general | solution.py:14
  212.8 0.6 all-to-all-done.2
  213.4 6.6 %all-to-all-start.1 = ((bf16[16,56,2048]{2,1,0:T(8,128)(2,1)}), bf16[16,56,2048]{2,1,0:T(8,128)(2,1)}, u32[]{:S(2)}, u32[]{:S(2)}) async-start(bf16[16,56,2048]{2,1,0:T(8,128)(2,1)} %bitcast.122), calls=%async_computation.1 | async-start | bytes 7340032 | tf_op jit(solution)/shard_map/all_to_all | solution.py:109
  220.1 7.0 %fusion.23 = (bf16[896,704]{0,1:T(8,128)(2,1)S(1)}, bf16[896,704]{0,1:T(8,128)(2,1)S(1)}) fusion(f32[1,2,896,704]{2,3,1,0:T(8,128)} %copy-done.2, bf16[1,704,2048]{2,1,0:T(8,128)(2,1)S(1)} %copy-done, f32[896]{0:T(1024)S(1)} %reshape.281, bf16[1,896,1,1,1,1,2048]{6,1,5,4,3,2,0:T(8,128)(2,1)} %bitcast.99), kind=kOutput, calls=%fused_computation.41 | convolution fusion | flops 2597396480 | bytes 14126592 | tf_op jit(solution)/shard_map/erd,ehd->erh/dot_general | solution.py:19
  227.1 5.8 %fusion.8 = f32[896,2048]{1,0:T(8,128)S(1)} fusion(bf16[896,704]{0,1:T(8,128)(2,1)S(1)} %get-tuple-element.16, bf16[1,2,704,2048]{3,2,1,0:T(8,128)(2,1)} %param.14), kind=kOutput, calls=%fused_computation.23 | convolution fusion | flops 2583691264 | bytes 11485184 | tf_op jit(solution)/shard_map/erh,ehd->erd/dot_general | solution.py:26
  232.9 7.0 %add_convert_fusion = bf16[896,2048]{1,0:T(8,128)(2,1)} fusion(f32[896,2048]{1,0:T(8,128)S(1)} %fusion.8, bf16[896,704]{0,1:T(8,128)(2,1)S(1)} %get-tuple-element.15, bf16[1,2,704,2048]{3,2,1,0:T(8,128)(2,1)} %param.14), kind=kOutput, calls=%fused_computation.10 | convolution fusion | flops 2587361280 | bytes 15155200 | tf_op jit(solution)/shard_map/erh,ehd->erd/dot_general | solution.py:28
  239.9 49.3 %all-to-all-done.1 = bf16[16,56,2048]{2,1,0:T(8,128)(2,1)} async-done(((bf16[16,56,2048]{2,1,0:T(8,128)(2,1)}), bf16[16,56,2048]{2,1,0:T(8,128)(2,1)}, u32[]{:S(2)}, u32[]{:S(2)}) %all-to-all-start.1) | async-done | bytes 3670048 | tf_op jit(solution)/shard_map/all_to_all | solution.py:109
  289.2 16.1 %all-to-all-start.4 = ((bf16[16,56,2048]{2,1,0:T(8,128)(2,1)}), bf16[16,56,2048]{2,1,0:T(8,128)(2,1)}, u32[]{:S(2)}, u32[]{:S(2)}) async-start(bf16[16,56,2048]{2,1,0:T(8,128)(2,1)} %bitcast.121), calls=%async_computation.5 | async-start | bytes 7340032 | tf_op jit(solution)/shard_map/all_to_all | solution.py:110
  305.3 0.3 reduce-scatter.3.cloned.1.call-start
  305.7 9.7 %gather_fusion.1 = bf16[768,2048]{1,0:T(8,128)(2,1)} fusion(bf16[896,2048]{1,0:T(8,128)(2,1)} %bitcast.13, s32[1024]{0:T(1024)S(1)} %pad_clamp_fusion), kind=kCustom, calls=%fused_computation.1 | custom fusion | bytes 6294528 | tf_op jit(solution)/shard_map/gather | solution.py:114
  315.4 6.6 %reshape.280 = f32[128,6,2048]{2,1,0:T(8,128)} reshape(bf16[768,2048]{1,0:T(8,128)(2,1)} %gather_fusion.1) | data formatting | bytes 9437184 | tf_op jit(solution)/shard_map/convert_element_type | solution.py:116
  321.9 7.5 %multiply_reduce_fusion = bf16[128,2048]{1,0:T(8,128)(2,1)} fusion(f32[128,6,2048]{2,1,0:T(8,128)} %reshape.280, f32[128,6]{1,0:T(8,128)S(1)} %copy.21), kind=kLoop, calls=%fused_computation.7 | loop fusion | flops 2883584 | bytes 6818816 | tf_op jit(solution)/shard_map/reduce_sum | solution.py:116
  329.5 0.3 reduce-scatter.5.cloned.1.call-start
  329.8 6.6 %fusion.5 = bf16[1,1,704,2048]{3,2,1,0:T(8,128)(2,1)} fusion(bf16[896,704]{0,1:T(8,128)(2,1)S(1)} %copy-done.11, bf16[896,2048]{1,0:T(8,128)(2,1)} %bitcast.2), kind=kOutput, calls=%fused_computation.20 | convolution fusion | flops 2585133056 | bytes 7815168 | tf_op jit(solution)/shard_map/erh,erd->ehd/dot_general | solution.py:32
  336.4 6.7 %fusion.6 = bf16[1,704,2048]{2,1,0:T(8,128)(2,1)} fusion(bf16[1,1,896,704]{2,3,1,0:T(8,128)(2,1)S(1)} %copy-done.3, f32[896]{0:T(1024)S(1)} %reshape.281, bf16[1,896,1,1,1,1,2048]{6,1,5,4,3,2,0:T(8,128)(2,1)} %bitcast.99), kind=kOutput, calls=%fused_computation.21 | convolution fusion | flops 2590638080 | bytes 7818752 | tf_op jit(solution)/shard_map/erh,erd->ehd/dot_general | solution.py:36
  343.1 31.9 %all-to-all-done.4 = bf16[16,56,2048]{2,1,0:T(8,128)(2,1)} async-done(((bf16[16,56,2048]{2,1,0:T(8,128)(2,1)}), bf16[16,56,2048]{2,1,0:T(8,128)(2,1)}, u32[]{:S(2)}, u32[]{:S(2)}) %all-to-all-start.4) | async-done | bytes 3670048 | tf_op jit(solution)/shard_map/all_to_all | solution.py:110
  375.0 9.6 %gather_fusion.3 = bf16[768,2048]{1,0:T(8,128)(2,1)} fusion(bf16[896,2048]{1,0:T(8,128)(2,1)} %bitcast.22, s32[1024]{0:T(1024)S(1)} %pad_clamp_fusion), kind=kCustom, calls=%fused_computation.3 | custom fusion | bytes 6294528 | tf_op jit(solution)/shard_map/gather | solution.py:115
  384.6 6.2 %reshape.278 = bf16[128,6,2048]{2,1,0:T(8,128)(2,1)} reshape(bf16[768,2048]{1,0:T(8,128)(2,1)} %gather_fusion.3) | data formatting | bytes 6291456 | tf_op jit(solution)/shard_map/reshape | solution.py:115
  390.8 5.8 %reduce_sum.44 = bf16[128,2048]{1,0:T(8,128)(2,1)} reduce(bf16[128,6,2048]{2,1,0:T(8,128)(2,1)} %reshape.278, bf16[]{:T(256)} %constant.11.clone.1), dimensions={1}, to_apply=%region_7.8 | reduce | flops 1310720 | bytes 3670018 | tf_op jit(solution)/shard_map/reduce_sum | solution.py:117
  396.6 6.6 %fusion.4 = bf16[1,1,704,2048]{3,2,1,0:T(8,128)(2,1)} fusion(bf16[896,704]{0,1:T(8,128)(2,1)S(1)} %copy-done.9, bf16[896,2048]{1,0:T(8,128)(2,1)} %bitcast.2), kind=kOutput, calls=%fused_computation.19 | convolution fusion | flops 2585133056 | bytes 7815168 | tf_op jit(solution)/shard_map/erh,erd->ehd/dot_general | solution.py:29
  403.2 0.7 convert_element_type.209
  403.9 16.5 %all-to-all-start.5 = ((bf16[16,1,56]{2,1,0:T(2,128)(2,1)}), bf16[16,1,56]{2,1,0:T(2,128)(2,1)S(1)}, u32[]{:S(2)}, u32[]{:S(2)}) async-start(bf16[16,1,56]{2,1,0:T(2,128)(2,1)} %convert_element_type.209), calls=%async_computation.7 | async-start | bytes 16384 | tf_op jit(solution)/shard_map/all_to_all | solution.py:111
  420.4 5.9 %pad_maximum_fusion = bf16[1,2,704,2048]{3,2,1,0:T(8,128)(2,1)} fusion(bf16[1,1,704,2048]{3,2,1,0:T(8,128)(2,1)} %fusion.5, bf16[1,1,704,2048]{3,2,1,0:T(8,128)(2,1)} %fusion.4), kind=kLoop, calls=%fused_computation.12 | loop fusion | flops 2883584 | bytes 11534336 | tf_op jit(solution)/shard_map/stack | solution.py:35
  426.3 1.3 all-to-all-done.5
  427.7 3.2 gather_fusion.4
  431.0 3.6 psum.7
  434.6 0.7 copy.29
  435.3 1.7 subtract_convert_fusion
  437.0 1.7 add_convert_fusion.1
  (49 shorter events, 1.6 us)
Async XLA Ops:
  7.2 199.0 %copy-start = (bf16[1,704,2048]{2,1,0:T(8,128)(2,1)S(1)}, bf16[1,704,2048]{2,1,0:T(8,128)(2,1)}, u32[]{:S(2)}) copy-start(bf16[1,704,2048]{2,1,0:T(8,128)(2,1)} %param.15) | copy-start | bytes 8650756
  22.4 8.4 %copy-start.4 = (bf16[128,1024]{1,0:T(8,128)(2,1)S(1)}, bf16[128,1024]{1,0:T(8,128)(2,1)}, u32[]{:S(2)}) copy-start(bf16[128,1024]{1,0:T(8,128)(2,1)} %param.11) | copy-start | bytes 786436
  22.4 79.2 %all-to-all-start = ((bf16[16,56,2048]{2,1,0:T(8,128)(2,1)}), bf16[16,56,2048]{2,1,0:T(8,128)(2,1)}, u32[]{:S(2)}, u32[]{:S(2)}) async-start(bf16[16,56,2048]{2,1,0:T(8,128)(2,1)} %bitcast.120), calls=%async_computation | async-start | bytes 7340032 | tf_op jit(solution)/shard_map/all_to_all | solution.py:95
  101.6 18.2 %copy-start.7 = (bf16[128,6]{0,1:T(8,128)(2,1)S(1)}, bf16[128,6]{0,1:T(8,128)(2,1)}, u32[]{:S(2)}) copy-start(bf16[128,6]{0,1:T(8,128)(2,1)} %param.13) | copy-start | bytes 4612
  101.6 87.9 %all-to-all-start.3 = ((bf16[16,56,2048]{2,1,0:T(8,128)(2,1)}), bf16[16,56,2048]{2,1,0:T(8,128)(2,1)}, u32[]{:S(2)}, u32[]{:S(2)}) async-start(bf16[16,56,2048]{2,1,0:T(8,128)(2,1)} %bitcast.119), calls=%async_computation.4 | async-start | bytes 7340032 | tf_op jit(solution)/shard_map/all_to_all | solution.py:96
  139.3 2.3 copy-start.2
  189.5 23.9 %all-to-all-start.2 = ((bf16[16,1,56]{2,1,0:T(2,128)(2,1)}), bf16[16,1,56]{2,1,0:T(2,128)(2,1)S(1)}, u32[]{:S(2)}, u32[]{:S(2)}) async-start(bf16[16,1,56]{2,1,0:T(2,128)(2,1)} %all_to_all.29), calls=%async_computation.3 | async-start | bytes 16384 | tf_op jit(solution)/shard_map/all_to_all | solution.py:97
  213.4 75.8 %all-to-all-start.1 = ((bf16[16,56,2048]{2,1,0:T(8,128)(2,1)}), bf16[16,56,2048]{2,1,0:T(8,128)(2,1)}, u32[]{:S(2)}, u32[]{:S(2)}) async-start(bf16[16,56,2048]{2,1,0:T(8,128)(2,1)} %bitcast.122), calls=%async_computation.1 | async-start | bytes 7340032 | tf_op jit(solution)/shard_map/all_to_all | solution.py:109
  227.1 5.9 %copy-start.8 = (bf16[896,704]{0,1:T(8,128)(2,1)}, bf16[896,704]{0,1:T(8,128)(2,1)S(1)}, u32[]{:S(2)}) copy-start(bf16[896,704]{0,1:T(8,128)(2,1)S(1)} %get-tuple-element.16) | copy-start | bytes 3784708
  227.1 5.9 %copy-start.10 = (bf16[896,704]{0,1:T(8,128)(2,1)}, bf16[896,704]{0,1:T(8,128)(2,1)S(1)}, u32[]{:S(2)}) copy-start(bf16[896,704]{0,1:T(8,128)(2,1)S(1)} %get-tuple-element.15) | copy-start | bytes 3784708
  289.2 85.8 %all-to-all-start.4 = ((bf16[16,56,2048]{2,1,0:T(8,128)(2,1)}), bf16[16,56,2048]{2,1,0:T(8,128)(2,1)}, u32[]{:S(2)}, u32[]{:S(2)}) async-start(bf16[16,56,2048]{2,1,0:T(8,128)(2,1)} %bitcast.121), calls=%async_computation.5 | async-start | bytes 7340032 | tf_op jit(solution)/shard_map/all_to_all | solution.py:110
  305.3 130.0 %reduce-scatter.3.cloned.1.call-start = ((), (), s32[]{:S(2)}) async-start(), calls=%async_computation.8 | async-start | bytes 786432 | tf_op jit(solution)/shard_map/reduce_scatter | solution.py:119
  321.9 7.8 %copy-start.11 = (bf16[896,704]{0,1:T(8,128)(2,1)S(1)}, bf16[896,704]{0,1:T(8,128)(2,1)}, u32[]{:S(2)}) copy-start(bf16[896,704]{0,1:T(8,128)(2,1)} %copy-done.10) | copy-start | bytes 3784708
  329.5 107.6 %reduce-scatter.5.cloned.1.call-start = ((), (), s32[]{:S(2)}) async-start(), calls=%async_computation.9 | async-start | bytes 786432 | tf_op jit(solution)/shard_map/reduce_scatter | solution.py:122
  329.8 6.6 %copy-start.3 = (bf16[1,1,896,704]{2,3,1,0:T(8,128)(2,1)S(1)}, bf16[1,1,896,704]{2,3,1,0:T(8,128)(2,1)}, u32[]{:S(2)}) copy-start(bf16[1,1,896,704]{2,3,1,0:T(8,128)(2,1)} %multiply_convert_fusion.1) | copy-start | bytes 3784708
  390.8 5.8 %copy-start.9 = (bf16[896,704]{0,1:T(8,128)(2,1)S(1)}, bf16[896,704]{0,1:T(8,128)(2,1)}, u32[]{:S(2)}) copy-start(bf16[896,704]{0,1:T(8,128)(2,1)} %copy-done.8) | copy-start | bytes 3784708
  403.9 23.7 %all-to-all-start.5 = ((bf16[16,1,56]{2,1,0:T(2,128)(2,1)}), bf16[16,1,56]{2,1,0:T(2,128)(2,1)S(1)}, u32[]{:S(2)}, u32[]{:S(2)}) async-start(bf16[16,1,56]{2,1,0:T(2,128)(2,1)} %convert_element_type.209), calls=%async_computation.7 | async-start | bytes 16384 | tf_op jit(solution)/shard_map/all_to_all | solution.py:111
  420.4 18.4 %copy-start.1 = (bf16[1,704,2048]{2,1,0:T(8,128)(2,1)S(1)}, bf16[1,704,2048]{2,1,0:T(8,128)(2,1)}, u32[]{:S(2)}) copy-start(bf16[1,704,2048]{2,1,0:T(8,128)(2,1)} %param.15) | copy-start | bytes 8650756
  426.3 9.0 %copy-start.5 = (bf16[128,1024]{1,0:T(8,128)(2,1)S(1)}, bf16[128,1024]{1,0:T(8,128)(2,1)}, u32[]{:S(2)}) copy-start(bf16[128,1024]{1,0:T(8,128)(2,1)} %param.9) | copy-start | bytes 786436
  426.3 10.7 %copy-start.6 = (bf16[128,1024]{1,0:T(8,128)(2,1)S(1)}, bf16[128,1024]{1,0:T(8,128)(2,1)}, u32[]{:S(2)}) copy-start(bf16[128,1024]{1,0:T(8,128)(2,1)} %param.10) | copy-start | bytes 786436
Sparse Core Ops, SparseCore 0:
  329.6 9.1 reduce-scatter.2
  396.8 18.8 reduce-scatter.4
where the time goes:
time: 454 us; the launch traced here: 446 us
  waiting for transfers between devices  193 us (43%)
  starting transfers between devices  83.1 us (18%)
  local copies, waits for them, and re-layouts  64.5 us (14%)
  matrix products  55.6 us (12%)
  other arithmetic  27.2 us (6%)
  between operations  14.6 us (3%)
  blocking collectives  8.24 us (2%)
    all_to_all x1, waiting for transfers between devices, body(): lax.all_to_all(to_slots(whole_first), 'expert', split_axis=0, concat_axis...  63.5 us
    all_to_all x1, waiting for transfers between devices, body(): lax.all_to_all(out_all, 'expert', split_axis=0, concat_axis=0, tiled=True)  49.3 us
    all_to_all x1, waiting for transfers between devices, body(): lax.all_to_all(to_slots(whole_cots), 'expert', split_axis=0, concat_axis=...  46.2 us
    all_to_all x1, waiting for transfers between devices, body(): lax.all_to_all(input_all, 'expert', split_axis=0, concat_axis=0, tiled=True)  31.9 us
    all_to_all x1, starting transfers between devices, body(): lax.all_to_all(to_slots(whole_cots), 'expert', split_axis=0, concat_axis=...  18.2 us
    all_to_all x1, starting transfers between devices, body(): lax.all_to_all(slot_gate, 'expert', split_axis=0, concat_axis=0, tiled=True)  16.7 us
    all_to_all x1, starting transfers between devices, body(): lax.all_to_all(gate_all, 'expert', split_axis=0, concat_axis=0, tiled=True)  16.5 us
    all_to_all x1, starting transfers between devices, body(): lax.all_to_all(input_all, 'expert', split_axis=0, concat_axis=0, tiled=True)  16.1 us
  transfers between devices with their start and end apart: 8, of which 6 were waited for; matrix products, arithmetic and copies ran while one was open for 29% of the time, Pallas kernels for 0%

commit v1 on v0

v1 whole, which is shorter than its diff:
```python
import functools

import jax
import jax.numpy as jnp
from jax import lax
from jax.experimental import pallas as pl
from jax.experimental.pallas import tpu as pltpu
from jax.sharding import PartitionSpec as P

PLANE = 4
TAIL = 16
VMEM_LIMIT = 56 * 1024 * 1024
F32 = jnp.float32
BF16 = jnp.bfloat16


def dot_nn(a, b):
    return lax.dot_general(a, b, (((1,), (0,)), ((), ())), preferred_element_type=F32)


def dot_nt(a, b):
    return lax.dot_general(a, b, (((1,), (1,)), ((), ())), preferred_element_type=F32)


def dot_tn(a, b):
    return lax.dot_general(a, b, (((0,), (0,)), ((), ())), preferred_element_type=F32)


def iota(shape, axis):
    return lax.broadcasted_iota(jnp.int32, shape, axis)


def call(kernel, outs, args, specs, scratch=(), out_specs=None, flops=0, name=None):
    vmem = pl.BlockSpec(memory_space=pltpu.VMEM)
    nbytes = sum(a.size * a.dtype.itemsize for a in args) + sum(
        o.size * o.dtype.itemsize for o in outs
    )
    return pl.pallas_call(
        kernel,
        out_shape=outs,
        in_specs=specs,
        out_specs=out_specs if out_specs is not None else [vmem] * len(outs),
        scratch_shapes=list(scratch),
        compiler_params=pltpu.CompilerParams(vmem_limit_bytes=VMEM_LIMIT),
        cost_estimate=pl.CostEstimate(flops=flops, bytes_accessed=nbytes, transcendentals=0),
        name=name,
    )(*args)


def route_kernel(info, meta, metat, sel, selt, *, zn, pn, tokens, picks, cap):
    rows = zn * cap
    base, inner = info[0], info[1]
    partner_r = iota((8, 1), 0)
    partner_c = iota((1, 8), 1)
    experts_r = jnp.where(partner_r < pn, base + (partner_r ^ inner), -2).astype(F32)
    experts_c = jnp.where(partner_c < pn, base + (partner_c ^ inner), -2).astype(F32)
    earlier_r = (iota((tokens, tokens), 0) < iota((tokens, tokens), 1)).astype(F32).astype(BF16)
    earlier_c = (iota((tokens, tokens), 1) < iota((tokens, tokens), 0)).astype(F32).astype(BF16)
    slot_r = iota((rows, tokens), 0).astype(F32)
    slot_c = iota((tokens, pn * rows), 1).astype(F32)
    for s in range(zn):
        here = slice(s * tokens, (s + 1) * tokens)
        ids_r = meta[0:8, here]
        ids_c = metat[here, 0:8]
        named_r = jnp.zeros((8, tokens), F32)
        named_c = jnp.zeros((tokens, 8), F32)
        for k in range(picks):
            named_r += (ids_r[k : k + 1, :] == experts_r).astype(F32)
            named_c += (ids_c[:, k : k + 1] == experts_c).astype(F32)
        dest_r = dot_nn(named_r.astype(BF16), earlier_r) + s * cap
        dest_c = dot_nn(earlier_c, named_c.astype(BF16)) + s * cap
        dest_r = jnp.where(named_r > 0, dest_r, -1.0)
        dest_c = jnp.where(named_c > 0, dest_c + rows * partner_c.astype(F32), -1.0)
        picked = jnp.zeros((tokens, pn * rows), F32)
        for q in range(pn):
            sel[q * rows : (q + 1) * rows, here] = (
                (slot_r == dest_r[q : q + 1, :]).astype(F32).astype(BF16)
            )
            picked += (slot_c == dest_c[:, q : q + 1]).astype(F32)
        selt[here, :] = picked.astype(BF16)


def pack_kernel(info, meta, sel, *refs, zn, pn, tokens, picks, rows, gates):
    sources, outs, whole = refs[:zn], refs[zn : zn + pn], refs[zn + pn]
    base, inner = info[0], info[1]
    for s in range(zn):
        whole[s * tokens : (s + 1) * tokens, :] = sources[s][...]
    for q in range(pn):
        chosen = sel[q * rows : (q + 1) * rows, :]
        outs[q][0:rows, :] = dot_nn(chosen, whole[...]).astype(BF16)
        if gates:
            expert = (base + (inner ^ q)).astype(F32)
            gate = jnp.zeros((1, zn * tokens), F32)
            for k in range(picks):
                gate += jnp.where(meta[k : k + 1, :] == expert, meta[8 + k : 9 + k, :], 0.0)
            gate = jnp.broadcast_to(gate, (TAIL, zn * tokens)).astype(BF16)
            outs[q][rows : rows + TAIL, :] = jnp.zeros((TAIL, outs[q].shape[1]), BF16)
            outs[q][rows : rows + TAIL, 0:rows] = dot_nt(gate, chosen).astype(BF16)


def combine_kernel(info, meta, sel, selt, *refs, zn, pn, tokens, rows, gates):
    sources, outs, whole = refs[:pn], refs[pn : pn + zn], refs[pn + zn]
    base, inner = info[0], info[1]
    for q in range(pn):
        whole[q * rows : (q + 1) * rows, :] = sources[q][0:rows, :]
    for s in range(zn):
        here = slice(s * tokens, (s + 1) * tokens)
        outs[s][0:tokens, :] = dot_nn(selt[here, :], whole[...]).astype(BF16)
    if gates:
        total = jnp.zeros((8, zn * tokens), F32)
        for q in range(pn):
            expert = (base + (inner ^ q)).astype(F32)
            row = sources[q][rows : rows + TAIL, 0:rows]
            spread = dot_nn(row, sel[q * rows : (q + 1) * rows, :])
            total += jnp.where(meta[0:8, :] == expert, spread[0:8, :], 0.0)
        total = jnp.concatenate([total, jnp.zeros((TAIL - 8, zn * tokens), F32)], axis=0)
        total = total.astype(BF16)
        for s in range(zn):
            outs[s][tokens : tokens + TAIL, :] = jnp.zeros((TAIL, outs[s].shape[1]), BF16)
            outs[s][tokens : tokens + TAIL, 0:tokens] = total[:, s * tokens : (s + 1) * tokens]


def column_block(info, j, nt, cols):
    block = lax.rem(info[2] - j + nt, nt)
    return pl.ds(pl.multiple_of(block * cols, 128), cols)


def forward_kernel(info, *refs, nt, pn, rows, cols):
    n = nt * pn
    xs, win, wout = refs[:n], refs[n], refs[n + 1]
    outs = refs[n + 2 : 2 * n + 2]
    hs, hid, a1, a2, wg, wu, wd, sems = refs[2 * n + 2 :]
    copies = []
    for j in range(nt):
        at = column_block(info, j, nt, cols)
        copies.append(pltpu.make_async_copy(win.at[0, 0, :, at], wg.at[j], sems.at[0, j]))
        copies.append(pltpu.make_async_copy(win.at[0, 1, :, at], wu.at[j], sems.at[1, j]))
    for j in range(nt):
        at = column_block(info, j, nt, cols)
        copies.append(pltpu.make_async_copy(wout.at[0, :, at], wd.at[j], sems.at[2, j]))
    for copy in copies:
        copy.start()
    for copy in copies[: 2 * nt]:
        copy.wait()
    same = iota((rows, rows), 0) == iota((rows, rows), 1)
    for q in range(pn):
        here = slice(q * rows, (q + 1) * rows)
        gate = xs[q][rows : rows + TAIL, 0:rows].astype(F32)[0:1, :]
        gate = jnp.sum(jnp.where(same, gate, 0.0), axis=1, keepdims=True)
        pre = [xs[j * pn + q][0:rows, :] for j in range(nt)]
        g = dot_nt(pre[0], wg[0])
        u = dot_nt(pre[0], wu[0])
        for j in range(1, nt):
            g += dot_nt(pre[j], wg[j])
            u += dot_nt(pre[j], wu[j])
        sigma = jax.nn.sigmoid(g)
        active = g * sigma
        hidden = active * u
        scaled = (gate * hidden).astype(BF16)
        hs[here, :] = scaled
        hid[here, :] = hidden.astype(BF16)
        a1[here, :] = (gate * (u * sigma * (1.0 + g * (1.0 - sigma)))).astype(BF16)
        a2[here, :] = (gate * active).astype(BF16)
        if q == 0:
            for copy in copies[2 * nt :]:
                copy.wait()
        for j in range(nt):
            outs[j * pn + q][...] = dot_nn(scaled, wd[(nt - j) % nt]).astype(BF16)


def backward_kernel(info, *refs, nt, pn, rows, cols):
    n = nt * pn
    cs, win, wout, hid, a1, a2 = refs[:n], *refs[n : n + 5]
    outs = refs[n + 5 : 2 * n + 5]
    gg, ug, wg, wu, wd, sems = refs[2 * n + 5 :]
    copies = []
    for j in range(nt):
        at = column_block(info, j, nt, cols)
        copies.append(pltpu.make_async_copy(wout.at[0, :, at], wd.at[j], sems.at[2, j]))
    for j in range(nt):
        at = column_block(info, j, nt, cols)
        copies.append(pltpu.make_async_copy(win.at[0, 0, :, at], wg.at[j], sems.at[0, j]))
        copies.append(pltpu.make_async_copy(win.at[0, 1, :, at], wu.at[j], sems.at[1, j]))
    for copy in copies:
        copy.start()
    for copy in copies[:nt]:
        copy.wait()
    same = iota((rows, rows), 0) == iota((rows, rows), 1)
    for q in range(pn):
        here = slice(q * rows, (q + 1) * rows)
        grad = dot_nt(cs[q][...], wd[0])
        for j in range(1, nt):
            grad += dot_nt(cs[j * pn + q][...], wd[j])
        piece = jnp.sum(grad * hid[here, :].astype(F32), axis=1, keepdims=True)
        piece = jnp.sum(jnp.where(same, piece, 0.0), axis=0, keepdims=True)
        piece = jnp.broadcast_to(piece, (TAIL, rows)).astype(BF16)
        gate_grad = (grad * a1[here, :].astype(F32)).astype(BF16)
        up_grad = (grad * a2[here, :].astype(F32)).astype(BF16)
        gg[here, :] = gate_grad
        ug[here, :] = up_grad
        if q == 0:
            for copy in copies[nt:]:
                copy.wait()
        for j in range(nt):
            out = outs[j * pn + q]
            w = (nt - j) % nt
            out[0:rows, :] = (dot_nn(gate_grad, wg[w]) + dot_nn(up_grad, wu[w])).astype(BF16)
            out[rows : rows + TAIL, :] = jnp.zeros((TAIL, cols), BF16)
            out[rows : rows + TAIL, 0:rows] = piece


def weights_kernel(info, *refs, nt, pn, rows, cols):
    n = nt * pn
    xs, cs, gg, ug, hs = refs[:n], refs[n : 2 * n], *refs[2 * n : 2 * n + 3]
    gin, gout, whole, stage, sems = refs[2 * n + 3 :]
    copies = []
    for j in range(nt):
        at = column_block(info, j, nt, cols)
        for q in range(pn):
            whole[0, q * rows : (q + 1) * rows, :] = xs[j * pn + q][0:rows, :]
            whole[1, q * rows : (q + 1) * rows, :] = cs[j * pn + q][...]
        for w, (left, right, out) in enumerate(
            ((gg, 0, gin.at[0, 0, :, at]), (ug, 0, gin.at[0, 1, :, at]), (hs, 1, gout.at[0, :, at]))
        ):
            stage[j, w] = dot_tn(left[...], whole[right]).astype(BF16)
            copy = pltpu.make_async_copy(stage.at[j, w], out, sems.at[j, w])
            copy.start()
            copies.append(copy)
    for copy in copies:
        copy.wait()


def body(
    first_half,
    second_half,
    first_grad,
    second_grad,
    expert_ids,
    gate_weights,
    expert_in,
    expert_out,
):
    tokens, picks = expert_ids.shape
    groups = lax.axis_size("expert")
    nt = lax.axis_size("tensor")
    pn = PLANE
    zn = groups // pn
    cap = tokens * picks * 7 // (6 * groups)
    rows = zn * cap
    cols = first_half.shape[1]
    hid_n = expert_out.shape[1]
    width = expert_out.shape[2]
    me = lax.axis_index("expert")
    info = jnp.stack(
        [(me // pn) * pn, me % pn, lax.axis_index("tensor")]
    ).astype(jnp.int32)

    smem = pl.BlockSpec(memory_space=pltpu.SMEM)
    vmem = pl.BlockSpec(memory_space=pltpu.VMEM)
    hbm = pl.BlockSpec(memory_space=pl.ANY)

    def outer_send(value, s):
        if s % zn == 0:
            return value
        return lax.ppermute(
            value,
            "expert",
            [(e, ((e // pn + s) % zn) * pn + e % pn) for e in range(groups)],
        )

    def inner_send(value, q):
        if q == 0:
            return value
        return lax.ppermute(value, "expert", [(e, e ^ q) for e in range(groups)])

    def tensor_send(value, j):
        if j == 0:
            return value
        return lax.ppermute(value, "tensor", [(c, (c + j) % nt) for c in range(nt)])

    def shape(*dims, dtype=BF16):
        return jax.ShapeDtypeStruct(dims, dtype)

    ids8 = jnp.full((8, tokens), -1.0, F32).at[:picks].set(expert_ids.T.astype(F32))
    gates8 = jnp.zeros((8, tokens), F32).at[:picks].set(gate_weights.T.astype(F32))
    own = jnp.concatenate([ids8, gates8], axis=0)
    x_parts = [outer_send(first_half, s) for s in range(zn)]
    meta = jnp.concatenate([outer_send(own, s) for s in range(zn)], axis=1)
    sel, selt = call(
        functools.partial(route_kernel, zn=zn, pn=pn, tokens=tokens, picks=picks, cap=cap),
        [shape(pn * rows, zn * tokens), shape(zn * tokens, pn * rows)],
        [info, meta, meta.T],
        [smem, vmem, vmem],
        name="route",
    )

    def pack(parts, gates):
        height = rows + TAIL if gates else rows
        return call(
            functools.partial(
                pack_kernel, zn=zn, pn=pn, tokens=tokens, picks=picks, rows=rows, gates=gates
            ),
            [shape(height, cols)] * pn,
            [info, meta, sel, *parts],
            [smem] + [vmem] * (2 + zn),
            scratch=[pltpu.VMEM((zn * tokens, cols), BF16)],
            flops=2 * pn * rows * zn * tokens * cols,
            name="pack_gates" if gates else "pack",
        )

    def combine(parts, gates):
        height = tokens + TAIL if gates else tokens
        return call(
            functools.partial(
                combine_kernel, zn=zn, pn=pn, tokens=tokens, rows=rows, gates=gates
            ),
            [shape(height, cols)] * zn,
            [info, meta, sel, selt, *parts],
            [smem] + [vmem] * (3 + pn),
            scratch=[pltpu.VMEM((pn * rows, cols), BF16)],
            flops=2 * pn * rows * zn * tokens * cols,
            name="combine_gates" if gates else "combine",
        )

    def dispatch(parts, gates):
        mine = [inner_send(piece, q) for q, piece in enumerate(pack(parts, gates))]
        return [tensor_send(piece, j) for j in range(nt) for piece in mine]

    def collect(pieces, gates):
        summed = []
        for q in range(pn):
            total = pieces[q].astype(F32)
            for j in range(1, nt):
                total += tensor_send(pieces[j * pn + q], j).astype(F32)
            summed.append(inner_send(total.astype(BF16), q))
        return [outer_send(part, -s) for s, part in enumerate(combine(summed, gates))]

    slots = pn * rows
    work = 2 * slots * hid_n * width
    weight_scratch = [pltpu.VMEM((nt, hid_n, cols), BF16)] * 3 + [
        pltpu.SemaphoreType.DMA((3, nt))
    ]

    xs = dispatch(x_parts, True)
    grad_whole, *_ = lax.optimization_barrier((second_grad, *x_parts))
    c_parts = [outer_send(grad_whole, s) for s in range(zn)]
    cs = dispatch(c_parts, False)

    forward = call(
        functools.partial(forward_kernel, nt=nt, pn=pn, rows=rows, cols=cols),
        [shape(rows, cols)] * (nt * pn) + [shape(slots, hid_n)] * 4,
        [info, *xs, expert_in, expert_out],
        [smem] + [vmem] * (nt * pn) + [hbm, hbm],
        scratch=weight_scratch,
        flops=3 * work,
        name="expert_forward",
    )
    out_parts = collect(forward[: nt * pn], False)
    hs, hid, a1, a2 = forward[nt * pn :]
    backward = call(
        functools.partial(backward_kernel, nt=nt, pn=pn, rows=rows, cols=cols),
        [shape(rows + TAIL, cols)] * (nt * pn) + [shape(slots, hid_n)] * 2,
        [info, *cs, expert_in, expert_out, hid, a1, a2],
        [smem] + [vmem] * (nt * pn) + [hbm, hbm] + [vmem] * 3,
        scratch=weight_scratch,
        flops=3 * work,
        name="expert_backward",
    )
    grad_parts = collect(backward[: nt * pn], True)
    gg, ug = backward[nt * pn :]
    grad_in, grad_out = call(
        functools.partial(weights_kernel, nt=nt, pn=pn, rows=rows, cols=cols),
        [shape(*expert_in.shape), shape(*expert_out.shape)],
        [info, *xs, *cs, gg, ug, hs],
        [smem] + [vmem] * (2 * nt * pn + 3),
        out_specs=[hbm, hbm],
        scratch=[
            pltpu.VMEM((2, slots, cols), BF16),
            pltpu.VMEM((nt, 3, hid_n, cols), BF16),
            pltpu.SemaphoreType.DMA((nt, 3)),
        ],
        flops=3 * work,
        name="expert_weights",
    )

    branch = sum(part.astype(F32) for part in out_parts)
    input_sum = sum(part[:tokens].astype(F32) for part in grad_parts)
    gate_sum = sum(part[tokens : tokens + picks, :tokens].astype(F32) for part in grad_parts)
    restored = (second_half.astype(F32) - branch).astype(BF16)
    carried_grad = (first_grad.astype(F32) + input_sum).astype(BF16)
    return (restored, carried_grad, gate_sum.T, grad_in, grad_out)


def solution(mesh):
    in_specs = (
        P("expert", "tensor"),
        P("expert", "tensor"),
        P("expert", "tensor"),
        P("expert", "tensor"),
        P("expert", None),
        P("expert", None),
        P("expert", None, "tensor", None),
        P("expert", "tensor", None),
    )
    out_specs = (
        P("expert", "tensor"),
        P("expert", "tensor"),
        P("expert", None),
        P("expert", None, "tensor", None),
        P("expert", "tensor", None),
    )
    return jax.shard_map(body, mesh=mesh, in_specs=in_specs, out_specs=out_specs, check_vma=False)
```

time: 454 us -> 215 us (0.47)
  the two profiles are of different devices: /device:TPU:0 before, /device:TPU:9 now
where the time goes in v1:
time: 215 us; the launch traced here: 214 us
  waiting for transfers between devices  89.3 us (42%)
  Pallas kernels  69.9 us (33%)
  starting transfers between devices  39.3 us (18%)
  other arithmetic  8.14 us (4%)
  local copies, waits for them, and re-layouts  6.81 us (3%)
    pallas_call x8, Pallas kernels, call(): pl.pallas_call(kernel, out_shape=outs, in_specs=specs, out_specs=out_spec...  69.9 us
    ppermute x12, waiting for transfers between devices, inner_send(): return lax.ppermute(value, 'expert', [(e, e ^ q) for e in range(groups)])  49 us
    ppermute x15, waiting for transfers between devices, outer_send(): lax.ppermute(value, 'expert', [(e, (e // pn + s) % zn * pn + e % pn) for...  39.5 us
    ppermute x16, starting transfers between devices, tensor_send(): return lax.ppermute(value, 'tensor', [(c, (c + j) % nt) for c in range(nt)])  15.2 us
    ppermute x15, starting transfers between devices, outer_send(): lax.ppermute(value, 'expert', [(e, (e // pn + s) % zn * pn + e % pn) for...  13.7 us
    ppermute x12, starting transfers between devices, inner_send(): return lax.ppermute(value, 'expert', [(e, e ^ q) for e in range(groups)])  10.5 us
    unnamed x84, local copies, waits for them, and re-layouts  5.97 us
  transfers between devices with their start and end apart: 43, of which 14 were waited for; matrix products, arithmetic and copies ran while one was open for 3% of the time, Pallas kernels for 33%

profile of v1, /device:TPU:9, one launch (start us, length us, event | category | flops | bytes accessed | tf_op | source)
XLA Modules:
  0.0 214.5 jit_solution(11561802688489101605)
XLA Ops:
  0.6 1.3 collective-permute-start.3
  2.0 1.1 collective-permute-start.4
  3.1 1.4 collective-permute-start.5
  5.8 1.1 collective-permute-start.2
  7.1 1.0 collective-permute-done.3.refs_1_
  8.1 1.4 collective-permute-start
  9.5 15.0 %collective-permute-done.4.refs_2_ = bf16[128,1024]{1,0:T(8,128)(2,1)S(1)} collective-permute-done((bf16[128,1024]{1,0:T(8,128)(2,1)}, bf16[128,1024]{1,0:T(8,128)(2,1)S(1)}, u32[]{:S(2)}, u32[]{:S(2)}) %collective-permute-start.4) | collective-permute-done | bytes 262176 | tf_op jit(solution)/shard_map/ppermute | solution.py:265
  24.5 2.8 %collective-permute-done.5.refs_3_ = bf16[128,1024]{1,0:T(8,128)(2,1)S(1)} collective-permute-done((bf16[128,1024]{1,0:T(8,128)(2,1)}, bf16[128,1024]{1,0:T(8,128)(2,1)S(1)}, u32[]{:S(2)}, u32[]{:S(2)}) %collective-permute-start.5) | collective-permute-done | bytes 262176 | tf_op jit(solution)/shard_map/ppermute | solution.py:265
  27.6 1.4 collective-permute-start.25
  30.2 0.8 copy.13.metat
  31.0 4.2 %route.1 = (bf16[896,512]{1,0:T(8,128)(2,1)}, bf16[512,896]{1,0:T(8,128)(2,1)}) custom-call(s32[3]{0:T(128)} %pad_add_fusion.info, f32[16,512]{1,0:T(8,128)} %get-tuple-element.116.meta, f32[512,16]{1,0:T(8,128)} %copy.13.metat), custom_call_target="tpu_custom_call" | custom-call | bytes 1900556 | tf_op jit(solution)/shard_map/route/pallas_call | solution.py:38
  35.3 3.6 %pack_gates.1 = (bf16[240,1024]{1,0:T(8,128)(2,1)}, bf16[240,1024]{1,0:T(8,128)(2,1)}, bf16[240,1024]{1,0:T(8,128)(2,1)}, bf16[240,1024]{1,0:T(8,128)(2,1)}) custom-call(s32[3]{0:T(128)} %pad_add_fusion.info, f32[16,512]{1,0:T(8,128)} %get-tuple-element.116.meta, bf16[896,512]{1,0:T(8,128)(2,1)} %get-tuple-element.72.sel, bf16[128,1024]{1,0:T(8,128)(2,1)} %refs_0_.1, ...), custom_call_target="tpu_custom_call" | custom-call | flops 939524096 | bytes 3964940 | tf_op jit(solution)/shard_map/pack_gates/pallas_call | solution.py:38
  38.9 1.2 collective-permute-start.6
  40.1 1.2 collective-permute-start.7
  41.5 8.3 %collective-permute-done.24.refs_2_ = bf16[128,1024]{1,0:T(8,128)(2,1)S(1)} collective-permute-done((bf16[128,1024]{1,0:T(8,128)(2,1)}, bf16[128,1024]{1,0:T(8,128)(2,1)S(1)}, u32[]{:S(2)}, u32[]{:S(2)}) %collective-permute-start.24) | collective-permute-done | bytes 262176 | tf_op jit(solution)/shard_map/ppermute | solution.py:265
  49.8 1.1 collective-permute-start.9
  52.1 3.4 %pack.1 = (bf16[224,1024]{1,0:T(8,128)(2,1)}, bf16[224,1024]{1,0:T(8,128)(2,1)}, bf16[224,1024]{1,0:T(8,128)(2,1)}, bf16[224,1024]{1,0:T(8,128)(2,1)}) custom-call(s32[3]{0:T(128)} %pad_add_fusion.info, f32[16,512]{1,0:T(8,128)} %get-tuple-element.116.meta, bf16[896,512]{1,0:T(8,128)(2,1)} %get-tuple-element.72.sel, bf16[128,1024]{1,0:T(8,128)(2,1)} %refs_0_.2, ...), custom_call_target="tpu_custom_call" | custom-call | flops 939524096 | bytes 3833868 | tf_op jit(solution)/shard_map/pack/pallas_call | solution.py:38
  55.5 1.2 collective-permute-start.26
  56.7 0.8 collective-permute-start.10
  57.5 4.1 %collective-permute-start.11 = (bf16[240,1024]{1,0:T(8,128)(2,1)S(1)}, bf16[240,1024]{1,0:T(8,128)(2,1)S(1)}, u32[]{:S(2)}, u32[]{:S(2)}) collective-permute-start(bf16[240,1024]{1,0:T(8,128)(2,1)S(1)} %collective-permute-done.7.refs_2_), channel_id=1, source_target_pairs={{0,1},{1,0},{2,3},{3,2},{4,5},{5,4},{6,7},{7,6},{8,9},{9,8},{10,11... | collective-permute-start | bytes 1474568 | tf_op jit(solution)/shard_map/ppermute | solution.py:279
  61.6 5.7 %collective-permute-start.12 = (bf16[240,1024]{1,0:T(8,128)(2,1)S(1)}, bf16[240,1024]{1,0:T(8,128)(2,1)S(1)}, u32[]{:S(2)}, u32[]{:S(2)}) collective-permute-start(bf16[240,1024]{1,0:T(8,128)(2,1)S(1)} %collective-permute-done.8.refs_3_), channel_id=1, source_target_pairs={{0,1},{1,0},{2,3},{3,2},{4,5},{5,4},{6,7},{7,6},{8,9},{9,8},{10,11... | collective-permute-start | bytes 1474568 | tf_op jit(solution)/shard_map/ppermute | solution.py:279
  67.6 2.1 collective-permute-done.26.refs_1_.refs_9_
  69.6 2.1 collective-permute-start.28
  71.8 17.7 %collective-permute-done.27.refs_2_.refs_10_ = bf16[224,1024]{1,0:T(8,128)(2,1)S(1)} collective-permute-done((bf16[224,1024]{1,0:T(8,128)(2,1)}, bf16[224,1024]{1,0:T(8,128)(2,1)S(1)}, u32[]{:S(2)}, u32[]{:S(2)}) %collective-permute-start.27) | collective-permute-done | bytes 458784 | tf_op jit(solution)/shard_map/ppermute | solution.py:274
  89.5 0.8 collective-permute-start.29
  91.7 0.8 copy-done.24
  92.4 17.7 %expert_forward.1 = (bf16[224,1024]{1,0:T(8,128)(2,1)}, bf16[224,1024]{1,0:T(8,128)(2,1)}, bf16[224,1024]{1,0:T(8,128)(2,1)}, bf16[224,1024]{1,0:T(8,128)(2,1)},...) custom-call(s32[3]{0:T(128)} %pad_add_fusion.info, ...), custom_call_target="tpu_custom_call" | custom-call | flops 7751073792 | bytes 21299212 | tf_op jit(solution)/shard_map/expert_forward/pallas_call | solution.py:38
  112.0 17.7 %expert_backward.1 = (bf16[240,1024]{1,0:T(8,128)(2,1)}, bf16[240,1024]{1,0:T(8,128)(2,1)}, bf16[240,1024]{1,0:T(8,128)(2,1)}, bf16[240,1024]{1,0:T(8,128)(2,1)}...) custom-call(s32[3]{0:T(128)} %pad_add_fusion.info, ...), custom_call_target="tpu_custom_call" | custom-call | flops 7751073792 | bytes 22560780 | tf_op jit(solution)/shard_map/expert_backward/pallas_call | solution.py:38
  131.8 0.8 collective-permute-done.34
  132.7 1.2 collective-permute-start.15
  134.6 1.3 collective-permute-start.19
  136.2 1.2 collective-permute-start.35
  137.5 7.1 %collective-permute-done.15.refs_1_ = bf16[224,1024]{1,0:T(8,128)(2,1)S(1)} collective-permute-done((bf16[224,1024]{1,0:T(8,128)(2,1)S(1)}, bf16[224,1024]{1,0:T(8,128)(2,1)S(1)}, u32[]{:S(2)}, u32[]{:S(2)}) %collective-permute-start.15) | collective-permute-done | bytes 458784 | tf_op jit(solution)/shard_map/ppermute | solution.py:274
  144.8 10.6 %collective-permute-done.17.refs_2_ = bf16[224,1024]{1,0:T(8,128)(2,1)S(1)} collective-permute-done((bf16[224,1024]{1,0:T(8,128)(2,1)S(1)}, bf16[224,1024]{1,0:T(8,128)(2,1)S(1)}, u32[]{:S(2)}, u32[]{:S(2)}) %collective-permute-start.17) | collective-permute-done | bytes 458784 | tf_op jit(solution)/shard_map/ppermute | solution.py:274
  155.5 0.9 add_convert_fusion.7.refs_0_
  156.4 0.8 copy-done.13
  157.2 4.0 %combine.1 = (bf16[128,1024]{1,0:T(8,128)(2,1)}, bf16[128,1024]{1,0:T(8,128)(2,1)}, bf16[128,1024]{1,0:T(8,128)(2,1)}, bf16[128,1024]{1,0:T(8,128)(2,1)}) custom-call(s32[3]{0:T(128)} %pad_add_fusion.info, f32[16,512]{1,0:T(8,128)} %get-tuple-element.116.meta, bf16[896,512]{1,0:T(8,128)(2,1)} %get-tuple-element.72.sel, ...), custom_call_target="tpu_custom_call" | custom-call | flops 939524096 | bytes 4751372 | tf_op jit(solution)/shard_map/combine/pallas_call | solution.py:38
  161.4 1.0 add_convert_fusion.3.refs_0_
  162.3 2.5 %collective-permute-start.21 = (bf16[128,1024]{1,0:T(8,128)(2,1)S(1)}, bf16[128,1024]{1,0:T(8,128)(2,1)S(1)}, u32[]{:S(2)}, u32[]{:S(2)}) collective-permute-start(bf16[128,1024]{1,0:T(8,128)(2,1)S(1)} %copy-done.38), channel_id=1, source_target_pairs={{0,16},{2,18},{4,20},{6,22},{8,24},{10,26},{12,28},{14,30},{16,0},... | collective-permute-start | bytes 786440 | tf_op jit(solution)/shard_map/ppermute | solution.py:265
  165.4 11.2 %collective-permute-done.37.refs_2_ = bf16[240,1024]{1,0:T(8,128)(2,1)S(1)} collective-permute-done((bf16[240,1024]{1,0:T(8,128)(2,1)S(1)}, bf16[240,1024]{1,0:T(8,128)(2,1)S(1)}, u32[]{:S(2)}, u32[]{:S(2)}) %collective-permute-start.37) | collective-permute-done | bytes 491552 | tf_op jit(solution)/shard_map/ppermute | solution.py:274
  177.4 0.8 copy-done.6
  178.2 4.5 %combine_gates.1 = (bf16[144,1024]{1,0:T(8,128)(2,1)}, bf16[144,1024]{1,0:T(8,128)(2,1)}, bf16[144,1024]{1,0:T(8,128)(2,1)}, bf16[144,1024]{1,0:T(8,128)(2,1)}) custom-call(s32[3]{0:T(128)} %pad_add_fusion.info, f32[16,512]{1,0:T(8,128)} %get-tuple-element.116.meta, bf16[896,512]{1,0:T(8,128)(2,1)} %get-tuple-element.72.sel, ...), custom_call_target="tpu_custom_call" | custom-call | flops 939524096 | bytes 5013516 | tf_op jit(solution)/shard_map/combine_gates/pallas_call | solution.py:38
  182.7 2.5 %collective-permute-start.41 = (bf16[144,1024]{1,0:T(8,128)(2,1)}, bf16[144,1024]{1,0:T(8,128)(2,1)S(1)}, u32[]{:S(2)}, u32[]{:S(2)}) collective-permute-start(bf16[144,1024]{1,0:T(8,128)(2,1)} %get-tuple-element.108), channel_id=1, source_target_pairs={{0,16},{2,18},{4,20},{6,22},{8,24},{10,26},{12,28},{14,30},{16,0},... | collective-permute-start | bytes 884744 | tf_op jit(solution)/shard_map/ppermute | solution.py:265
  185.2 14.7 %expert_weights.1 = (bf16[1,2,704,2048]{3,2,1,0:T(8,128)(2,1)}, bf16[1,704,2048]{2,1,0:T(8,128)(2,1)}) custom-call(s32[3]{0:T(128)} %pad_add_fusion.info, bf16[240,1024]{1,0:T(8,128)(2,1)} %get-tuple-element.74.refs_0_, bf16[240,1024]{1,0:T(8,128)(2,1)} %copy-done.18, bf16[240,1024]{1,0:T(8,128)(2,1)} %copy-done.19, bf16[240,1024]{1,0:T(8,128)(2,1)} %copy-done.20, ...), custom_call_target="tpu_custom_call" | custom-call | flops 7751073792 | bytes 20037644 | tf_op jit(solution)/shard_map/expert_weights/pallas_call | solution.py:38
  200.0 0.9 subtract_convert_fusion
  201.0 7.9 %collective-permute-done.41 = bf16[144,1024]{1,0:T(8,128)(2,1)S(1)} collective-permute-done((bf16[144,1024]{1,0:T(8,128)(2,1)}, bf16[144,1024]{1,0:T(8,128)(2,1)S(1)}, u32[]{:S(2)}, u32[]{:S(2)}) %collective-permute-start.41) | collective-permute-done | bytes 294944 | tf_op jit(solution)/shard_map/ppermute | solution.py:265
  208.9 4.1 %collective-permute-done.40 = bf16[144,1024]{1,0:T(8,128)(2,1)S(1)} collective-permute-done((bf16[144,1024]{1,0:T(8,128)(2,1)}, bf16[144,1024]{1,0:T(8,128)(2,1)S(1)}, u32[]{:S(2)}, u32[]{:S(2)}) %collective-permute-start.40) | collective-permute-done | bytes 294944 | tf_op jit(solution)/shard_map/ppermute | solution.py:265
  213.5 0.9 add_convert_fusion.8
  (148 shorter events, 13.4 us)
Async XLA Ops:
  0.6 7.4 %collective-permute-start.3 = (bf16[128,1024]{1,0:T(8,128)(2,1)}, bf16[128,1024]{1,0:T(8,128)(2,1)S(1)}, u32[]{:S(2)}, u32[]{:S(2)}) collective-permute-start(bf16[128,1024]{1,0:T(8,128)(2,1)} %refs_0_.1), channel_id=1, source_target_pairs={{0,8},{2,10},{4,12},{6,14},{8,16},{10,18},{12,20},{14,22},{16,24},... | collective-permute-start | bytes 786440 | tf_op jit(solution)/shard_map/ppermute | solution.py:265
  2.0 22.5 %collective-permute-start.4 = (bf16[128,1024]{1,0:T(8,128)(2,1)}, bf16[128,1024]{1,0:T(8,128)(2,1)S(1)}, u32[]{:S(2)}, u32[]{:S(2)}) collective-permute-start(bf16[128,1024]{1,0:T(8,128)(2,1)} %refs_0_.1), channel_id=1, source_target_pairs={{0,16},{2,18},{4,20},{6,22},{8,24},{10,26},{12,28},{14,30},{16,0},... | collective-permute-start | bytes 786440 | tf_op jit(solution)/shard_map/ppermute | solution.py:265
  3.1 24.2 %collective-permute-start.5 = (bf16[128,1024]{1,0:T(8,128)(2,1)}, bf16[128,1024]{1,0:T(8,128)(2,1)S(1)}, u32[]{:S(2)}, u32[]{:S(2)}) collective-permute-start(bf16[128,1024]{1,0:T(8,128)(2,1)} %refs_0_.1), channel_id=1, source_target_pairs={{0,24},{2,26},{4,28},{6,30},{8,0},{10,2},{12,4},{14,6},{16,8},{18,... | collective-permute-start | bytes 786440 | tf_op jit(solution)/shard_map/ppermute | solution.py:265
  5.8 21.8 %collective-permute-start.2 = (f32[16,128]{1,0:T(8,128)S(1)}, f32[16,128]{1,0:T(8,128)S(1)}, u32[]{:S(2)}, u32[]{:S(2)}) collective-permute-start(f32[16,128]{1,0:T(8,128)S(1)} %pad_maximum_fusion.1), channel_id=1, source_target_pairs={{0,24},{2,26},{4,28},{6,30},{8,0},{10,2},{12,4},{14,6},{16,8},{18,... | collective-permute-start | bytes 24584 | tf_op jit(solution)/shard_map/ppermute | solution.py:265
  6.9 22.7 %collective-permute-start.1 = (f32[16,128]{1,0:T(8,128)S(1)}, f32[16,128]{1,0:T(8,128)S(1)}, u32[]{:S(2)}, u32[]{:S(2)}) collective-permute-start(f32[16,128]{1,0:T(8,128)S(1)} %pad_maximum_fusion.1), channel_id=1, source_target_pairs={{0,16},{2,18},{4,20},{6,22},{8,24},{10,26},{12,28},{14,30},{16,0},... | collective-permute-start | bytes 24584 | tf_op jit(solution)/shard_map/ppermute | solution.py:265
  8.1 27.2 %copy-start.34 = (bf16[128,1024]{1,0:T(8,128)(2,1)}, bf16[128,1024]{1,0:T(8,128)(2,1)S(1)}, u32[]{:S(2)}) copy-start(bf16[128,1024]{1,0:T(8,128)(2,1)S(1)} %collective-permute-done.3.refs_1_) | copy-start | bytes 786436
  8.1 21.5 %collective-permute-start = (f32[16,128]{1,0:T(8,128)S(1)}, f32[16,128]{1,0:T(8,128)S(1)}, u32[]{:S(2)}, u32[]{:S(2)}) collective-permute-start(f32[16,128]{1,0:T(8,128)S(1)} %pad_maximum_fusion.1), channel_id=1, source_target_pairs={{0,8},{2,10},{4,12},{6,14},{8,16},{10,18},{12,20},{14,22},{16,24},... | collective-permute-start | bytes 24584 | tf_op jit(solution)/shard_map/ppermute | solution.py:265
  27.3 14.1 %collective-permute-start.23 = (bf16[128,1024]{1,0:T(8,128)(2,1)}, bf16[128,1024]{1,0:T(8,128)(2,1)S(1)}, u32[]{:S(2)}, u32[]{:S(2)}) collective-permute-start(bf16[128,1024]{1,0:T(8,128)(2,1)} %refs_0_.2), channel_id=1, source_target_pairs={{0,8},{2,10},{4,12},{6,14},{8,16},{10,18},{12,20},{14,22},{16,24},... | collective-permute-start | bytes 786440 | tf_op jit(solution)/shard_map/ppermute | solution.py:265
  27.3 22.6 %collective-permute-start.24 = (bf16[128,1024]{1,0:T(8,128)(2,1)}, bf16[128,1024]{1,0:T(8,128)(2,1)S(1)}, u32[]{:S(2)}, u32[]{:S(2)}) collective-permute-start(bf16[128,1024]{1,0:T(8,128)(2,1)} %refs_0_.2), channel_id=1, source_target_pairs={{0,16},{2,18},{4,20},{6,22},{8,24},{10,26},{12,28},{14,30},{16,0},... | collective-permute-start | bytes 786440 | tf_op jit(solution)/shard_map/ppermute | solution.py:265
  27.6 23.8 %collective-permute-start.25 = (bf16[128,1024]{1,0:T(8,128)(2,1)}, bf16[128,1024]{1,0:T(8,128)(2,1)S(1)}, u32[]{:S(2)}, u32[]{:S(2)}) collective-permute-start(bf16[128,1024]{1,0:T(8,128)(2,1)} %refs_0_.2), channel_id=1, source_target_pairs={{0,24},{2,26},{4,28},{6,30},{8,0},{10,2},{12,4},{14,6},{16,8},{18,... | collective-permute-start | bytes 786440 | tf_op jit(solution)/shard_map/ppermute | solution.py:265
  38.9 17.9 %collective-permute-start.6 = (bf16[240,1024]{1,0:T(8,128)(2,1)}, bf16[240,1024]{1,0:T(8,128)(2,1)S(1)}, u32[]{:S(2)}, u32[]{:S(2)}) collective-permute-start(bf16[240,1024]{1,0:T(8,128)(2,1)} %get-tuple-element.75), channel_id=1, source_target_pairs={{0,2},{2,0},{4,6},{6,4},{8,10},{10,8},{12,14},{14,12},{16,18},{18,... | collective-permute-start | bytes 1474568 | tf_op jit(solution)/shard_map/ppermute | solution.py:274
  40.1 17.4 %collective-permute-start.7 = (bf16[240,1024]{1,0:T(8,128)(2,1)}, bf16[240,1024]{1,0:T(8,128)(2,1)S(1)}, u32[]{:S(2)}, u32[]{:S(2)}) collective-permute-start(bf16[240,1024]{1,0:T(8,128)(2,1)} %get-tuple-element.76), channel_id=1, source_target_pairs={{0,4},{2,6},{4,0},{6,2},{8,12},{10,14},{12,8},{14,10},{16,20},{18,... | collective-permute-start | bytes 1474568 | tf_op jit(solution)/shard_map/ppermute | solution.py:274
  41.3 20.3 %collective-permute-start.8 = (bf16[240,1024]{1,0:T(8,128)(2,1)}, bf16[240,1024]{1,0:T(8,128)(2,1)S(1)}, u32[]{:S(2)}, u32[]{:S(2)}) collective-permute-start(bf16[240,1024]{1,0:T(8,128)(2,1)} %get-tuple-element.77), channel_id=1, source_target_pairs={{0,6},{2,4},{4,2},{6,0},{8,14},{10,12},{12,10},{14,8},{16,22},{18,... | collective-permute-start | bytes 1474568 | tf_op jit(solution)/shard_map/ppermute | solution.py:274
  49.8 17.5 %collective-permute-start.9 = (bf16[240,1024]{1,0:T(8,128)(2,1)}, bf16[240,1024]{1,0:T(8,128)(2,1)S(1)}, u32[]{:S(2)}, u32[]{:S(2)}) collective-permute-start(bf16[240,1024]{1,0:T(8,128)(2,1)} %get-tuple-element.74.refs_0_), channel_id=1, source_target_pairs={{0,1},{1,0},{2,3},{3,2},{4,5},{5,4},{6,7},{7,6},{8,9},{9,8},{10,11... | collective-permute-start | bytes 1474568 | tf_op jit(solution)/shard_map/ppermute | solution.py:279
  55.5 14.1 %collective-permute-start.26 = (bf16[224,1024]{1,0:T(8,128)(2,1)}, bf16[224,1024]{1,0:T(8,128)(2,1)S(1)}, u32[]{:S(2)}, u32[]{:S(2)}) collective-permute-start(bf16[224,1024]{1,0:T(8,128)(2,1)} %get-tuple-element.92), channel_id=1, source_target_pairs={{0,2},{2,0},{4,6},{6,4},{8,10},{10,8},{12,14},{14,12},{16,18},{18,... | collective-permute-start | bytes 1376264 | tf_op jit(solution)/shard_map/ppermute | solution.py:274
  56.7 34.2 %copy-start.18 = (bf16[240,1024]{1,0:T(8,128)(2,1)}, bf16[240,1024]{1,0:T(8,128)(2,1)S(1)}, u32[]{:S(2)}) copy-start(bf16[240,1024]{1,0:T(8,128)(2,1)S(1)} %collective-permute-done.6.refs_1_) | copy-start | bytes 1474564
  56.7 33.7 %collective-permute-start.10 = (bf16[240,1024]{1,0:T(8,128)(2,1)S(1)}, bf16[240,1024]{1,0:T(8,128)(2,1)S(1)}, u32[]{:S(2)}, u32[]{:S(2)}) collective-permute-start(bf16[240,1024]{1,0:T(8,128)(2,1)S(1)} %collective-permute-done.6.refs_1_), channel_id=1, source_target_pairs={{0,1},{1,0},{2,3},{3,2},{4,5},{5,4},{6,7},{7,6},{8,9},{9,8},{10,11... | collective-permute-start | bytes 1474568 | tf_op jit(solution)/shard_map/ppermute | solution.py:279
  57.5 33.4 %copy-start.19 = (bf16[240,1024]{1,0:T(8,128)(2,1)}, bf16[240,1024]{1,0:T(8,128)(2,1)S(1)}, u32[]{:S(2)}) copy-start(bf16[240,1024]{1,0:T(8,128)(2,1)S(1)} %collective-permute-done.7.refs_2_) | copy-start | bytes 1474564
  57.5 33.3 %collective-permute-start.11 = (bf16[240,1024]{1,0:T(8,128)(2,1)S(1)}, bf16[240,1024]{1,0:T(8,128)(2,1)S(1)}, u32[]{:S(2)}, u32[]{:S(2)}) collective-permute-start(bf16[240,1024]{1,0:T(8,128)(2,1)S(1)} %collective-permute-done.7.refs_2_), channel_id=1, source_target_pairs={{0,1},{1,0},{2,3},{3,2},{4,5},{5,4},{6,7},{7,6},{8,9},{9,8},{10,11... | collective-permute-start | bytes 1474568 | tf_op jit(solution)/shard_map/ppermute | solution.py:279
  61.6 29.4 %copy-start.20 = (bf16[240,1024]{1,0:T(8,128)(2,1)}, bf16[240,1024]{1,0:T(8,128)(2,1)S(1)}, u32[]{:S(2)}) copy-start(bf16[240,1024]{1,0:T(8,128)(2,1)S(1)} %collective-permute-done.8.refs_3_) | copy-start | bytes 1474564
  61.6 29.3 %collective-permute-start.12 = (bf16[240,1024]{1,0:T(8,128)(2,1)S(1)}, bf16[240,1024]{1,0:T(8,128)(2,1)S(1)}, u32[]{:S(2)}, u32[]{:S(2)}) collective-permute-start(bf16[240,1024]{1,0:T(8,128)(2,1)S(1)} %collective-permute-done.8.refs_3_), channel_id=1, source_target_pairs={{0,1},{1,0},{2,3},{3,2},{4,5},{5,4},{6,7},{7,6},{8,9},{9,8},{10,11... | collective-permute-start | bytes 1474568 | tf_op jit(solution)/shard_map/ppermute | solution.py:279
  67.3 22.1 %collective-permute-start.27 = (bf16[224,1024]{1,0:T(8,128)(2,1)}, bf16[224,1024]{1,0:T(8,128)(2,1)S(1)}, u32[]{:S(2)}, u32[]{:S(2)}) collective-permute-start(bf16[224,1024]{1,0:T(8,128)(2,1)} %get-tuple-element.93), channel_id=1, source_target_pairs={{0,4},{2,6},{4,0},{6,2},{8,12},{10,14},{12,8},{14,10},{16,20},{18,... | collective-permute-start | bytes 1376264 | tf_op jit(solution)/shard_map/ppermute | solution.py:274
  69.6 40.5 %copy-start.27 = (bf16[224,1024]{1,0:T(8,128)(2,1)}, bf16[224,1024]{1,0:T(8,128)(2,1)S(1)}, u32[]{:S(2)}) copy-start(bf16[224,1024]{1,0:T(8,128)(2,1)S(1)} %collective-permute-done.26.refs_1_.refs_9_) | copy-start | bytes 1376260
  69.6 20.7 %collective-permute-start.28 = (bf16[224,1024]{1,0:T(8,128)(2,1)}, bf16[224,1024]{1,0:T(8,128)(2,1)S(1)}, u32[]{:S(2)}, u32[]{:S(2)}) collective-permute-start(bf16[224,1024]{1,0:T(8,128)(2,1)} %get-tuple-element.94), channel_id=1, source_target_pairs={{0,6},{2,4},{4,2},{6,0},{8,14},{10,12},{12,10},{14,8},{16,22},{18,... | collective-permute-start | bytes 1376264 | tf_op jit(solution)/shard_map/ppermute | solution.py:274
  89.5 20.9 %collective-permute-start.29 = (bf16[224,1024]{1,0:T(8,128)(2,1)}, bf16[224,1024]{1,0:T(8,128)(2,1)S(1)}, u32[]{:S(2)}, u32[]{:S(2)}) collective-permute-start(bf16[224,1024]{1,0:T(8,128)(2,1)} %get-tuple-element.91.refs_0_.refs_8_), channel_id=1, source_target_pairs={{0,1},{1,0},{2,3},{3,2},{4,5},{5,4},{6,7},{7,6},{8,9},{9,8},{10,11... | collective-permute-start | bytes 1376264 | tf_op jit(solution)/shard_map/ppermute | solution.py:279
  90.3 20.4 %collective-permute-start.30 = (bf16[224,1024]{1,0:T(8,128)(2,1)S(1)}, bf16[224,1024]{1,0:T(8,128)(2,1)S(1)}, u32[]{:S(2)}, u32[]{:S(2)}) collective-permute-start(bf16[224,1024]{1,0:T(8,128)(2,1)S(1)} %collective-permute-done.26.refs_1_.refs_9_), channel_id=1, source_target_pairs={{0,1},{1,0},{2,3},{3,2},{4,5},{5,4},{6,7},{7,6},{8,9},{9,8},{10,11... | collective-permute-start | bytes 1376264 | tf_op jit(solution)/shard_map/ppermute | solution.py:279
  90.4 20.5 %collective-permute-start.31 = (bf16[224,1024]{1,0:T(8,128)(2,1)S(1)}, bf16[224,1024]{1,0:T(8,128)(2,1)S(1)}, u32[]{:S(2)}, u32[]{:S(2)}) collective-permute-start(bf16[224,1024]{1,0:T(8,128)(2,1)S(1)} %collective-permute-done.27.refs_2_.refs_10_), channel_id=1, source_target_pairs={{0,1},{1,0},{2,3},{3,2},{4,5},{5,4},{6,7},{7,6},{8,9},{9,8},{10,11... | collective-permute-start | bytes 1376264 | tf_op jit(solution)/shard_map/ppermute | solution.py:279
  90.9 20.4 %collective-permute-start.32 = (bf16[224,1024]{1,0:T(8,128)(2,1)S(1)}, bf16[224,1024]{1,0:T(8,128)(2,1)S(1)}, u32[]{:S(2)}, u32[]{:S(2)}) collective-permute-start(bf16[224,1024]{1,0:T(8,128)(2,1)S(1)} %collective-permute-done.28.refs_3_.refs_11_), channel_id=1, source_target_pairs={{0,1},{1,0},{2,3},{3,2},{4,5},{5,4},{6,7},{7,6},{8,9},{9,8},{10,11... | collective-permute-start | bytes 1376264 | tf_op jit(solution)/shard_map/ppermute | solution.py:279
  110.2 26.1 %collective-permute-start.13 = (bf16[224,1024]{1,0:T(8,128)(2,1)}, bf16[224,1024]{1,0:T(8,128)(2,1)S(1)}, u32[]{:S(2)}, u32[]{:S(2)}) collective-permute-start(bf16[224,1024]{1,0:T(8,128)(2,1)} %get-tuple-element.79), channel_id=1, source_target_pairs={{0,1},{1,0},{2,3},{3,2},{4,5},{5,4},{6,7},{7,6},{8,9},{9,8},{10,11... | collective-permute-start | bytes 1376264 | tf_op jit(solution)/shard_map/ppermute | solution.py:279
  110.4 19.7 %collective-permute-start.14 = (bf16[224,1024]{1,0:T(8,128)(2,1)}, bf16[224,1024]{1,0:T(8,128)(2,1)S(1)}, u32[]{:S(2)}, u32[]{:S(2)}) collective-permute-start(bf16[224,1024]{1,0:T(8,128)(2,1)} %get-tuple-element.81), channel_id=1, source_target_pairs={{0,1},{1,0},{2,3},{3,2},{4,5},{5,4},{6,7},{7,6},{8,9},{9,8},{10,11... | collective-permute-start | bytes 1376264 | tf_op jit(solution)/shard_map/ppermute | solution.py:279
  110.7 19.8 %collective-permute-start.16 = (bf16[224,1024]{1,0:T(8,128)(2,1)}, bf16[224,1024]{1,0:T(8,128)(2,1)S(1)}, u32[]{:S(2)}, u32[]{:S(2)}) collective-permute-start(bf16[224,1024]{1,0:T(8,128)(2,1)} %get-tuple-element.83), channel_id=1, source_target_pairs={{0,1},{1,0},{2,3},{3,2},{4,5},{5,4},{6,7},{7,6},{8,9},{9,8},{10,11... | collective-permute-start | bytes 1376264 | tf_op jit(solution)/shard_map/ppermute | solution.py:279
  110.9 20.3 %collective-permute-start.18 = (bf16[224,1024]{1,0:T(8,128)(2,1)}, bf16[224,1024]{1,0:T(8,128)(2,1)S(1)}, u32[]{:S(2)}, u32[]{:S(2)}) collective-permute-start(bf16[224,1024]{1,0:T(8,128)(2,1)} %get-tuple-element.85), channel_id=1, source_target_pairs={{0,1},{1,0},{2,3},{3,2},{4,5},{5,4},{6,7},{7,6},{8,9},{9,8},{10,11... | collective-permute-start | bytes 1376264 | tf_op jit(solution)/shard_map/ppermute | solution.py:279
  129.8 31.5 %collective-permute-start.33 = (bf16[240,1024]{1,0:T(8,128)(2,1)}, bf16[240,1024]{1,0:T(8,128)(2,1)S(1)}, u32[]{:S(2)}, u32[]{:S(2)}) collective-permute-start(bf16[240,1024]{1,0:T(8,128)(2,1)} %get-tuple-element.99), channel_id=1, source_target_pairs={{0,1},{1,0},{2,3},{3,2},{4,5},{5,4},{6,7},{7,6},{8,9},{9,8},{10,11... | collective-permute-start | bytes 1474568 | tf_op jit(solution)/shard_map/ppermute | solution.py:279
  130.1 2.6 %collective-permute-start.34 = (bf16[240,1024]{1,0:T(8,128)(2,1)}, bf16[240,1024]{1,0:T(8,128)(2,1)S(1)}, u32[]{:S(2)}, u32[]{:S(2)}) collective-permute-start(bf16[240,1024]{1,0:T(8,128)(2,1)} %get-tuple-element.101), channel_id=1, source_target_pairs={{0,1},{1,0},{2,3},{3,2},{4,5},{5,4},{6,7},{7,6},{8,9},{9,8},{10,11... | collective-permute-start | bytes 1474568 | tf_op jit(solution)/shard_map/ppermute | solution.py:279
  130.8 3.2 %collective-permute-start.36 = (bf16[240,1024]{1,0:T(8,128)(2,1)S(1)}, bf16[240,1024]{1,0:T(8,128)(2,1)S(1)}, u32[]{:S(2)}, u32[]{:S(2)}) collective-permute-start(bf16[240,1024]{1,0:T(8,128)(2,1)S(1)} %copy-done.26), channel_id=1, source_target_pairs={{0,1},{1,0},{2,3},{3,2},{4,5},{5,4},{6,7},{7,6},{8,9},{9,8},{10,11... | collective-permute-start | bytes 1474568 | tf_op jit(solution)/shard_map/ppermute | solution.py:279
  131.5 3.1 %collective-permute-start.38 = (bf16[240,1024]{1,0:T(8,128)(2,1)S(1)}, bf16[240,1024]{1,0:T(8,128)(2,1)S(1)}, u32[]{:S(2)}, u32[]{:S(2)}) collective-permute-start(bf16[240,1024]{1,0:T(8,128)(2,1)S(1)} %copy-done.25), channel_id=1, source_target_pairs={{0,1},{1,0},{2,3},{3,2},{4,5},{5,4},{6,7},{7,6},{8,9},{9,8},{10,11... | collective-permute-start | bytes 1474568 | tf_op jit(solution)/shard_map/ppermute | solution.py:279
  132.7 12.0 %collective-permute-start.15 = (bf16[224,1024]{1,0:T(8,128)(2,1)S(1)}, bf16[224,1024]{1,0:T(8,128)(2,1)S(1)}, u32[]{:S(2)}, u32[]{:S(2)}) collective-permute-start(bf16[224,1024]{1,0:T(8,128)(2,1)S(1)} %add_convert_fusion.6), channel_id=1, source_target_pairs={{0,2},{2,0},{4,6},{6,4},{8,10},{10,8},{12,14},{14,12},{16,18},{18,... | collective-permute-start | bytes 1376264 | tf_op jit(solution)/shard_map/ppermute | solution.py:274
  134.0 21.5 %collective-permute-start.17 = (bf16[224,1024]{1,0:T(8,128)(2,1)S(1)}, bf16[224,1024]{1,0:T(8,128)(2,1)S(1)}, u32[]{:S(2)}, u32[]{:S(2)}) collective-permute-start(bf16[224,1024]{1,0:T(8,128)(2,1)S(1)} %add_convert_fusion.5), channel_id=1, source_target_pairs={{0,4},{2,6},{4,0},{6,2},{8,12},{10,14},{12,8},{14,10},{16,20},{18,... | collective-permute-start | bytes 1376264 | tf_op jit(solution)/shard_map/ppermute | solution.py:274
  134.6 21.9 %collective-permute-start.19 = (bf16[224,1024]{1,0:T(8,128)(2,1)S(1)}, bf16[224,1024]{1,0:T(8,128)(2,1)S(1)}, u32[]{:S(2)}, u32[]{:S(2)}) collective-permute-start(bf16[224,1024]{1,0:T(8,128)(2,1)S(1)} %add_convert_fusion.4), channel_id=1, source_target_pairs={{0,6},{2,4},{4,2},{6,0},{8,14},{10,12},{12,10},{14,8},{16,22},{18,... | collective-permute-start | bytes 1376264 | tf_op jit(solution)/shard_map/ppermute | solution.py:274
  136.2 28.8 %collective-permute-start.35 = (bf16[240,1024]{1,0:T(8,128)(2,1)S(1)}, bf16[240,1024]{1,0:T(8,128)(2,1)S(1)}, u32[]{:S(2)}, u32[]{:S(2)}) collective-permute-start(bf16[240,1024]{1,0:T(8,128)(2,1)S(1)} %add_convert_fusion.2), channel_id=1, source_target_pairs={{0,2},{2,0},{4,6},{6,4},{8,10},{10,8},{12,14},{14,12},{16,18},{18,... | collective-permute-start | bytes 1474568 | tf_op jit(solution)/shard_map/ppermute | solution.py:274
  144.6 32.0 %collective-permute-start.37 = (bf16[240,1024]{1,0:T(8,128)(2,1)S(1)}, bf16[240,1024]{1,0:T(8,128)(2,1)S(1)}, u32[]{:S(2)}, u32[]{:S(2)}) collective-permute-start(bf16[240,1024]{1,0:T(8,128)(2,1)S(1)} %add_convert_fusion.1), channel_id=1, source_target_pairs={{0,4},{2,6},{4,0},{6,2},{8,12},{10,14},{12,8},{14,10},{16,20},{18,... | collective-permute-start | bytes 1474568 | tf_op jit(solution)/shard_map/ppermute | solution.py:274
  155.5 21.1 %collective-permute-start.39 = (bf16[240,1024]{1,0:T(8,128)(2,1)S(1)}, bf16[240,1024]{1,0:T(8,128)(2,1)S(1)}, u32[]{:S(2)}, u32[]{:S(2)}) collective-permute-start(bf16[240,1024]{1,0:T(8,128)(2,1)S(1)} %add_convert_fusion), channel_id=1, source_target_pairs={{0,6},{2,4},{4,2},{6,0},{8,14},{10,12},{12,10},{14,8},{16,22},{18,... | collective-permute-start | bytes 1474568 | tf_op jit(solution)/shard_map/ppermute | solution.py:274
  161.3 23.9 %collective-permute-start.22 = (bf16[128,1024]{1,0:T(8,128)(2,1)}, bf16[128,1024]{1,0:T(8,128)(2,1)S(1)}, u32[]{:S(2)}, u32[]{:S(2)}) collective-permute-start(bf16[128,1024]{1,0:T(8,128)(2,1)} %get-tuple-element.89), channel_id=1, source_target_pairs={{0,8},{2,10},{4,12},{6,14},{8,16},{10,18},{12,20},{14,22},{16,24},... | collective-permute-start | bytes 786440 | tf_op jit(solution)/shard_map/ppermute | solution.py:265
  162.3 37.7 %collective-permute-start.21 = (bf16[128,1024]{1,0:T(8,128)(2,1)S(1)}, bf16[128,1024]{1,0:T(8,128)(2,1)S(1)}, u32[]{:S(2)}, u32[]{:S(2)}) collective-permute-start(bf16[128,1024]{1,0:T(8,128)(2,1)S(1)} %copy-done.38), channel_id=1, source_target_pairs={{0,16},{2,18},{4,20},{6,22},{8,24},{10,26},{12,28},{14,30},{16,0},... | collective-permute-start | bytes 786440 | tf_op jit(solution)/shard_map/ppermute | solution.py:265
  165.0 35.0 %collective-permute-start.20 = (bf16[128,1024]{1,0:T(8,128)(2,1)S(1)}, bf16[128,1024]{1,0:T(8,128)(2,1)S(1)}, u32[]{:S(2)}, u32[]{:S(2)}) collective-permute-start(bf16[128,1024]{1,0:T(8,128)(2,1)S(1)} %copy-done.37), channel_id=1, source_target_pairs={{0,24},{2,26},{4,28},{6,30},{8,0},{10,2},{12,4},{14,6},{16,8},{18,... | collective-permute-start | bytes 786440 | tf_op jit(solution)/shard_map/ppermute | solution.py:265
  182.7 18.3 %collective-permute-start.42 = (bf16[144,1024]{1,0:T(8,128)(2,1)}, bf16[144,1024]{1,0:T(8,128)(2,1)S(1)}, u32[]{:S(2)}, u32[]{:S(2)}) collective-permute-start(bf16[144,1024]{1,0:T(8,128)(2,1)} %get-tuple-element.109), channel_id=1, source_target_pairs={{0,8},{2,10},{4,12},{6,14},{8,16},{10,18},{12,20},{14,22},{16,24},... | collective-permute-start | bytes 884744 | tf_op jit(solution)/shard_map/ppermute | solution.py:265
  182.7 26.2 %collective-permute-start.41 = (bf16[144,1024]{1,0:T(8,128)(2,1)}, bf16[144,1024]{1,0:T(8,128)(2,1)S(1)}, u32[]{:S(2)}, u32[]{:S(2)}) collective-permute-start(bf16[144,1024]{1,0:T(8,128)(2,1)} %get-tuple-element.108), channel_id=1, source_target_pairs={{0,16},{2,18},{4,20},{6,22},{8,24},{10,26},{12,28},{14,30},{16,0},... | collective-permute-start | bytes 884744 | tf_op jit(solution)/shard_map/ppermute | solution.py:265
  185.2 27.7 %collective-permute-start.40 = (bf16[144,1024]{1,0:T(8,128)(2,1)}, bf16[144,1024]{1,0:T(8,128)(2,1)S(1)}, u32[]{:S(2)}, u32[]{:S(2)}) collective-permute-start(bf16[144,1024]{1,0:T(8,128)(2,1)} %get-tuple-element.107), channel_id=1, source_target_pairs={{0,24},{2,26},{4,28},{6,30},{8,0},{10,2},{12,4},{14,6},{16,8},{18,... | collective-permute-start | bytes 884744 | tf_op jit(solution)/shard_map/ppermute | solution.py:265
  (37 other events, 246.0 us)

commit v2 on v0

v2 whole, which is shorter than its diff:
```python
import functools

import jax
import jax.numpy as jnp
from jax import lax
from jax.experimental import pallas as pl
from jax.experimental.pallas import tpu as pltpu
from jax.sharding import PartitionSpec as P

PLANE = 4
CHUNKS = 2
TAIL = 16
VMEM_LIMIT = 56 * 1024 * 1024
F32 = jnp.float32
BF16 = jnp.bfloat16


def dot_nn(a, b):
    return lax.dot_general(a, b, (((1,), (0,)), ((), ())), preferred_element_type=F32)


def dot_nt(a, b):
    return lax.dot_general(a, b, (((1,), (1,)), ((), ())), preferred_element_type=F32)


def dot_tn(a, b):
    return lax.dot_general(a, b, (((0,), (0,)), ((), ())), preferred_element_type=F32)


def iota(shape, axis):
    return lax.broadcasted_iota(jnp.int32, shape, axis)


SMEM = pl.BlockSpec(memory_space=pltpu.SMEM)
VMEM = pl.BlockSpec(memory_space=pltpu.VMEM)
HBM = pl.BlockSpec(memory_space=pl.ANY)


def call(kernel, outs, args, specs, out_specs=None, scratch=(), flops=0, name=None):
    nbytes = sum(a.size * a.dtype.itemsize for a in (*args, *outs))
    return pl.pallas_call(
        kernel,
        out_shape=outs,
        in_specs=specs,
        out_specs=out_specs if out_specs is not None else [VMEM] * len(outs),
        scratch_shapes=list(scratch),
        compiler_params=pltpu.CompilerParams(vmem_limit_bytes=VMEM_LIMIT),
        cost_estimate=pl.CostEstimate(flops=flops, bytes_accessed=nbytes, transcendentals=0),
        name=name,
    )(*args)


def shape(*dims, dtype=BF16):
    return jax.ShapeDtypeStruct(dims, dtype)


def earlier(tokens):
    return (iota((tokens, tokens), 0) < iota((tokens, tokens), 1)).astype(F32).astype(BF16)


def select_kernel(info, meta, *sels, zn, pn, tokens, picks, cap):
    zc = zn // CHUNKS
    rows = zc * cap
    partner = iota((8, 1), 0)
    experts = jnp.where(partner < pn, info[0] + (partner ^ info[1]), -2).astype(F32)
    before = earlier(tokens)
    slot = iota((rows, tokens), 0).astype(F32)
    for s in range(zn):
        g, local = divmod(s, zc)
        source = lax.rem(info[3] - s + zn, zn) * pn + info[1]
        ids = meta[source]
        named = jnp.zeros((8, tokens), F32)
        for k in range(picks):
            named += (ids[k : k + 1, :] == experts).astype(F32)
        dest = dot_nn(named.astype(BF16), before) + local * cap
        dest = jnp.where(named > 0, dest, -1.0)
        for q in range(pn):
            sels[g][q * rows : (q + 1) * rows, local * tokens : (local + 1) * tokens] = (
                (slot == dest[q : q + 1, :]).astype(F32).astype(BF16)
            )


def route_kernel(info, meta, *refs, zn, pn, tokens, picks, cap):
    zc = zn // CHUNKS
    rows = zc * cap
    ones, gated, (ids_out, gate_out) = refs[:CHUNKS], refs[CHUNKS : 2 * CHUNKS], refs[-2:]
    partner = iota((1, 8), 1)
    experts = jnp.where(partner < pn, info[0] + (partner ^ info[1]), -2).astype(F32)
    after = (iota((tokens, tokens), 1) < iota((tokens, tokens), 0)).astype(F32).astype(BF16)
    before = earlier(tokens)
    eye = (iota((16, 16), 0) == iota((16, 16), 1)).astype(F32).astype(BF16)
    lane = iota((tokens, pn * rows), 1).astype(F32)
    slot = iota((rows, tokens), 0).astype(F32)
    own = (info[0] + info[1]).astype(F32)
    for s in range(zn):
        g, local = divmod(s, zc)
        here = slice(local * tokens, (local + 1) * tokens)
        outer = lax.rem(info[3] - s + zn, zn) * pn
        rowed = meta[outer + info[1]]
        ids_out[:, s * tokens : (s + 1) * tokens] = rowed[0:8, :]
        columned = dot_tn(rowed.astype(BF16), eye)
        named = jnp.zeros((tokens, 8), F32)
        gate = jnp.zeros((tokens, 8), F32)
        for k in range(picks):
            match = (columned[:, k : k + 1] == experts).astype(F32)
            named += match
            gate += match * columned[:, 8 + k : 9 + k]
        dest = dot_nn(after, named.astype(BF16)) + local * cap
        dest = jnp.where(named > 0, dest + rows * partner.astype(F32), -1.0)
        picked = jnp.zeros((tokens, pn * rows), F32)
        weighed = jnp.zeros((tokens, pn * rows), F32)
        for q in range(pn):
            match = lane == dest[:, q : q + 1]
            picked += match.astype(F32)
            weighed += jnp.where(match, gate[:, q : q + 1], 0.0)
        ones[g][here, :] = picked.astype(BF16)
        gated[g][here, :] = weighed.astype(BF16)
    for g in range(CHUNKS):
        for q in range(pn):
            column = jnp.zeros((rows, 1), F32)
            for local in range(zc):
                s = g * zc + local
                outer = lax.rem(info[3] - s + zn, zn) * pn
                rowed = meta[outer + (info[1] ^ q)]
                match = (rowed[0:8, :] == own).astype(F32)
                named = jnp.sum(match[0:picks, :], axis=0, keepdims=True)
                gate = jnp.sum(match[0:picks, :] * rowed[8 : 8 + picks, :], axis=0, keepdims=True)
                many = jnp.broadcast_to(named, (8, tokens)).astype(BF16)
                dest = dot_nn(many, before)[0:1, :] + local * cap
                dest = jnp.where(named > 0, dest, -1.0)
                column += jnp.sum(
                    jnp.where(slot == dest, gate, 0.0), axis=1, keepdims=True
                )
            gate_out[(g * pn + q) * rows : (g * pn + q + 1) * rows, :] = column


def pack_kernel(sel, *refs, zc, pn, tokens, rows):
    sources, outs, whole = refs[:zc], refs[zc : zc + pn], refs[zc + pn]
    for s in range(zc):
        whole[s * tokens : (s + 1) * tokens, :] = sources[s][...]
    for q in range(pn):
        outs[q][...] = dot_nn(sel[q * rows : (q + 1) * rows, :], whole[...]).astype(BF16)


def add_kernel(first, second, *outs, pn, rows, tail):
    for q in range(pn):
        here = slice(q * rows, (q + 1) * rows)
        outs[q][0:rows, :] = (first[here, :].astype(F32) + second[here, :].astype(F32)).astype(BF16)
    if tail:
        here = slice(pn * rows, pn * rows + TAIL)
        total = (first[here, :].astype(F32) + second[here, :].astype(F32)).astype(BF16)
        for q in range(pn):
            outs[q][rows : rows + TAIL, :] = total


def combine_kernel(chosen, *refs, zc, pn, tokens, rows):
    sources, outs, whole = refs[:pn], refs[pn : pn + zc], refs[pn + zc]
    for q in range(pn):
        whole[q * rows : (q + 1) * rows, :] = sources[q][0:rows, :]
    for s in range(zc):
        outs[s][...] = dot_nn(chosen[s * tokens : (s + 1) * tokens, :], whole[...]).astype(BF16)


def combine_far_kernel(info, ids, *refs, zc, pn, tokens, rows):
    sels, chosen, sources = refs[:CHUNKS], refs[CHUNKS], refs[CHUNKS + 1 : CHUNKS + 1 + pn]
    *outs, gate_out, whole = refs[CHUNKS + 1 + pn :]
    for q in range(pn):
        whole[q * rows : (q + 1) * rows, :] = sources[q][0:rows, :]
    gate_out[...] = jnp.zeros(gate_out.shape, BF16)
    for g in range(CHUNKS):
        span = slice(g * zc * tokens, (g + 1) * zc * tokens)
        total = jnp.zeros((8, zc * tokens), F32)
        for q in range(pn):
            expert = (info[0] + (info[1] ^ q)).astype(F32)
            row = g * pn + q
            values = sources[q][rows : rows + TAIL, 0:rows].astype(F32)[row : row + 1, :]
            values = jnp.broadcast_to(values, (8, rows)).astype(BF16)
            spread = dot_nn(values, sels[g][q * rows : (q + 1) * rows, :])
            total += jnp.where(ids[:, span] == expert, spread, 0.0)
        total = jnp.concatenate([total, jnp.zeros((TAIL - 8, zc * tokens), F32)], axis=0)
        gate_out[:, span] = total.astype(BF16)
    for s in range(zc):
        part = dot_nn(chosen[s * tokens : (s + 1) * tokens, :], whole[...]).astype(BF16)
        outs[s][0:tokens, :] = part
        at = (CHUNKS - 1) * zc + s
        outs[s][tokens : tokens + TAIL, :] = jnp.zeros((TAIL, part.shape[1]), BF16)
        outs[s][tokens : tokens + TAIL, 0:tokens] = gate_out[:, at * tokens : (at + 1) * tokens]


def combine_near_kernel(gates, chosen, *refs, zc, pn, tokens, rows, first):
    sources, outs, whole = refs[:pn], refs[pn : pn + zc], refs[pn + zc]
    for q in range(pn):
        whole[q * rows : (q + 1) * rows, :] = sources[q][0:rows, :]
    for s in range(zc):
        part = dot_nn(chosen[s * tokens : (s + 1) * tokens, :], whole[...]).astype(BF16)
        outs[s][0:tokens, :] = part
        at = first + s
        outs[s][tokens : tokens + TAIL, :] = jnp.zeros((TAIL, part.shape[1]), BF16)
        outs[s][tokens : tokens + TAIL, 0:tokens] = gates[:, at * tokens : (at + 1) * tokens]


class Loads:
    def __init__(self, sems):
        self.sems, self.copies, self.waited = sems, {}, set()

    def add(self, key, source, target):
        self.copies[key] = pltpu.make_async_copy(source, target, self.sems.at[len(self.copies)])
        self.copies[key].start()

    def need(self, *keys):
        for key in keys:
            if key not in self.waited:
                self.waited.add(key)
                self.copies[key].wait()

    def finish(self):
        self.need(*self.copies)


def column_block(info, j, nt, cols):
    block = lax.rem(info[2] - j + nt, nt)
    return pl.ds(pl.multiple_of(block * cols, 128), cols)


def forward_kernel(info, *refs, nt, rows, cols):
    n = nt * CHUNKS
    xs, win, wout = refs[:n], refs[n], refs[n + 1]
    outs, hid, a1, a2 = refs[n + 2 : 2 * n + 2], *refs[2 * n + 2 : 2 * n + 5]
    x, wg, wu, wd, stage, in_sems, out_sems = refs[2 * n + 5 :]
    loads, stores = Loads(in_sems), Loads(out_sems)
    for j in range(nt):
        at = column_block(info, j, nt, cols)
        loads.add(("x", 0, j), xs[j], x.at[0, j])
        loads.add(("g", j), win.at[0, 0, :, at], wg.at[j])
        loads.add(("u", j), win.at[0, 1, :, at], wu.at[j])
    for g in range(1, CHUNKS):
        for j in range(nt):
            loads.add(("x", g, j), xs[g * nt + j], x.at[g, j])
    for j in range(nt):
        loads.add(("d", j), wout.at[0, :, column_block(info, j, nt, cols)], wd.at[j])
    for g in range(CHUNKS):
        here = slice(g * rows, (g + 1) * rows)
        loads.need(("x", g, 0), ("g", 0))
        gate = dot_nt(x[g, 0], wg[0])
        loads.need(("u", 0))
        up = dot_nt(x[g, 0], wu[0])
        for j in range(1, nt):
            loads.need(("x", g, j), ("g", j), ("u", j))
            gate += dot_nt(x[g, j], wg[j])
            up += dot_nt(x[g, j], wu[j])
        sigma = jax.nn.sigmoid(gate)
        active = gate * sigma
        hidden = (active * up).astype(BF16)
        hid[here, :] = hidden
        a1[here, :] = (up * sigma * (1.0 + gate * (1.0 - sigma))).astype(BF16)
        a2[here, :] = active.astype(BF16)
        for j in reversed(range(nt)):
            w = (nt - j) % nt
            loads.need(("d", w))
            stage[g, j] = dot_nn(hidden, wd[w]).astype(BF16)
            stores.add((g, j), stage.at[g, j], outs[g * nt + j])
    loads.finish()
    stores.finish()


def backward_kernel(info, *refs, nt, pn, rows, cols):
    n = nt * CHUNKS
    cs, win, wout, hid, a1, a2, gates = refs[:n], *refs[n : n + 6]
    outs, gg, ug, hs = refs[n + 6 : 2 * n + 6], *refs[2 * n + 6 : 2 * n + 9]
    c, h, b1, b2, wg, wu, wd, stage, in_sems, out_sems = refs[2 * n + 9 :]
    loads, stores = Loads(in_sems), Loads(out_sems)
    for j in range(nt):
        at = column_block(info, j, nt, cols)
        loads.add(("c", 0, j), cs[j], c.at[0, j])
        loads.add(("d", j), wout.at[0, :, at], wd.at[j])
    for key, source, target in (("h", hid, h), ("1", a1, b1), ("2", a2, b2)):
        loads.add(key, source, target)
    for j in range(nt):
        at = column_block(info, j, nt, cols)
        loads.add(("g", j), win.at[0, 0, :, at], wg.at[j])
        loads.add(("u", j), win.at[0, 1, :, at], wu.at[j])
    for g in range(1, CHUNKS):
        for j in range(nt):
            loads.add(("c", g, j), cs[g * nt + j], c.at[g, j])
    piece_rows = rows // pn
    same = iota((piece_rows, piece_rows), 0) == iota((piece_rows, piece_rows), 1)
    tail_row = iota((TAIL, piece_rows), 0)
    tail = jnp.zeros((TAIL, piece_rows), F32)
    for g in range(CHUNKS):
        here = slice(g * rows, (g + 1) * rows)
        loads.need(("c", g, 0), ("d", 0))
        grad = dot_nt(c[g, 0], wd[0])
        for j in range(1, nt):
            loads.need(("c", g, j), ("d", j))
            grad += dot_nt(c[g, j], wd[j])
        loads.need("h", "1", "2")
        hidden = h[here, :].astype(F32)
        piece = jnp.sum(grad * hidden, axis=1, keepdims=True)
        for q in range(pn):
            part = piece[q * piece_rows : (q + 1) * piece_rows, :]
            part = jnp.sum(jnp.where(same, part, 0.0), axis=0, keepdims=True)
            tail += jnp.where(tail_row == g * pn + q, part, 0.0)
        gate = gates[here, :]
        grad = gate * grad
        hs[here, :] = (gate * hidden).astype(BF16)
        gate_grad = (grad * b1[here, :].astype(F32)).astype(BF16)
        up_grad = (grad * b2[here, :].astype(F32)).astype(BF16)
        gg[here, :] = gate_grad
        ug[here, :] = up_grad
        for j in reversed(range(nt)):
            w = (nt - j) % nt
            loads.need(("g", w), ("u", w))
            part = dot_nn(gate_grad, wg[w]) + dot_nn(up_grad, wu[w])
            stage[g, j, 0:rows, :] = part.astype(BF16)
            if g == CHUNKS - 1:
                stage[g, j, rows : rows + TAIL, :] = jnp.zeros((TAIL, cols), BF16)
                stage[g, j, rows : rows + TAIL, 0:piece_rows] = tail.astype(BF16)
                stores.add((g, j), stage.at[g, j], outs[g * nt + j])
            else:
                stores.add((g, j), stage.at[g, j, pl.ds(0, rows)], outs[g * nt + j])
    loads.finish()
    stores.finish()


def weights_kernel(info, *refs, nt, rows, cols):
    n = nt * CHUNKS
    xs, cs, lefts = refs[:n], refs[n : 2 * n], refs[2 * n : 2 * n + 3]
    gin, gout, left, right, stage, in_sems, out_sems = refs[2 * n + 3 :]
    loads, stores = Loads(in_sems), Loads(out_sems)
    order = ((0, 0, xs), (1, 0, xs), (2, 1, cs))
    for w, side, sources in order:
        loads.add(("l", w), lefts[w], left.at[w])
        if w == 1:
            continue
        for j in range(nt):
            for g in range(CHUNKS):
                target = right.at[side, j, pl.ds(g * rows, rows)]
                loads.add((side, j, g), sources[g * nt + j], target)
    for w, side, _ in order:
        loads.need(("l", w))
        for j in range(nt):
            loads.need(*((side, j, g) for g in range(CHUNKS)))
            at = column_block(info, j, nt, cols)
            stage[j, w] = dot_tn(left[w], right[side, j]).astype(BF16)
            target = gout.at[0, :, at] if w == 2 else gin.at[0, w, :, at]
            stores.add((j, w), stage.at[j, w], target)
    loads.finish()
    stores.finish()


def body(
    first_half,
    second_half,
    first_grad,
    second_grad,
    expert_ids,
    gate_weights,
    expert_in,
    expert_out,
):
    tokens, picks = expert_ids.shape
    groups = lax.axis_size("expert")
    nt = lax.axis_size("tensor")
    pn = PLANE
    zn = groups // pn
    zc = zn // CHUNKS
    cap = tokens * picks * 7 // (6 * groups)
    rows = zc * cap
    chunk = pn * rows
    slots = CHUNKS * chunk
    cols = first_half.shape[1]
    hid_n = expert_out.shape[1]
    width = expert_out.shape[2]
    me = lax.axis_index("expert")
    info = jnp.stack([(me // pn) * pn, me % pn, lax.axis_index("tensor"), me // pn]).astype(jnp.int32)

    def outer_send(value, s):
        if s % zn == 0:
            return value
        return lax.ppermute(
            value, "expert", [(e, ((e // pn + s) % zn) * pn + e % pn) for e in range(groups)]
        )

    def inner_send(value, q):
        if q == 0:
            return value
        return lax.ppermute(value, "expert", [(e, e ^ q) for e in range(groups)])

    def tensor_send(value, j):
        if j == 0:
            return value
        return lax.ppermute(value, "tensor", [(c, (c + j) % nt) for c in range(nt)])

    fixed = dict(zn=zn, pn=pn, tokens=tokens, picks=picks, cap=cap)
    near = dict(zc=zc, pn=pn, tokens=tokens, rows=rows)

    own = jnp.concatenate(
        [
            jnp.pad(expert_ids.T.astype(F32), ((0, 8 - picks), (0, 0)), constant_values=-1.0),
            jnp.pad(gate_weights.T.astype(F32), ((0, 8 - picks), (0, 0))),
        ],
        axis=0,
    )
    x_parts = [outer_send(first_half, s) for s in range(zn)]
    meta = lax.all_gather(own, "expert")
    sels = call(
        functools.partial(select_kernel, **fixed),
        [shape(chunk, zc * tokens)] * CHUNKS,
        [info, meta],
        [SMEM, VMEM],
        name="select",
    )
    routed = call(
        functools.partial(route_kernel, **fixed),
        [shape(zc * tokens, chunk)] * (2 * CHUNKS)
        + [shape(8, zn * tokens, dtype=F32), shape(slots, 1, dtype=F32)],
        [info, meta],
        [SMEM, VMEM],
        name="route",
    )
    ones, gated, (ids, gates) = routed[:CHUNKS], routed[CHUNKS : 2 * CHUNKS], routed[-2:]

    def dispatch(parts):
        arrays = []
        for g in range(CHUNKS):
            pieces = call(
                functools.partial(pack_kernel, **near),
                [shape(rows, cols)] * pn,
                [sels[g], *parts[g * zc : (g + 1) * zc]],
                [VMEM] * (1 + zc),
                scratch=[pltpu.VMEM((zc * tokens, cols), BF16)],
                flops=2 * chunk * zc * tokens * cols,
                name="pack",
            )
            mine = jnp.concatenate([inner_send(piece, q) for q, piece in enumerate(pieces)], axis=0)
            arrays += [tensor_send(mine, j) for j in range(nt)]
        return arrays

    def collect(g, arrays, tail):
        height = rows + TAIL if tail else rows
        total = arrays[0]
        for j in range(1, nt):
            pieces = call(
                functools.partial(add_kernel, pn=pn, rows=rows, tail=tail),
                [shape(height, cols)] * pn,
                [total, tensor_send(arrays[j], j)],
                [VMEM] * 2,
                name="add",
            )
            if j < nt - 1:
                total = jnp.concatenate(
                    [piece[:rows] for piece in pieces] + ([pieces[0][rows:]] if tail else []), axis=0
                )
        return [inner_send(piece, q) for q, piece in enumerate(pieces)]

    def combine(g, pieces):
        parts = call(
            functools.partial(combine_kernel, **near),
            [shape(tokens, cols)] * zc,
            [gated[g], *pieces],
            [VMEM] * (1 + pn),
            scratch=[pltpu.VMEM((chunk, cols), BF16)],
            flops=2 * chunk * zc * tokens * cols,
            name="combine",
        )
        return [outer_send(part, -(g * zc + s)) for s, part in enumerate(parts)]

    work = 2 * slots * hid_n * width
    weights = [pltpu.VMEM((nt, hid_n, cols), BF16)] * 3
    last = CHUNKS - 1

    xs = dispatch(x_parts)
    grad_whole, *_ = lax.optimization_barrier((second_grad, *x_parts[1:]))
    cs = dispatch([outer_send(grad_whole, s) for s in range(zn)])

    forward = call(
        functools.partial(forward_kernel, nt=nt, rows=chunk, cols=cols),
        [shape(chunk, cols)] * (nt * CHUNKS) + [shape(slots, hid_n)] * 3,
        [info, *xs, expert_in, expert_out],
        [SMEM] + [HBM] * (nt * CHUNKS + 2),
        out_specs=[HBM] * (nt * CHUNKS) + [VMEM] * 3,
        scratch=[pltpu.VMEM((CHUNKS, nt, chunk, cols), BF16)]
        + weights
        + [
            pltpu.VMEM((CHUNKS, nt, chunk, cols), BF16),
            pltpu.SemaphoreType.DMA((3 * nt + CHUNKS * nt,)),
            pltpu.SemaphoreType.DMA((CHUNKS * nt,)),
        ],
        flops=3 * work,
        name="expert_forward",
    )
    outs, (hid, a1, a2) = forward[: nt * CHUNKS], forward[nt * CHUNKS :]
    out_parts = {}
    for g in reversed(range(CHUNKS)):
        out_parts[g] = combine(g, collect(g, outs[g * nt : (g + 1) * nt], False))

    backward = call(
        functools.partial(backward_kernel, nt=nt, pn=pn, rows=chunk, cols=cols),
        [
            shape(chunk + (TAIL if g == last else 0), cols)
            for g in range(CHUNKS)
            for _ in range(nt)
        ]
        + [shape(slots, hid_n)] * 3,
        [info, *cs, expert_in, expert_out, hid, a1, a2, gates],
        [SMEM] + [HBM] * (nt * CHUNKS + 5) + [VMEM],
        out_specs=[HBM] * (nt * CHUNKS) + [VMEM] * 3,
        scratch=[pltpu.VMEM((CHUNKS, nt, chunk, cols), BF16)]
        + [pltpu.VMEM((slots, hid_n), BF16)] * 3
        + weights
        + [
            pltpu.VMEM((CHUNKS, nt, chunk + TAIL, cols), BF16),
            pltpu.SemaphoreType.DMA((3 * nt + CHUNKS * nt + 3,)),
            pltpu.SemaphoreType.DMA((CHUNKS * nt,)),
        ],
        flops=3 * work,
        name="expert_backward",
    )
    grads, (gg, ug, hs) = backward[: nt * CHUNKS], backward[nt * CHUNKS :]
    grad_parts = {}
    pieces = collect(last, grads[last * nt :], True)
    *parts, gate_parts = call(
        functools.partial(combine_far_kernel, **near),
        [shape(tokens + TAIL, cols)] * zc + [shape(TAIL, zn * tokens)],
        [info, ids, *sels, ones[last], *pieces],
        [SMEM] + [VMEM] * (2 + CHUNKS + pn),
        scratch=[pltpu.VMEM((chunk, cols), BF16)],
        flops=2 * chunk * zc * tokens * cols,
        name="combine_far",
    )
    grad_parts[last] = [outer_send(part, -(last * zc + s)) for s, part in enumerate(parts)]
    for g in reversed(range(last)):
        parts = call(
            functools.partial(combine_near_kernel, **near, first=g * zc),
            [shape(tokens + TAIL, cols)] * zc,
            [gate_parts, ones[g], *collect(g, grads[g * nt : (g + 1) * nt], False)],
            [VMEM] * (2 + pn),
            scratch=[pltpu.VMEM((chunk, cols), BF16)],
            flops=2 * chunk * zc * tokens * cols,
            name="combine_near",
        )
        grad_parts[g] = [outer_send(part, -(g * zc + s)) for s, part in enumerate(parts)]

    grad_in, grad_out = call(
        functools.partial(weights_kernel, nt=nt, rows=chunk, cols=cols),
        [shape(*expert_in.shape), shape(*expert_out.shape)],
        [info, *xs, *cs, gg, ug, hs],
        [SMEM] + [HBM] * (2 * nt * CHUNKS + 3),
        out_specs=[HBM, HBM],
        scratch=[
            pltpu.VMEM((3, slots, hid_n), BF16),
            pltpu.VMEM((2, nt, slots, cols), BF16),
            pltpu.VMEM((nt, 3, hid_n, cols), BF16),
            pltpu.SemaphoreType.DMA((3 + 2 * nt * CHUNKS,)),
            pltpu.SemaphoreType.DMA((3 * nt,)),
        ],
        flops=3 * work,
        name="expert_weights",
    )

    out_all = [part for g in range(CHUNKS) for part in out_parts[g]]
    grad_all = [part for g in range(CHUNKS) for part in grad_parts[g]]
    branch = sum(part.astype(F32) for part in out_all)
    input_sum = sum(part[:tokens].astype(F32) for part in grad_all)
    gate_sum = sum(part[tokens : tokens + picks, :tokens].astype(F32) for part in grad_all)
    restored = (second_half.astype(F32) - branch).astype(BF16)
    carried_grad = (first_grad.astype(F32) + input_sum).astype(BF16)
    return (restored, carried_grad, gate_sum.T, grad_in, grad_out)


def solution(mesh):
    in_specs = (
        P("expert", "tensor"),
        P("expert", "tensor"),
        P("expert", "tensor"),
        P("expert", "tensor"),
        P("expert", None),
        P("expert", None),
        P("expert", None, "tensor", None),
        P("expert", "tensor", None),
    )
    out_specs = (
        P("expert", "tensor"),
        P("expert", "tensor"),
        P("expert", None),
        P("expert", None, "tensor", None),
        P("expert", "tensor", None),
    )
    return jax.shard_map(body, mesh=mesh, in_specs=in_specs, out_specs=out_specs, check_vma=False)
```

time: 454 us -> 252 us (0.56)
  the two profiles are of different devices: /device:TPU:0 before, /device:TPU:9 now
where the time goes in v2:
time: 252 us; the launch traced here: 251 us
  Pallas kernels  85.9 us (34%)
  starting transfers between devices  61.6 us (24%)
  waiting for transfers between devices  48.5 us (19%)
  blocking collectives  40.8 us (16%)
  local copies, waits for them, and re-layouts  8.63 us (3%)
  other arithmetic  4.4 us (2%)
    pallas_call x17, Pallas kernels, call(): pl.pallas_call(kernel, out_shape=outs, in_specs=specs, out_specs=out_spec...  85.9 us
    all_gather x1, blocking collectives, body(): meta = lax.all_gather(own, 'expert')  40.8 us
    ppermute x24, waiting for transfers between devices, inner_send(): return lax.ppermute(value, 'expert', [(e, e ^ q) for e in range(groups)])  28.8 us
    ppermute x24, starting transfers between devices, inner_send(): return lax.ppermute(value, 'expert', [(e, e ^ q) for e in range(groups)])  26.9 us
    ppermute x8, starting transfers between devices, tensor_send(): return lax.ppermute(value, 'tensor', [(c, (c + j) % nt) for c in range(nt)])  20.2 us
    ppermute x12, waiting for transfers between devices, outer_send(): lax.ppermute(value, 'expert', [(e, (e // pn + s) % zn * pn + e % pn) for...  19.7 us
    ppermute x12, starting transfers between devices, outer_send(): lax.ppermute(value, 'expert', [(e, (e // pn + s) % zn * pn + e % pn) for...  14.5 us
    unnamed x94, local copies, waits for them, and re-layouts  8.56 us
  transfers between devices with their start and end apart: 44, of which 17 were waited for; matrix products, arithmetic and copies ran while one was open for 3% of the time, Pallas kernels for 34%

profile of v2, /device:TPU:9, one launch (start us, length us, event | category | flops | bytes accessed | tf_op | source)
XLA Modules:
  0.0 250.9 jit_solution(16503830757682556474)
XLA Ops:
  5.8 40.8 %all-gather = f32[256,128]{1,0:T(8,128)} all-gather(f32[16,128]{1,0:T(8,128)S(1)} %select_maximum_fusion), channel_id=2, replica_groups=mesh['expert'=16,'tensor'=2] {'expert'}, dimensions={0}, use_global_device_ids=true | all-gather | bytes 139264 | tf_op jit(solution)/shard_map/all_gather | solution.py:405
  47.2 1.9 select.11
  49.1 2.9 %collective-permute-start.22 = (bf16[128,1024]{1,0:T(8,128)(2,1)}, bf16[128,1024]{1,0:T(8,128)(2,1)S(1)}, u32[]{:S(2)}, u32[]{:S(2)}) collective-permute-start(bf16[128,1024]{1,0:T(8,128)(2,1)} %refs_0_.2), channel_id=1, source_target_pairs={{0,8},{2,10},{4,12},{6,14},{8,16},{10,18},{12,20},{14,22},{16,24},... | collective-permute-start | bytes 786440 | tf_op jit(solution)/shard_map/ppermute | solution.py:380
  52.0 1.9 collective-permute-start.27
  53.9 2.3 pack.4
  56.6 2.3 pack.5
  61.2 2.0 collective-permute-start.3
  63.8 5.5 %collective-permute-done.3 = bf16[112,1024]{1,0:T(8,128)(2,1)S(1)} collective-permute-done((bf16[112,1024]{1,0:T(8,128)(2,1)S(1)}, bf16[112,1024]{1,0:T(8,128)(2,1)S(1)}, u32[]{:S(2)}, u32[]{:S(2)}) %collective-permute-start.3) | collective-permute-done | bytes 229408 | tf_op jit(solution)/shard_map/ppermute | solution.py:387
  69.2 1.9 collective-permute-done.7
  71.1 1.6 collective-permute-start.9
  72.7 1.6 collective-permute-done.8
  74.4 11.7 %collective-permute-start.4 = (bf16[448,1024]{1,0:T(8,128)(2,1)S(1)}, bf16[448,1024]{1,0:T(8,128)(2,1)S(1)}, u32[]{:S(2)}, u32[]{:S(2)}) collective-permute-start(bf16[448,1024]{1,0:T(8,128)(2,1)S(1)} %constant_dynamic-update-slice_fusion.refs_0_), channel_id=1, source_target_pairs={{0,1},{1,0},{2,3},{3,2},{4,5},{5,4},{6,7},{7,6},{8,9},{9,8},{10,11... | collective-permute-start | bytes 2752520 | tf_op jit(solution)/shard_map/ppermute | solution.py:392
  86.1 3.3 %collective-permute-start.10 = (bf16[448,1024]{1,0:T(8,128)(2,1)S(1)}, bf16[448,1024]{1,0:T(8,128)(2,1)S(1)}, u32[]{:S(2)}, u32[]{:S(2)}) collective-permute-start(bf16[448,1024]{1,0:T(8,128)(2,1)S(1)} %constant_dynamic-update-slice_fusion.4.refs_2_), channel_id=1, source_target_pairs={{0,1},{1,0},{2,3},{3,2},{4,5},{5,4},{6,7},{7,6},{8,9},{9,8},{10,11... | collective-permute-start | bytes 2752520 | tf_op jit(solution)/shard_map/ppermute | solution.py:392
  90.1 2.3 pack.6
  92.4 1.5 collective-permute-start.23
  95.7 2.3 pack.7
  101.0 3.4 %collective-permute-done.24 = bf16[112,1024]{1,0:T(8,128)(2,1)S(1)} collective-permute-done((bf16[112,1024]{1,0:T(8,128)(2,1)}, bf16[112,1024]{1,0:T(8,128)(2,1)S(1)}, u32[]{:S(2)}, u32[]{:S(2)}) %collective-permute-start.24) | collective-permute-done | bytes 229408 | tf_op jit(solution)/shard_map/ppermute | solution.py:387
  104.3 2.6 %collective-permute-start.30 = (bf16[112,1024]{1,0:T(8,128)(2,1)S(1)}, bf16[112,1024]{1,0:T(8,128)(2,1)S(1)}, u32[]{:S(2)}, u32[]{:S(2)}) collective-permute-start(bf16[112,1024]{1,0:T(8,128)(2,1)S(1)} %copy-done.38), channel_id=1, source_target_pairs={{0,4},{2,6},{4,0},{6,2},{8,12},{10,14},{12,8},{14,10},{16,20},{18,... | collective-permute-start | bytes 688136 | tf_op jit(solution)/shard_map/ppermute | solution.py:387
  107.1 2.6 %collective-permute-done.29 = bf16[112,1024]{1,0:T(8,128)(2,1)S(1)} collective-permute-done((bf16[112,1024]{1,0:T(8,128)(2,1)}, bf16[112,1024]{1,0:T(8,128)(2,1)S(1)}, u32[]{:S(2)}, u32[]{:S(2)}) %collective-permute-start.29) | collective-permute-done | bytes 229408 | tf_op jit(solution)/shard_map/ppermute | solution.py:387
  111.1 4.7 %collective-permute-done.30 = bf16[112,1024]{1,0:T(8,128)(2,1)S(1)} collective-permute-done((bf16[112,1024]{1,0:T(8,128)(2,1)S(1)}, bf16[112,1024]{1,0:T(8,128)(2,1)S(1)}, u32[]{:S(2)}, u32[]{:S(2)}) %collective-permute-start.30) | collective-permute-done | bytes 229408 | tf_op jit(solution)/shard_map/ppermute | solution.py:387
  115.8 2.7 %collective-permute-start.32 = (bf16[448,1024]{1,0:T(8,128)(2,1)S(1)}, bf16[448,1024]{1,0:T(8,128)(2,1)}, u32[]{:S(2)}, u32[]{:S(2)}) collective-permute-start(bf16[448,1024]{1,0:T(8,128)(2,1)S(1)} %constant_dynamic-update-slice_fusion.12.refs_2_.refs_6_), channel_id=1, source_target_pairs={{0,1},{1,0},{2,3},{3,2},{4,5},{5,4},{6,7},{7,6},{8,9},{9,8},{10,11... | collective-permute-start | bytes 2752520 | tf_op jit(solution)/shard_map/ppermute | solution.py:392
  118.5 4.5 %route.1 = (bf16[256,448]{1,0:T(8,128)(2,1)}, bf16[256,448]{1,0:T(8,128)(2,1)}, bf16[256,448]{1,0:T(8,128)(2,1)}, bf16[256,448]{1,0:T(8,128)(2,1)}, f32[8,512]{1,0:T(8,128)}, /*index=5*/f32[896,1]{1,0:T(8,128)}) custom-call(s32[4]{0:T(128)} %pad_add_fusion.info, f32[16,16,128]{2,1,0:T(8,128)} %bitcast.11), custom_call_target="tpu_custom_call" | custom-call | bytes 1068560 | tf_op jit(solution)/shard_map/route/pallas_call | solution.py:41
  125.0 17.1 %expert_forward.1 = (bf16[448,1024]{1,0:T(8,128)(2,1)}, bf16[448,1024]{1,0:T(8,128)(2,1)}, bf16[448,1024]{1,0:T(8,128)(2,1)}, bf16[448,1024]{1,0:T(8,128)(2,1)},...) custom-call(s32[4]{0:T(128)} %pad_add_fusion.info, bf16[448,1024]{1,0:T(8,128)(2,1)} %copy-done.22, ...), custom_call_target="tpu_custom_call" | custom-call | flops 7751073792 | bytes 19775504 | tf_op jit(solution)/shard_map/expert_forward/pallas_call | solution.py:41
  142.7 19.1 %expert_backward.1 = (bf16[448,1024]{1,0:T(8,128)(2,1)}, bf16[448,1024]{1,0:T(8,128)(2,1)}, bf16[464,1024]{1,0:T(8,128)(2,1)}, bf16[464,1024]{1,0:T(8,128)(2,1)}...) custom-call(s32[4]{0:T(128)} %pad_add_fusion.info, bf16[448,1024]{1,0:T(8,128)(2,1)} %copy-done.23, ...), custom_call_target="tpu_custom_call" | custom-call | flops 7751073792 | bytes 23629328 | tf_op jit(solution)/shard_map/expert_backward/pallas_call | solution.py:41
  163.4 2.4 add.71
  165.8 1.4 collective-permute-start.18
  168.5 2.5 add.70
  171.0 2.1 collective-permute-done.17.refs_1_
  173.3 1.5 collective-permute-start.13
  174.8 2.5 %add.72 = (bf16[128,1024]{1,0:T(8,128)(2,1)}, bf16[128,1024]{1,0:T(8,128)(2,1)}, bf16[128,1024]{1,0:T(8,128)(2,1)}, bf16[128,1024]{1,0:T(8,128)(2,1)}) custom-call(bf16[464,1024]{1,0:T(8,128)(2,1)} %get-tuple-element.114.first, bf16[464,1024]{1,0:T(8,128)(2,1)} %copy-done), custom_call_target="tpu_custom_call" | custom-call | bytes 2949120 | tf_op jit(solution)/shard_map/add/pallas_call | solution.py:41
  177.4 1.4 collective-permute-start.34
  179.2 1.4 collective-permute-start.35
  180.5 2.4 collective-permute-done.12.refs_1_
  182.9 1.5 collective-permute-start.14
  185.3 2.5 combine.3
  188.8 2.5 %add.73 = (bf16[112,1024]{1,0:T(8,128)(2,1)}, bf16[112,1024]{1,0:T(8,128)(2,1)}, bf16[112,1024]{1,0:T(8,128)(2,1)}, bf16[112,1024]{1,0:T(8,128)(2,1)}) custom-call(bf16[448,1024]{1,0:T(8,128)(2,1)} %get-tuple-element.122.first, bf16[448,1024]{1,0:T(8,128)(2,1)} %copy-done.1), custom_call_target="tpu_custom_call" | custom-call | bytes 2752512 | tf_op jit(solution)/shard_map/add/pallas_call | solution.py:41
  191.4 3.2 %collective-permute-done.14.refs_3_ = bf16[112,1024]{1,0:T(8,128)(2,1)S(1)} collective-permute-done((bf16[112,1024]{1,0:T(8,128)(2,1)S(1)}, bf16[112,1024]{1,0:T(8,128)(2,1)S(1)}, u32[]{:S(2)}, u32[]{:S(2)}) %collective-permute-start.14) | collective-permute-done | bytes 229408 | tf_op jit(solution)/shard_map/ppermute | solution.py:387
  194.8 6.5 %collective-permute-start.40 = (bf16[112,1024]{1,0:T(8,128)(2,1)}, bf16[112,1024]{1,0:T(8,128)(2,1)S(1)}, u32[]{:S(2)}, u32[]{:S(2)}) collective-permute-start(bf16[112,1024]{1,0:T(8,128)(2,1)} %get-tuple-element.127), channel_id=1, source_target_pairs={{0,6},{2,4},{4,2},{6,0},{8,14},{10,12},{12,10},{14,8},{16,22},{18,... | collective-permute-start | bytes 688136 | tf_op jit(solution)/shard_map/ppermute | solution.py:387
  201.2 2.5 combine.2
  204.4 2.7 %combine_far.1 = (bf16[144,1024]{1,0:T(8,128)(2,1)}, bf16[144,1024]{1,0:T(8,128)(2,1)}, bf16[16,512]{1,0:T(8,128)(2,1)}) custom-call(s32[4]{0:T(128)} %pad_add_fusion.info, f32[8,512]{1,0:T(8,128)} %get-tuple-element.99.ids, bf16[448,256]{1,0:T(8,128)(2,1)} %get-tuple-element.72.sel.refs_0_, bf16[448,256]{1,0:T(8,128)(2,1)} %get-tuple-element.77.sel.refs_1_, ...), custom_call_target="tpu_custom_call" | custom-call | flops 234881024 | bytes 2359312 | tf_op jit(solution)/shard_map/combine_far/pallas_call | solution.py:41
  207.2 1.7 collective-permute-start.15
  210.1 2.1 collective-permute-start.42
  212.2 2.5 %combine_near.1 = (bf16[144,1024]{1,0:T(8,128)(2,1)}, bf16[144,1024]{1,0:T(8,128)(2,1)}) custom-call(bf16[16,512]{1,0:T(8,128)(2,1)} %get-tuple-element.120.gates, bf16[256,448]{1,0:T(8,128)(2,1)} %get-tuple-element.121.chosen, bf16[112,1024]{1,0:T(8,128)(2,1)} %get-tuple-element.124.refs_0_, bf16[112,1024]{1,0:T(8,128)(2,1)} %copy-done.14, ...), custom_call_target="tpu_custom_call" | custom-call | flops 234881024 | bytes 1753088 | tf_op jit(solution)/shard_map/combine_near/pallas_call | solution.py:41
  214.9 13.8 %expert_weights.1 = (bf16[1,2,704,2048]{3,2,1,0:T(8,128)(2,1)}, bf16[1,704,2048]{2,1,0:T(8,128)(2,1)}) custom-call(s32[4]{0:T(128)} %pad_add_fusion.info, bf16[448,1024]{1,0:T(8,128)(2,1)} %copy-done.22, bf16[448,1024]{1,0:T(8,128)(2,1)} %copy-done.24, bf16[448,1024]{1,0:T(8,128)(2,1)} %copy-done.20, bf16[448,1024]{1,0:T(8,128)(2,1)} %copy-done.25, ...), custom_call_target="tpu_custom_call" | custom-call | flops 7751073792 | bytes 19775504 | tf_op jit(solution)/shard_map/expert_weights/pallas_call | solution.py:41
  228.8 7.9 %collective-permute-done.15 = bf16[128,1024]{1,0:T(8,128)(2,1)S(1)} collective-permute-done((bf16[128,1024]{1,0:T(8,128)(2,1)S(1)}, bf16[128,1024]{1,0:T(8,128)(2,1)S(1)}, u32[]{:S(2)}, u32[]{:S(2)}) %collective-permute-start.15) | collective-permute-done | bytes 262176 | tf_op jit(solution)/shard_map/ppermute | solution.py:380
  237.6 1.4 collective-permute-done.43
  239.0 6.3 %collective-permute-done.42 = bf16[144,1024]{1,0:T(8,128)(2,1)S(1)} collective-permute-done((bf16[144,1024]{1,0:T(8,128)(2,1)}, bf16[144,1024]{1,0:T(8,128)(2,1)S(1)}, u32[]{:S(2)}, u32[]{:S(2)}) %collective-permute-start.42) | collective-permute-done | bytes 294944 | tf_op jit(solution)/shard_map/ppermute | solution.py:380
  245.4 4.0 %collective-permute-done.41 = bf16[144,1024]{1,0:T(8,128)(2,1)S(1)} collective-permute-done((bf16[144,1024]{1,0:T(8,128)(2,1)}, bf16[144,1024]{1,0:T(8,128)(2,1)S(1)}, u32[]{:S(2)}, u32[]{:S(2)}) %collective-permute-start.41) | collective-permute-done | bytes 294944 | tf_op jit(solution)/shard_map/ppermute | solution.py:380
  (163 shorter events, 28.7 us)
Async XLA Ops:
  0.6 48.4 %collective-permute-start = (bf16[128,1024]{1,0:T(8,128)(2,1)}, bf16[128,1024]{1,0:T(8,128)(2,1)S(1)}, u32[]{:S(2)}, u32[]{:S(2)}) collective-permute-start(bf16[128,1024]{1,0:T(8,128)(2,1)} %refs_0_.1), channel_id=1, source_target_pairs={{0,8},{2,10},{4,12},{6,14},{8,16},{10,18},{12,20},{14,22},{16,24},... | collective-permute-start | bytes 786440 | tf_op jit(solution)/shard_map/ppermute | solution.py:380
  2.0 47.1 %collective-permute-start.5 = (bf16[128,1024]{1,0:T(8,128)(2,1)}, bf16[128,1024]{1,0:T(8,128)(2,1)S(1)}, u32[]{:S(2)}, u32[]{:S(2)}) collective-permute-start(bf16[128,1024]{1,0:T(8,128)(2,1)} %refs_0_.1), channel_id=1, source_target_pairs={{0,16},{2,18},{4,20},{6,22},{8,24},{10,26},{12,28},{14,30},{16,0},... | collective-permute-start | bytes 786440 | tf_op jit(solution)/shard_map/ppermute | solution.py:380
  3.1 46.0 %collective-permute-start.6 = (bf16[128,1024]{1,0:T(8,128)(2,1)}, bf16[128,1024]{1,0:T(8,128)(2,1)S(1)}, u32[]{:S(2)}, u32[]{:S(2)}) collective-permute-start(bf16[128,1024]{1,0:T(8,128)(2,1)} %refs_0_.1), channel_id=1, source_target_pairs={{0,24},{2,26},{4,28},{6,30},{8,0},{10,2},{12,4},{14,6},{16,8},{18,... | collective-permute-start | bytes 786440 | tf_op jit(solution)/shard_map/ppermute | solution.py:380
  49.1 40.3 %collective-permute-start.22 = (bf16[128,1024]{1,0:T(8,128)(2,1)}, bf16[128,1024]{1,0:T(8,128)(2,1)S(1)}, u32[]{:S(2)}, u32[]{:S(2)}) collective-permute-start(bf16[128,1024]{1,0:T(8,128)(2,1)} %refs_0_.2), channel_id=1, source_target_pairs={{0,8},{2,10},{4,12},{6,14},{8,16},{10,18},{12,20},{14,22},{16,24},... | collective-permute-start | bytes 786440 | tf_op jit(solution)/shard_map/ppermute | solution.py:380
  52.0 41.9 %collective-permute-start.27 = (bf16[128,1024]{1,0:T(8,128)(2,1)}, bf16[128,1024]{1,0:T(8,128)(2,1)S(1)}, u32[]{:S(2)}, u32[]{:S(2)}) collective-permute-start(bf16[128,1024]{1,0:T(8,128)(2,1)} %refs_0_.2), channel_id=1, source_target_pairs={{0,16},{2,18},{4,20},{6,22},{8,24},{10,26},{12,28},{14,30},{16,0},... | collective-permute-start | bytes 786440 | tf_op jit(solution)/shard_map/ppermute | solution.py:380
  53.8 41.1 %collective-permute-start.28 = (bf16[128,1024]{1,0:T(8,128)(2,1)}, bf16[128,1024]{1,0:T(8,128)(2,1)S(1)}, u32[]{:S(2)}, u32[]{:S(2)}) collective-permute-start(bf16[128,1024]{1,0:T(8,128)(2,1)} %refs_0_.2), channel_id=1, source_target_pairs={{0,24},{2,26},{4,28},{6,30},{8,0},{10,2},{12,4},{14,6},{16,8},{18,... | collective-permute-start | bytes 786440 | tf_op jit(solution)/shard_map/ppermute | solution.py:380
  56.2 5.1 %collective-permute-start.1 = (bf16[112,1024]{1,0:T(8,128)(2,1)}, bf16[112,1024]{1,0:T(8,128)(2,1)S(1)}, u32[]{:S(2)}, u32[]{:S(2)}) collective-permute-start(bf16[112,1024]{1,0:T(8,128)(2,1)} %get-tuple-element.74), channel_id=1, source_target_pairs={{0,2},{2,0},{4,6},{6,4},{8,10},{10,8},{12,14},{14,12},{16,18},{18,... | collective-permute-start | bytes 688136 | tf_op jit(solution)/shard_map/ppermute | solution.py:387
  56.6 6.6 %collective-permute-start.2 = (bf16[112,1024]{1,0:T(8,128)(2,1)}, bf16[112,1024]{1,0:T(8,128)(2,1)S(1)}, u32[]{:S(2)}, u32[]{:S(2)}) collective-permute-start(bf16[112,1024]{1,0:T(8,128)(2,1)} %get-tuple-element.75), channel_id=1, source_target_pairs={{0,4},{2,6},{4,0},{6,2},{8,12},{10,14},{12,8},{14,10},{16,20},{18,... | collective-permute-start | bytes 688136 | tf_op jit(solution)/shard_map/ppermute | solution.py:387
  61.2 8.0 %collective-permute-start.3 = (bf16[112,1024]{1,0:T(8,128)(2,1)S(1)}, bf16[112,1024]{1,0:T(8,128)(2,1)S(1)}, u32[]{:S(2)}, u32[]{:S(2)}) collective-permute-start(bf16[112,1024]{1,0:T(8,128)(2,1)S(1)} %copy-done.39), channel_id=1, source_target_pairs={{0,6},{2,4},{4,2},{6,0},{8,14},{10,12},{12,10},{14,8},{16,22},{18,... | collective-permute-start | bytes 688136 | tf_op jit(solution)/shard_map/ppermute | solution.py:387
  63.2 7.9 %collective-permute-start.7 = (bf16[112,1024]{1,0:T(8,128)(2,1)S(1)}, bf16[112,1024]{1,0:T(8,128)(2,1)S(1)}, u32[]{:S(2)}, u32[]{:S(2)}) collective-permute-start(bf16[112,1024]{1,0:T(8,128)(2,1)S(1)} %copy-done.40), channel_id=1, source_target_pairs={{0,2},{2,0},{4,6},{6,4},{8,10},{10,8},{12,14},{14,12},{16,18},{18,... | collective-permute-start | bytes 688136 | tf_op jit(solution)/shard_map/ppermute | solution.py:387
  69.2 5.2 %collective-permute-start.8 = (bf16[112,1024]{1,0:T(8,128)(2,1)S(1)}, bf16[112,1024]{1,0:T(8,128)(2,1)S(1)}, u32[]{:S(2)}, u32[]{:S(2)}) collective-permute-start(bf16[112,1024]{1,0:T(8,128)(2,1)S(1)} %copy-done.37), channel_id=1, source_target_pairs={{0,4},{2,6},{4,0},{6,2},{8,12},{10,14},{12,8},{14,10},{16,20},{18,... | collective-permute-start | bytes 688136 | tf_op jit(solution)/shard_map/ppermute | solution.py:387
  69.2 28.8 %copy-start.22 = (bf16[448,1024]{1,0:T(8,128)(2,1)}, bf16[448,1024]{1,0:T(8,128)(2,1)S(1)}, u32[]{:S(2)}) copy-start(bf16[448,1024]{1,0:T(8,128)(2,1)S(1)} %constant_dynamic-update-slice_fusion.refs_0_) | copy-start | bytes 2752516
  71.1 15.0 %collective-permute-start.9 = (bf16[112,1024]{1,0:T(8,128)(2,1)S(1)}, bf16[112,1024]{1,0:T(8,128)(2,1)S(1)}, u32[]{:S(2)}, u32[]{:S(2)}) collective-permute-start(bf16[112,1024]{1,0:T(8,128)(2,1)S(1)} %copy-done.35), channel_id=1, source_target_pairs={{0,6},{2,4},{4,2},{6,0},{8,14},{10,12},{12,10},{14,8},{16,22},{18,... | collective-permute-start | bytes 688136 | tf_op jit(solution)/shard_map/ppermute | solution.py:387
  74.4 48.7 %collective-permute-start.4 = (bf16[448,1024]{1,0:T(8,128)(2,1)S(1)}, bf16[448,1024]{1,0:T(8,128)(2,1)S(1)}, u32[]{:S(2)}, u32[]{:S(2)}) collective-permute-start(bf16[448,1024]{1,0:T(8,128)(2,1)S(1)} %constant_dynamic-update-slice_fusion.refs_0_), channel_id=1, source_target_pairs={{0,1},{1,0},{2,3},{3,2},{4,5},{5,4},{6,7},{7,6},{8,9},{9,8},{10,11... | collective-permute-start | bytes 2752520 | tf_op jit(solution)/shard_map/ppermute | solution.py:392
  86.1 36.9 %collective-permute-start.10 = (bf16[448,1024]{1,0:T(8,128)(2,1)S(1)}, bf16[448,1024]{1,0:T(8,128)(2,1)S(1)}, u32[]{:S(2)}, u32[]{:S(2)}) collective-permute-start(bf16[448,1024]{1,0:T(8,128)(2,1)S(1)} %constant_dynamic-update-slice_fusion.4.refs_2_), channel_id=1, source_target_pairs={{0,1},{1,0},{2,3},{3,2},{4,5},{5,4},{6,7},{7,6},{8,9},{9,8},{10,11... | collective-permute-start | bytes 2752520 | tf_op jit(solution)/shard_map/ppermute | solution.py:392
  92.4 7.6 %collective-permute-start.23 = (bf16[112,1024]{1,0:T(8,128)(2,1)}, bf16[112,1024]{1,0:T(8,128)(2,1)S(1)}, u32[]{:S(2)}, u32[]{:S(2)}) collective-permute-start(bf16[112,1024]{1,0:T(8,128)(2,1)} %get-tuple-element.103), channel_id=1, source_target_pairs={{0,2},{2,0},{4,6},{6,4},{8,10},{10,8},{12,14},{14,12},{16,18},{18,... | collective-permute-start | bytes 688136 | tf_op jit(solution)/shard_map/ppermute | solution.py:387
  93.9 10.4 %collective-permute-start.24 = (bf16[112,1024]{1,0:T(8,128)(2,1)}, bf16[112,1024]{1,0:T(8,128)(2,1)S(1)}, u32[]{:S(2)}, u32[]{:S(2)}) collective-permute-start(bf16[112,1024]{1,0:T(8,128)(2,1)} %get-tuple-element.104), channel_id=1, source_target_pairs={{0,4},{2,6},{4,0},{6,2},{8,12},{10,14},{12,8},{14,10},{16,20},{18,... | collective-permute-start | bytes 688136 | tf_op jit(solution)/shard_map/ppermute | solution.py:387
  95.0 12.0 %collective-permute-start.25 = (bf16[112,1024]{1,0:T(8,128)(2,1)}, bf16[112,1024]{1,0:T(8,128)(2,1)S(1)}, u32[]{:S(2)}, u32[]{:S(2)}) collective-permute-start(bf16[112,1024]{1,0:T(8,128)(2,1)} %get-tuple-element.105), channel_id=1, source_target_pairs={{0,6},{2,4},{4,2},{6,0},{8,14},{10,12},{12,10},{14,8},{16,22},{18,... | collective-permute-start | bytes 688136 | tf_op jit(solution)/shard_map/ppermute | solution.py:387
  100.0 9.7 %collective-permute-start.29 = (bf16[112,1024]{1,0:T(8,128)(2,1)}, bf16[112,1024]{1,0:T(8,128)(2,1)S(1)}, u32[]{:S(2)}, u32[]{:S(2)}) collective-permute-start(bf16[112,1024]{1,0:T(8,128)(2,1)} %get-tuple-element.107), channel_id=1, source_target_pairs={{0,2},{2,0},{4,6},{6,4},{8,10},{10,8},{12,14},{14,12},{16,18},{18,... | collective-permute-start | bytes 688136 | tf_op jit(solution)/shard_map/ppermute | solution.py:387
  104.3 11.4 %collective-permute-start.30 = (bf16[112,1024]{1,0:T(8,128)(2,1)S(1)}, bf16[112,1024]{1,0:T(8,128)(2,1)S(1)}, u32[]{:S(2)}, u32[]{:S(2)}) collective-permute-start(bf16[112,1024]{1,0:T(8,128)(2,1)S(1)} %copy-done.38), channel_id=1, source_target_pairs={{0,4},{2,6},{4,0},{6,2},{8,12},{10,14},{12,8},{14,10},{16,20},{18,... | collective-permute-start | bytes 688136 | tf_op jit(solution)/shard_map/ppermute | solution.py:387
  107.0 8.8 %collective-permute-start.31 = (bf16[112,1024]{1,0:T(8,128)(2,1)S(1)}, bf16[112,1024]{1,0:T(8,128)(2,1)S(1)}, u32[]{:S(2)}, u32[]{:S(2)}) collective-permute-start(bf16[112,1024]{1,0:T(8,128)(2,1)S(1)} %copy-done.36), channel_id=1, source_target_pairs={{0,6},{2,4},{4,2},{6,0},{8,14},{10,12},{12,10},{14,8},{16,22},{18,... | collective-permute-start | bytes 688136 | tf_op jit(solution)/shard_map/ppermute | solution.py:387
  107.1 35.0 %copy-start.23 = (bf16[448,1024]{1,0:T(8,128)(2,1)}, bf16[448,1024]{1,0:T(8,128)(2,1)S(1)}, u32[]{:S(2)}) copy-start(bf16[448,1024]{1,0:T(8,128)(2,1)S(1)} %constant_dynamic-update-slice_fusion.8.refs_0_.refs_4_) | copy-start | bytes 2752516
  109.7 33.0 %collective-permute-start.26 = (bf16[448,1024]{1,0:T(8,128)(2,1)S(1)}, bf16[448,1024]{1,0:T(8,128)(2,1)}, u32[]{:S(2)}, u32[]{:S(2)}) collective-permute-start(bf16[448,1024]{1,0:T(8,128)(2,1)S(1)} %constant_dynamic-update-slice_fusion.8.refs_0_.refs_4_), channel_id=1, source_target_pairs={{0,1},{1,0},{2,3},{3,2},{4,5},{5,4},{6,7},{7,6},{8,9},{9,8},{10,11... | collective-permute-start | bytes 2752520 | tf_op jit(solution)/shard_map/ppermute | solution.py:392
  115.8 26.3 %copy-start.21 = (bf16[448,1024]{1,0:T(8,128)(2,1)}, bf16[448,1024]{1,0:T(8,128)(2,1)S(1)}, u32[]{:S(2)}) copy-start(bf16[448,1024]{1,0:T(8,128)(2,1)S(1)} %constant_dynamic-update-slice_fusion.12.refs_2_.refs_6_) | copy-start | bytes 2752516
  115.8 26.9 %collective-permute-start.32 = (bf16[448,1024]{1,0:T(8,128)(2,1)S(1)}, bf16[448,1024]{1,0:T(8,128)(2,1)}, u32[]{:S(2)}, u32[]{:S(2)}) collective-permute-start(bf16[448,1024]{1,0:T(8,128)(2,1)S(1)} %constant_dynamic-update-slice_fusion.12.refs_2_.refs_6_), channel_id=1, source_target_pairs={{0,1},{1,0},{2,3},{3,2},{4,5},{5,4},{6,7},{7,6},{8,9},{9,8},{10,11... | collective-permute-start | bytes 2752520 | tf_op jit(solution)/shard_map/ppermute | solution.py:392
  142.1 20.3 %collective-permute-start.16 = (bf16[448,1024]{1,0:T(8,128)(2,1)}, bf16[448,1024]{1,0:T(8,128)(2,1)S(1)}, u32[]{:S(2)}, u32[]{:S(2)}) collective-permute-start(bf16[448,1024]{1,0:T(8,128)(2,1)} %get-tuple-element.92), channel_id=1, source_target_pairs={{0,1},{1,0},{2,3},{3,2},{4,5},{5,4},{6,7},{7,6},{8,9},{9,8},{10,11... | collective-permute-start | bytes 2752520 | tf_op jit(solution)/shard_map/ppermute | solution.py:392
  142.4 24.9 %collective-permute-start.11 = (bf16[448,1024]{1,0:T(8,128)(2,1)}, bf16[448,1024]{1,0:T(8,128)(2,1)S(1)}, u32[]{:S(2)}, u32[]{:S(2)}) collective-permute-start(bf16[448,1024]{1,0:T(8,128)(2,1)} %get-tuple-element.83), channel_id=1, source_target_pairs={{0,1},{1,0},{2,3},{3,2},{4,5},{5,4},{6,7},{7,6},{8,9},{9,8},{10,11... | collective-permute-start | bytes 2752520 | tf_op jit(solution)/shard_map/ppermute | solution.py:392
  161.9 11.4 %collective-permute-start.33 = (bf16[464,1024]{1,0:T(8,128)(2,1)}, bf16[464,1024]{1,0:T(8,128)(2,1)S(1)}, u32[]{:S(2)}, u32[]{:S(2)}) collective-permute-start(bf16[464,1024]{1,0:T(8,128)(2,1)} %get-tuple-element.115), channel_id=1, source_target_pairs={{0,1},{1,0},{2,3},{3,2},{4,5},{5,4},{6,7},{7,6},{8,9},{9,8},{10,11... | collective-permute-start | bytes 2850824 | tf_op jit(solution)/shard_map/ppermute | solution.py:392
  162.1 25.7 %collective-permute-start.37 = (bf16[448,1024]{1,0:T(8,128)(2,1)}, bf16[448,1024]{1,0:T(8,128)(2,1)S(1)}, u32[]{:S(2)}, u32[]{:S(2)}) collective-permute-start(bf16[448,1024]{1,0:T(8,128)(2,1)} %get-tuple-element.123), channel_id=1, source_target_pairs={{0,1},{1,0},{2,3},{3,2},{4,5},{5,4},{6,7},{7,6},{8,9},{9,8},{10,11... | collective-permute-start | bytes 2752520 | tf_op jit(solution)/shard_map/ppermute | solution.py:392
  165.8 7.3 %collective-permute-start.17 = (bf16[112,1024]{1,0:T(8,128)(2,1)}, bf16[112,1024]{1,0:T(8,128)(2,1)S(1)}, u32[]{:S(2)}, u32[]{:S(2)}) collective-permute-start(bf16[112,1024]{1,0:T(8,128)(2,1)} %get-tuple-element.94), channel_id=1, source_target_pairs={{0,2},{2,0},{4,6},{6,4},{8,10},{10,8},{12,14},{14,12},{16,18},{18,... | collective-permute-start | bytes 688136 | tf_op jit(solution)/shard_map/ppermute | solution.py:387
  165.8 11.6 %collective-permute-start.18 = (bf16[112,1024]{1,0:T(8,128)(2,1)}, bf16[112,1024]{1,0:T(8,128)(2,1)S(1)}, u32[]{:S(2)}, u32[]{:S(2)}) collective-permute-start(bf16[112,1024]{1,0:T(8,128)(2,1)} %get-tuple-element.95), channel_id=1, source_target_pairs={{0,4},{2,6},{4,0},{6,2},{8,12},{10,14},{12,8},{14,10},{16,20},{18,... | collective-permute-start | bytes 688136 | tf_op jit(solution)/shard_map/ppermute | solution.py:387
  167.2 11.9 %collective-permute-start.19 = (bf16[112,1024]{1,0:T(8,128)(2,1)}, bf16[112,1024]{1,0:T(8,128)(2,1)S(1)}, u32[]{:S(2)}, u32[]{:S(2)}) collective-permute-start(bf16[112,1024]{1,0:T(8,128)(2,1)} %get-tuple-element.96), channel_id=1, source_target_pairs={{0,6},{2,4},{4,2},{6,0},{8,14},{10,12},{12,10},{14,8},{16,22},{18,... | collective-permute-start | bytes 688136 | tf_op jit(solution)/shard_map/ppermute | solution.py:387
  173.0 9.9 %collective-permute-start.12 = (bf16[112,1024]{1,0:T(8,128)(2,1)}, bf16[112,1024]{1,0:T(8,128)(2,1)S(1)}, u32[]{:S(2)}, u32[]{:S(2)}) collective-permute-start(bf16[112,1024]{1,0:T(8,128)(2,1)} %get-tuple-element.85), channel_id=1, source_target_pairs={{0,2},{2,0},{4,6},{6,4},{8,10},{10,8},{12,14},{14,12},{16,18},{18,... | collective-permute-start | bytes 688136 | tf_op jit(solution)/shard_map/ppermute | solution.py:387
  173.3 11.2 %collective-permute-start.13 = (bf16[112,1024]{1,0:T(8,128)(2,1)}, bf16[112,1024]{1,0:T(8,128)(2,1)S(1)}, u32[]{:S(2)}, u32[]{:S(2)}) collective-permute-start(bf16[112,1024]{1,0:T(8,128)(2,1)} %get-tuple-element.86), channel_id=1, source_target_pairs={{0,4},{2,6},{4,0},{6,2},{8,12},{10,14},{12,8},{14,10},{16,20},{18,... | collective-permute-start | bytes 688136 | tf_op jit(solution)/shard_map/ppermute | solution.py:387
  177.4 17.3 %collective-permute-start.34 = (bf16[128,1024]{1,0:T(8,128)(2,1)}, bf16[128,1024]{1,0:T(8,128)(2,1)S(1)}, u32[]{:S(2)}, u32[]{:S(2)}) collective-permute-start(bf16[128,1024]{1,0:T(8,128)(2,1)} %get-tuple-element.117), channel_id=1, source_target_pairs={{0,2},{2,0},{4,6},{6,4},{8,10},{10,8},{12,14},{14,12},{16,18},{18,... | collective-permute-start | bytes 786440 | tf_op jit(solution)/shard_map/ppermute | solution.py:387
  179.2 15.6 %collective-permute-start.35 = (bf16[128,1024]{1,0:T(8,128)(2,1)}, bf16[128,1024]{1,0:T(8,128)(2,1)S(1)}, u32[]{:S(2)}, u32[]{:S(2)}) collective-permute-start(bf16[128,1024]{1,0:T(8,128)(2,1)} %get-tuple-element.118), channel_id=1, source_target_pairs={{0,4},{2,6},{4,0},{6,2},{8,12},{10,14},{12,8},{14,10},{16,20},{18,... | collective-permute-start | bytes 786440 | tf_op jit(solution)/shard_map/ppermute | solution.py:387
  182.9 11.7 %collective-permute-start.14 = (bf16[112,1024]{1,0:T(8,128)(2,1)S(1)}, bf16[112,1024]{1,0:T(8,128)(2,1)S(1)}, u32[]{:S(2)}, u32[]{:S(2)}) collective-permute-start(bf16[112,1024]{1,0:T(8,128)(2,1)S(1)} %copy-done.34), channel_id=1, source_target_pairs={{0,6},{2,4},{4,2},{6,0},{8,14},{10,12},{12,10},{14,8},{16,22},{18,... | collective-permute-start | bytes 688136 | tf_op jit(solution)/shard_map/ppermute | solution.py:387
  184.5 19.2 %collective-permute-start.36 = (bf16[128,1024]{1,0:T(8,128)(2,1)}, bf16[128,1024]{1,0:T(8,128)(2,1)S(1)}, u32[]{:S(2)}, u32[]{:S(2)}) collective-permute-start(bf16[128,1024]{1,0:T(8,128)(2,1)} %get-tuple-element.119), channel_id=1, source_target_pairs={{0,6},{2,4},{4,2},{6,0},{8,14},{10,12},{12,10},{14,8},{16,22},{18,... | collective-permute-start | bytes 786440 | tf_op jit(solution)/shard_map/ppermute | solution.py:387
  187.8 27.0 %collective-permute-start.21 = (bf16[128,1024]{1,0:T(8,128)(2,1)}, bf16[128,1024]{1,0:T(8,128)(2,1)S(1)}, u32[]{:S(2)}, u32[]{:S(2)}) collective-permute-start(bf16[128,1024]{1,0:T(8,128)(2,1)} %get-tuple-element.98), channel_id=1, source_target_pairs={{0,8},{2,10},{4,12},{6,14},{8,16},{10,18},{12,20},{14,22},{16,24},... | collective-permute-start | bytes 786440 | tf_op jit(solution)/shard_map/ppermute | solution.py:380
  194.6 12.6 %collective-permute-start.38 = (bf16[112,1024]{1,0:T(8,128)(2,1)}, bf16[112,1024]{1,0:T(8,128)(2,1)S(1)}, u32[]{:S(2)}, u32[]{:S(2)}) collective-permute-start(bf16[112,1024]{1,0:T(8,128)(2,1)} %get-tuple-element.125), channel_id=1, source_target_pairs={{0,2},{2,0},{4,6},{6,4},{8,10},{10,8},{12,14},{14,12},{16,18},{18,... | collective-permute-start | bytes 688136 | tf_op jit(solution)/shard_map/ppermute | solution.py:387
  194.6 14.2 %collective-permute-start.39 = (bf16[112,1024]{1,0:T(8,128)(2,1)}, bf16[112,1024]{1,0:T(8,128)(2,1)S(1)}, u32[]{:S(2)}, u32[]{:S(2)}) collective-permute-start(bf16[112,1024]{1,0:T(8,128)(2,1)} %get-tuple-element.126), channel_id=1, source_target_pairs={{0,4},{2,6},{4,0},{6,2},{8,12},{10,14},{12,8},{14,10},{16,20},{18,... | collective-permute-start | bytes 688136 | tf_op jit(solution)/shard_map/ppermute | solution.py:387
  194.8 15.3 %collective-permute-start.40 = (bf16[112,1024]{1,0:T(8,128)(2,1)}, bf16[112,1024]{1,0:T(8,128)(2,1)S(1)}, u32[]{:S(2)}, u32[]{:S(2)}) collective-permute-start(bf16[112,1024]{1,0:T(8,128)(2,1)} %get-tuple-element.127), channel_id=1, source_target_pairs={{0,6},{2,4},{4,2},{6,0},{8,14},{10,12},{12,10},{14,8},{16,22},{18,... | collective-permute-start | bytes 688136 | tf_op jit(solution)/shard_map/ppermute | solution.py:387
  203.7 25.0 %collective-permute-start.20 = (bf16[128,1024]{1,0:T(8,128)(2,1)S(1)}, bf16[128,1024]{1,0:T(8,128)(2,1)S(1)}, u32[]{:S(2)}, u32[]{:S(2)}) collective-permute-start(bf16[128,1024]{1,0:T(8,128)(2,1)S(1)} %copy-done.26), channel_id=1, source_target_pairs={{0,16},{2,18},{4,20},{6,22},{8,24},{10,26},{12,28},{14,30},{16,0},... | collective-permute-start | bytes 786440 | tf_op jit(solution)/shard_map/ppermute | solution.py:380
  207.2 29.5 %collective-permute-start.15 = (bf16[128,1024]{1,0:T(8,128)(2,1)S(1)}, bf16[128,1024]{1,0:T(8,128)(2,1)S(1)}, u32[]{:S(2)}, u32[]{:S(2)}) collective-permute-start(bf16[128,1024]{1,0:T(8,128)(2,1)S(1)} %copy-done.33), channel_id=1, source_target_pairs={{0,24},{2,26},{4,28},{6,30},{8,0},{10,2},{12,4},{14,6},{16,8},{18,... | collective-permute-start | bytes 786440 | tf_op jit(solution)/shard_map/ppermute | solution.py:380
  208.8 30.2 %collective-permute-start.43 = (bf16[144,1024]{1,0:T(8,128)(2,1)}, bf16[144,1024]{1,0:T(8,128)(2,1)S(1)}, u32[]{:S(2)}, u32[]{:S(2)}) collective-permute-start(bf16[144,1024]{1,0:T(8,128)(2,1)} %get-tuple-element.131), channel_id=1, source_target_pairs={{0,8},{2,10},{4,12},{6,14},{8,16},{10,18},{12,20},{14,22},{16,24},... | collective-permute-start | bytes 884744 | tf_op jit(solution)/shard_map/ppermute | solution.py:380
  210.1 35.3 %collective-permute-start.42 = (bf16[144,1024]{1,0:T(8,128)(2,1)}, bf16[144,1024]{1,0:T(8,128)(2,1)S(1)}, u32[]{:S(2)}, u32[]{:S(2)}) collective-permute-start(bf16[144,1024]{1,0:T(8,128)(2,1)} %get-tuple-element.130), channel_id=1, source_target_pairs={{0,16},{2,18},{4,20},{6,22},{8,24},{10,26},{12,28},{14,30},{16,0},... | collective-permute-start | bytes 884744 | tf_op jit(solution)/shard_map/ppermute | solution.py:380
  214.8 34.6 %collective-permute-start.41 = (bf16[144,1024]{1,0:T(8,128)(2,1)}, bf16[144,1024]{1,0:T(8,128)(2,1)S(1)}, u32[]{:S(2)}, u32[]{:S(2)}) collective-permute-start(bf16[144,1024]{1,0:T(8,128)(2,1)} %get-tuple-element.129), channel_id=1, source_target_pairs={{0,24},{2,26},{4,28},{6,30},{8,0},{10,2},{12,4},{14,6},{16,8},{18,... | collective-permute-start | bytes 884744 | tf_op jit(solution)/shard_map/ppermute | solution.py:380
  214.9 21.8 %copy-start.7 = (bf16[128,1024]{1,0:T(8,128)(2,1)S(1)}, bf16[128,1024]{1,0:T(8,128)(2,1)}, u32[]{:S(2)}) copy-start(bf16[128,1024]{1,0:T(8,128)(2,1)} %get-tuple-element.88) | copy-start | bytes 786436
  (37 other events, 263.4 us)

commit v3 on v0

v3 whole, which is shorter than its diff:
```python
import functools

import jax
import jax.numpy as jnp
from jax import lax
from jax.experimental import pallas as pl
from jax.experimental.pallas import tpu as pltpu
from jax.sharding import PartitionSpec as P

PLANE = 4
TAIL = 16
VMEM_LIMIT = 56 * 1024 * 1024
F32 = jnp.float32
BF16 = jnp.bfloat16


def dot_nn(a, b):
    return lax.dot_general(a, b, (((1,), (0,)), ((), ())), preferred_element_type=F32)


def dot_nt(a, b):
    return lax.dot_general(a, b, (((1,), (1,)), ((), ())), preferred_element_type=F32)


def dot_tn(a, b):
    return lax.dot_general(a, b, (((0,), (0,)), ((), ())), preferred_element_type=F32)


def iota(shape, axis):
    return lax.broadcasted_iota(jnp.int32, shape, axis)


SMEM = pl.BlockSpec(memory_space=pltpu.SMEM)
VMEM = pl.BlockSpec(memory_space=pltpu.VMEM)
HBM = pl.BlockSpec(memory_space=pl.ANY)


def call(kernel, outs, args, specs, out_specs=None, scratch=(), flops=0, name=None):
    nbytes = sum(a.size * a.dtype.itemsize for a in (*args, *outs))
    return pl.pallas_call(
        kernel,
        out_shape=outs,
        in_specs=specs,
        out_specs=out_specs if out_specs is not None else [VMEM] * len(outs),
        scratch_shapes=list(scratch),
        compiler_params=pltpu.CompilerParams(vmem_limit_bytes=VMEM_LIMIT),
        cost_estimate=pl.CostEstimate(flops=flops, bytes_accessed=nbytes, transcendentals=0),
        name=name,
    )(*args)


def shape(*dims, dtype=BF16):
    return jax.ShapeDtypeStruct(dims, dtype)


def select_kernel(info, meta, sel, *, zn, pn, tokens, picks, cap):
    rows = zn * cap
    expert = iota((8, 1), 0)
    experts = jnp.where(expert < pn, info[0] + expert, -2).astype(F32)
    before = (iota((tokens, tokens), 0) < iota((tokens, tokens), 1)).astype(F32).astype(BF16)
    slot = iota((rows, tokens), 0).astype(F32)
    for s in range(zn):
        here = slice(s * tokens, (s + 1) * tokens)
        ids = meta[0:8, here]
        named = jnp.zeros((8, tokens), F32)
        for k in range(picks):
            named += (ids[k : k + 1, :] == experts).astype(F32)
        dest = dot_nn(named.astype(BF16), before) + s * cap
        dest = jnp.where(named > 0, dest, -1.0)
        for q in range(pn):
            sel[q * rows : (q + 1) * rows, here] = (
                (slot == dest[q : q + 1, :]).astype(F32).astype(BF16)
            )


def route_kernel(info, meta, ones, gated, *, zn, pn, tokens, picks, cap):
    rows = zn * cap
    expert = iota((1, 8), 1)
    experts = jnp.where(expert < pn, info[0] + expert, -2).astype(F32)
    after = (iota((tokens, tokens), 1) < iota((tokens, tokens), 0)).astype(F32).astype(BF16)
    eye = (iota((16, 16), 0) == iota((16, 16), 1)).astype(F32).astype(BF16)
    lane = iota((tokens, pn * rows), 1).astype(F32)
    for s in range(zn):
        here = slice(s * tokens, (s + 1) * tokens)
        columned = dot_tn(meta[:, here].astype(BF16), eye)
        named = jnp.zeros((tokens, 8), F32)
        gate = jnp.zeros((tokens, 8), F32)
        for k in range(picks):
            match = (columned[:, k : k + 1] == experts).astype(F32)
            named += match
            gate += match * columned[:, 8 + k : 9 + k]
        dest = dot_nn(after, named.astype(BF16)) + s * cap
        dest = jnp.where(named > 0, dest + rows * expert.astype(F32), -1.0)
        picked = jnp.zeros((tokens, pn * rows), F32)
        weighed = jnp.zeros((tokens, pn * rows), F32)
        for q in range(pn):
            match = lane == dest[:, q : q + 1]
            picked += match.astype(F32)
            weighed += jnp.where(match, gate[:, q : q + 1], 0.0)
        ones[here, :] = picked.astype(BF16)
        gated[here, :] = weighed.astype(BF16)


def pack_kernel(info, meta, sel, *refs, zn, pn, tokens, picks, rows, gates):
    sources, out, whole = refs[:zn], refs[zn], refs[zn + 1]
    for s in range(zn):
        whole[s * tokens : (s + 1) * tokens, :] = sources[s][...]
    for q in range(pn):
        chosen = sel[q * rows : (q + 1) * rows, :]
        out[q, 0:rows, :] = dot_nn(chosen, whole[...]).astype(BF16)
        if gates:
            expert = (info[0] + q).astype(F32)
            gate = jnp.zeros((1, zn * tokens), F32)
            for k in range(picks):
                gate += jnp.where(meta[k : k + 1, :] == expert, meta[8 + k : 9 + k, :], 0.0)
            gate = jnp.broadcast_to(gate, (TAIL, zn * tokens)).astype(BF16)
            out[q, rows : rows + TAIL, :] = jnp.zeros((TAIL, out.shape[2]), BF16)
            out[q, rows : rows + TAIL, 0:rows] = dot_nt(gate, chosen).astype(BF16)


def combine_kernel(info, meta, sel, chosen, back, *outs, zn, pn, tokens, rows, gates):
    cols = back.shape[2]
    whole = back[:, 0:rows, :].reshape(pn * rows, cols)
    if gates:
        total = jnp.zeros((8, zn * tokens), F32)
        for q in range(pn):
            expert = (info[0] + q).astype(F32)
            row = back[q, rows : rows + TAIL, 0:rows]
            spread = dot_nn(row, sel[q * rows : (q + 1) * rows, :])
            total += jnp.where(meta[0:8, :] == expert, spread[0:8, :], 0.0)
        total = jnp.concatenate([total, jnp.zeros((TAIL - 8, zn * tokens), F32)], axis=0)
        total = total.astype(BF16)
    for s in range(zn):
        here = slice(s * tokens, (s + 1) * tokens)
        outs[s][0:tokens, :] = dot_nn(chosen[here, :], whole).astype(BF16)
        if gates:
            outs[s][tokens : tokens + TAIL, :] = jnp.zeros((TAIL, cols), BF16)
            outs[s][tokens : tokens + TAIL, 0:tokens] = total[:, here]


class Loads:
    def __init__(self, sems):
        self.sems, self.copies, self.waited = sems, {}, set()

    def add(self, key, source, target):
        self.copies[key] = pltpu.make_async_copy(source, target, self.sems.at[len(self.copies)])
        self.copies[key].start()

    def need(self, *keys):
        for key in keys:
            if key not in self.waited:
                self.waited.add(key)
                self.copies[key].wait()

    def finish(self):
        self.need(*self.copies)


def column_block(info, j, nt, cols):
    block = lax.rem(info[2] - j + nt, nt)
    return pl.ds(pl.multiple_of(block * cols, 128), cols)


def load_weights(loads, info, win, wout, wg, wu, wd, nt, cols, kinds):
    for kind in kinds:
        for j in range(nt):
            at = column_block(info, j, nt, cols)
            to = pl.ds(j * cols, cols)
            if kind == "g":
                loads.add(("g", j), win.at[0, 0, :, at], wg.at[:, to])
            elif kind == "u":
                loads.add(("u", j), win.at[0, 1, :, at], wu.at[:, to])
            else:
                loads.add(("d", j), wout.at[0, :, at], wd.at[:, to])


def forward_kernel(info, *refs, nt, pn, rows, cols):
    xs, win, wout = refs[:nt], refs[nt], refs[nt + 1]
    outs, hid, a1, a2 = refs[nt + 2 : 2 * nt + 2], *refs[2 * nt + 2 : 2 * nt + 5]
    x, wg, wu, wd, stage, in_sems, out_sems = refs[2 * nt + 5 :]
    loads, stores = Loads(in_sems), Loads(out_sems)
    every = range(nt)

    def load_rows(g):
        for j in every:
            for q in (2 * g, 2 * g + 1):
                target = x.at[pl.ds(q * rows, rows), pl.ds(j * cols, cols)]
                loads.add(("x", j, q), xs[j].at[q], target)

    load_rows(0)
    load_weights(loads, info, win, wout, wg, wu, wd, nt, cols, "gu")
    for g in range(1, pn // 2):
        load_rows(g)
    load_weights(loads, info, win, wout, wg, wu, wd, nt, cols, "d")
    for g in range(pn // 2):
        here = slice(2 * g * rows, 2 * (g + 1) * rows)
        loads.need(*(("x", j, q) for j in every for q in (2 * g, 2 * g + 1)))
        loads.need(*(("g", j) for j in every))
        gate = dot_nt(x[here, :], wg[...])
        loads.need(*(("u", j) for j in every))
        up = dot_nt(x[here, :], wu[...])
        sigma = jax.nn.sigmoid(gate)
        active = gate * sigma
        hidden = (active * up).astype(BF16)
        hid[here, :] = hidden
        a1[here, :] = (up * sigma * (1.0 + gate * (1.0 - sigma))).astype(BF16)
        a2[here, :] = active.astype(BF16)
        loads.need(*(("d", j) for j in every))
        part = dot_nn(hidden, wd[...]).astype(BF16)
        for j in every:
            w = (nt - j) % nt
            stage[j, 2 * g : 2 * g + 2] = part[:, w * cols : (w + 1) * cols].reshape(2, rows, cols)
            span = pl.ds(2 * g, 2)
            stores.add((g, j), stage.at[j, span], outs[j].at[span])
    loads.finish()
    stores.finish()


def backward_kernel(info, *refs, nt, pn, rows, cols):
    cs, win, wout, hid, a1, a2 = refs[:nt], *refs[nt : nt + 5]
    outs, gg, ug, hs = refs[nt + 5 : 2 * nt + 5], *refs[2 * nt + 5 : 2 * nt + 8]
    c, tails, h, b1, b2, wg, wu, wd, stage, in_sems, out_sems = refs[2 * nt + 8 :]
    loads, stores = Loads(in_sems), Loads(out_sems)
    every = range(nt)

    def load_rows(g):
        for j in every:
            for q in (2 * g, 2 * g + 1):
                target = c.at[pl.ds(q * rows, rows), pl.ds(j * cols, cols)]
                loads.add(("c", j, q), cs[j].at[q, pl.ds(0, rows)], target)

    load_rows(0)
    load_weights(loads, info, win, wout, wg, wu, wd, nt, cols, "d")
    loads.add("t", cs[0].at[:, pl.ds(rows, TAIL)], tails)
    for key, source, target in (("h", hid, h), ("1", a1, b1), ("2", a2, b2)):
        loads.add(key, source, target)
    load_weights(loads, info, win, wout, wg, wu, wd, nt, cols, "gu")
    for g in range(1, pn // 2):
        load_rows(g)
    same = iota((rows, rows), 0) == iota((rows, rows), 1)
    for g in range(pn // 2):
        here = slice(2 * g * rows, 2 * (g + 1) * rows)
        both = (2 * g, 2 * g + 1)
        loads.need(*(("c", j, q) for j in every for q in both), *(("d", j) for j in every))
        grad = dot_nt(c[here, :], wd[...])
        loads.need("t", "h", "1", "2")
        hidden = h[here, :].astype(F32)
        piece = jnp.sum(grad * hidden, axis=1, keepdims=True)
        gates = []
        for at, q in enumerate(both):
            row = tails[q, :, 0:rows].astype(F32)[0:1, :]
            gates.append(jnp.sum(jnp.where(same, row, 0.0), axis=1, keepdims=True))
            part = piece[at * rows : (at + 1) * rows, :]
            part = jnp.sum(jnp.where(same, part, 0.0), axis=0, keepdims=True)
            part = jnp.broadcast_to(part, (TAIL, rows)).astype(BF16)
            for j in every:
                stage[j, q, rows : rows + TAIL, :] = jnp.zeros((TAIL, cols), BF16)
                stage[j, q, rows : rows + TAIL, 0:rows] = part
        gate = jnp.concatenate(gates, axis=0)
        grad = gate * grad
        hs[here, :] = (gate * hidden).astype(BF16)
        gate_grad = (grad * b1[here, :].astype(F32)).astype(BF16)
        up_grad = (grad * b2[here, :].astype(F32)).astype(BF16)
        gg[here, :] = gate_grad
        ug[here, :] = up_grad
        loads.need(*((k, j) for k in "gu" for j in every))
        part = (dot_nn(gate_grad, wg[...]) + dot_nn(up_grad, wu[...])).astype(BF16)
        for j in every:
            w = (nt - j) % nt
            block = part[:, w * cols : (w + 1) * cols].reshape(2, rows, cols)
            stage[j, 2 * g : 2 * g + 2, 0:rows, :] = block
            span = pl.ds(2 * g, 2)
            stores.add((g, j), stage.at[j, span], outs[j].at[span])
    loads.finish()
    stores.finish()


def weights_kernel(info, *refs, nt, pn, rows, cols):
    xs, cs, lefts = refs[:nt], refs[nt : 2 * nt], refs[2 * nt : 2 * nt + 3]
    gin, gout, left, right, stage, in_sems, out_sems = refs[2 * nt + 3 :]
    loads, stores = Loads(in_sems), Loads(out_sems)
    order = ((0, 0, xs), (1, 0, xs), (2, 1, cs))
    for w, side, sources in order:
        loads.add(("l", w), lefts[w], left.at[w])
        if w == 1:
            continue
        for j in range(nt):
            for q in range(pn):
                target = right.at[side, j, pl.ds(q * rows, rows)]
                loads.add((side, j, q), sources[j].at[q, pl.ds(0, rows)], target)
    for w, side, _ in order:
        loads.need(("l", w))
        for j in range(nt):
            loads.need(*((side, j, q) for q in range(pn)))
            at = column_block(info, j, nt, cols)
            stage[j, w] = dot_tn(left[w], right[side, j]).astype(BF16)
            target = gout.at[0, :, at] if w == 2 else gin.at[0, w, :, at]
            stores.add((j, w), stage.at[j, w], target)
    loads.finish()
    stores.finish()


def after(value, *others):
    return lax.optimization_barrier((value, *others))[0]


def body(
    first_half,
    second_half,
    first_grad,
    second_grad,
    expert_ids,
    gate_weights,
    expert_in,
    expert_out,
):
    tokens, picks = expert_ids.shape
    groups = lax.axis_size("expert")
    nt = lax.axis_size("tensor")
    pn = PLANE
    zn = groups // pn
    cap = tokens * picks * 7 // (6 * groups)
    rows = zn * cap
    slots = pn * rows
    cols = first_half.shape[1]
    hid_n = expert_out.shape[1]
    width = expert_out.shape[2]
    me = lax.axis_index("expert")
    info = jnp.stack([(me // pn) * pn, me % pn, lax.axis_index("tensor")]).astype(jnp.int32)

    def outer_send(value, s):
        if s % zn == 0:
            return value
        return lax.ppermute(
            value, "expert", [(e, ((e // pn + s) % zn) * pn + e % pn) for e in range(groups)]
        )

    def inner_exchange(value):
        planes = [[z * pn + q for q in range(pn)] for z in range(zn)]
        return lax.all_to_all(
            value, "expert", split_axis=0, concat_axis=0, axis_index_groups=planes, tiled=True
        )

    def tensor_send(value, j):
        if j == 0:
            return value
        return lax.ppermute(value, "tensor", [(c, (c + j) % nt) for c in range(nt)])

    fixed = dict(zn=zn, pn=pn, tokens=tokens)

    own = jnp.concatenate(
        [
            jnp.pad(expert_ids.T.astype(F32), ((0, 8 - picks), (0, 0)), constant_values=-1.0),
            jnp.pad(gate_weights.T.astype(F32), ((0, 8 - picks), (0, 0))),
        ],
        axis=0,
    )
    meta = jnp.concatenate([outer_send(own, s) for s in range(zn)], axis=1)
    sel = call(
        functools.partial(select_kernel, **fixed, picks=picks, cap=cap),
        [shape(slots, zn * tokens)],
        [info, meta],
        [SMEM, VMEM],
        name="select",
    )[0]
    late = zn // 2
    x_parts = [
        outer_send(after(first_half, sel) if s == late else first_half, s) for s in range(zn)
    ]

    def pack(parts, gates):
        return call(
            functools.partial(pack_kernel, **fixed, picks=picks, rows=rows, gates=gates),
            [shape(pn, rows + TAIL if gates else rows, cols)],
            [info, meta, sel, *parts],
            [SMEM] + [VMEM] * (2 + zn),
            scratch=[pltpu.VMEM((zn * tokens, cols), BF16)],
            flops=2 * slots * zn * tokens * cols,
            name="pack_gates" if gates else "pack",
        )[0]

    def combine(chosen, back, gates):
        parts = call(
            functools.partial(combine_kernel, **fixed, rows=rows, gates=gates),
            [shape(tokens + TAIL if gates else tokens, cols)] * zn,
            [info, meta, sel, chosen, back],
            [SMEM] + [VMEM] * 4,
            flops=2 * slots * zn * tokens * cols,
            name="combine_gates" if gates else "combine",
        )
        return [outer_send(part, -s) for s, part in enumerate(parts)]

    def core_sum(parts):
        total = parts[0].astype(F32)
        for j in range(1, nt):
            total += tensor_send(parts[j], j).astype(F32)
        return total.astype(BF16)

    work = 2 * slots * hid_n * width
    weights = [pltpu.VMEM((hid_n, nt * cols), BF16)] * 3
    sizes = dict(nt=nt, pn=pn, rows=rows, cols=cols)

    x_packed = pack(x_parts, False)
    x_here = inner_exchange(x_packed)
    xs = [tensor_send(x_here, j) for j in range(nt)]
    grad_whole = after(second_grad, *x_parts[1:])
    c_parts = [outer_send(grad_whole, s) for s in range(zn)]
    ones, gated = call(
        functools.partial(route_kernel, **fixed, picks=picks, cap=cap),
        [shape(zn * tokens, slots)] * 2,
        [info, after(meta, x_packed)],
        [SMEM, VMEM],
        name="route",
    )
    c_packed = pack(c_parts, True)
    c_here = inner_exchange(c_packed)

    forward = call(
        functools.partial(forward_kernel, **sizes),
        [shape(pn, rows, cols)] * nt + [shape(slots, hid_n)] * 3,
        [info, *xs, expert_in, expert_out],
        [SMEM] + [HBM] * (nt + 2),
        out_specs=[HBM] * nt + [VMEM] * 3,
        scratch=[pltpu.VMEM((slots, nt * cols), BF16)]
        + weights
        + [
            pltpu.VMEM((nt, pn, rows, cols), BF16),
            pltpu.SemaphoreType.DMA(((3 + pn) * nt,)),
            pltpu.SemaphoreType.DMA((pn // 2 * nt,)),
        ],
        flops=3 * work,
        name="expert_forward",
    )
    outs, (hid, a1, a2) = forward[:nt], forward[nt:]
    c_here = after(c_here, hid)
    cs = [tensor_send(c_here, j) for j in range(nt)]
    out_here = core_sum(outs)
    out_back = inner_exchange(out_here)

    backward = call(
        functools.partial(backward_kernel, **sizes),
        [shape(pn, rows + TAIL, cols)] * nt + [shape(slots, hid_n)] * 3,
        [info, *cs, expert_in, expert_out, after(hid, out_here), a1, a2],
        [SMEM] + [HBM] * (nt + 5),
        out_specs=[HBM] * nt + [VMEM] * 3,
        scratch=[pltpu.VMEM((slots, nt * cols), BF16), pltpu.VMEM((pn, TAIL, cols), BF16)]
        + [pltpu.VMEM((slots, hid_n), BF16)] * 3
        + weights
        + [
            pltpu.VMEM((nt, pn, rows + TAIL, cols), BF16),
            pltpu.SemaphoreType.DMA(((3 + pn) * nt + 4,)),
            pltpu.SemaphoreType.DMA((pn // 2 * nt,)),
        ],
        flops=3 * work,
        name="expert_backward",
    )
    grads, (gg, ug, hs) = backward[:nt], backward[nt:]
    dx_here = core_sum(grads)
    dx_back = inner_exchange(dx_here)
    out_parts = combine(gated, out_back, False)
    grad_parts = combine(ones, dx_back, True)

    grad_in, grad_out = call(
        functools.partial(weights_kernel, **sizes),
        [shape(*expert_in.shape), shape(*expert_out.shape)],
        [info, *xs, *cs, gg, ug, after(hs, dx_here)],
        [SMEM] + [HBM] * (2 * nt + 3),
        out_specs=[HBM, HBM],
        scratch=[
            pltpu.VMEM((3, slots, hid_n), BF16),
            pltpu.VMEM((2, nt, slots, cols), BF16),
            pltpu.VMEM((nt, 3, hid_n, cols), BF16),
            pltpu.SemaphoreType.DMA((3 + 2 * nt * pn,)),
            pltpu.SemaphoreType.DMA((3 * nt,)),
        ],
        flops=3 * work,
        name="expert_weights",
    )

    branch = sum(part.astype(F32) for part in out_parts)
    input_sum = sum(part[:tokens].astype(F32) for part in grad_parts)
    gate_sum = sum(part[tokens : tokens + picks, :tokens].astype(F32) for part in grad_parts)
    restored = (second_half.astype(F32) - branch).astype(BF16)
    carried_grad = (first_grad.astype(F32) + input_sum).astype(BF16)
    return (restored, carried_grad, gate_sum.T, grad_in, grad_out)


def solution(mesh):
    in_specs = (
        P("expert", "tensor"),
        P("expert", "tensor"),
        P("expert", "tensor"),
        P("expert", "tensor"),
        P("expert", None),
        P("expert", None),
        P("expert", None, "tensor", None),
        P("expert", "tensor", None),
    )
    out_specs = (
        P("expert", "tensor"),
        P("expert", "tensor"),
        P("expert", None),
        P("expert", None, "tensor", None),
        P("expert", "tensor", None),
    )
    return jax.shard_map(body, mesh=mesh, in_specs=in_specs, out_specs=out_specs, check_vma=False)
```

time: 454 us -> 250 us (0.55)
  the two profiles are of different devices: /device:TPU:0 before, /device:TPU:9 now
where the time goes in v3:
time: 250 us; the launch traced here: 249 us
  waiting for transfers between devices  96.2 us (38%)
  Pallas kernels  73.1 us (29%)
  starting transfers between devices  33.7 us (13%)
  blocking collectives  25.7 us (10%)
  other arithmetic  14.5 us (6%)
  local copies, waits for them, and re-layouts  5.29 us (2%)
    ppermute x15, waiting for transfers between devices, outer_send(): lax.ppermute(value, 'expert', [(e, (e // pn + s) % zn * pn + e % pn) for...  73.3 us
    pallas_call x9, Pallas kernels, call(): pl.pallas_call(kernel, out_shape=outs, in_specs=specs, out_specs=out_spec...  73.1 us
    all_to_all x1, blocking collectives, inner_exchange(): lax.all_to_all(value, 'expert', split_axis=0, concat_axis=0, axis_index_g...  25.7 us
    all_to_all x3, waiting for transfers between devices, inner_exchange(): lax.all_to_all(value, 'expert', split_axis=0, concat_axis=0, axis_index_g...  22.6 us
    ppermute x15, starting transfers between devices, outer_send(): lax.ppermute(value, 'expert', [(e, (e // pn + s) % zn * pn + e % pn) for...  17.2 us
    all_to_all x3, starting transfers between devices, inner_exchange(): lax.all_to_all(value, 'expert', split_axis=0, concat_axis=0, axis_index_g...  11 us
    convert_element_type x2, other arithmetic, core_sum(): return total.astype(BF16)  8.49 us
    ppermute x4, starting transfers between devices, tensor_send(): return lax.ppermute(value, 'tensor', [(c, (c + j) % nt) for c in range(nt)])  5.51 us
  transfers between devices with their start and end apart: 22, of which 14 were waited for; matrix products, arithmetic and copies ran while one was open for 5% of the time, Pallas kernels for 18%

profile of v3, /device:TPU:9, one launch (start us, length us, event | category | flops | bytes accessed | tf_op | source)
XLA Modules:
  0.0 249.3 jit_solution(2514786695609505941)
XLA Ops:
  2.1 2.5 collective-permute-start.1
  4.5 2.2 collective-permute-start
  6.8 1.4 collective-permute-start.5
  9.4 2.0 select.9.sel
  11.5 0.9 collective-permute-start.4
  12.4 0.9 collective-permute-done.3.refs_1_
  13.2 9.3 %collective-permute-done.5.refs_3_ = bf16[128,1024]{1,0:T(8,128)(2,1)S(1)} collective-permute-done((bf16[128,1024]{1,0:T(8,128)(2,1)}, bf16[128,1024]{1,0:T(8,128)(2,1)S(1)}, u32[]{:S(2)}, u32[]{:S(2)}) %collective-permute-start.5) | collective-permute-done | bytes 262176 | tf_op jit(solution)/shard_map/ppermute | solution.py:334
  22.5 7.0 %collective-permute-done.4.refs_2_ = bf16[128,1024]{1,0:T(8,128)(2,1)S(1)} collective-permute-done((bf16[128,1024]{1,0:T(8,128)(2,1)}, bf16[128,1024]{1,0:T(8,128)(2,1)S(1)}, u32[]{:S(2)}, u32[]{:S(2)}) %collective-permute-start.4) | collective-permute-done | bytes 262176 | tf_op jit(solution)/shard_map/ppermute | solution.py:334
  29.5 0.7 copy-done.8
  30.2 3.8 %pack.1 = bf16[4,224,1024]{2,1,0:T(8,128)(2,1)} custom-call(s32[3]{0:T(128)} %pad_add_fusion.info, f32[16,512]{1,0:T(8,128)} %pad_maximum_fusion.meta, bf16[896,512]{1,0:T(8,128)(2,1)} %select.9.sel, bf16[128,1024]{1,0:T(8,128)(2,1)} %refs_0_.1, bf16[128,1024]{1,0:T(8,128)(2,1)} %copy-done.4, bf16[128,1024]{1,0:T(8,128)(2,1)} %copy-done.8, ...), custom_call_target="tpu_custom_call" | custom-call | flops 939524096 | bytes 3833868 | tf_op jit(solution)/shard_map/pack/pallas_call | solution.py:40
  34.1 25.7 %all_to_all.20.refs_0_ = bf16[4,224,1024]{2,1,0:T(8,128)(2,1)} all-to-all(bf16[4,224,1024]{2,1,0:T(8,128)(2,1)} %pack.1), channel_id=1, replica_groups={{0,2,4,6},{8,10,12,14},{16,18,20,22},{24,26,28,30},{1,3,5,7},{9,11,13,1..., dimensions={0} | all-to-all | bytes 3670016 | tf_op jit(solution)/shard_map/all_to_all | solution.py:340
  59.8 2.3 collective-permute-start.6
  62.1 1.9 collective-permute-start.11
  64.0 3.9 %collective-permute-start.12 = (bf16[128,1024]{1,0:T(8,128)(2,1)S(1)}, bf16[128,1024]{1,0:T(8,128)(2,1)S(1)}, u32[]{:S(2)}, u32[]{:S(2)}) collective-permute-start(bf16[128,1024]{1,0:T(8,128)(2,1)S(1)} %copy-done.3), channel_id=1, source_target_pairs={{0,16},{2,18},{4,20},{6,22},{8,24},{10,26},{12,28},{14,30},{16,0},... | collective-permute-start | bytes 786440 | tf_op jit(solution)/shard_map/ppermute | solution.py:334
  67.9 4.6 %collective-permute-done.11.refs_1_ = bf16[128,1024]{1,0:T(8,128)(2,1)S(1)} collective-permute-done((bf16[128,1024]{1,0:T(8,128)(2,1)S(1)}, bf16[128,1024]{1,0:T(8,128)(2,1)S(1)}, u32[]{:S(2)}, u32[]{:S(2)}) %collective-permute-start.11) | collective-permute-done | bytes 262176 | tf_op jit(solution)/shard_map/ppermute | solution.py:334
  72.5 14.1 %collective-permute-done.12.refs_2_ = bf16[128,1024]{1,0:T(8,128)(2,1)S(1)} collective-permute-done((bf16[128,1024]{1,0:T(8,128)(2,1)S(1)}, bf16[128,1024]{1,0:T(8,128)(2,1)S(1)}, u32[]{:S(2)}, u32[]{:S(2)}) %collective-permute-start.12) | collective-permute-done | bytes 262176 | tf_op jit(solution)/shard_map/ppermute | solution.py:334
  86.6 3.7 %collective-permute-done.13.refs_3_ = bf16[128,1024]{1,0:T(8,128)(2,1)S(1)} collective-permute-done((bf16[128,1024]{1,0:T(8,128)(2,1)S(1)}, bf16[128,1024]{1,0:T(8,128)(2,1)S(1)}, u32[]{:S(2)}, u32[]{:S(2)}) %collective-permute-start.13) | collective-permute-done | bytes 262176 | tf_op jit(solution)/shard_map/ppermute | solution.py:334
  90.3 0.7 copy-done.9
  91.0 4.1 %pack_gates.1 = bf16[4,240,1024]{2,1,0:T(8,128)(2,1)} custom-call(s32[3]{0:T(128)} %pad_add_fusion.info, f32[16,512]{1,0:T(8,128)} %pad_maximum_fusion.meta, bf16[896,512]{1,0:T(8,128)(2,1)} %select.9.sel, bf16[128,1024]{1,0:T(8,128)(2,1)} %refs_0_.2, bf16[128,1024]{1,0:T(8,128)(2,1)} %copy-done.6, bf16[128,1024]{1,0:T(8,128)(2,1)} %copy-done.7, ...), custom_call_target="tpu_custom_call" | custom-call | flops 939524096 | bytes 3964940 | tf_op jit(solution)/shard_map/pack_gates/pallas_call | solution.py:40
  95.1 3.8 %all-to-all-start.2 = ((bf16[4,240,1024]{2,1,0:T(8,128)(2,1)}), bf16[4,240,1024]{2,1,0:T(8,128)(2,1)S(1)}, u32[]{:S(2)}, u32[]{:S(2)}) async-start(bf16[4,240,1024]{2,1,0:T(8,128)(2,1)} %pack_gates.1), calls=%async_computation.2 | async-start | bytes 3932160 | tf_op jit(solution)/shard_map/all_to_all | solution.py:340
  98.9 16.6 %expert_forward.1 = (bf16[4,224,1024]{2,1,0:T(8,128)(2,1)}, bf16[4,224,1024]{2,1,0:T(8,128)(2,1)}, bf16[896,704]{1,0:T(8,128)(2,1)}, bf16[896,704]{1,0:T(8,128)(2,1)}, bf16[896,704]{1,0:T(8,128)(2,1)}) custom-call(s32[3]{0:T(128)} %pad_add_fusion.info, bf16[4,224,1024]{2,1,0:T(8,128)(2,1)} %all_to_all.20.refs_0_, ...), custom_call_target="tpu_custom_call" | custom-call | flops 7751073792 | bytes 19775500 | tf_op jit(solution)/shard_map/expert_forward/pallas_call | solution.py:40
  115.5 0.9 collective-permute-start.7
  116.4 5.1 %all-to-all-done.2.refs_0_.refs_2_ = bf16[4,240,1024]{2,1,0:T(8,128)(2,1)S(1)} async-done(((bf16[4,240,1024]{2,1,0:T(8,128)(2,1)}), bf16[4,240,1024]{2,1,0:T(8,128)(2,1)S(1)}, u32[]{:S(2)}, u32[]{:S(2)}) %all-to-all-start.2) | async-done | bytes 1966112 | tf_op jit(solution)/shard_map/all_to_all | solution.py:340
  121.6 1.5 collective-permute-start.14
  123.1 4.2 %add_convert_fusion.1 = bf16[4,224,1024]{2,1,0:T(8,128)(2,1)} fusion(bf16[4,224,1024]{2,1,0:T(8,128)(2,1)} %collective-permute-done.7, bf16[4,224,1024]{2,1,0:T(8,128)(2,1)} %get-tuple-element.36), kind=kLoop, calls=%fused_computation.1 | loop fusion | flops 3670016 | bytes 5505024 | tf_op jit(solution)/shard_map/convert_element_type | solution.py:397
  127.2 1.3 copy-done.13
  128.6 19.1 %expert_backward.1 = (bf16[4,240,1024]{2,1,0:T(8,128)(2,1)}, bf16[4,240,1024]{2,1,0:T(8,128)(2,1)}, bf16[896,704]{1,0:T(8,128)(2,1)}, bf16[896,704]{1,0:T(8,128)(2,1)}, bf16[896,704]{1,0:T(8,128)(2,1)}) custom-call(s32[3]{0:T(128)} %pad_add_fusion.info, bf16[4,240,1024]{2,1,0:T(8,128)(2,1)} %copy-done.2, bf16[4,240,1024]{2,1,0:T(8,128)(2,1)} %copy-done.13, ...), custom_call_target="tpu_custom_call" | custom-call | flops 7751073792 | bytes 24084492 | tf_op jit(solution)/shard_map/expert_backward/pallas_call | solution.py:40
  147.7 0.8 collective-permute-start.15
  148.5 3.6 %all-to-all-start.1 = ((bf16[4,224,1024]{2,1,0:T(8,128)(2,1)}), bf16[4,224,1024]{2,1,0:T(8,128)(2,1)S(1)}, u32[]{:S(2)}, u32[]{:S(2)}) async-start(bf16[4,224,1024]{2,1,0:T(8,128)(2,1)} %add_convert_fusion.1), calls=%async_computation.1 | async-start | bytes 3670016 | tf_op jit(solution)/shard_map/all_to_all | solution.py:340
  152.4 4.3 %add_convert_fusion = bf16[4,240,1024]{2,1,0:T(8,128)(2,1)} fusion(bf16[4,240,1024]{2,1,0:T(8,128)(2,1)} %collective-permute-done.15, bf16[4,240,1024]{2,1,0:T(8,128)(2,1)} %get-tuple-element.49), kind=kLoop, calls=%fused_computation | loop fusion | flops 3932160 | bytes 5898240 | tf_op jit(solution)/shard_map/convert_element_type | solution.py:397
  156.7 17.5 %all-to-all-done.1.back = bf16[4,224,1024]{2,1,0:T(8,128)(2,1)S(1)} async-done(((bf16[4,224,1024]{2,1,0:T(8,128)(2,1)}), bf16[4,224,1024]{2,1,0:T(8,128)(2,1)S(1)}, u32[]{:S(2)}, u32[]{:S(2)}) %all-to-all-start.1) | async-done | bytes 1835040 | tf_op jit(solution)/shard_map/all_to_all | solution.py:340
  174.2 1.2 copy-done.1
  175.5 3.6 %all-to-all-start.3 = ((bf16[4,240,1024]{2,1,0:T(8,128)(2,1)}), bf16[4,240,1024]{2,1,0:T(8,128)(2,1)S(1)}, u32[]{:S(2)}, u32[]{:S(2)}) async-start(bf16[4,240,1024]{2,1,0:T(8,128)(2,1)} %add_convert_fusion), calls=%async_computation.3 | async-start | bytes 3932160 | tf_op jit(solution)/shard_map/all_to_all | solution.py:340
  179.1 5.1 %route.1 = (bf16[512,896]{1,0:T(8,128)(2,1)}, bf16[512,896]{1,0:T(8,128)(2,1)}) custom-call(s32[3]{0:T(128)} %pad_add_fusion.info, f32[16,512]{1,0:T(8,128)} %pad_maximum_fusion.meta), custom_call_target="tpu_custom_call" | custom-call | bytes 1867788 | tf_op jit(solution)/shard_map/route/pallas_call | solution.py:40
  184.2 4.1 %combine.1 = (bf16[128,1024]{1,0:T(8,128)(2,1)}, bf16[128,1024]{1,0:T(8,128)(2,1)}, bf16[128,1024]{1,0:T(8,128)(2,1)}, bf16[128,1024]{1,0:T(8,128)(2,1)}) custom-call(s32[3]{0:T(128)} %pad_add_fusion.info, f32[16,512]{1,0:T(8,128)} %pad_maximum_fusion.meta, bf16[896,512]{1,0:T(8,128)(2,1)} %select.9.sel, bf16[512,896]{1,0:T(8,128)(2,1)} %get-tuple-element.35.chosen, ...), custom_call_target="tpu_custom_call" | custom-call | flops 939524096 | bytes 4751372 | tf_op jit(solution)/shard_map/combine/pallas_call | solution.py:40
  188.4 1.5 collective-permute-start.8
  189.8 5.6 %collective-permute-done.10 = bf16[128,1024]{1,0:T(8,128)(2,1)S(1)} collective-permute-done((bf16[128,1024]{1,0:T(8,128)(2,1)}, bf16[128,1024]{1,0:T(8,128)(2,1)S(1)}, u32[]{:S(2)}, u32[]{:S(2)}) %collective-permute-start.10) | collective-permute-done | bytes 262176 | tf_op jit(solution)/shard_map/ppermute | solution.py:334
  195.5 15.1 %collective-permute-done.9 = bf16[128,1024]{1,0:T(8,128)(2,1)S(1)} collective-permute-done((bf16[128,1024]{1,0:T(8,128)(2,1)}, bf16[128,1024]{1,0:T(8,128)(2,1)S(1)}, u32[]{:S(2)}, u32[]{:S(2)}) %collective-permute-start.9) | collective-permute-done | bytes 262176 | tf_op jit(solution)/shard_map/ppermute | solution.py:334
  210.6 1.7 collective-permute-done.8
  212.2 1.9 subtract_convert_fusion
  214.1 1.3 copy-done
  215.4 4.4 %combine_gates.1 = (bf16[144,1024]{1,0:T(8,128)(2,1)}, bf16[144,1024]{1,0:T(8,128)(2,1)}, bf16[144,1024]{1,0:T(8,128)(2,1)}, bf16[144,1024]{1,0:T(8,128)(2,1)}) custom-call(s32[3]{0:T(128)} %pad_add_fusion.info, f32[16,512]{1,0:T(8,128)} %pad_maximum_fusion.meta, bf16[896,512]{1,0:T(8,128)(2,1)} %select.9.sel, bf16[512,896]{1,0:T(8,128)(2,1)} %get-tuple-element.42.chosen, ...), custom_call_target="tpu_custom_call" | custom-call | flops 939524096 | bytes 5013516 | tf_op jit(solution)/shard_map/combine_gates/pallas_call | solution.py:40
  219.8 1.3 collective-permute-start.17
  221.1 1.5 collective-permute-start.16
  222.6 13.9 %expert_weights.1 = (bf16[1,2,704,2048]{3,2,1,0:T(8,128)(2,1)}, bf16[1,704,2048]{2,1,0:T(8,128)(2,1)}) custom-call(s32[3]{0:T(128)} %pad_add_fusion.info, bf16[4,224,1024]{2,1,0:T(8,128)(2,1)} %all_to_all.20.refs_0_, bf16[4,224,1024]{2,1,0:T(8,128)(2,1)} %collective-permute-done.6.refs_1_, bf16[4,240,1024]{2,1,0:T(8,128)(2,1)} %copy-done.2, ...), custom_call_target="tpu_custom_call" | custom-call | flops 7751073792 | bytes 20037644 | tf_op jit(solution)/shard_map/expert_weights/pallas_call | solution.py:40
  236.5 8.8 %collective-permute-done.17 = bf16[144,1024]{1,0:T(8,128)(2,1)S(1)} collective-permute-done((bf16[144,1024]{1,0:T(8,128)(2,1)}, bf16[144,1024]{1,0:T(8,128)(2,1)S(1)}, u32[]{:S(2)}, u32[]{:S(2)}) %collective-permute-start.17) | collective-permute-done | bytes 294944 | tf_op jit(solution)/shard_map/ppermute | solution.py:334
  245.3 2.5 %collective-permute-done.16 = bf16[144,1024]{1,0:T(8,128)(2,1)S(1)} collective-permute-done((bf16[144,1024]{1,0:T(8,128)(2,1)}, bf16[144,1024]{1,0:T(8,128)(2,1)S(1)}, u32[]{:S(2)}, u32[]{:S(2)}) %collective-permute-start.16) | collective-permute-done | bytes 294944 | tf_op jit(solution)/shard_map/ppermute | solution.py:334
  248.4 0.9 add_convert_fusion.2
  (45 shorter events, 3.8 us)
Async XLA Ops:
  2.0 6.8 %collective-permute-start.2 = (f32[16,128]{1,0:T(8,128)S(1)}, f32[16,128]{1,0:T(8,128)S(1)}, u32[]{:S(2)}, u32[]{:S(2)}) collective-permute-start(f32[16,128]{1,0:T(8,128)S(1)} %pad_maximum_fusion.1), channel_id=1, source_target_pairs={{0,24},{2,26},{4,28},{6,30},{8,0},{10,2},{12,4},{14,6},{16,8},{18,... | collective-permute-start | bytes 24584 | tf_op jit(solution)/shard_map/ppermute | solution.py:334
  2.1 6.7 %collective-permute-start.1 = (f32[16,128]{1,0:T(8,128)S(1)}, f32[16,128]{1,0:T(8,128)S(1)}, u32[]{:S(2)}, u32[]{:S(2)}) collective-permute-start(f32[16,128]{1,0:T(8,128)S(1)} %pad_maximum_fusion.1), channel_id=1, source_target_pairs={{0,16},{2,18},{4,20},{6,22},{8,24},{10,26},{12,28},{14,30},{16,0},... | collective-permute-start | bytes 24584 | tf_op jit(solution)/shard_map/ppermute | solution.py:334
  4.5 4.3 %collective-permute-start = (f32[16,128]{1,0:T(8,128)S(1)}, f32[16,128]{1,0:T(8,128)S(1)}, u32[]{:S(2)}, u32[]{:S(2)}) collective-permute-start(f32[16,128]{1,0:T(8,128)S(1)} %pad_maximum_fusion.1), channel_id=1, source_target_pairs={{0,8},{2,10},{4,12},{6,14},{8,16},{10,18},{12,20},{14,22},{16,24},... | collective-permute-start | bytes 24584 | tf_op jit(solution)/shard_map/ppermute | solution.py:334
  6.7 6.5 %collective-permute-start.3 = (bf16[128,1024]{1,0:T(8,128)(2,1)}, bf16[128,1024]{1,0:T(8,128)(2,1)S(1)}, u32[]{:S(2)}, u32[]{:S(2)}) collective-permute-start(bf16[128,1024]{1,0:T(8,128)(2,1)} %refs_0_.1), channel_id=1, source_target_pairs={{0,8},{2,10},{4,12},{6,14},{8,16},{10,18},{12,20},{14,22},{16,24},... | collective-permute-start | bytes 786440 | tf_op jit(solution)/shard_map/ppermute | solution.py:334
  6.8 15.8 %collective-permute-start.5 = (bf16[128,1024]{1,0:T(8,128)(2,1)}, bf16[128,1024]{1,0:T(8,128)(2,1)S(1)}, u32[]{:S(2)}, u32[]{:S(2)}) collective-permute-start(bf16[128,1024]{1,0:T(8,128)(2,1)} %refs_0_.1), channel_id=1, source_target_pairs={{0,24},{2,26},{4,28},{6,30},{8,0},{10,2},{12,4},{14,6},{16,8},{18,... | collective-permute-start | bytes 786440 | tf_op jit(solution)/shard_map/ppermute | solution.py:334
  11.5 18.1 %collective-permute-start.4 = (bf16[128,1024]{1,0:T(8,128)(2,1)}, bf16[128,1024]{1,0:T(8,128)(2,1)S(1)}, u32[]{:S(2)}, u32[]{:S(2)}) collective-permute-start(bf16[128,1024]{1,0:T(8,128)(2,1)} %refs_0_.1), channel_id=1, source_target_pairs={{0,16},{2,18},{4,20},{6,22},{8,24},{10,26},{12,28},{14,30},{16,0},... | collective-permute-start | bytes 786440 | tf_op jit(solution)/shard_map/ppermute | solution.py:334
  13.2 16.3 %copy-start.4 = (bf16[128,1024]{1,0:T(8,128)(2,1)}, bf16[128,1024]{1,0:T(8,128)(2,1)S(1)}, u32[]{:S(2)}) copy-start(bf16[128,1024]{1,0:T(8,128)(2,1)S(1)} %collective-permute-done.3.refs_1_) | copy-start | bytes 786436
  22.5 7.0 %copy-start.5 = (bf16[128,1024]{1,0:T(8,128)(2,1)}, bf16[128,1024]{1,0:T(8,128)(2,1)S(1)}, u32[]{:S(2)}) copy-start(bf16[128,1024]{1,0:T(8,128)(2,1)S(1)} %collective-permute-done.5.refs_3_) | copy-start | bytes 786436
  29.5 0.7 copy-start.8
  34.1 28.1 %copy-start.3 = (bf16[128,1024]{1,0:T(8,128)(2,1)S(1)}, bf16[128,1024]{1,0:T(8,128)(2,1)}, u32[]{:S(2)}) copy-start(bf16[128,1024]{1,0:T(8,128)(2,1)} %refs_0_.2) | copy-start | bytes 786436
  59.8 39.0 %collective-permute-start.6 = (bf16[4,224,1024]{2,1,0:T(8,128)(2,1)}, bf16[4,224,1024]{2,1,0:T(8,128)(2,1)}, u32[]{:S(2)}, u32[]{:S(2)}) collective-permute-start(bf16[4,224,1024]{2,1,0:T(8,128)(2,1)} %all_to_all.20.refs_0_), channel_id=1, source_target_pairs={{0,1},{1,0},{2,3},{3,2},{4,5},{5,4},{6,7},{7,6},{8,9},{9,8},{10,11... | collective-permute-start | bytes 5505032 | tf_op jit(solution)/shard_map/ppermute | solution.py:347
  62.1 10.4 %collective-permute-start.11 = (bf16[128,1024]{1,0:T(8,128)(2,1)S(1)}, bf16[128,1024]{1,0:T(8,128)(2,1)S(1)}, u32[]{:S(2)}, u32[]{:S(2)}) collective-permute-start(bf16[128,1024]{1,0:T(8,128)(2,1)S(1)} %copy-done.3), channel_id=1, source_target_pairs={{0,8},{2,10},{4,12},{6,14},{8,16},{10,18},{12,20},{14,22},{16,24},... | collective-permute-start | bytes 786440 | tf_op jit(solution)/shard_map/ppermute | solution.py:334
  64.0 22.6 %collective-permute-start.12 = (bf16[128,1024]{1,0:T(8,128)(2,1)S(1)}, bf16[128,1024]{1,0:T(8,128)(2,1)S(1)}, u32[]{:S(2)}, u32[]{:S(2)}) collective-permute-start(bf16[128,1024]{1,0:T(8,128)(2,1)S(1)} %copy-done.3), channel_id=1, source_target_pairs={{0,16},{2,18},{4,20},{6,22},{8,24},{10,26},{12,28},{14,30},{16,0},... | collective-permute-start | bytes 786440 | tf_op jit(solution)/shard_map/ppermute | solution.py:334
  67.9 22.4 %collective-permute-start.13 = (bf16[128,1024]{1,0:T(8,128)(2,1)S(1)}, bf16[128,1024]{1,0:T(8,128)(2,1)S(1)}, u32[]{:S(2)}, u32[]{:S(2)}) collective-permute-start(bf16[128,1024]{1,0:T(8,128)(2,1)S(1)} %copy-done.3), channel_id=1, source_target_pairs={{0,24},{2,26},{4,28},{6,30},{8,0},{10,2},{12,4},{14,6},{16,8},{18,... | collective-permute-start | bytes 786440 | tf_op jit(solution)/shard_map/ppermute | solution.py:334
  72.5 17.8 %copy-start.6 = (bf16[128,1024]{1,0:T(8,128)(2,1)}, bf16[128,1024]{1,0:T(8,128)(2,1)S(1)}, u32[]{:S(2)}) copy-start(bf16[128,1024]{1,0:T(8,128)(2,1)S(1)} %collective-permute-done.11.refs_1_) | copy-start | bytes 786436
  86.6 3.7 %copy-start.7 = (bf16[128,1024]{1,0:T(8,128)(2,1)}, bf16[128,1024]{1,0:T(8,128)(2,1)S(1)}, u32[]{:S(2)}) copy-start(bf16[128,1024]{1,0:T(8,128)(2,1)S(1)} %collective-permute-done.12.refs_2_) | copy-start | bytes 786436
  90.3 0.7 copy-start.9
  95.1 26.5 %all-to-all-start.2 = ((bf16[4,240,1024]{2,1,0:T(8,128)(2,1)}), bf16[4,240,1024]{2,1,0:T(8,128)(2,1)S(1)}, u32[]{:S(2)}, u32[]{:S(2)}) async-start(bf16[4,240,1024]{2,1,0:T(8,128)(2,1)} %pack_gates.1), calls=%async_computation.2 | async-start | bytes 3932160 | tf_op jit(solution)/shard_map/all_to_all | solution.py:340
  115.5 7.5 %collective-permute-start.7 = (bf16[4,224,1024]{2,1,0:T(8,128)(2,1)}, bf16[4,224,1024]{2,1,0:T(8,128)(2,1)}, u32[]{:S(2)}, u32[]{:S(2)}) collective-permute-start(bf16[4,224,1024]{2,1,0:T(8,128)(2,1)} %get-tuple-element.37), channel_id=1, source_target_pairs={{0,1},{1,0},{2,3},{3,2},{4,5},{5,4},{6,7},{7,6},{8,9},{9,8},{10,11... | collective-permute-start | bytes 5505032 | tf_op jit(solution)/shard_map/ppermute | solution.py:347
  121.6 5.7 %copy-start.2 = (bf16[4,240,1024]{2,1,0:T(8,128)(2,1)}, bf16[4,240,1024]{2,1,0:T(8,128)(2,1)S(1)}, u32[]{:S(2)}) copy-start(bf16[4,240,1024]{2,1,0:T(8,128)(2,1)S(1)} %all-to-all-done.2.refs_0_.refs_2_) | copy-start | bytes 5898244
  121.6 5.7 %collective-permute-start.14 = (bf16[4,240,1024]{2,1,0:T(8,128)(2,1)S(1)}, bf16[4,240,1024]{2,1,0:T(8,128)(2,1)S(1)}, u32[]{:S(2)}, u32[]{:S(2)}) collective-permute-start(bf16[4,240,1024]{2,1,0:T(8,128)(2,1)S(1)} %all-to-all-done.2.refs_0_.refs_2_), channel_id=1, source_target_pairs={{0,1},{1,0},{2,3},{3,2},{4,5},{5,4},{6,7},{7,6},{8,9},{9,8},{10,11... | collective-permute-start | bytes 5898248 | tf_op jit(solution)/shard_map/ppermute | solution.py:347
  127.2 1.3 copy-start.13
  147.7 4.7 %collective-permute-start.15 = (bf16[4,240,1024]{2,1,0:T(8,128)(2,1)}, bf16[4,240,1024]{2,1,0:T(8,128)(2,1)}, u32[]{:S(2)}, u32[]{:S(2)}) collective-permute-start(bf16[4,240,1024]{2,1,0:T(8,128)(2,1)} %get-tuple-element.50), channel_id=1, source_target_pairs={{0,1},{1,0},{2,3},{3,2},{4,5},{5,4},{6,7},{7,6},{8,9},{9,8},{10,11... | collective-permute-start | bytes 5898248 | tf_op jit(solution)/shard_map/ppermute | solution.py:347
  148.5 25.8 %all-to-all-start.1 = ((bf16[4,224,1024]{2,1,0:T(8,128)(2,1)}), bf16[4,224,1024]{2,1,0:T(8,128)(2,1)S(1)}, u32[]{:S(2)}, u32[]{:S(2)}) async-start(bf16[4,224,1024]{2,1,0:T(8,128)(2,1)} %add_convert_fusion.1), calls=%async_computation.1 | async-start | bytes 3670016 | tf_op jit(solution)/shard_map/all_to_all | solution.py:340
  174.2 1.2 copy-start.1
  175.5 38.6 %all-to-all-start.3 = ((bf16[4,240,1024]{2,1,0:T(8,128)(2,1)}), bf16[4,240,1024]{2,1,0:T(8,128)(2,1)S(1)}, u32[]{:S(2)}, u32[]{:S(2)}) async-start(bf16[4,240,1024]{2,1,0:T(8,128)(2,1)} %add_convert_fusion), calls=%async_computation.3 | async-start | bytes 3932160 | tf_op jit(solution)/shard_map/all_to_all | solution.py:340
  179.1 33.2 %copy-start.10 = (bf16[128,1024]{1,0:T(8,128)(2,1)S(1)}, bf16[128,1024]{1,0:T(8,128)(2,1)}, u32[]{:S(2)}) copy-start(bf16[128,1024]{1,0:T(8,128)(2,1)} %param.9) | copy-start | bytes 786436
  188.2 7.2 %collective-permute-start.10 = (bf16[128,1024]{1,0:T(8,128)(2,1)}, bf16[128,1024]{1,0:T(8,128)(2,1)S(1)}, u32[]{:S(2)}, u32[]{:S(2)}) collective-permute-start(bf16[128,1024]{1,0:T(8,128)(2,1)} %get-tuple-element.41), channel_id=1, source_target_pairs={{0,8},{2,10},{4,12},{6,14},{8,16},{10,18},{12,20},{14,22},{16,24},... | collective-permute-start | bytes 786440 | tf_op jit(solution)/shard_map/ppermute | solution.py:334
  188.2 22.3 %collective-permute-start.9 = (bf16[128,1024]{1,0:T(8,128)(2,1)}, bf16[128,1024]{1,0:T(8,128)(2,1)S(1)}, u32[]{:S(2)}, u32[]{:S(2)}) collective-permute-start(bf16[128,1024]{1,0:T(8,128)(2,1)} %get-tuple-element.40), channel_id=1, source_target_pairs={{0,16},{2,18},{4,20},{6,22},{8,24},{10,26},{12,28},{14,30},{16,0},... | collective-permute-start | bytes 786440 | tf_op jit(solution)/shard_map/ppermute | solution.py:334
  188.4 23.9 %collective-permute-start.8 = (bf16[128,1024]{1,0:T(8,128)(2,1)}, bf16[128,1024]{1,0:T(8,128)(2,1)S(1)}, u32[]{:S(2)}, u32[]{:S(2)}) collective-permute-start(bf16[128,1024]{1,0:T(8,128)(2,1)} %get-tuple-element.39), channel_id=1, source_target_pairs={{0,24},{2,26},{4,28},{6,30},{8,0},{10,2},{12,4},{14,6},{16,8},{18,... | collective-permute-start | bytes 786440 | tf_op jit(solution)/shard_map/ppermute | solution.py:334
  214.1 1.3 copy-start
  219.8 16.7 %collective-permute-start.18 = (bf16[144,1024]{1,0:T(8,128)(2,1)}, bf16[144,1024]{1,0:T(8,128)(2,1)S(1)}, u32[]{:S(2)}, u32[]{:S(2)}) collective-permute-start(bf16[144,1024]{1,0:T(8,128)(2,1)} %get-tuple-element.54), channel_id=1, source_target_pairs={{0,8},{2,10},{4,12},{6,14},{8,16},{10,18},{12,20},{14,22},{16,24},... | collective-permute-start | bytes 884744 | tf_op jit(solution)/shard_map/ppermute | solution.py:334
  219.8 25.5 %collective-permute-start.17 = (bf16[144,1024]{1,0:T(8,128)(2,1)}, bf16[144,1024]{1,0:T(8,128)(2,1)S(1)}, u32[]{:S(2)}, u32[]{:S(2)}) collective-permute-start(bf16[144,1024]{1,0:T(8,128)(2,1)} %get-tuple-element.53), channel_id=1, source_target_pairs={{0,16},{2,18},{4,20},{6,22},{8,24},{10,26},{12,28},{14,30},{16,0},... | collective-permute-start | bytes 884744 | tf_op jit(solution)/shard_map/ppermute | solution.py:334
  221.1 26.7 %collective-permute-start.16 = (bf16[144,1024]{1,0:T(8,128)(2,1)}, bf16[144,1024]{1,0:T(8,128)(2,1)S(1)}, u32[]{:S(2)}, u32[]{:S(2)}) collective-permute-start(bf16[144,1024]{1,0:T(8,128)(2,1)} %get-tuple-element.52), channel_id=1, source_target_pairs={{0,24},{2,26},{4,28},{6,30},{8,0},{10,2},{12,4},{14,6},{16,8},{18,... | collective-permute-start | bytes 884744 | tf_op jit(solution)/shard_map/ppermute | solution.py:334
  222.6 25.2 %copy-start.12 = (bf16[144,1024]{1,0:T(8,128)(2,1)S(1)}, bf16[144,1024]{1,0:T(8,128)(2,1)}, u32[]{:S(2)}) copy-start(bf16[144,1024]{1,0:T(8,128)(2,1)} %get-tuple-element.51) | copy-start | bytes 884740
  222.6 25.8 %copy-start.11 = (bf16[128,1024]{1,0:T(8,128)(2,1)S(1)}, bf16[128,1024]{1,0:T(8,128)(2,1)}, u32[]{:S(2)}) copy-start(bf16[128,1024]{1,0:T(8,128)(2,1)} %param.10) | copy-start | bytes 786436

commit v4 on v3

v4 whole, which is shorter than its diff:
```python
import functools

import jax
import jax.numpy as jnp
from jax import lax
from jax.experimental import pallas as pl
from jax.experimental.pallas import tpu as pltpu
from jax.sharding import PartitionSpec as P

PLANE = 4
TAIL = 16
VMEM_LIMIT = 56 * 1024 * 1024
F32 = jnp.float32
BF16 = jnp.bfloat16


def dot_nn(a, b):
    return lax.dot_general(a, b, (((1,), (0,)), ((), ())), preferred_element_type=F32)


def dot_nt(a, b):
    return lax.dot_general(a, b, (((1,), (1,)), ((), ())), preferred_element_type=F32)


def dot_tn(a, b):
    return lax.dot_general(a, b, (((0,), (0,)), ((), ())), preferred_element_type=F32)


def iota(shape, axis):
    return lax.broadcasted_iota(jnp.int32, shape, axis)


SMEM = pl.BlockSpec(memory_space=pltpu.SMEM)
VMEM = pl.BlockSpec(memory_space=pltpu.VMEM)
HBM = pl.BlockSpec(memory_space=pl.ANY)


def call(kernel, outs, args, specs, out_specs=None, scratch=(), name=None):
    return pl.pallas_call(
        kernel,
        out_shape=outs,
        in_specs=specs,
        out_specs=out_specs if out_specs is not None else [VMEM] * len(outs),
        scratch_shapes=list(scratch),
        compiler_params=pltpu.CompilerParams(vmem_limit_bytes=VMEM_LIMIT),
        cost_estimate=pl.CostEstimate(flops=1024, bytes_accessed=1024, transcendentals=0),
        name=name,
    )(*args)


def shape(*dims, dtype=BF16):
    return jax.ShapeDtypeStruct(dims, dtype)


def outer_meta(info, meta, s, zn):
    return meta[lax.rem(info[3] - s + zn, zn)]


def select_kernel(info, meta, sel, *, zn, pn, tokens, picks, cap):
    rows = zn * cap
    partner = iota((8, 1), 0)
    experts = jnp.where(partner < pn, info[0] + (partner ^ info[1]), -2).astype(F32)
    before = (iota((tokens, tokens), 0) < iota((tokens, tokens), 1)).astype(F32).astype(BF16)
    slot = iota((rows, tokens), 0).astype(F32)
    for s in range(zn):
        here = slice(s * tokens, (s + 1) * tokens)
        ids = outer_meta(info, meta, s, zn)
        named = jnp.zeros((8, tokens), F32)
        for k in range(picks):
            named += (ids[k : k + 1, :] == experts).astype(F32)
        dest = dot_nn(named.astype(BF16), before) + s * cap
        dest = jnp.where(named > 0, dest, -1.0)
        for q in range(pn):
            sel[q * rows : (q + 1) * rows, here] = (
                (slot == dest[q : q + 1, :]).astype(F32).astype(BF16)
            )


def route_kernel(info, meta, ones, gated, *, zn, pn, tokens, picks, cap):
    rows = zn * cap
    partner = iota((1, 8), 1)
    experts = jnp.where(partner < pn, info[0] + (partner ^ info[1]), -2).astype(F32)
    after = (iota((tokens, tokens), 1) < iota((tokens, tokens), 0)).astype(F32).astype(BF16)
    eye = (iota((16, 16), 0) == iota((16, 16), 1)).astype(F32).astype(BF16)
    lane = iota((tokens, pn * rows), 1).astype(F32)
    for s in range(zn):
        here = slice(s * tokens, (s + 1) * tokens)
        columned = dot_tn(outer_meta(info, meta, s, zn).astype(BF16), eye)
        named = jnp.zeros((tokens, 8), F32)
        gate = jnp.zeros((tokens, 8), F32)
        for k in range(picks):
            match = (columned[:, k : k + 1] == experts).astype(F32)
            named += match
            gate += match * columned[:, 8 + k : 9 + k]
        dest = dot_nn(after, named.astype(BF16)) + s * cap
        dest = jnp.where(named > 0, dest + rows * partner.astype(F32), -1.0)
        picked = jnp.zeros((tokens, pn * rows), F32)
        weighed = jnp.zeros((tokens, pn * rows), F32)
        for q in range(pn):
            match = lane == dest[:, q : q + 1]
            picked += match.astype(F32)
            weighed += jnp.where(match, gate[:, q : q + 1], 0.0)
        ones[here, :] = picked.astype(BF16)
        gated[here, :] = weighed.astype(BF16)


def pack_kernel(info, meta, sel, *refs, zn, pn, tokens, picks, rows, gates):
    sources, outs, whole = refs[:zn], refs[zn : zn + pn], refs[zn + pn]
    for s in range(zn):
        whole[s * tokens : (s + 1) * tokens, :] = sources[s][...]
    for q in range(pn):
        chosen = sel[q * rows : (q + 1) * rows, :]
        out = outs[q]
        out[0:rows, :] = dot_nn(chosen, whole[...]).astype(BF16)
        if gates:
            expert = (info[0] + (info[1] ^ q)).astype(F32)
            tail = jnp.zeros((TAIL, rows), F32)
            for s in range(zn):
                known = outer_meta(info, meta, s, zn)
                gate = jnp.zeros((1, tokens), F32)
                for k in range(picks):
                    gate += jnp.where(known[k : k + 1, :] == expert, known[8 + k : 9 + k, :], 0.0)
                gate = jnp.broadcast_to(gate, (TAIL, tokens)).astype(BF16)
                tail += dot_nt(gate, chosen[:, s * tokens : (s + 1) * tokens])
            out[rows : rows + TAIL, :] = jnp.zeros((TAIL, out.shape[1]), BF16)
            out[rows : rows + TAIL, 0:rows] = tail.astype(BF16)


def combine_kernel(info, meta, sel, chosen, *refs, zn, pn, tokens, rows, gates):
    backs, outs, whole = refs[:pn], refs[pn : pn + zn], refs[pn + zn]
    cols = whole.shape[1]
    for q in range(pn):
        whole[q * rows : (q + 1) * rows, :] = backs[q][0:rows, :]
    if gates:
        spreads = []
        for q in range(pn):
            row = backs[q][rows : rows + TAIL, 0:rows]
            spreads.append(dot_nn(row, sel[q * rows : (q + 1) * rows, :])[0:8, :])
    for s in range(zn):
        here = slice(s * tokens, (s + 1) * tokens)
        outs[s][0:tokens, :] = dot_nn(chosen[here, :], whole[...]).astype(BF16)
        if gates:
            outs[s][tokens : tokens + TAIL, :] = jnp.zeros((TAIL, cols), BF16)
            ids = outer_meta(info, meta, s, zn)[0:8, :]
            total = jnp.zeros((8, tokens), F32)
            for q in range(pn):
                expert = (info[0] + (info[1] ^ q)).astype(F32)
                total += jnp.where(ids == expert, spreads[q][:, here], 0.0)
            total = jnp.concatenate([total, jnp.zeros((TAIL - 8, tokens), F32)], axis=0)
            outs[s][tokens : tokens + TAIL, 0:tokens] = total.astype(BF16)


class Loads:
    def __init__(self, sems):
        self.sems, self.copies, self.waited = sems, {}, set()

    def add(self, key, source, target):
        self.copies[key] = pltpu.make_async_copy(source, target, self.sems.at[len(self.copies)])
        self.copies[key].start()

    def need(self, *keys):
        for key in keys:
            if key not in self.waited:
                self.waited.add(key)
                self.copies[key].wait()

    def finish(self):
        self.need(*self.copies)


def column_block(info, j, nt, cols):
    block = lax.rem(info[2] - j + nt, nt)
    return pl.ds(pl.multiple_of(block * cols, 128), cols)


def load_weight(loads, info, kind, source, target, blocks, nt, cols):
    for at, j in enumerate(blocks):
        block = source.at[:, column_block(info, j, nt, cols)]
        loads.add((kind, j), block, target.at[:, pl.ds(at * cols, cols)])


def by_core(refs, nt, pn):
    return [refs[j * pn : (j + 1) * pn] for j in range(nt)]


def load_rows(loads, sources, target, group, rows, cols):
    for j, pieces in enumerate(sources):
        for q in group:
            to = target.at[pl.ds(q * rows, rows), pl.ds(j * cols, cols)]
            loads.add(("r", j, q), pieces[q].at[pl.ds(0, rows)], to)


def forward_kernel(info, *refs, nt, pn, rows, cols):
    xs, refs = by_core(refs, nt, pn), refs[nt * pn :]
    win, wout, outs, refs = refs[0], refs[1], refs[2 : nt + 1], refs[nt + 1 :]
    hid, a1, a2, x, wg, wu, wd, stage, in_sems, out_sems = refs
    loads, stores = Loads(in_sems), Loads(out_sems)
    every, others = range(nt), [(nt - j) % nt for j in range(1, nt)]
    groups = [(2 * g, 2 * g + 1) for g in range(pn // 2)]
    load_rows(loads, xs, x, groups[0], rows, cols)
    load_weight(loads, info, "g", win.at[0, 0], wg, every, nt, cols)
    load_weight(loads, info, "u", win.at[0, 1], wu, every, nt, cols)
    for group in groups[1:]:
        load_rows(loads, xs, x, group, rows, cols)
    load_weight(loads, info, "d", wout.at[0], wd, others, nt, cols)
    for g, group in enumerate(groups):
        here = slice(2 * g * rows, 2 * (g + 1) * rows)
        loads.need(*(("r", j, q) for j in every for q in group), *(("g", j) for j in every))
        gate = dot_nt(x[here, :], wg[...])
        loads.need(*(("u", j) for j in every))
        up = dot_nt(x[here, :], wu[...])
        sigma = jax.nn.sigmoid(gate)
        active = gate * sigma
        hidden = (active * up).astype(BF16)
        hid[here, :] = hidden
        a1[here, :] = (up * sigma * (1.0 + gate * (1.0 - sigma))).astype(BF16)
        a2[here, :] = active.astype(BF16)
        loads.need(*(("d", j) for j in others))
        part = dot_nn(hidden, wd[...]).astype(BF16)
        span = pl.ds(2 * g, 2)
        for j in range(nt - 1):
            stage[j, 2 * g : 2 * g + 2] = part[:, j * cols : (j + 1) * cols].reshape(2, rows, cols)
            stores.add((g, j), stage.at[j, span], outs[j].at[span])
    loads.finish()
    stores.finish()


def output_kernel(info, *refs, nt, pn, rows, cols):
    hid, recvs, wout, outs = refs[0], refs[1:nt], refs[nt], refs[nt + 1 : nt + 1 + pn]
    h, got, wd, stage, in_sems, out_sems = refs[nt + 1 + pn :]
    loads, stores = Loads(in_sems), Loads(out_sems)
    loads.add("h", hid, h)
    load_weight(loads, info, "d", wout.at[0], wd, (0,), nt, cols)
    for j in range(nt - 1):
        for g in range(pn // 2):
            span = pl.ds(2 * g, 2)
            loads.add(("r", j, g), recvs[j].at[span], got.at[j, span])
    for g in range(pn // 2):
        here = slice(2 * g * rows, 2 * (g + 1) * rows)
        loads.need("h", ("d", 0))
        part = dot_nn(h[here, :], wd[...])
        for j in range(nt - 1):
            loads.need(("r", j, g))
            part += got[j, 2 * g : 2 * g + 2].reshape(2 * rows, cols).astype(F32)
        stage[2 * g : 2 * g + 2] = part.astype(BF16).reshape(2, rows, cols)
        for q in (2 * g, 2 * g + 1):
            stores.add(q, stage.at[q], outs[q])
    loads.finish()
    stores.finish()


def backward_kernel(info, *refs, nt, pn, rows, cols):
    cs, refs = by_core(refs, nt, pn), refs[nt * pn :]
    (win, wout, hid, a1, a2), refs = refs[:5], refs[5:]
    outs, (own_tails, gg, ug, hs), refs = refs[: nt - 1], refs[nt - 1 : nt + 3], refs[nt + 3 :]
    c, tails, h, b1, b2, wg, wu, wd, stage, in_sems, out_sems = refs
    loads, stores = Loads(in_sems), Loads(out_sems)
    every, others = range(nt), [(nt - j) % nt for j in range(1, nt)]
    groups = [(2 * g, 2 * g + 1) for g in range(pn // 2)]
    load_rows(loads, cs, c, groups[0], rows, cols)
    load_weight(loads, info, "d", wout.at[0], wd, every, nt, cols)
    for q in range(pn):
        loads.add(("t", q), cs[0][q].at[pl.ds(rows, TAIL)], tails.at[q])
    for key, source, target in (("h", hid, h), ("1", a1, b1), ("2", a2, b2)):
        loads.add(key, source, target)
    load_weight(loads, info, "g", win.at[0, 0], wg, others, nt, cols)
    load_weight(loads, info, "u", win.at[0, 1], wu, others, nt, cols)
    for group in groups[1:]:
        load_rows(loads, cs, c, group, rows, cols)
    same = iota((rows, rows), 0) == iota((rows, rows), 1)
    for g, group in enumerate(groups):
        here = slice(2 * g * rows, 2 * (g + 1) * rows)
        loads.need(*(("r", j, q) for j in every for q in group), *(("d", j) for j in every))
        grad = dot_nt(c[here, :], wd[...])
        loads.need("h", "1", "2", *(("t", q) for q in group))
        hidden = h[here, :].astype(F32)
        piece = jnp.sum(grad * hidden, axis=1, keepdims=True)
        gates = []
        for at, q in enumerate(group):
            row = tails[q, :, 0:rows].astype(F32)[0:1, :]
            gates.append(jnp.sum(jnp.where(same, row, 0.0), axis=1, keepdims=True))
            part = piece[at * rows : (at + 1) * rows, :]
            part = jnp.sum(jnp.where(same, part, 0.0), axis=0, keepdims=True)
            part = jnp.broadcast_to(part, (TAIL, rows)).astype(BF16)
            own_tails[q] = jnp.zeros((TAIL, cols), BF16)
            own_tails[q, :, 0:rows] = part
            for j in range(nt - 1):
                stage[j, q, rows : rows + TAIL, :] = jnp.zeros((TAIL, cols), BF16)
                stage[j, q, rows : rows + TAIL, 0:rows] = part
        gate = jnp.concatenate(gates, axis=0)
        grad = gate * grad
        hs[here, :] = (gate * hidden).astype(BF16)
        gate_grad = (grad * b1[here, :].astype(F32)).astype(BF16)
        up_grad = (grad * b2[here, :].astype(F32)).astype(BF16)
        gg[here, :] = gate_grad
        ug[here, :] = up_grad
        loads.need(*((k, j) for k in "gu" for j in others))
        part = (dot_nn(gate_grad, wg[...]) + dot_nn(up_grad, wu[...])).astype(BF16)
        span = pl.ds(2 * g, 2)
        for j in range(nt - 1):
            block = part[:, j * cols : (j + 1) * cols].reshape(2, rows, cols)
            stage[j, 2 * g : 2 * g + 2, 0:rows, :] = block
            stores.add((g, j), stage.at[j, span], outs[j].at[span])
    loads.finish()
    stores.finish()


def input_kernel(info, *refs, nt, pn, rows, cols):
    gg, ug, own_tails, recvs, win = *refs[:3], refs[3 : nt + 2], refs[nt + 2]
    outs, refs = refs[nt + 3 : nt + 3 + pn], refs[nt + 3 + pn :]
    left, got, wg, wu, stage, in_sems, out_sems = refs
    loads, stores = Loads(in_sems), Loads(out_sems)
    loads.add("gg", gg, left.at[0])
    load_weight(loads, info, "g", win.at[0, 0], wg, (0,), nt, cols)
    loads.add("ug", ug, left.at[1])
    load_weight(loads, info, "u", win.at[0, 1], wu, (0,), nt, cols)
    for j in range(nt - 1):
        for g in range(pn // 2):
            span = pl.ds(2 * g, 2)
            loads.add(("r", j, g), recvs[j].at[span], got.at[j, span])
    for g in range(pn // 2):
        here = slice(2 * g * rows, 2 * (g + 1) * rows)
        both = slice(2 * g, 2 * g + 2)
        loads.need("gg", ("g", 0))
        part = dot_nn(left[0, here, :], wg[...])
        loads.need("ug", ("u", 0))
        part += dot_nn(left[1, here, :], wu[...])
        tail = own_tails[both].astype(F32)
        for j in range(nt - 1):
            loads.need(("r", j, g))
            part += got[j, both, 0:rows, :].reshape(2 * rows, cols).astype(F32)
            tail += got[j, both, rows : rows + TAIL, :].astype(F32)
        stage[both, 0:rows, :] = part.astype(BF16).reshape(2, rows, cols)
        stage[both, rows : rows + TAIL, :] = tail.astype(BF16)
        for q in (2 * g, 2 * g + 1):
            stores.add(q, stage.at[q], outs[q])
    loads.finish()
    stores.finish()


def weights_kernel(info, *refs, nt, pn, rows, cols):
    n = nt * pn
    xs, cs, lefts = by_core(refs, nt, pn), by_core(refs[n:], nt, pn), refs[2 * n : 2 * n + 3]
    gin, gout, left, right, stage, in_sems, out_sems = refs[2 * n + 3 :]
    loads, stores = Loads(in_sems), Loads(out_sems)
    order = ((0, 0, xs), (1, 0, xs), (2, 1, cs))
    for w, side, sources in order:
        loads.add(("l", w), lefts[w], left.at[w])
        if w == 1:
            continue
        for j in range(nt):
            for q in range(pn):
                target = right.at[side, j, pl.ds(q * rows, rows)]
                loads.add((side, j, q), sources[j][q].at[pl.ds(0, rows)], target)
    for w, side, _ in order:
        loads.need(("l", w))
        for j in range(nt):
            loads.need(*((side, j, q) for q in range(pn)))
            at = column_block(info, j, nt, cols)
            stage[j, w] = dot_tn(left[w], right[side, j]).astype(BF16)
            target = gout.at[0, :, at] if w == 2 else gin.at[0, w, :, at]
            stores.add((j, w), stage.at[j, w], target)
    loads.finish()
    stores.finish()


def after(value, *others):
    return lax.optimization_barrier((value, *others))[0]


def body(
    first_half,
    second_half,
    first_grad,
    second_grad,
    expert_ids,
    gate_weights,
    expert_in,
    expert_out,
):
    tokens, picks = expert_ids.shape
    groups = lax.axis_size("expert")
    nt = lax.axis_size("tensor")
    pn = PLANE
    zn = groups // pn
    cap = tokens * picks * 7 // (6 * groups)
    rows = zn * cap
    slots = pn * rows
    cols = first_half.shape[1]
    hid_n = expert_out.shape[1]
    me = lax.axis_index("expert")
    info = jnp.stack([(me // pn) * pn, me % pn, lax.axis_index("tensor"), me // pn]).astype(jnp.int32)

    def outer_send(value, s):
        if s % zn == 0:
            return value
        return lax.ppermute(
            value, "expert", [(e, ((e // pn + s) % zn) * pn + e % pn) for e in range(groups)]
        )

    def inner_send(value, q):
        if q == 0:
            return value
        return lax.ppermute(value, "expert", [(e, e ^ q) for e in range(groups)])

    def inner_exchange(pieces):
        return [inner_send(piece, q) for q, piece in enumerate(pieces)]

    def tensor_send(value, j):
        if j == 0:
            return value
        return lax.ppermute(value, "tensor", [(c, (c + j) % nt) for c in range(nt)])

    fixed = dict(zn=zn, pn=pn, tokens=tokens)

    own = jnp.concatenate(
        [
            jnp.pad(expert_ids.T.astype(F32), ((0, 8 - picks), (0, 0)), constant_values=-1.0),
            jnp.pad(gate_weights.T.astype(F32), ((0, 8 - picks), (0, 0))),
        ],
        axis=0,
    )
    columns = [[z * pn + q for z in range(zn)] for q in range(pn)]
    meta = lax.all_to_all(
        jnp.broadcast_to(own[None], (zn,) + own.shape),
        "expert",
        split_axis=0,
        concat_axis=0,
        axis_index_groups=columns,
        tiled=True,
    )
    sel = call(
        functools.partial(select_kernel, **fixed, picks=picks, cap=cap),
        [shape(slots, zn * tokens)],
        [info, meta],
        [SMEM, VMEM],
        name="select",
    )[0]
    x_parts = [outer_send(first_half, s) for s in range(zn)]

    def pack(sel, parts, gates):
        return call(
            functools.partial(pack_kernel, **fixed, picks=picks, rows=rows, gates=gates),
            [shape(rows + TAIL if gates else rows, cols)] * pn,
            [info, meta, sel, *parts],
            [SMEM] + [VMEM] * (2 + zn),
            scratch=[pltpu.VMEM((zn * tokens, cols), BF16)],
                name="pack_gates" if gates else "pack",
        )

    def combine(chosen, backs, gates):
        parts = call(
            functools.partial(combine_kernel, **fixed, rows=rows, gates=gates),
            [shape(tokens + TAIL if gates else tokens, cols)] * zn,
            [info, meta, sel, chosen, *backs],
            [SMEM] + [VMEM] * (3 + pn),
            scratch=[pltpu.VMEM((slots, cols), BF16)],
                name="combine_gates" if gates else "combine",
        )
        return [outer_send(part, -s) for s, part in enumerate(parts)]

    sizes = dict(nt=nt, pn=pn, rows=rows, cols=cols)

    x_packed = pack(sel, x_parts, False)
    x_here = inner_exchange(x_packed)
    xs = [tensor_send(piece, j) for j in range(nt) for piece in x_here]
    grad_whole = after(second_grad, *x_parts[1:])
    c_parts = [outer_send(grad_whole, s) for s in range(zn)]
    ones, gated = call(
        functools.partial(route_kernel, **fixed, picks=picks, cap=cap),
        [shape(zn * tokens, slots)] * 2,
        [info, after(meta, *x_packed)],
        [SMEM, VMEM],
        name="route",
    )
    c_packed = pack(after(sel, ones), c_parts, True)
    c_here = inner_exchange(c_packed)

    dma = pltpu.SemaphoreType.DMA
    forward = call(
        functools.partial(forward_kernel, **sizes),
        [shape(pn, rows, cols)] * (nt - 1) + [shape(slots, hid_n)] * 3,
        [after(info, *c_packed), *xs, expert_in, expert_out],
        [SMEM] + [HBM] * (nt * pn + 2),
        out_specs=[HBM] * (nt - 1) + [VMEM] * 3,
        scratch=[pltpu.VMEM((slots, nt * cols), BF16)]
        + [pltpu.VMEM((hid_n, nt * cols), BF16)] * 2
        + [pltpu.VMEM((hid_n, (nt - 1) * cols), BF16)]
        + [pltpu.VMEM((nt - 1, pn, rows, cols), BF16), dma(((3 + pn) * nt - 1,))]
        + [dma((pn // 2 * (nt - 1),))],
        name="expert_forward",
    )
    outs, (hid, a1, a2) = forward[: nt - 1], forward[nt - 1 :]
    outs = [after(part, *c_here) for part in outs]
    c_here = [after(piece, hid) for piece in c_here]
    cs = [tensor_send(piece, j) for j in range(nt) for piece in c_here]
    out_here = call(
        functools.partial(output_kernel, **sizes),
        [shape(rows, cols)] * pn,
        [info, hid, *(tensor_send(out, j + 1) for j, out in enumerate(outs)), expert_out],
        [SMEM] + [HBM] * (nt + 1),
        out_specs=[HBM] * pn,
        scratch=[pltpu.VMEM((slots, hid_n), BF16), pltpu.VMEM((nt - 1, pn, rows, cols), BF16)]
        + [pltpu.VMEM((hid_n, cols), BF16), pltpu.VMEM((pn, rows, cols), BF16)]
        + [dma((2 + pn // 2 * (nt - 1),)), dma((pn,))],
        name="expert_output",
    )
    out_back = inner_exchange(out_here)

    backward = call(
        functools.partial(backward_kernel, **sizes),
        [shape(pn, rows + TAIL, cols)] * (nt - 1)
        + [shape(pn, TAIL, cols)]
        + [shape(slots, hid_n)] * 3,
        [info, *cs, expert_in, expert_out, after(hid, *out_here), a1, a2],
        [SMEM] + [HBM] * (nt * pn + 5),
        out_specs=[HBM] * (nt - 1) + [VMEM] * 4,
        scratch=[pltpu.VMEM((slots, nt * cols), BF16), pltpu.VMEM((pn, TAIL, cols), BF16)]
        + [pltpu.VMEM((slots, hid_n), BF16)] * 3
        + [pltpu.VMEM((hid_n, (nt - 1) * cols), BF16)] * 2
        + [pltpu.VMEM((hid_n, nt * cols), BF16)]
        + [pltpu.VMEM((nt - 1, pn, rows + TAIL, cols), BF16), dma(((3 + pn) * nt + 1 + pn,))]
        + [dma((pn // 2 * (nt - 1),))],
        name="expert_backward",
    )
    grads, (tails, gg, ug, hs) = backward[: nt - 1], backward[nt - 1 :]
    grads = [after(part, *out_back) for part in grads]
    dx_here = call(
        functools.partial(input_kernel, **sizes),
        [shape(rows + TAIL, cols)] * pn,
        [info, gg, ug, tails, *(tensor_send(part, j + 1) for j, part in enumerate(grads)), expert_in],
        [SMEM] + [HBM] * 2 + [VMEM] + [HBM] * nt,
        out_specs=[HBM] * pn,
        scratch=[pltpu.VMEM((2, slots, hid_n), BF16)]
        + [pltpu.VMEM((nt - 1, pn, rows + TAIL, cols), BF16)]
        + [pltpu.VMEM((hid_n, cols), BF16)] * 2
        + [pltpu.VMEM((pn, rows + TAIL, cols), BF16)]
        + [dma((4 + pn // 2 * (nt - 1),)), dma((pn,))],
        name="expert_input",
    )
    dx_back = inner_exchange(dx_here)
    out_parts = combine(gated, out_back, False)
    grad_parts = combine(ones, dx_back, True)

    grad_in, grad_out = call(
        functools.partial(weights_kernel, **sizes),
        [shape(*expert_in.shape), shape(*expert_out.shape)],
        [info, *xs, *cs, gg, ug, after(hs, *dx_here)],
        [SMEM] + [HBM] * (2 * nt * pn + 3),
        out_specs=[HBM, HBM],
        scratch=[
            pltpu.VMEM((3, slots, hid_n), BF16),
            pltpu.VMEM((2, nt, slots, cols), BF16),
            pltpu.VMEM((nt, 3, hid_n, cols), BF16),
            pltpu.SemaphoreType.DMA((3 + 2 * nt * pn,)),
            pltpu.SemaphoreType.DMA((3 * nt,)),
        ],
        name="expert_weights",
    )

    branch = sum(part.astype(F32) for part in out_parts)
    input_sum = sum(part[:tokens].astype(F32) for part in grad_parts)
    gate_sum = sum(part[tokens : tokens + picks, :tokens].astype(F32) for part in grad_parts)
    restored = (second_half.astype(F32) - branch).astype(BF16)
    carried_grad = (first_grad.astype(F32) + input_sum).astype(BF16)
    return (restored, carried_grad, gate_sum.T, grad_in, grad_out)


def solution(mesh):
    in_specs = (
        P("expert", "tensor"),
        P("expert", "tensor"),
        P("expert", "tensor"),
        P("expert", "tensor"),
        P("expert", None),
        P("expert", None),
        P("expert", None, "tensor", None),
        P("expert", "tensor", None),
    )
    out_specs = (
        P("expert", "tensor"),
        P("expert", "tensor"),
        P("expert", None),
        P("expert", None, "tensor", None),
        P("expert", "tensor", None),
    )
    return jax.shard_map(body, mesh=mesh, in_specs=in_specs, out_specs=out_specs, check_vma=False)
```

time: 250 us -> 204 us (0.82)
  waiting for transfers between devices: 96.2 us -> 54.4 us
  blocking collectives: 25.7 us -> 0 us
  starting transfers between devices: 33.7 us -> 50.7 us
  other arithmetic: 14.5 us -> 4.42 us
  Pallas kernels: 73.1 us -> 82.8 us
  local copies, waits for them, and re-layouts: 5.29 us -> 8.6 us
    ppermute x15 -> x12, waiting for transfers between devices: 73.3 us -> 13.9 us  [outer_send(): lax.ppermute(value, 'expert', [(e, (e // pn + s) % zn * pn + e % pn) for...]
    all_to_all x1 -> x0, blocking collectives: 25.7 us -> none  [inner_exchange(): lax.all_to_all(value, 'expert', split_axis=0, concat_axis=0, axis_index_g...]
    ppermute x0 -> x12, waiting for transfers between devices: none -> 14 us  [inner_send(): return lax.ppermute(value, 'expert', [(e, e ^ q) for e in range(groups)])]
    ppermute x0 -> x12, starting transfers between devices: none -> 10.7 us  [inner_send(): return lax.ppermute(value, 'expert', [(e, e ^ q) for e in range(groups)])]
    ppermute x4 -> x10, waiting for transfers between devices: 0.36 us -> 10.3 us  [tensor_send(): return lax.ppermute(value, 'tensor', [(c, (c + j) % nt) for c in range(nt)])]
    pallas_call x9 -> x11, Pallas kernels: 73.1 us -> 82.8 us  [call(): pl.pallas_call(kernel, out_shape=outs, in_specs=specs, out_specs=out_spec...]
    convert_element_type x2 -> x0, other arithmetic: 8.49 us -> none  [core_sum(): return total.astype(BF16)]
    ppermute x4 -> x10, starting transfers between devices: 5.51 us -> 13.8 us  [tensor_send(): return lax.ppermute(value, 'tensor', [(c, (c + j) % nt) for c in range(nt)])]
  transfers between devices with their start and end apart: 22 -> 35, of which waited for: 14 -> 12; matrix products, arithmetic and copies ran while one was open for 5% -> 2% of each run, Pallas kernels for 18% -> 35%
where the time goes in v4:
time: 204 us; the launch traced here: 202 us
  Pallas kernels  82.8 us (41%)
  waiting for transfers between devices  54.4 us (27%)
  starting transfers between devices  50.7 us (25%)
  local copies, waits for them, and re-layouts  8.6 us (4%)
  other arithmetic  4.42 us (2%)
    pallas_call x11, Pallas kernels, call(): pl.pallas_call(kernel, out_shape=outs, in_specs=specs, out_specs=out_spec...  82.8 us
    ppermute x12, starting transfers between devices, outer_send(): lax.ppermute(value, 'expert', [(e, (e // pn + s) % zn * pn + e % pn) for...  21.8 us
    all_to_all x1, waiting for transfers between devices, body(): lax.all_to_all(jnp.broadcast_to(own[None], (zn,) + own.shape), 'expert',...  16.1 us
    ppermute x12, waiting for transfers between devices, inner_send(): return lax.ppermute(value, 'expert', [(e, e ^ q) for e in range(groups)])  14 us
    ppermute x12, waiting for transfers between devices, outer_send(): lax.ppermute(value, 'expert', [(e, (e // pn + s) % zn * pn + e % pn) for...  13.9 us
    ppermute x10, starting transfers between devices, tensor_send(): return lax.ppermute(value, 'tensor', [(c, (c + j) % nt) for c in range(nt)])  13.8 us
    ppermute x12, starting transfers between devices, inner_send(): return lax.ppermute(value, 'expert', [(e, e ^ q) for e in range(groups)])  10.7 us
    ppermute x10, waiting for transfers between devices, tensor_send(): return lax.ppermute(value, 'tensor', [(c, (c + j) % nt) for c in range(nt)])  10.3 us
  transfers between devices with their start and end apart: 35, of which 12 were waited for; matrix products, arithmetic and copies ran while one was open for 2% of the time, Pallas kernels for 35%

profile of v4, /device:TPU:9, one launch (start us, length us, event | category | flops | bytes accessed | tf_op | source)
XLA Modules:
  0.0 201.8 jit_solution(9236148595034785308)
XLA Ops:
  0.6 1.3 collective-permute-start
  2.0 1.1 collective-permute-start.1
  3.1 1.4 collective-permute-start.2
  6.5 4.3 %all-to-all-start = ((f32[4,16,128]{2,1,0:T(8,128)}), f32[4,16,128]{2,1,0:T(8,128)S(1)}, u32[]{:S(2)}, u32[]{:S(2)}) async-start(f32[4,16,128]{2,1,0:T(8,128)} %broadcast_in_dim.2), calls=%async_computation | async-start | bytes 65536 | tf_op jit(solution)/shard_map/all_to_all | solution.py:424
  11.4 16.1 %all-to-all-done.meta = f32[4,16,128]{2,1,0:T(8,128)S(1)} async-done(((f32[4,16,128]{2,1,0:T(8,128)}), f32[4,16,128]{2,1,0:T(8,128)S(1)}, u32[]{:S(2)}, u32[]{:S(2)}) %all-to-all-start) | async-done | bytes 32800 | tf_op jit(solution)/shard_map/all_to_all | solution.py:424
  28.1 2.1 %select.11.sel = bf16[896,512]{1,0:T(8,128)(2,1)} custom-call(s32[4]{0:T(128)} %pad_add_fusion.info, f32[4,16,128]{2,1,0:T(8,128)} %copy-done.17), custom_call_target="tpu_custom_call" | custom-call | flops 1024 | bytes 1024 | tf_op jit(solution)/shard_map/select/pallas_call | solution.py:39
  31.7 3.4 %pack.1 = (bf16[224,1024]{1,0:T(8,128)(2,1)}, bf16[224,1024]{1,0:T(8,128)(2,1)}, bf16[224,1024]{1,0:T(8,128)(2,1)}, bf16[224,1024]{1,0:T(8,128)(2,1)}) custom-call(s32[4]{0:T(128)} %pad_add_fusion.info, f32[4,16,128]{2,1,0:T(8,128)} %copy-done.17, bf16[896,512]{1,0:T(8,128)(2,1)} %select.11.sel, bf16[128,1024]{1,0:T(8,128)(2,1)} %refs_0_.1, ...), custom_call_target="tpu_custom_call" | custom-call | flops 1024 | bytes 1024 | tf_op jit(solution)/shard_map/pack/pallas_call | solution.py:39
  35.1 1.2 collective-permute-start.6
  36.3 3.1 %collective-permute-start.4 = (bf16[128,1024]{1,0:T(8,128)(2,1)S(1)}, bf16[128,1024]{1,0:T(8,128)(2,1)S(1)}, u32[]{:S(2)}, u32[]{:S(2)}) collective-permute-start(bf16[128,1024]{1,0:T(8,128)(2,1)S(1)} %copy-done.24), channel_id=1, source_target_pairs={{0,16},{2,18},{4,20},{6,22},{8,24},{10,26},{12,28},{14,30},{16,0},... | collective-permute-start | bytes 786440 | tf_op jit(solution)/shard_map/ppermute | solution.py:397
  39.4 1.2 collective-permute-start.7
  40.9 2.4 %collective-permute-done.3.refs_1_ = bf16[128,1024]{1,0:T(8,128)(2,1)S(1)} collective-permute-done((bf16[128,1024]{1,0:T(8,128)(2,1)S(1)}, bf16[128,1024]{1,0:T(8,128)(2,1)S(1)}, u32[]{:S(2)}, u32[]{:S(2)}) %collective-permute-start.3) | collective-permute-done | bytes 262176 | tf_op jit(solution)/shard_map/ppermute | solution.py:397
  43.2 6.8 %collective-permute-start.9 = (bf16[224,1024]{1,0:T(8,128)(2,1)}, bf16[224,1024]{1,0:T(8,128)(2,1)S(1)}, u32[]{:S(2)}, u32[]{:S(2)}) collective-permute-start(bf16[224,1024]{1,0:T(8,128)(2,1)} %get-tuple-element.54.refs_0_), channel_id=1, source_target_pairs={{0,1},{1,0},{2,3},{3,2},{4,5},{5,4},{6,7},{7,6},{8,9},{9,8},{10,11... | collective-permute-start | bytes 1376264 | tf_op jit(solution)/shard_map/ppermute | solution.py:412
  50.1 1.8 collective-permute-done.4.refs_2_
  51.9 5.6 %collective-permute-start.5 = (bf16[128,1024]{1,0:T(8,128)(2,1)S(1)}, bf16[128,1024]{1,0:T(8,128)(2,1)S(1)}, u32[]{:S(2)}, u32[]{:S(2)}) collective-permute-start(bf16[128,1024]{1,0:T(8,128)(2,1)S(1)} %copy-done.24), channel_id=1, source_target_pairs={{0,24},{2,26},{4,28},{6,30},{8,0},{10,2},{12,4},{14,6},{16,8},{18,... | collective-permute-start | bytes 786440 | tf_op jit(solution)/shard_map/ppermute | solution.py:397
  57.5 5.1 %route.1 = (bf16[512,896]{1,0:T(8,128)(2,1)}, bf16[512,896]{1,0:T(8,128)(2,1)}) custom-call(s32[4]{0:T(128)} %pad_add_fusion.info, f32[4,16,128]{2,1,0:T(8,128)} %copy-done.17), custom_call_target="tpu_custom_call" | custom-call | flops 1024 | bytes 1024 | tf_op jit(solution)/shard_map/route/pallas_call | solution.py:39
  63.3 3.9 %pack_gates.1 = (bf16[240,1024]{1,0:T(8,128)(2,1)}, bf16[240,1024]{1,0:T(8,128)(2,1)}, bf16[240,1024]{1,0:T(8,128)(2,1)}, bf16[240,1024]{1,0:T(8,128)(2,1)}) custom-call(s32[4]{0:T(128)} %pad_add_fusion.info, f32[4,16,128]{2,1,0:T(8,128)} %copy-done.17, bf16[896,512]{1,0:T(8,128)(2,1)} %select.11.sel, bf16[128,1024]{1,0:T(8,128)(2,1)} %refs_0_.2, ...), custom_call_target="tpu_custom_call" | custom-call | flops 1024 | bytes 1024 | tf_op jit(solution)/shard_map/pack_gates/pallas_call | solution.py:39
  67.5 1.2 collective-permute-start.14
  68.8 1.2 collective-permute-start.15
  69.9 2.3 %collective-permute-start.11 = (bf16[224,1024]{1,0:T(8,128)(2,1)S(1)}, bf16[224,1024]{1,0:T(8,128)(2,1)S(1)}, u32[]{:S(2)}, u32[]{:S(2)}) collective-permute-start(bf16[224,1024]{1,0:T(8,128)(2,1)S(1)} %collective-permute-done.7.refs_2_), channel_id=1, source_target_pairs={{0,1},{1,0},{2,3},{3,2},{4,5},{5,4},{6,7},{7,6},{8,9},{9,8},{10,11... | collective-permute-start | bytes 1376264 | tf_op jit(solution)/shard_map/ppermute | solution.py:412
  72.3 1.4 collective-permute-done.11.refs_6_
  75.2 15.2 %expert_forward.1 = (bf16[4,224,1024]{2,1,0:T(8,128)(2,1)}, bf16[896,704]{1,0:T(8,128)(2,1)}, bf16[896,704]{1,0:T(8,128)(2,1)}, bf16[896,704]{1,0:T(8,128)(2,1)}) custom-call(s32[4]{0:T(128)} %pad_add_fusion.info, bf16[224,1024]{1,0:T(8,128)(2,1)} %get-tuple-element.54.refs_0_, bf16[224,1024]{1,0:T(8,128)(2,1)} %copy-done.10, bf16[224,1024]{1,0:T(8,128)(2,1)} %copy-done.11, ...), custom_call_target="tpu_custom_call" | custom-call | flops 1024 | bytes 1024 | tf_op jit(solution)/shard_map/expert_forward/pallas_call | solution.py:39
  90.5 2.1 %collective-permute-start.16 = (bf16[4,224,1024]{2,1,0:T(8,128)(2,1)}, bf16[4,224,1024]{2,1,0:T(8,128)(2,1)S(1)}, u32[]{:S(2)}, u32[]{:S(2)}) collective-permute-start(bf16[4,224,1024]{2,1,0:T(8,128)(2,1)} %get-tuple-element.70), channel_id=1, source_target_pairs={{0,1},{1,0},{2,3},{3,2},{4,5},{5,4},{6,7},{7,6},{8,9},{9,8},{10,11... | collective-permute-start | bytes 5505032 | tf_op jit(solution)/shard_map/ppermute | solution.py:412
  93.6 4.5 %collective-permute-done.16.refs_1_ = bf16[4,224,1024]{2,1,0:T(8,128)(2,1)S(1)} collective-permute-done((bf16[4,224,1024]{2,1,0:T(8,128)(2,1)}, bf16[4,224,1024]{2,1,0:T(8,128)(2,1)S(1)}, u32[]{:S(2)}, u32[]{:S(2)}) %collective-permute-start.16) | collective-permute-done | bytes 1835040 | tf_op jit(solution)/shard_map/ppermute | solution.py:412
  98.1 1.2 copy-done.9
  99.3 5.7 %expert_output.1 = (bf16[224,1024]{1,0:T(8,128)(2,1)}, bf16[224,1024]{1,0:T(8,128)(2,1)}, bf16[224,1024]{1,0:T(8,128)(2,1)}, bf16[224,1024]{1,0:T(8,128)(2,1)}) custom-call(s32[4]{0:T(128)} %pad_add_fusion.info, bf16[896,704]{1,0:T(8,128)(2,1)} %get-tuple-element.83.refs_0_.refs_10_, bf16[4,224,1024]{2,1,0:T(8,128)(2,1)} %copy-done.9, ...), custom_call_target="tpu_custom_call" | custom-call | flops 1024 | bytes 1024 | tf_op jit(solution)/shard_map/expert_output/pallas_call | solution.py:39
  105.6 1.2 collective-permute-start.18
  106.9 1.0 collective-permute-start.19
  108.8 16.5 %expert_backward.1 = (bf16[4,240,1024]{2,1,0:T(8,128)(2,1)}, bf16[4,16,1024]{2,1,0:T(8,128)(2,1)}, bf16[896,704]{1,0:T(8,128)(2,1)}, bf16[896,704]{1,0:T(8,128)(2,1)}, bf16[896,704]{1,0:T(8,128)(2,1)}) custom-call(s32[4]{0:T(128)} %pad_add_fusion.info, bf16[240,1024]{1,0:T(8,128)(2,1)} %get-tuple-element.79.refs_0_.refs_8_, bf16[240,1024]{1,0:T(8,128)(2,1)} %copy-done.2, ...), custom_call_target="tpu_custom_call" | custom-call | flops 1024 | bytes 1024 | tf_op jit(solution)/shard_map/expert_backward/pallas_call | solution.py:39
  125.4 1.8 collective-permute-done.19.refs_3_
  127.2 1.5 collective-permute-start.27
  128.7 3.8 %collective-permute-done.27.refs_3_ = bf16[4,240,1024]{2,1,0:T(8,128)(2,1)S(1)} collective-permute-done((bf16[4,240,1024]{2,1,0:T(8,128)(2,1)}, bf16[4,240,1024]{2,1,0:T(8,128)(2,1)S(1)}, u32[]{:S(2)}, u32[]{:S(2)}) %collective-permute-start.27) | collective-permute-done | bytes 1966112 | tf_op jit(solution)/shard_map/ppermute | solution.py:412
  132.5 1.3 copy-done
  133.8 8.5 %expert_input.1 = (bf16[240,1024]{1,0:T(8,128)(2,1)}, bf16[240,1024]{1,0:T(8,128)(2,1)}, bf16[240,1024]{1,0:T(8,128)(2,1)}, bf16[240,1024]{1,0:T(8,128)(2,1)}) custom-call(s32[4]{0:T(128)} %pad_add_fusion.info, bf16[896,704]{1,0:T(8,128)(2,1)} %get-tuple-element.86.refs_0_.refs_16_, bf16[896,704]{1,0:T(8,128)(2,1)} %get-tuple-element.87.refs_1_.refs_17_, ...), custom_call_target="tpu_custom_call" | custom-call | flops 1024 | bytes 1024 | tf_op jit(solution)/shard_map/expert_input/pallas_call | solution.py:39
  142.2 1.0 collective-permute-start.28
  143.8 1.2 collective-permute-start.30
  145.0 4.0 %combine.1 = (bf16[128,1024]{1,0:T(8,128)(2,1)}, bf16[128,1024]{1,0:T(8,128)(2,1)}, bf16[128,1024]{1,0:T(8,128)(2,1)}, bf16[128,1024]{1,0:T(8,128)(2,1)}) custom-call(s32[4]{0:T(128)} %pad_add_fusion.info, f32[4,16,128]{2,1,0:T(8,128)} %copy-done.17, bf16[896,512]{1,0:T(8,128)(2,1)} %select.11.sel, bf16[512,896]{1,0:T(8,128)(2,1)} %get-tuple-element.59.chosen, ...), custom_call_target="tpu_custom_call" | custom-call | flops 1024 | bytes 1024 | tf_op jit(solution)/shard_map/combine/pallas_call | solution.py:39
  149.0 3.7 %collective-permute-start.21 = (bf16[128,1024]{1,0:T(8,128)(2,1)}, bf16[128,1024]{1,0:T(8,128)(2,1)S(1)}, u32[]{:S(2)}, u32[]{:S(2)}) collective-permute-start(bf16[128,1024]{1,0:T(8,128)(2,1)} %get-tuple-element.77), channel_id=1, source_target_pairs={{0,16},{2,18},{4,20},{6,22},{8,24},{10,26},{12,28},{14,30},{16,0},... | collective-permute-start | bytes 786440 | tf_op jit(solution)/shard_map/ppermute | solution.py:397
  152.6 2.3 %collective-permute-done.28.refs_1_ = bf16[240,1024]{1,0:T(8,128)(2,1)S(1)} collective-permute-done((bf16[240,1024]{1,0:T(8,128)(2,1)}, bf16[240,1024]{1,0:T(8,128)(2,1)S(1)}, u32[]{:S(2)}, u32[]{:S(2)}) %collective-permute-start.28) | collective-permute-done | bytes 491552 | tf_op jit(solution)/shard_map/ppermute | solution.py:404
  154.9 1.6 collective-permute-start.20
  156.5 9.9 %collective-permute-done.30.refs_3_ = bf16[240,1024]{1,0:T(8,128)(2,1)S(1)} collective-permute-done((bf16[240,1024]{1,0:T(8,128)(2,1)}, bf16[240,1024]{1,0:T(8,128)(2,1)S(1)}, u32[]{:S(2)}, u32[]{:S(2)}) %collective-permute-start.30) | collective-permute-done | bytes 491552 | tf_op jit(solution)/shard_map/ppermute | solution.py:404
  166.4 0.8 copy-done.20
  167.3 4.5 %combine_gates.1 = (bf16[144,1024]{1,0:T(8,128)(2,1)}, bf16[144,1024]{1,0:T(8,128)(2,1)}, bf16[144,1024]{1,0:T(8,128)(2,1)}, bf16[144,1024]{1,0:T(8,128)(2,1)}) custom-call(s32[4]{0:T(128)} %pad_add_fusion.info, f32[4,16,128]{2,1,0:T(8,128)} %copy-done.17, bf16[896,512]{1,0:T(8,128)(2,1)} %select.11.sel, bf16[512,896]{1,0:T(8,128)(2,1)} %get-tuple-element.60.chosen, ...), custom_call_target="tpu_custom_call" | custom-call | flops 1024 | bytes 1024 | tf_op jit(solution)/shard_map/combine_gates/pallas_call | solution.py:39
  171.7 3.7 %collective-permute-start.32 = (bf16[144,1024]{1,0:T(8,128)(2,1)}, bf16[144,1024]{1,0:T(8,128)(2,1)S(1)}, u32[]{:S(2)}, u32[]{:S(2)}) collective-permute-start(bf16[144,1024]{1,0:T(8,128)(2,1)} %get-tuple-element.97), channel_id=1, source_target_pairs={{0,16},{2,18},{4,20},{6,22},{8,24},{10,26},{12,28},{14,30},{16,0},... | collective-permute-start | bytes 884744 | tf_op jit(solution)/shard_map/ppermute | solution.py:397
  175.7 0.9 subtract_convert_fusion
  176.6 13.9 %expert_weights.1 = (bf16[1,2,704,2048]{3,2,1,0:T(8,128)(2,1)}, bf16[1,704,2048]{2,1,0:T(8,128)(2,1)}) custom-call(s32[4]{0:T(128)} %pad_add_fusion.info, bf16[224,1024]{1,0:T(8,128)(2,1)} %get-tuple-element.54.refs_0_, bf16[224,1024]{1,0:T(8,128)(2,1)} %copy-done.10, bf16[224,1024]{1,0:T(8,128)(2,1)} %copy-done.11, bf16[224,1024]{1,0:T(8,128)(2,1)} %copy-done.12, ...), custom_call_target="tpu_custom_call" | custom-call | flops 1024 | bytes 1024 | tf_op jit(solution)/shard_map/expert_weights/pallas_call | solution.py:39
  190.5 5.8 %collective-permute-done.32 = bf16[144,1024]{1,0:T(8,128)(2,1)S(1)} collective-permute-done((bf16[144,1024]{1,0:T(8,128)(2,1)}, bf16[144,1024]{1,0:T(8,128)(2,1)S(1)}, u32[]{:S(2)}, u32[]{:S(2)}) %collective-permute-start.32) | collective-permute-done | bytes 294944 | tf_op jit(solution)/shard_map/ppermute | solution.py:397
  196.4 3.9 %collective-permute-done.31 = bf16[144,1024]{1,0:T(8,128)(2,1)S(1)} collective-permute-done((bf16[144,1024]{1,0:T(8,128)(2,1)}, bf16[144,1024]{1,0:T(8,128)(2,1)S(1)}, u32[]{:S(2)}, u32[]{:S(2)}) %collective-permute-start.31) | collective-permute-done | bytes 294944 | tf_op jit(solution)/shard_map/ppermute | solution.py:397
  200.9 0.9 add_convert_fusion
  (111 shorter events, 11.6 us)
Async XLA Ops:
  0.6 35.6 %copy-start.24 = (bf16[128,1024]{1,0:T(8,128)(2,1)S(1)}, bf16[128,1024]{1,0:T(8,128)(2,1)}, u32[]{:S(2)}) copy-start(bf16[128,1024]{1,0:T(8,128)(2,1)} %refs_0_.2) | copy-start | bytes 786436
  0.6 29.5 %collective-permute-start = (bf16[128,1024]{1,0:T(8,128)(2,1)}, bf16[128,1024]{1,0:T(8,128)(2,1)S(1)}, u32[]{:S(2)}, u32[]{:S(2)}) collective-permute-start(bf16[128,1024]{1,0:T(8,128)(2,1)} %refs_0_.1), channel_id=1, source_target_pairs={{0,8},{2,10},{4,12},{6,14},{8,16},{10,18},{12,20},{14,22},{16,24},... | collective-permute-start | bytes 786440 | tf_op jit(solution)/shard_map/ppermute | solution.py:397
  2.0 28.2 %collective-permute-start.1 = (bf16[128,1024]{1,0:T(8,128)(2,1)}, bf16[128,1024]{1,0:T(8,128)(2,1)S(1)}, u32[]{:S(2)}, u32[]{:S(2)}) collective-permute-start(bf16[128,1024]{1,0:T(8,128)(2,1)} %refs_0_.1), channel_id=1, source_target_pairs={{0,16},{2,18},{4,20},{6,22},{8,24},{10,26},{12,28},{14,30},{16,0},... | collective-permute-start | bytes 786440 | tf_op jit(solution)/shard_map/ppermute | solution.py:397
  3.1 27.1 %collective-permute-start.2 = (bf16[128,1024]{1,0:T(8,128)(2,1)}, bf16[128,1024]{1,0:T(8,128)(2,1)S(1)}, u32[]{:S(2)}, u32[]{:S(2)}) collective-permute-start(bf16[128,1024]{1,0:T(8,128)(2,1)} %refs_0_.1), channel_id=1, source_target_pairs={{0,24},{2,26},{4,28},{6,30},{8,0},{10,2},{12,4},{14,6},{16,8},{18,... | collective-permute-start | bytes 786440 | tf_op jit(solution)/shard_map/ppermute | solution.py:397
  6.5 21.0 %all-to-all-start = ((f32[4,16,128]{2,1,0:T(8,128)}), f32[4,16,128]{2,1,0:T(8,128)S(1)}, u32[]{:S(2)}, u32[]{:S(2)}) async-start(f32[4,16,128]{2,1,0:T(8,128)} %broadcast_in_dim.2), calls=%async_computation | async-start | bytes 65536 | tf_op jit(solution)/shard_map/all_to_all | solution.py:424
  35.1 15.0 %collective-permute-start.6 = (bf16[224,1024]{1,0:T(8,128)(2,1)}, bf16[224,1024]{1,0:T(8,128)(2,1)S(1)}, u32[]{:S(2)}, u32[]{:S(2)}) collective-permute-start(bf16[224,1024]{1,0:T(8,128)(2,1)} %get-tuple-element.55), channel_id=1, source_target_pairs={{0,2},{2,0},{4,6},{6,4},{8,10},{10,8},{12,14},{14,12},{16,18},{18,... | collective-permute-start | bytes 1376264 | tf_op jit(solution)/shard_map/ppermute | solution.py:404
  36.3 7.0 %collective-permute-start.3 = (bf16[128,1024]{1,0:T(8,128)(2,1)S(1)}, bf16[128,1024]{1,0:T(8,128)(2,1)S(1)}, u32[]{:S(2)}, u32[]{:S(2)}) collective-permute-start(bf16[128,1024]{1,0:T(8,128)(2,1)S(1)} %copy-done.24), channel_id=1, source_target_pairs={{0,8},{2,10},{4,12},{6,14},{8,16},{10,18},{12,20},{14,22},{16,24},... | collective-permute-start | bytes 786440 | tf_op jit(solution)/shard_map/ppermute | solution.py:397
  36.3 15.6 %collective-permute-start.4 = (bf16[128,1024]{1,0:T(8,128)(2,1)S(1)}, bf16[128,1024]{1,0:T(8,128)(2,1)S(1)}, u32[]{:S(2)}, u32[]{:S(2)}) collective-permute-start(bf16[128,1024]{1,0:T(8,128)(2,1)S(1)} %copy-done.24), channel_id=1, source_target_pairs={{0,16},{2,18},{4,20},{6,22},{8,24},{10,26},{12,28},{14,30},{16,0},... | collective-permute-start | bytes 786440 | tf_op jit(solution)/shard_map/ppermute | solution.py:397
  39.4 28.1 %collective-permute-start.7 = (bf16[224,1024]{1,0:T(8,128)(2,1)}, bf16[224,1024]{1,0:T(8,128)(2,1)S(1)}, u32[]{:S(2)}, u32[]{:S(2)}) collective-permute-start(bf16[224,1024]{1,0:T(8,128)(2,1)} %get-tuple-element.56), channel_id=1, source_target_pairs={{0,4},{2,6},{4,0},{6,2},{8,12},{10,14},{12,8},{14,10},{16,20},{18,... | collective-permute-start | bytes 1376264 | tf_op jit(solution)/shard_map/ppermute | solution.py:404
  40.7 28.1 %collective-permute-start.8 = (bf16[224,1024]{1,0:T(8,128)(2,1)}, bf16[224,1024]{1,0:T(8,128)(2,1)S(1)}, u32[]{:S(2)}, u32[]{:S(2)}) collective-permute-start(bf16[224,1024]{1,0:T(8,128)(2,1)} %get-tuple-element.57), channel_id=1, source_target_pairs={{0,6},{2,4},{4,2},{6,0},{8,14},{10,12},{12,10},{14,8},{16,22},{18,... | collective-permute-start | bytes 1376264 | tf_op jit(solution)/shard_map/ppermute | solution.py:404
  43.2 19.4 %copy-start.28 = (bf16[128,1024]{1,0:T(8,128)(2,1)}, bf16[128,1024]{1,0:T(8,128)(2,1)S(1)}, u32[]{:S(2)}) copy-start(bf16[128,1024]{1,0:T(8,128)(2,1)S(1)} %collective-permute-done.3.refs_1_) | copy-start | bytes 786436
  43.2 26.7 %collective-permute-start.9 = (bf16[224,1024]{1,0:T(8,128)(2,1)}, bf16[224,1024]{1,0:T(8,128)(2,1)S(1)}, u32[]{:S(2)}, u32[]{:S(2)}) collective-permute-start(bf16[224,1024]{1,0:T(8,128)(2,1)} %get-tuple-element.54.refs_0_), channel_id=1, source_target_pairs={{0,1},{1,0},{2,3},{3,2},{4,5},{5,4},{6,7},{7,6},{8,9},{9,8},{10,11... | collective-permute-start | bytes 1376264 | tf_op jit(solution)/shard_map/ppermute | solution.py:412
  50.0 24.3 %copy-start.10 = (bf16[224,1024]{1,0:T(8,128)(2,1)}, bf16[224,1024]{1,0:T(8,128)(2,1)S(1)}, u32[]{:S(2)}) copy-start(bf16[224,1024]{1,0:T(8,128)(2,1)S(1)} %collective-permute-done.6.refs_1_) | copy-start | bytes 1376260
  50.0 22.2 %collective-permute-start.10 = (bf16[224,1024]{1,0:T(8,128)(2,1)S(1)}, bf16[224,1024]{1,0:T(8,128)(2,1)S(1)}, u32[]{:S(2)}, u32[]{:S(2)}) collective-permute-start(bf16[224,1024]{1,0:T(8,128)(2,1)S(1)} %collective-permute-done.6.refs_1_), channel_id=1, source_target_pairs={{0,1},{1,0},{2,3},{3,2},{4,5},{5,4},{6,7},{7,6},{8,9},{9,8},{10,11... | collective-permute-start | bytes 1376264 | tf_op jit(solution)/shard_map/ppermute | solution.py:412
  51.9 10.7 %collective-permute-start.5 = (bf16[128,1024]{1,0:T(8,128)(2,1)S(1)}, bf16[128,1024]{1,0:T(8,128)(2,1)S(1)}, u32[]{:S(2)}, u32[]{:S(2)}) collective-permute-start(bf16[128,1024]{1,0:T(8,128)(2,1)S(1)} %copy-done.24), channel_id=1, source_target_pairs={{0,24},{2,26},{4,28},{6,30},{8,0},{10,2},{12,4},{14,6},{16,8},{18,... | collective-permute-start | bytes 786440 | tf_op jit(solution)/shard_map/ppermute | solution.py:397
  67.3 23.2 %collective-permute-start.13 = (bf16[240,1024]{1,0:T(8,128)(2,1)}, bf16[240,1024]{1,0:T(8,128)(2,1)S(1)}, u32[]{:S(2)}, u32[]{:S(2)}) collective-permute-start(bf16[240,1024]{1,0:T(8,128)(2,1)} %get-tuple-element.64), channel_id=1, source_target_pairs={{0,2},{2,0},{4,6},{6,4},{8,10},{10,8},{12,14},{14,12},{16,18},{18,... | collective-permute-start | bytes 1474568 | tf_op jit(solution)/shard_map/ppermute | solution.py:404
  67.5 23.0 %collective-permute-start.14 = (bf16[240,1024]{1,0:T(8,128)(2,1)}, bf16[240,1024]{1,0:T(8,128)(2,1)S(1)}, u32[]{:S(2)}, u32[]{:S(2)}) collective-permute-start(bf16[240,1024]{1,0:T(8,128)(2,1)} %get-tuple-element.65), channel_id=1, source_target_pairs={{0,4},{2,6},{4,0},{6,2},{8,12},{10,14},{12,8},{14,10},{16,20},{18,... | collective-permute-start | bytes 1474568 | tf_op jit(solution)/shard_map/ppermute | solution.py:404
  68.8 21.7 %collective-permute-start.15 = (bf16[240,1024]{1,0:T(8,128)(2,1)}, bf16[240,1024]{1,0:T(8,128)(2,1)S(1)}, u32[]{:S(2)}, u32[]{:S(2)}) collective-permute-start(bf16[240,1024]{1,0:T(8,128)(2,1)} %get-tuple-element.66), channel_id=1, source_target_pairs={{0,6},{2,4},{4,2},{6,0},{8,14},{10,12},{12,10},{14,8},{16,22},{18,... | collective-permute-start | bytes 1474568 | tf_op jit(solution)/shard_map/ppermute | solution.py:404
  69.9 3.7 %collective-permute-start.11 = (bf16[224,1024]{1,0:T(8,128)(2,1)S(1)}, bf16[224,1024]{1,0:T(8,128)(2,1)S(1)}, u32[]{:S(2)}, u32[]{:S(2)}) collective-permute-start(bf16[224,1024]{1,0:T(8,128)(2,1)S(1)} %collective-permute-done.7.refs_2_), channel_id=1, source_target_pairs={{0,1},{1,0},{2,3},{3,2},{4,5},{5,4},{6,7},{7,6},{8,9},{9,8},{10,11... | collective-permute-start | bytes 1376264 | tf_op jit(solution)/shard_map/ppermute | solution.py:412
  72.2 2.1 %collective-permute-start.12 = (bf16[224,1024]{1,0:T(8,128)(2,1)S(1)}, bf16[224,1024]{1,0:T(8,128)(2,1)S(1)}, u32[]{:S(2)}, u32[]{:S(2)}) collective-permute-start(bf16[224,1024]{1,0:T(8,128)(2,1)S(1)} %collective-permute-done.8.refs_3_), channel_id=1, source_target_pairs={{0,1},{1,0},{2,3},{3,2},{4,5},{5,4},{6,7},{7,6},{8,9},{9,8},{10,11... | collective-permute-start | bytes 1376264 | tf_op jit(solution)/shard_map/ppermute | solution.py:412
  72.3 20.3 %copy-start.1 = (bf16[240,1024]{1,0:T(8,128)(2,1)S(1)}, bf16[240,1024]{1,0:T(8,128)(2,1)}, u32[]{:S(2)}) copy-start(bf16[240,1024]{1,0:T(8,128)(2,1)} %get-tuple-element.79.refs_0_.refs_8_) | copy-start | bytes 1474564
  90.5 14.6 %copy-start.2 = (bf16[240,1024]{1,0:T(8,128)(2,1)}, bf16[240,1024]{1,0:T(8,128)(2,1)S(1)}, u32[]{:S(2)}) copy-start(bf16[240,1024]{1,0:T(8,128)(2,1)S(1)} %collective-permute-done.13.refs_1_.refs_9_) | copy-start | bytes 1474564
  90.5 14.6 %copy-start.3 = (bf16[240,1024]{1,0:T(8,128)(2,1)}, bf16[240,1024]{1,0:T(8,128)(2,1)S(1)}, u32[]{:S(2)}) copy-start(bf16[240,1024]{1,0:T(8,128)(2,1)S(1)} %collective-permute-done.14.refs_2_.refs_10_) | copy-start | bytes 1474564
  90.5 14.6 %copy-start.4 = (bf16[240,1024]{1,0:T(8,128)(2,1)}, bf16[240,1024]{1,0:T(8,128)(2,1)S(1)}, u32[]{:S(2)}) copy-start(bf16[240,1024]{1,0:T(8,128)(2,1)S(1)} %collective-permute-done.15.refs_3_.refs_11_) | copy-start | bytes 1474564
  90.5 7.6 %collective-permute-start.16 = (bf16[4,224,1024]{2,1,0:T(8,128)(2,1)}, bf16[4,224,1024]{2,1,0:T(8,128)(2,1)S(1)}, u32[]{:S(2)}, u32[]{:S(2)}) collective-permute-start(bf16[4,224,1024]{2,1,0:T(8,128)(2,1)} %get-tuple-element.70), channel_id=1, source_target_pairs={{0,1},{1,0},{2,3},{3,2},{4,5},{5,4},{6,7},{7,6},{8,9},{9,8},{10,11... | collective-permute-start | bytes 5505032 | tf_op jit(solution)/shard_map/ppermute | solution.py:412
  92.6 13.0 %collective-permute-start.23 = (bf16[240,1024]{1,0:T(8,128)(2,1)S(1)}, bf16[240,1024]{1,0:T(8,128)(2,1)S(1)}, u32[]{:S(2)}, u32[]{:S(2)}) collective-permute-start(bf16[240,1024]{1,0:T(8,128)(2,1)S(1)} %copy-done.1), channel_id=1, source_target_pairs={{0,1},{1,0},{2,3},{3,2},{4,5},{5,4},{6,7},{7,6},{8,9},{9,8},{10,11... | collective-permute-start | bytes 1474568 | tf_op jit(solution)/shard_map/ppermute | solution.py:412
  92.7 14.2 %collective-permute-start.24 = (bf16[240,1024]{1,0:T(8,128)(2,1)S(1)}, bf16[240,1024]{1,0:T(8,128)(2,1)S(1)}, u32[]{:S(2)}, u32[]{:S(2)}) collective-permute-start(bf16[240,1024]{1,0:T(8,128)(2,1)S(1)} %collective-permute-done.13.refs_1_.refs_9_), channel_id=1, source_target_pairs={{0,1},{1,0},{2,3},{3,2},{4,5},{5,4},{6,7},{7,6},{8,9},{9,8},{10,11... | collective-permute-start | bytes 1474568 | tf_op jit(solution)/shard_map/ppermute | solution.py:412
  93.1 14.7 %collective-permute-start.25 = (bf16[240,1024]{1,0:T(8,128)(2,1)S(1)}, bf16[240,1024]{1,0:T(8,128)(2,1)S(1)}, u32[]{:S(2)}, u32[]{:S(2)}) collective-permute-start(bf16[240,1024]{1,0:T(8,128)(2,1)S(1)} %collective-permute-done.14.refs_2_.refs_10_), channel_id=1, source_target_pairs={{0,1},{1,0},{2,3},{3,2},{4,5},{5,4},{6,7},{7,6},{8,9},{9,8},{10,11... | collective-permute-start | bytes 1474568 | tf_op jit(solution)/shard_map/ppermute | solution.py:412
  93.2 14.7 %collective-permute-start.26 = (bf16[240,1024]{1,0:T(8,128)(2,1)S(1)}, bf16[240,1024]{1,0:T(8,128)(2,1)S(1)}, u32[]{:S(2)}, u32[]{:S(2)}) collective-permute-start(bf16[240,1024]{1,0:T(8,128)(2,1)S(1)} %collective-permute-done.15.refs_3_.refs_11_), channel_id=1, source_target_pairs={{0,1},{1,0},{2,3},{3,2},{4,5},{5,4},{6,7},{7,6},{8,9},{9,8},{10,11... | collective-permute-start | bytes 1474568 | tf_op jit(solution)/shard_map/ppermute | solution.py:412
  105.1 20.2 %collective-permute-start.17 = (bf16[224,1024]{1,0:T(8,128)(2,1)}, bf16[224,1024]{1,0:T(8,128)(2,1)S(1)}, u32[]{:S(2)}, u32[]{:S(2)}) collective-permute-start(bf16[224,1024]{1,0:T(8,128)(2,1)} %get-tuple-element.72), channel_id=1, source_target_pairs={{0,2},{2,0},{4,6},{6,4},{8,10},{10,8},{12,14},{14,12},{16,18},{18,... | collective-permute-start | bytes 1376264 | tf_op jit(solution)/shard_map/ppermute | solution.py:404
  105.6 19.7 %collective-permute-start.18 = (bf16[224,1024]{1,0:T(8,128)(2,1)}, bf16[224,1024]{1,0:T(8,128)(2,1)S(1)}, u32[]{:S(2)}, u32[]{:S(2)}) collective-permute-start(bf16[224,1024]{1,0:T(8,128)(2,1)} %get-tuple-element.73), channel_id=1, source_target_pairs={{0,4},{2,6},{4,0},{6,2},{8,12},{10,14},{12,8},{14,10},{16,20},{18,... | collective-permute-start | bytes 1376264 | tf_op jit(solution)/shard_map/ppermute | solution.py:404
  106.9 20.3 %collective-permute-start.19 = (bf16[224,1024]{1,0:T(8,128)(2,1)}, bf16[224,1024]{1,0:T(8,128)(2,1)S(1)}, u32[]{:S(2)}, u32[]{:S(2)}) collective-permute-start(bf16[224,1024]{1,0:T(8,128)(2,1)} %get-tuple-element.74), channel_id=1, source_target_pairs={{0,6},{2,4},{4,2},{6,0},{8,14},{10,12},{12,10},{14,8},{16,22},{18,... | collective-permute-start | bytes 1376264 | tf_op jit(solution)/shard_map/ppermute | solution.py:404
  125.4 19.6 %copy-start.21 = (bf16[224,1024]{1,0:T(8,128)(2,1)}, bf16[224,1024]{1,0:T(8,128)(2,1)S(1)}, u32[]{:S(2)}) copy-start(bf16[224,1024]{1,0:T(8,128)(2,1)S(1)} %collective-permute-done.17.refs_1_) | copy-start | bytes 1376260
  125.4 19.6 %copy-start.22 = (bf16[224,1024]{1,0:T(8,128)(2,1)}, bf16[224,1024]{1,0:T(8,128)(2,1)S(1)}, u32[]{:S(2)}) copy-start(bf16[224,1024]{1,0:T(8,128)(2,1)S(1)} %collective-permute-done.18.refs_2_) | copy-start | bytes 1376260
  127.2 17.8 %copy-start.23 = (bf16[224,1024]{1,0:T(8,128)(2,1)}, bf16[224,1024]{1,0:T(8,128)(2,1)S(1)}, u32[]{:S(2)}) copy-start(bf16[224,1024]{1,0:T(8,128)(2,1)S(1)} %collective-permute-done.19.refs_3_) | copy-start | bytes 1376260
  127.2 5.3 %collective-permute-start.27 = (bf16[4,240,1024]{2,1,0:T(8,128)(2,1)}, bf16[4,240,1024]{2,1,0:T(8,128)(2,1)S(1)}, u32[]{:S(2)}, u32[]{:S(2)}) collective-permute-start(bf16[4,240,1024]{2,1,0:T(8,128)(2,1)} %get-tuple-element.90), channel_id=1, source_target_pairs={{0,1},{1,0},{2,3},{3,2},{4,5},{5,4},{6,7},{7,6},{8,9},{9,8},{10,11... | collective-permute-start | bytes 5898248 | tf_op jit(solution)/shard_map/ppermute | solution.py:412
  142.2 12.7 %collective-permute-start.28 = (bf16[240,1024]{1,0:T(8,128)(2,1)}, bf16[240,1024]{1,0:T(8,128)(2,1)S(1)}, u32[]{:S(2)}, u32[]{:S(2)}) collective-permute-start(bf16[240,1024]{1,0:T(8,128)(2,1)} %get-tuple-element.92), channel_id=1, source_target_pairs={{0,2},{2,0},{4,6},{6,4},{8,10},{10,8},{12,14},{14,12},{16,18},{18,... | collective-permute-start | bytes 1474568 | tf_op jit(solution)/shard_map/ppermute | solution.py:404
  143.3 13.3 %collective-permute-start.29 = (bf16[240,1024]{1,0:T(8,128)(2,1)}, bf16[240,1024]{1,0:T(8,128)(2,1)S(1)}, u32[]{:S(2)}, u32[]{:S(2)}) collective-permute-start(bf16[240,1024]{1,0:T(8,128)(2,1)} %get-tuple-element.93), channel_id=1, source_target_pairs={{0,4},{2,6},{4,0},{6,2},{8,12},{10,14},{12,8},{14,10},{16,20},{18,... | collective-permute-start | bytes 1474568 | tf_op jit(solution)/shard_map/ppermute | solution.py:404
  143.8 22.6 %collective-permute-start.30 = (bf16[240,1024]{1,0:T(8,128)(2,1)}, bf16[240,1024]{1,0:T(8,128)(2,1)S(1)}, u32[]{:S(2)}, u32[]{:S(2)}) collective-permute-start(bf16[240,1024]{1,0:T(8,128)(2,1)} %get-tuple-element.94), channel_id=1, source_target_pairs={{0,6},{2,4},{4,2},{6,0},{8,14},{10,12},{12,10},{14,8},{16,22},{18,... | collective-permute-start | bytes 1474568 | tf_op jit(solution)/shard_map/ppermute | solution.py:404
  149.0 26.4 %collective-permute-start.22 = (bf16[128,1024]{1,0:T(8,128)(2,1)}, bf16[128,1024]{1,0:T(8,128)(2,1)S(1)}, u32[]{:S(2)}, u32[]{:S(2)}) collective-permute-start(bf16[128,1024]{1,0:T(8,128)(2,1)} %get-tuple-element.78), channel_id=1, source_target_pairs={{0,8},{2,10},{4,12},{6,14},{8,16},{10,18},{12,20},{14,22},{16,24},... | collective-permute-start | bytes 786440 | tf_op jit(solution)/shard_map/ppermute | solution.py:397
  149.0 26.7 %collective-permute-start.21 = (bf16[128,1024]{1,0:T(8,128)(2,1)}, bf16[128,1024]{1,0:T(8,128)(2,1)S(1)}, u32[]{:S(2)}, u32[]{:S(2)}) collective-permute-start(bf16[128,1024]{1,0:T(8,128)(2,1)} %get-tuple-element.77), channel_id=1, source_target_pairs={{0,16},{2,18},{4,20},{6,22},{8,24},{10,26},{12,28},{14,30},{16,0},... | collective-permute-start | bytes 786440 | tf_op jit(solution)/shard_map/ppermute | solution.py:397
  154.9 11.5 %copy-start.18 = (bf16[240,1024]{1,0:T(8,128)(2,1)}, bf16[240,1024]{1,0:T(8,128)(2,1)S(1)}, u32[]{:S(2)}) copy-start(bf16[240,1024]{1,0:T(8,128)(2,1)S(1)} %collective-permute-done.28.refs_1_) | copy-start | bytes 1474564
  154.9 20.7 %collective-permute-start.20 = (bf16[128,1024]{1,0:T(8,128)(2,1)}, bf16[128,1024]{1,0:T(8,128)(2,1)S(1)}, u32[]{:S(2)}, u32[]{:S(2)}) collective-permute-start(bf16[128,1024]{1,0:T(8,128)(2,1)} %get-tuple-element.76), channel_id=1, source_target_pairs={{0,24},{2,26},{4,28},{6,30},{8,0},{10,2},{12,4},{14,6},{16,8},{18,... | collective-permute-start | bytes 786440 | tf_op jit(solution)/shard_map/ppermute | solution.py:397
  171.7 18.8 %collective-permute-start.33 = (bf16[144,1024]{1,0:T(8,128)(2,1)}, bf16[144,1024]{1,0:T(8,128)(2,1)S(1)}, u32[]{:S(2)}, u32[]{:S(2)}) collective-permute-start(bf16[144,1024]{1,0:T(8,128)(2,1)} %get-tuple-element.98), channel_id=1, source_target_pairs={{0,8},{2,10},{4,12},{6,14},{8,16},{10,18},{12,20},{14,22},{16,24},... | collective-permute-start | bytes 884744 | tf_op jit(solution)/shard_map/ppermute | solution.py:397
  171.7 24.7 %collective-permute-start.32 = (bf16[144,1024]{1,0:T(8,128)(2,1)}, bf16[144,1024]{1,0:T(8,128)(2,1)S(1)}, u32[]{:S(2)}, u32[]{:S(2)}) collective-permute-start(bf16[144,1024]{1,0:T(8,128)(2,1)} %get-tuple-element.97), channel_id=1, source_target_pairs={{0,16},{2,18},{4,20},{6,22},{8,24},{10,26},{12,28},{14,30},{16,0},... | collective-permute-start | bytes 884744 | tf_op jit(solution)/shard_map/ppermute | solution.py:397
  175.4 24.9 %collective-permute-start.31 = (bf16[144,1024]{1,0:T(8,128)(2,1)}, bf16[144,1024]{1,0:T(8,128)(2,1)S(1)}, u32[]{:S(2)}, u32[]{:S(2)}) collective-permute-start(bf16[144,1024]{1,0:T(8,128)(2,1)} %get-tuple-element.96), channel_id=1, source_target_pairs={{0,24},{2,26},{4,28},{6,30},{8,0},{10,2},{12,4},{14,6},{16,8},{18,... | collective-permute-start | bytes 884744 | tf_op jit(solution)/shard_map/ppermute | solution.py:397
  176.6 23.6 %copy-start.34 = (bf16[144,1024]{1,0:T(8,128)(2,1)S(1)}, bf16[144,1024]{1,0:T(8,128)(2,1)}, u32[]{:S(2)}) copy-start(bf16[144,1024]{1,0:T(8,128)(2,1)} %get-tuple-element.95) | copy-start | bytes 884740
  176.6 24.2 %copy-start.32 = (bf16[128,1024]{1,0:T(8,128)(2,1)S(1)}, bf16[128,1024]{1,0:T(8,128)(2,1)}, u32[]{:S(2)}) copy-start(bf16[128,1024]{1,0:T(8,128)(2,1)} %param.10) | copy-start | bytes 786436
  (22 other events, 69.8 us)

commit v5 on v3

v5 whole, which is shorter than its diff:
```python
import functools

import jax
import jax.numpy as jnp
from jax import lax
from jax.experimental import pallas as pl
from jax.experimental.pallas import tpu as pltpu
from jax.sharding import PartitionSpec as P

PLANE = 4
CHUNKS = 1
TAIL = 16
VMEM_LIMIT = 60 * 1024 * 1024
F32 = jnp.float32
BF16 = jnp.bfloat16


def dot_nn(a, b):
    return lax.dot_general(a, b, (((1,), (0,)), ((), ())), preferred_element_type=F32)


def dot_nt(a, b):
    return lax.dot_general(a, b, (((1,), (1,)), ((), ())), preferred_element_type=F32)


def dot_tn(a, b):
    return lax.dot_general(a, b, (((0,), (0,)), ((), ())), preferred_element_type=F32)


def iota(shape, axis):
    return lax.broadcasted_iota(jnp.int32, shape, axis)


SMEM = pl.BlockSpec(memory_space=pltpu.SMEM)
VMEM = pl.BlockSpec(memory_space=pltpu.VMEM)
HBM = pl.BlockSpec(memory_space=pl.ANY)


def call(kernel, outs, args, specs, out_specs=None, scratch=(), name=None):
    return pl.pallas_call(
        kernel,
        out_shape=outs,
        in_specs=specs,
        out_specs=out_specs if out_specs is not None else [VMEM] * len(outs),
        scratch_shapes=list(scratch),
        compiler_params=pltpu.CompilerParams(vmem_limit_bytes=VMEM_LIMIT),
        cost_estimate=pl.CostEstimate(flops=1024, bytes_accessed=1024, transcendentals=0),
        name=name,
    )(*args)


def shape(*dims, dtype=BF16):
    return jax.ShapeDtypeStruct(dims, dtype)


def outer_meta(info, meta, s, zn):
    return meta[lax.rem(info[3] - s + zn, zn)]


def select_kernel(info, meta, *sels, zn, pn, tokens, picks, cap):
    zc = zn // CHUNKS
    rows = zc * cap
    partner = iota((8, 1), 0)
    experts = jnp.where(partner < pn, info[0] + (partner ^ info[1]), -2).astype(F32)
    before = (iota((tokens, tokens), 0) < iota((tokens, tokens), 1)).astype(F32).astype(BF16)
    slot = iota((rows, tokens), 0).astype(F32)
    for s in range(zn):
        g, local = divmod(s, zc)
        ids = outer_meta(info, meta, s, zn)
        named = jnp.zeros((8, tokens), F32)
        for k in range(picks):
            named += (ids[k : k + 1, :] == experts).astype(F32)
        dest = dot_nn(named.astype(BF16), before) + local * cap
        dest = jnp.where(named > 0, dest, -1.0)
        for q in range(pn):
            sels[g][q * rows : (q + 1) * rows, local * tokens : (local + 1) * tokens] = (
                (slot == dest[q : q + 1, :]).astype(F32).astype(BF16)
            )


def route_kernel(info, meta, ones, *, zn, pn, tokens, picks, cap):
    rows = zn * cap
    partner = iota((1, 8), 1)
    experts = jnp.where(partner < pn, info[0] + (partner ^ info[1]), -2).astype(F32)
    after = (iota((tokens, tokens), 1) < iota((tokens, tokens), 0)).astype(F32).astype(BF16)
    eye = (iota((16, 16), 0) == iota((16, 16), 1)).astype(F32).astype(BF16)
    lane = iota((tokens, pn * rows), 1).astype(F32)
    for s in range(zn):
        here = slice(s * tokens, (s + 1) * tokens)
        columned = dot_tn(outer_meta(info, meta, s, zn).astype(BF16), eye)
        named = jnp.zeros((tokens, 8), F32)
        for k in range(picks):
            named += (columned[:, k : k + 1] == experts).astype(F32)
        dest = dot_nn(after, named.astype(BF16)) + s * cap
        dest = jnp.where(named > 0, dest + rows * partner.astype(F32), -1.0)
        picked = jnp.zeros((tokens, pn * rows), F32)
        for q in range(pn):
            picked += (lane == dest[:, q : q + 1]).astype(F32)
        ones[here, :] = picked.astype(BF16)


def tail_lanes(rows):
    return -(-rows // 128) * 128


class Loads:
    def __init__(self, sems):
        self.sems, self.copies, self.waited = sems, {}, set()

    def add(self, key, source, target):
        self.copies[key] = pltpu.make_async_copy(source, target, self.sems.at[len(self.copies)])
        self.copies[key].start()

    def need(self, *keys):
        for key in keys:
            if key not in self.waited:
                self.waited.add(key)
                self.copies[key].wait()

    def finish(self):
        self.need(*self.copies)


def pack_kernel(info, sel, source, *refs, zn, pn, tokens, rows):
    outs, whole, sems = refs[:pn], refs[-2], refs[-1]
    loads = Loads(sems)
    for s in range(zn):
        place = lax.rem(info[3] - s + zn, zn)
        loads.add(s, source.at[place], whole.at[pl.ds(s * tokens, tokens)])
    loads.finish()
    for q in range(pn):
        outs[q][...] = dot_nn(sel[q * rows : (q + 1) * rows, :], whole[...]).astype(BF16)


def pack_gates_kernel(info, meta, *refs, zn, pn, tokens, picks, rows):
    zc = zn // CHUNKS
    sels, sources = refs[:CHUNKS], refs[CHUNKS : CHUNKS + zc]
    outs, whole, sems = refs[CHUNKS + zc : CHUNKS + zc + pn], refs[-2], refs[-1]
    loads = Loads(sems)
    for s in range(zc):
        loads.add(s, sources[s], whole.at[pl.ds(s * tokens, tokens)])
    for q in range(pn):
        expert = (info[0] + (info[1] ^ q)).astype(F32)
        outs[q][rows : rows + TAIL, :] = jnp.zeros((TAIL, outs[q].shape[1]), BF16)
        for g in range(CHUNKS):
            tail = jnp.zeros((TAIL, rows), F32)
            for local in range(zc):
                known = outer_meta(info, meta, g * zc + local, zn)
                gate = jnp.zeros((1, tokens), F32)
                for k in range(picks):
                    gate += jnp.where(known[k : k + 1, :] == expert, known[8 + k : 9 + k, :], 0.0)
                gate = jnp.broadcast_to(gate, (TAIL, tokens)).astype(BF16)
                here = slice(local * tokens, (local + 1) * tokens)
                tail += dot_nt(gate, sels[g][q * rows : (q + 1) * rows, here])
            at = g * tail_lanes(rows)
            outs[q][rows : rows + TAIL, at : at + rows] = tail.astype(BF16)
    loads.finish()
    for q in range(pn):
        chosen = sels[0][q * rows : (q + 1) * rows, :]
        outs[q][0:rows, :] = dot_nn(chosen, whole[...]).astype(BF16)


def combine_kernel(info, meta, *refs, zn, pn, tokens, rows, gates):
    zc, part_rows = zn // CHUNKS, rows // CHUNKS
    sels, chosen, backs = refs[:CHUNKS], refs[CHUNKS], refs[CHUNKS + 1 : CHUNKS + 1 + pn]
    outs, (whole, tails, sems) = refs[CHUNKS + 1 + pn : -3], refs[-3:]
    cols = whole.shape[1]
    loads = Loads(sems)
    for q in range(pn):
        if gates:
            loads.add(("t", q), backs[q].at[pl.ds(rows, TAIL)], tails.at[q])
        loads.add(q, backs[q].at[pl.ds(0, rows)], whole.at[pl.ds(q * rows, rows)])
    totals = {}
    if gates:
        loads.need(*(("t", q) for q in range(pn)))
        for g in range(CHUNKS):
            spreads = []
            for q in range(pn):
                at = g * tail_lanes(part_rows)
                row = tails[q, :, at : at + part_rows]
                spreads.append(dot_nn(row, sels[g][q * part_rows : (q + 1) * part_rows, :])[0:8, :])
            for local in range(zc):
                ids = outer_meta(info, meta, g * zc + local, zn)[0:8, :]
                total = jnp.zeros((8, tokens), F32)
                for q in range(pn):
                    expert = (info[0] + (info[1] ^ q)).astype(F32)
                    spread = spreads[q][:, local * tokens : (local + 1) * tokens]
                    total += jnp.where(ids == expert, spread, 0.0)
                totals[g * zc + local] = jnp.concatenate(
                    [total, jnp.zeros((TAIL - 8, tokens), F32)], axis=0
                ).astype(BF16)
    loads.finish()
    for s in range(zn):
        here = slice(s * tokens, (s + 1) * tokens)
        part = dot_nn(chosen[here, :], whole[...]).astype(BF16)
        if not gates:
            outs[0][lax.rem(info[3] - s + zn, zn)] = part
        else:
            outs[s][0:tokens, :] = part
            outs[s][tokens : tokens + TAIL, :] = jnp.zeros((TAIL, cols), BF16)
            outs[s][tokens : tokens + TAIL, 0:tokens] = totals[s]


def column_block(info, j, nt, cols):
    block = lax.rem(info[2] - j + nt, nt)
    return pl.ds(pl.multiple_of(block * cols, 128), cols)


def load_weight(loads, info, kind, source, target, blocks, nt, cols):
    for at, j in enumerate(blocks):
        block = source.at[:, column_block(info, j, nt, cols)]
        loads.add((kind, j), block, target.at[:, pl.ds(at * cols, cols)])


def by_core(refs, nt, pn):
    return [refs[j * pn : (j + 1) * pn] for j in range(nt)]


def load_chunk(loads, sources, target, g, pn, rows, cols):
    for j, pieces in enumerate(sources):
        for q in range(pn):
            to = target.at[pl.ds((g * pn + q) * rows, rows), pl.ds(j * cols, cols)]
            loads.add(("r", g, j, q), pieces[g * pn + q].at[pl.ds(0, rows)], to)


def halves(pn):
    units = [(g, q) for g in range(CHUNKS) for q in range(pn)]
    return units[: len(units) // 2], units[len(units) // 2 :]


def forward_kernel(info, *refs, nt, pn, rows, cols):
    n = CHUNKS * pn
    xs, refs = by_core(refs, nt, n), refs[nt * n :]
    (win, wout), outs, refs = refs[:2], by_core(refs[2:], nt, pn), refs[2 + nt * pn :]
    hs, hid, a1, a2, x, tails, wg, wu, wd, stage, in_sems, out_sems = refs
    loads, stores = Loads(in_sems), Loads(out_sems)
    every = range(nt)
    load_chunk(loads, xs, x, 0, pn, rows, cols)
    load_weight(loads, info, "g", win.at[0, 0], wg, every, nt, cols)
    load_weight(loads, info, "u", win.at[0, 1], wu, every, nt, cols)
    for q in range(pn):
        loads.add(("t", q), xs[0][q].at[pl.ds(rows, TAIL)], tails.at[q])
    for g in range(1, CHUNKS):
        load_chunk(loads, xs, x, g, pn, rows, cols)
    load_weight(loads, info, "d", wout.at[0], wd, every, nt, cols)
    same = iota((rows, rows), 0) == iota((rows, rows), 1)
    tail_step = tail_lanes(rows)
    for b, units in enumerate(halves(pn)):
        here = slice(b * len(units) * rows, (b + 1) * len(units) * rows)
        loads.need(*(("r", g, j, q) for j in every for g, q in units))
        loads.need(*(("g", j) for j in every))
        gate = dot_nt(x[here, :], wg[...])
        loads.need(*(("u", j) for j in every), *(("t", q) for q in range(pn)))
        up = dot_nt(x[here, :], wu[...])
        columns = []
        for g, q in units:
            row = tails[q, :, g * tail_step : g * tail_step + rows].astype(F32)[0:1, :]
            columns.append(jnp.sum(jnp.where(same, row, 0.0), axis=1, keepdims=True))
        weight = jnp.concatenate(columns, axis=0)
        sigma = jax.nn.sigmoid(gate)
        active = gate * sigma
        hidden = active * up
        scaled = (weight * hidden).astype(BF16)
        hs[here, :] = scaled
        hid[here, :] = hidden.astype(BF16)
        a1[here, :] = (weight * (up * sigma * (1.0 + gate * (1.0 - sigma)))).astype(BF16)
        a2[here, :] = (weight * active).astype(BF16)
        loads.need(*(("d", j) for j in every))
        part = dot_nn(scaled, wd[...]).astype(BF16)
        for j in reversed(every):
            w = (nt - j) % nt
            for u, (g, q) in enumerate(units):
                block = part[u * rows : (u + 1) * rows, w * cols : (w + 1) * cols]
                stage[j, q, g * rows : (g + 1) * rows, :] = block
                if g == CHUNKS - 1:
                    stores.add((j, q), stage.at[j, q], outs[j][q])
    loads.finish()
    stores.finish()


def backward_kernel(info, *refs, nt, pn, rows, cols):
    n = CHUNKS * pn
    cs, refs = by_core(refs, nt, n), refs[nt * n :]
    (win, wout, hid, a1, a2), outs, refs = refs[:5], by_core(refs[5:], nt, pn), refs[5 + nt * pn :]
    gg, ug, c, h, b1, b2, wg, wu, wd, stage, in_sems, out_sems = refs
    loads, stores = Loads(in_sems), Loads(out_sems)
    every = range(nt)
    load_chunk(loads, cs, c, 0, pn, rows, cols)
    load_weight(loads, info, "d", wout.at[0], wd, every, nt, cols)
    for key, source, target in (("h", hid, h), ("1", a1, b1), ("2", a2, b2)):
        loads.add(key, source, target)
    load_weight(loads, info, "g", win.at[0, 0], wg, every, nt, cols)
    load_weight(loads, info, "u", win.at[0, 1], wu, every, nt, cols)
    for g in range(1, CHUNKS):
        load_chunk(loads, cs, c, g, pn, rows, cols)
    same = iota((rows, rows), 0) == iota((rows, rows), 1)
    tail_step = tail_lanes(rows)
    bottom = slice(CHUNKS * rows, CHUNKS * rows + TAIL)
    for b, units in enumerate(halves(pn)):
        here = slice(b * len(units) * rows, (b + 1) * len(units) * rows)
        loads.need(*(("r", g, j, q) for j in every for g, q in units))
        loads.need(*(("d", j) for j in every))
        grad = dot_nt(c[here, :], wd[...])
        loads.need("h", "1", "2")
        piece = jnp.sum(grad * h[here, :].astype(F32), axis=1, keepdims=True)
        gate_grad = (grad * b1[here, :].astype(F32)).astype(BF16)
        up_grad = (grad * b2[here, :].astype(F32)).astype(BF16)
        gg[here, :] = gate_grad
        ug[here, :] = up_grad
        for u, (g, q) in enumerate(units):
            part = piece[u * rows : (u + 1) * rows, :]
            part = jnp.sum(jnp.where(same, part, 0.0), axis=0, keepdims=True)
            part = jnp.broadcast_to(part, (TAIL, rows)).astype(BF16)
            for j in every:
                if g == 0:
                    stage[j, q, bottom, :] = jnp.zeros((TAIL, cols), BF16)
                stage[j, q, bottom, g * tail_step : g * tail_step + rows] = part
        loads.need(*((k, j) for k in "gu" for j in every))
        part = (dot_nn(gate_grad, wg[...]) + dot_nn(up_grad, wu[...])).astype(BF16)
        for j in reversed(every):
            w = (nt - j) % nt
            for u, (g, q) in enumerate(units):
                block = part[u * rows : (u + 1) * rows, w * cols : (w + 1) * cols]
                stage[j, q, g * rows : (g + 1) * rows, :] = block
                if g == CHUNKS - 1:
                    stores.add((j, q), stage.at[j, q], outs[j][q])
    loads.finish()
    stores.finish()


def weights_kernel(info, *refs, nt, pn, rows, cols):
    n = CHUNKS * pn
    xs, cs, refs = by_core(refs, nt, n), by_core(refs[nt * n :], nt, n), refs[2 * nt * n :]
    lefts, (gin, gout, left, right, stage, in_sems, out_sems) = refs[:3], refs[3:]
    loads, stores = Loads(in_sems), Loads(out_sems)
    order = ((0, 0, xs), (1, 0, xs), (2, 1, cs))
    for w, side, sources in order:
        loads.add(("l", w), lefts[w], left.at[w])
        if w == 1:
            continue
        for j in range(nt):
            for q in range(n):
                target = right.at[side, j, pl.ds(q * rows, rows)]
                loads.add((side, j, q), sources[j][q].at[pl.ds(0, rows)], target)
    for w, side, _ in order:
        loads.need(("l", w))
        for j in range(nt):
            loads.need(*((side, j, q) for q in range(n)))
            at = column_block(info, j, nt, cols)
            stage[j, w] = dot_tn(left[w], right[side, j]).astype(BF16)
            target = gout.at[0, :, at] if w == 2 else gin.at[0, w, :, at]
            stores.add((j, w), stage.at[j, w], target)
    loads.finish()
    stores.finish()


def after(value, *others):
    return lax.optimization_barrier((value, *others))[0]


def body(
    first_half,
    second_half,
    first_grad,
    second_grad,
    expert_ids,
    gate_weights,
    expert_in,
    expert_out,
):
    tokens, picks = expert_ids.shape
    groups = lax.axis_size("expert")
    nt = lax.axis_size("tensor")
    pn = PLANE
    zn = groups // pn
    cap = tokens * picks * 7 // (6 * groups)
    zc = zn // CHUNKS
    part_rows = zc * cap
    rows = CHUNKS * part_rows
    slots = pn * rows
    cols = first_half.shape[1]
    hid_n = expert_out.shape[1]
    me = lax.axis_index("expert")
    info = jnp.stack([(me // pn) * pn, me % pn, lax.axis_index("tensor"), me // pn]).astype(jnp.int32)

    def outer_send(value, s):
        if s % zn == 0:
            return value
        return lax.ppermute(
            value, "expert", [(e, ((e // pn + s) % zn) * pn + e % pn) for e in range(groups)]
        )

    def inner_send(value, q):
        if q == 0:
            return value
        return lax.ppermute(value, "expert", [(e, e ^ q) for e in range(groups)])

    def inner_exchange(pieces):
        return [inner_send(piece, q) for q, piece in enumerate(pieces)]

    def tensor_send(value, j):
        if j == 0:
            return value
        return lax.ppermute(value, "tensor", [(c, (c + j) % nt) for c in range(nt)])

    fixed = dict(zn=zn, pn=pn, tokens=tokens)

    own = jnp.concatenate(
        [
            jnp.pad(expert_ids.T.astype(F32), ((0, 8 - picks), (0, 0)), constant_values=-1.0),
            jnp.pad(gate_weights.T.astype(F32), ((0, 8 - picks), (0, 0))),
        ],
        axis=0,
    )
    columns = [[z * pn + q for z in range(zn)] for q in range(pn)]
    meta = lax.all_to_all(
        jnp.broadcast_to(own[None], (zn,) + own.shape),
        "expert",
        split_axis=0,
        concat_axis=0,
        axis_index_groups=columns,
        tiled=True,
    )
    sels = call(
        functools.partial(select_kernel, **fixed, picks=picks, cap=cap),
        [shape(pn * part_rows, zc * tokens)] * CHUNKS,
        [info, meta],
        [SMEM, VMEM],
        name="select",
    )
    dma = pltpu.SemaphoreType.DMA
    sizes = dict(nt=nt, pn=pn, rows=part_rows, cols=cols)

    def pack(gathered):
        return call(
            functools.partial(pack_kernel, **fixed, rows=part_rows),
            [shape(part_rows, cols)] * pn,
            [info, sels[0], gathered],
            [SMEM, VMEM, HBM],
            scratch=[pltpu.VMEM((zn * tokens, cols), BF16), dma((zn,))],
            name="pack",
        )

    def pack_gates(parts):
        return call(
            functools.partial(pack_gates_kernel, **fixed, picks=picks, rows=part_rows),
            [shape(part_rows + TAIL, cols)] * pn,
            [info, meta, *sels, *parts[:zc]],
            [SMEM] + [VMEM] * (1 + CHUNKS) + [HBM] * zc,
            scratch=[pltpu.VMEM((zc * tokens, cols), BF16), dma((zc,))],
            name="pack_gates",
        )

    def combine(backs, gates):
        parts = call(
            functools.partial(combine_kernel, **fixed, rows=rows, gates=gates),
            [shape(tokens + TAIL, cols)] * zn if gates else [shape(zn, tokens, cols)],
            [info, meta, *sels, chosen, *backs],
            [SMEM] + [VMEM] * (2 + CHUNKS) + [HBM] * pn,
            scratch=[pltpu.VMEM((slots, cols), BF16), pltpu.VMEM((pn, TAIL, cols), BF16)]
            + [dma((2 * pn,))],
            name="combine_gates" if gates else "combine",
        )
        if not gates:
            return lax.psum_scatter(
                parts[0], "expert", scatter_dimension=0, axis_index_groups=columns, tiled=False
            )
        return [outer_send(part, -s) for s, part in enumerate(parts)]

    def swapped(chunks):
        return [tensor_send(piece, j) for j in range(nt) for pieces in chunks for piece in pieces]

    def core_sum(arrays):
        sums = []
        for q in range(pn):
            total = arrays[q].astype(F32)
            for j in range(1, nt):
                total += tensor_send(arrays[j * pn + q], j).astype(F32)
            sums.append(total.astype(BF16))
        return sums

    x_parts = [outer_send(first_half, s) for s in range(zn)]
    x_packed = pack_gates(x_parts)
    x_here = inner_exchange(x_packed)
    gathered = lax.all_gather(
        after(second_grad, *x_parts[1:]), "expert", axis_index_groups=columns, tiled=False
    )
    chosen = call(
        functools.partial(route_kernel, **fixed, picks=picks, cap=cap),
        [shape(zn * tokens, slots)],
        [info, after(meta, *x_packed)],
        [SMEM, VMEM],
        name="route",
    )[0]
    c_packed = pack(after(gathered, chosen))
    c_here = inner_exchange(c_packed)

    xs = swapped((x_here,))
    pieces = nt * CHUNKS * pn
    forward = call(
        functools.partial(forward_kernel, **sizes),
        [shape(rows, cols)] * (nt * pn) + [shape(slots, hid_n)] * 4,
        [after(info, *c_packed), *xs, expert_in, expert_out],
        [SMEM] + [HBM] * (pieces + 2),
        out_specs=[HBM] * (nt * pn) + [VMEM] * 4,
        scratch=[pltpu.VMEM((slots, nt * cols), BF16), pltpu.VMEM((pn, TAIL, cols), BF16)]
        + [pltpu.VMEM((hid_n, nt * cols), BF16)] * 3
        + [pltpu.VMEM((nt, pn, rows, cols), BF16), dma((3 * nt + pieces + pn,))]
        + [dma((nt * pn,))],
        name="expert_forward",
    )
    outs, (hs, hid, a1, a2) = forward[: nt * pn], forward[nt * pn :]
    outs = [after(part, *c_here) for part in outs]
    cs = swapped(([after(piece, hid) for piece in c_here],))
    out_here = core_sum(outs)
    out_back = inner_exchange(out_here)

    backward = call(
        functools.partial(backward_kernel, **sizes),
        [shape(rows + TAIL, cols)] * (nt * pn) + [shape(slots, hid_n)] * 2,
        [info, *cs, expert_in, expert_out, after(hid, *out_here), a1, a2],
        [SMEM] + [HBM] * (pieces + 5),
        out_specs=[HBM] * (nt * pn) + [VMEM] * 2,
        scratch=[pltpu.VMEM((slots, nt * cols), BF16)]
        + [pltpu.VMEM((slots, hid_n), BF16)] * 3
        + [pltpu.VMEM((hid_n, nt * cols), BF16)] * 3
        + [pltpu.VMEM((nt, pn, rows + TAIL, cols), BF16), dma((3 * nt + pieces + 3,))]
        + [dma((nt * pn,))],
        name="expert_backward",
    )
    grads, (gg, ug) = backward[: nt * pn], backward[nt * pn :]
    dx_here = core_sum([after(part, *out_back) for part in grads])
    dx_back = inner_exchange(dx_here)
    branch = combine(out_back, False).astype(F32)
    grad_parts = combine(dx_back, True)

    grad_in, grad_out = call(
        functools.partial(weights_kernel, **sizes),
        [shape(*expert_in.shape), shape(*expert_out.shape)],
        [info, *xs, *cs, gg, ug, after(hs, *dx_here)],
        [SMEM] + [HBM] * (2 * pieces + 3),
        out_specs=[HBM, HBM],
        scratch=[
            pltpu.VMEM((3, slots, hid_n), BF16),
            pltpu.VMEM((2, nt, slots, cols), BF16),
            pltpu.VMEM((nt, 3, hid_n, cols), BF16),
            dma((3 + 2 * pieces,)),
            dma((3 * nt,)),
        ],
        name="expert_weights",
    )

    input_sum = sum(part[:tokens].astype(F32) for part in grad_parts)
    gate_sum = sum(part[tokens : tokens + picks, :tokens].astype(F32) for part in grad_parts)
    restored = (second_half.astype(F32) - branch).astype(BF16)
    carried_grad = (first_grad.astype(F32) + input_sum).astype(BF16)
    return (restored, carried_grad, gate_sum.T, grad_in, grad_out)


def solution(mesh):
    in_specs = (
        P("expert", "tensor"),
        P("expert", "tensor"),
        P("expert", "tensor"),
        P("expert", "tensor"),
        P("expert", None),
        P("expert", None),
        P("expert", None, "tensor", None),
        P("expert", "tensor", None),
    )
    out_specs = (
        P("expert", "tensor"),
        P("expert", "tensor"),
        P("expert", None),
        P("expert", None, "tensor", None),
        P("expert", "tensor", None),
    )
    return jax.shard_map(body, mesh=mesh, in_specs=in_specs, out_specs=out_specs, check_vma=False)
```

time: 250 us -> 219 us (0.88); the launches traced: 249 us -> 215 us
  waiting for transfers between devices: 96.2 us -> 62.5 us
  blocking collectives: 25.7 us -> 0 us
  between operations: 0.76 us -> 14.4 us
  starting transfers between devices: 33.7 us -> 44.8 us
  Pallas kernels: 73.1 us -> 77.1 us
  other arithmetic: 14.5 us -> 10.8 us
    ppermute x15 -> x6, waiting for transfers between devices: 73.3 us -> 32.3 us  [outer_send(): lax.ppermute(value, 'expert', [(e, (e // pn + s) % zn * pn + e % pn) for...]
    ppermute x0 -> x12, waiting for transfers between devices: none -> 26.2 us  [inner_send(): return lax.ppermute(value, 'expert', [(e, e ^ q) for e in range(groups)])]
    all_to_all x1 -> x0, blocking collectives: 25.7 us -> none  [inner_exchange(): lax.all_to_all(value, 'expert', split_axis=0, concat_axis=0, axis_index_g...]
    all_to_all x3 -> x1, waiting for transfers between devices: 22.6 us -> 2.84 us  [body(): lax.all_to_all(jnp.broadcast_to(own[None], (zn,) + own.shape), 'expert',...]
    ppermute x4 -> x16, starting transfers between devices: 5.51 us -> 22.7 us  [tensor_send(): return lax.ppermute(value, 'tensor', [(c, (c + j) % nt) for c in range(nt)])]
    ppermute x0 -> x12, starting transfers between devices: none -> 10.9 us  [inner_send(): return lax.ppermute(value, 'expert', [(e, e ^ q) for e in range(groups)])]
    ppermute x15 -> x6, starting transfers between devices: 17.2 us -> 6.67 us  [outer_send(): lax.ppermute(value, 'expert', [(e, (e // pn + s) % zn * pn + e % pn) for...]
    all_to_all x3 -> x1, starting transfers between devices: 11 us -> 4.54 us  [body(): lax.all_to_all(jnp.broadcast_to(own[None], (zn,) + own.shape), 'expert',...]
  transfers between devices with their start and end apart: 22 -> 37, of which waited for: 14 -> 10; matrix products, arithmetic and copies ran while one was open for 5% -> 5% of each run, Pallas kernels for 18% -> 36%
where the time goes in v5:
time: 219 us; the launch traced here: 215 us
  Pallas kernels  77.1 us (35%)
  waiting for transfers between devices  62.5 us (29%)
  starting transfers between devices  44.8 us (20%)
  between operations  14.4 us (7%)
  other arithmetic  10.8 us (5%)
  local copies, waits for them, and re-layouts  5.4 us (2%)
    pallas_call x9, Pallas kernels, call(): pl.pallas_call(kernel, out_shape=outs, in_specs=specs, out_specs=out_spec...  77.1 us
    ppermute x6, waiting for transfers between devices, outer_send(): lax.ppermute(value, 'expert', [(e, (e // pn + s) % zn * pn + e % pn) for...  32.3 us
    ppermute x12, waiting for transfers between devices, inner_send(): return lax.ppermute(value, 'expert', [(e, e ^ q) for e in range(groups)])  26.2 us
    ppermute x16, starting transfers between devices, tensor_send(): return lax.ppermute(value, 'tensor', [(c, (c + j) % nt) for c in range(nt)])  22.7 us
    ppermute x12, starting transfers between devices, inner_send(): return lax.ppermute(value, 'expert', [(e, e ^ q) for e in range(groups)])  10.9 us
    ppermute x6, starting transfers between devices, outer_send(): lax.ppermute(value, 'expert', [(e, (e // pn + s) % zn * pn + e % pn) for...  6.67 us
    convert_element_type x8, other arithmetic, core_sum(): sums.append(total.astype(BF16))  5.52 us
    unnamed x70, local copies, waits for them, and re-layouts  4.78 us
  transfers between devices with their start and end apart: 37, of which 10 were waited for; matrix products, arithmetic and copies ran while one was open for 5% of the time, Pallas kernels for 36%

profile of v5, /device:TPU:9, one launch (start us, length us, event | category | flops | bytes accessed | tf_op | source)
XLA Modules:
  0.0 215.1 jit_solution(4508799598754454162)
XLA Ops:
  7.2 2.4 %collective-permute-start.1 = (bf16[128,1024]{1,0:T(8,128)(2,1)}, bf16[128,1024]{1,0:T(8,128)(2,1)S(1)}, u32[]{:S(2)}, u32[]{:S(2)}) collective-permute-start(bf16[128,1024]{1,0:T(8,128)(2,1)} %refs_1_.1), channel_id=1, source_target_pairs={{0,16},{2,18},{4,20},{6,22},{8,24},{10,26},{12,28},{14,30},{16,0},... | collective-permute-start | bytes 786440 | tf_op jit(solution)/shard_map/ppermute | solution.py:389
  9.6 1.5 collective-permute-start.2
  11.1 10.9 %collective-permute-done.1.refs_3_ = bf16[128,1024]{1,0:T(8,128)(2,1)S(1)} collective-permute-done((bf16[128,1024]{1,0:T(8,128)(2,1)}, bf16[128,1024]{1,0:T(8,128)(2,1)S(1)}, u32[]{:S(2)}, u32[]{:S(2)}) %collective-permute-start.1) | collective-permute-done | bytes 262176 | tf_op jit(solution)/shard_map/ppermute | solution.py:389
  21.9 10.7 %collective-permute-done.refs_2_ = bf16[128,1024]{1,0:T(8,128)(2,1)S(1)} collective-permute-done((bf16[128,1024]{1,0:T(8,128)(2,1)}, bf16[128,1024]{1,0:T(8,128)(2,1)S(1)}, u32[]{:S(2)}, u32[]{:S(2)}) %collective-permute-start) | collective-permute-done | bytes 262176 | tf_op jit(solution)/shard_map/ppermute | solution.py:389
  34.7 4.5 %all-to-all-start = ((f32[4,16,128]{2,1,0:T(8,128)}), f32[4,16,128]{2,1,0:T(8,128)S(1)}, u32[]{:S(2)}, u32[]{:S(2)}) async-start(f32[4,16,128]{2,1,0:T(8,128)} %broadcast_in_dim.2), calls=%async_computation | async-start | bytes 65536 | tf_op jit(solution)/shard_map/all_to_all | solution.py:416
  39.9 2.8 %all-to-all-done.meta = f32[4,16,128]{2,1,0:T(8,128)S(1)} async-done(((f32[4,16,128]{2,1,0:T(8,128)}), f32[4,16,128]{2,1,0:T(8,128)S(1)}, u32[]{:S(2)}, u32[]{:S(2)}) %all-to-all-start) | async-done | bytes 32800 | tf_op jit(solution)/shard_map/all_to_all | solution.py:416
  43.4 2.0 select.11.refs_0_.sel
  45.5 4.6 %pack_gates.1 = (bf16[240,1024]{1,0:T(8,128)(2,1)}, bf16[240,1024]{1,0:T(8,128)(2,1)}, bf16[240,1024]{1,0:T(8,128)(2,1)}, bf16[240,1024]{1,0:T(8,128)(2,1)}) custom-call(s32[4]{0:T(128)} %pad_add_fusion.info, f32[4,16,128]{2,1,0:T(8,128)} %copy-done.13, bf16[896,512]{1,0:T(8,128)(2,1)} %select.11.refs_0_.sel, bf16[128,1024]{1,0:T(8,128)(2,1)} %refs_1_.1, ...), custom_call_target="tpu_custom_call" | custom-call | flops 1024 | bytes 1024 | tf_op jit(solution)/shard_map/pack_gates/pallas_call | solution.py:40
  50.0 1.3 collective-permute-start.3
  51.3 1.2 collective-permute-start.4
  52.8 2.8 %collective-permute-start.6 = (bf16[240,1024]{1,0:T(8,128)(2,1)}, bf16[240,1024]{1,0:T(8,128)(2,1)S(1)}, u32[]{:S(2)}, u32[]{:S(2)}) collective-permute-start(bf16[240,1024]{1,0:T(8,128)(2,1)} %get-tuple-element.67.refs_0_), channel_id=1, source_target_pairs={{0,1},{1,0},{2,3},{3,2},{4,5},{5,4},{6,7},{7,6},{8,9},{9,8},{10,11... | collective-permute-start | bytes 1474568 | tf_op jit(solution)/shard_map/ppermute | solution.py:404
  55.5 5.7 %collective-permute-done.3.refs_1_ = bf16[240,1024]{1,0:T(8,128)(2,1)S(1)} collective-permute-done((bf16[240,1024]{1,0:T(8,128)(2,1)}, bf16[240,1024]{1,0:T(8,128)(2,1)S(1)}, u32[]{:S(2)}, u32[]{:S(2)}) %collective-permute-start.3) | collective-permute-done | bytes 491552 | tf_op jit(solution)/shard_map/ppermute | solution.py:396
  61.2 5.2 %collective-permute-start.7 = (bf16[240,1024]{1,0:T(8,128)(2,1)S(1)}, bf16[240,1024]{1,0:T(8,128)(2,1)S(1)}, u32[]{:S(2)}, u32[]{:S(2)}) collective-permute-start(bf16[240,1024]{1,0:T(8,128)(2,1)S(1)} %collective-permute-done.3.refs_1_), channel_id=1, source_target_pairs={{0,1},{1,0},{2,3},{3,2},{4,5},{5,4},{6,7},{7,6},{8,9},{9,8},{10,11... | collective-permute-start | bytes 1474568 | tf_op jit(solution)/shard_map/ppermute | solution.py:404
  66.4 9.3 %collective-permute-start.8 = (bf16[240,1024]{1,0:T(8,128)(2,1)S(1)}, bf16[240,1024]{1,0:T(8,128)(2,1)S(1)}, u32[]{:S(2)}, u32[]{:S(2)}) collective-permute-start(bf16[240,1024]{1,0:T(8,128)(2,1)S(1)} %collective-permute-done.4.refs_2_), channel_id=1, source_target_pairs={{0,1},{1,0},{2,3},{3,2},{4,5},{5,4},{6,7},{7,6},{8,9},{9,8},{10,11... | collective-permute-start | bytes 1474568 | tf_op jit(solution)/shard_map/ppermute | solution.py:404
  75.8 3.6 %route.1.refs_1_ = bf16[512,896]{1,0:T(8,128)(2,1)} custom-call(s32[4]{0:T(128)} %pad_add_fusion.info, f32[4,16,128]{2,1,0:T(8,128)} %copy-done.13), custom_call_target="tpu_custom_call" | custom-call | flops 1024 | bytes 1024 | tf_op jit(solution)/shard_map/route/pallas_call | solution.py:40
  79.4 4.3 %pack.1 = (bf16[224,1024]{1,0:T(8,128)(2,1)}, bf16[224,1024]{1,0:T(8,128)(2,1)}, bf16[224,1024]{1,0:T(8,128)(2,1)}, bf16[224,1024]{1,0:T(8,128)(2,1)}) custom-call(s32[4]{0:T(128)} %pad_add_fusion.info, bf16[896,512]{1,0:T(8,128)(2,1)} %select.11.refs_0_.sel, bf16[4,128,1024]{2,1,0:T(8,128)(2,1)} %bitcast.13), custom_call_target="tpu_custom_call" | custom-call | flops 1024 | bytes 1024 | tf_op jit(solution)/shard_map/pack/pallas_call | solution.py:40
  83.8 0.9 collective-permute-start.10
  85.3 1.2 collective-permute-start.12
  86.5 0.8 copy-done.5
  87.3 0.8 copy-done.6
  88.1 18.7 %expert_forward.1 = (bf16[224,1024]{1,0:T(8,128)(2,1)}, bf16[224,1024]{1,0:T(8,128)(2,1)}, bf16[224,1024]{1,0:T(8,128)(2,1)}, bf16[224,1024]{1,0:T(8,128)(2,1)},...) custom-call(s32[4]{0:T(128)} %pad_add_fusion.info, ...), custom_call_target="tpu_custom_call" | custom-call | flops 1024 | bytes 1024 | tf_op jit(solution)/shard_map/expert_forward/pallas_call | solution.py:40
  106.8 1.3 collective-permute-start.18
  110.1 1.2 add_convert_fusion.4
  111.6 1.0 add_convert_fusion.5
  113.4 0.9 add_convert_fusion.6
  114.4 1.3 collective-permute-start.19
  116.0 1.0 collective-permute-start.15
  117.0 1.0 add_convert_fusion.7.refs_2_
  118.0 0.7 copy-done.11
  118.9 19.3 %expert_backward.1 = (bf16[240,1024]{1,0:T(8,128)(2,1)}, bf16[240,1024]{1,0:T(8,128)(2,1)}, bf16[240,1024]{1,0:T(8,128)(2,1)}, bf16[240,1024]{1,0:T(8,128)(2,1)}...) custom-call(s32[4]{0:T(128)} %pad_add_fusion.info, ...), custom_call_target="tpu_custom_call" | custom-call | flops 1024 | bytes 1024 | tf_op jit(solution)/shard_map/expert_backward/pallas_call | solution.py:40
  138.3 1.1 collective-permute-start.29
  139.4 5.5 %combine.1 = bf16[4,128,1024]{2,1,0:T(8,128)(2,1)} custom-call(s32[4]{0:T(128)} %pad_add_fusion.info, f32[4,16,128]{2,1,0:T(8,128)} %copy-done.13, bf16[896,512]{1,0:T(8,128)(2,1)} %select.11.refs_0_.sel, bf16[512,896]{1,0:T(8,128)(2,1)} %route.1.refs_1_, bf16[224,1024]{1,0:T(8,128)(2,1)} %add_convert_fusion.7.refs_2_, bf16[224,1024]{1,0:T(8,128)(2,1)} %copy-done.23, ...), custom_call_target="tpu_custom_call" | custom-call | flops 1024 | bytes 1024 | tf_op jit(solution)/shard_map/combine/pallas_call | solution.py:40
  145.0 0.9 collective-permute-start.25
  146.2 1.3 collective-permute-start.30
  148.4 1.0 collective-permute-start.26
  149.4 1.0 add_convert_fusion.3.refs_2_
  150.4 8.8 %collective-permute-done.30.refs_5_ = bf16[240,1024]{1,0:T(8,128)(2,1)S(1)} collective-permute-done((bf16[240,1024]{1,0:T(8,128)(2,1)S(1)}, bf16[240,1024]{1,0:T(8,128)(2,1)S(1)}, u32[]{:S(2)}, u32[]{:S(2)}) %collective-permute-start.30) | collective-permute-done | bytes 491552 | tf_op jit(solution)/shard_map/ppermute | solution.py:396
  159.1 11.7 %collective-permute-done.28.refs_4_ = bf16[240,1024]{1,0:T(8,128)(2,1)S(1)} collective-permute-done((bf16[240,1024]{1,0:T(8,128)(2,1)S(1)}, bf16[240,1024]{1,0:T(8,128)(2,1)S(1)}, u32[]{:S(2)}, u32[]{:S(2)}) %collective-permute-start.28) | collective-permute-done | bytes 491552 | tf_op jit(solution)/shard_map/ppermute | solution.py:396
  170.8 0.8 copy-done.19
  171.6 0.8 copy-done.20
  172.4 5.2 %combine_gates.1 = (bf16[144,1024]{1,0:T(8,128)(2,1)}, bf16[144,1024]{1,0:T(8,128)(2,1)}, bf16[144,1024]{1,0:T(8,128)(2,1)}, bf16[144,1024]{1,0:T(8,128)(2,1)}) custom-call(s32[4]{0:T(128)} %pad_add_fusion.info, f32[4,16,128]{2,1,0:T(8,128)} %copy-done.13, bf16[896,512]{1,0:T(8,128)(2,1)} %select.11.refs_0_.sel, bf16[512,896]{1,0:T(8,128)(2,1)} %route.1.refs_1_, ...), custom_call_target="tpu_custom_call" | custom-call | flops 1024 | bytes 1024 | tf_op jit(solution)/shard_map/combine_gates/pallas_call | solution.py:40
  177.6 1.1 collective-permute-start.31
  179.2 1.2 collective-permute-start.33
  180.5 13.9 %expert_weights.1 = (bf16[1,2,704,2048]{3,2,1,0:T(8,128)(2,1)}, bf16[1,704,2048]{2,1,0:T(8,128)(2,1)}) custom-call(s32[4]{0:T(128)} %pad_add_fusion.info, bf16[240,1024]{1,0:T(8,128)(2,1)} %get-tuple-element.67.refs_0_, bf16[240,1024]{1,0:T(8,128)(2,1)} %copy-done, bf16[240,1024]{1,0:T(8,128)(2,1)} %copy-done.1, bf16[240,1024]{1,0:T(8,128)(2,1)} %copy-done.2, ...), custom_call_target="tpu_custom_call" | custom-call | flops 1024 | bytes 1024 | tf_op jit(solution)/shard_map/expert_weights/pallas_call | solution.py:40
  194.4 4.4 %collective-permute-done.32 = bf16[144,1024]{1,0:T(8,128)(2,1)S(1)} collective-permute-done((bf16[144,1024]{1,0:T(8,128)(2,1)}, bf16[144,1024]{1,0:T(8,128)(2,1)S(1)}, u32[]{:S(2)}, u32[]{:S(2)}) %collective-permute-start.32) | collective-permute-done | bytes 294944 | tf_op jit(solution)/shard_map/ppermute | solution.py:389
  198.7 6.3 %collective-permute-done.33 = bf16[144,1024]{1,0:T(8,128)(2,1)S(1)} collective-permute-done((bf16[144,1024]{1,0:T(8,128)(2,1)}, bf16[144,1024]{1,0:T(8,128)(2,1)S(1)}, u32[]{:S(2)}, u32[]{:S(2)}) %collective-permute-start.33) | collective-permute-done | bytes 294944 | tf_op jit(solution)/shard_map/ppermute | solution.py:389
  205.6 0.9 add_convert_fusion.8
  206.6 1.7 fusion
  (123 shorter events, 10.5 us)
Async XLA Ops:
  7.2 72.3 %all-gather.3.cloned.1.call-start = ((), (), s32[]{:S(2)}) async-start(), calls=%async_computation.3 | async-start | bytes 1310720 | tf_op jit(solution)/shard_map/all_gather | solution.py:485
  7.2 14.7 %collective-permute-start.1 = (bf16[128,1024]{1,0:T(8,128)(2,1)}, bf16[128,1024]{1,0:T(8,128)(2,1)S(1)}, u32[]{:S(2)}, u32[]{:S(2)}) collective-permute-start(bf16[128,1024]{1,0:T(8,128)(2,1)} %refs_1_.1), channel_id=1, source_target_pairs={{0,16},{2,18},{4,20},{6,22},{8,24},{10,26},{12,28},{14,30},{16,0},... | collective-permute-start | bytes 786440 | tf_op jit(solution)/shard_map/ppermute | solution.py:389
  9.6 23.1 %collective-permute-start = (bf16[128,1024]{1,0:T(8,128)(2,1)}, bf16[128,1024]{1,0:T(8,128)(2,1)S(1)}, u32[]{:S(2)}, u32[]{:S(2)}) collective-permute-start(bf16[128,1024]{1,0:T(8,128)(2,1)} %refs_1_.1), channel_id=1, source_target_pairs={{0,8},{2,10},{4,12},{6,14},{8,16},{10,18},{12,20},{14,22},{16,24},... | collective-permute-start | bytes 786440 | tf_op jit(solution)/shard_map/ppermute | solution.py:389
  9.6 23.1 %collective-permute-start.2 = (bf16[128,1024]{1,0:T(8,128)(2,1)}, bf16[128,1024]{1,0:T(8,128)(2,1)S(1)}, u32[]{:S(2)}, u32[]{:S(2)}) collective-permute-start(bf16[128,1024]{1,0:T(8,128)(2,1)} %refs_1_.1), channel_id=1, source_target_pairs={{0,24},{2,26},{4,28},{6,30},{8,0},{10,2},{12,4},{14,6},{16,8},{18,... | collective-permute-start | bytes 786440 | tf_op jit(solution)/shard_map/ppermute | solution.py:389
  21.9 23.5 %copy-start.28 = (bf16[128,1024]{1,0:T(8,128)(2,1)}, bf16[128,1024]{1,0:T(8,128)(2,1)S(1)}, u32[]{:S(2)}) copy-start(bf16[128,1024]{1,0:T(8,128)(2,1)S(1)} %collective-permute-done.1.refs_3_) | copy-start | bytes 786436
  32.7 12.8 %copy-start.29 = (bf16[128,1024]{1,0:T(8,128)(2,1)}, bf16[128,1024]{1,0:T(8,128)(2,1)S(1)}, u32[]{:S(2)}) copy-start(bf16[128,1024]{1,0:T(8,128)(2,1)S(1)} %collective-permute-done.refs_2_) | copy-start | bytes 786436
  32.7 12.8 %copy-start.30 = (bf16[128,1024]{1,0:T(8,128)(2,1)}, bf16[128,1024]{1,0:T(8,128)(2,1)S(1)}, u32[]{:S(2)}) copy-start(bf16[128,1024]{1,0:T(8,128)(2,1)S(1)} %collective-permute-done.2.refs_4_) | copy-start | bytes 786436
  34.7 8.0 %all-to-all-start = ((f32[4,16,128]{2,1,0:T(8,128)}), f32[4,16,128]{2,1,0:T(8,128)S(1)}, u32[]{:S(2)}, u32[]{:S(2)}) async-start(f32[4,16,128]{2,1,0:T(8,128)} %broadcast_in_dim.2), calls=%async_computation | async-start | bytes 65536 | tf_op jit(solution)/shard_map/all_to_all | solution.py:416
  39.3 167.3 %reduce-scatter.2.cloned.1.call-start = ((), (), s32[]{:S(2)}) async-start(), calls=%async_computation.2 | async-start | bytes 1310720 | tf_op jit(solution)/shard_map/reduce_scatter | solution.py:465
  50.0 11.2 %collective-permute-start.3 = (bf16[240,1024]{1,0:T(8,128)(2,1)}, bf16[240,1024]{1,0:T(8,128)(2,1)S(1)}, u32[]{:S(2)}, u32[]{:S(2)}) collective-permute-start(bf16[240,1024]{1,0:T(8,128)(2,1)} %get-tuple-element.68), channel_id=1, source_target_pairs={{0,2},{2,0},{4,6},{6,4},{8,10},{10,8},{12,14},{14,12},{16,18},{18,... | collective-permute-start | bytes 1474568 | tf_op jit(solution)/shard_map/ppermute | solution.py:396
  51.3 15.1 %collective-permute-start.4 = (bf16[240,1024]{1,0:T(8,128)(2,1)}, bf16[240,1024]{1,0:T(8,128)(2,1)S(1)}, u32[]{:S(2)}, u32[]{:S(2)}) collective-permute-start(bf16[240,1024]{1,0:T(8,128)(2,1)} %get-tuple-element.69), channel_id=1, source_target_pairs={{0,4},{2,6},{4,0},{6,2},{8,12},{10,14},{12,8},{14,10},{16,20},{18,... | collective-permute-start | bytes 1474568 | tf_op jit(solution)/shard_map/ppermute | solution.py:396
  52.6 23.1 %collective-permute-start.5 = (bf16[240,1024]{1,0:T(8,128)(2,1)}, bf16[240,1024]{1,0:T(8,128)(2,1)S(1)}, u32[]{:S(2)}, u32[]{:S(2)}) collective-permute-start(bf16[240,1024]{1,0:T(8,128)(2,1)} %get-tuple-element.70), channel_id=1, source_target_pairs={{0,6},{2,4},{4,2},{6,0},{8,14},{10,12},{12,10},{14,8},{16,22},{18,... | collective-permute-start | bytes 1474568 | tf_op jit(solution)/shard_map/ppermute | solution.py:396
  52.8 31.9 %collective-permute-start.6 = (bf16[240,1024]{1,0:T(8,128)(2,1)}, bf16[240,1024]{1,0:T(8,128)(2,1)S(1)}, u32[]{:S(2)}, u32[]{:S(2)}) collective-permute-start(bf16[240,1024]{1,0:T(8,128)(2,1)} %get-tuple-element.67.refs_0_), channel_id=1, source_target_pairs={{0,1},{1,0},{2,3},{3,2},{4,5},{5,4},{6,7},{7,6},{8,9},{9,8},{10,11... | collective-permute-start | bytes 1474568 | tf_op jit(solution)/shard_map/ppermute | solution.py:404
  61.2 22.5 %copy-start = (bf16[240,1024]{1,0:T(8,128)(2,1)}, bf16[240,1024]{1,0:T(8,128)(2,1)S(1)}, u32[]{:S(2)}) copy-start(bf16[240,1024]{1,0:T(8,128)(2,1)S(1)} %collective-permute-done.3.refs_1_) | copy-start | bytes 1474564
  61.2 24.1 %collective-permute-start.7 = (bf16[240,1024]{1,0:T(8,128)(2,1)S(1)}, bf16[240,1024]{1,0:T(8,128)(2,1)S(1)}, u32[]{:S(2)}, u32[]{:S(2)}) collective-permute-start(bf16[240,1024]{1,0:T(8,128)(2,1)S(1)} %collective-permute-done.3.refs_1_), channel_id=1, source_target_pairs={{0,1},{1,0},{2,3},{3,2},{4,5},{5,4},{6,7},{7,6},{8,9},{9,8},{10,11... | collective-permute-start | bytes 1474568 | tf_op jit(solution)/shard_map/ppermute | solution.py:404
  66.4 17.3 %copy-start.1 = (bf16[240,1024]{1,0:T(8,128)(2,1)}, bf16[240,1024]{1,0:T(8,128)(2,1)S(1)}, u32[]{:S(2)}) copy-start(bf16[240,1024]{1,0:T(8,128)(2,1)S(1)} %collective-permute-done.4.refs_2_) | copy-start | bytes 1474564
  66.4 20.1 %collective-permute-start.8 = (bf16[240,1024]{1,0:T(8,128)(2,1)S(1)}, bf16[240,1024]{1,0:T(8,128)(2,1)S(1)}, u32[]{:S(2)}, u32[]{:S(2)}) collective-permute-start(bf16[240,1024]{1,0:T(8,128)(2,1)S(1)} %collective-permute-done.4.refs_2_), channel_id=1, source_target_pairs={{0,1},{1,0},{2,3},{3,2},{4,5},{5,4},{6,7},{7,6},{8,9},{9,8},{10,11... | collective-permute-start | bytes 1474568 | tf_op jit(solution)/shard_map/ppermute | solution.py:404
  75.7 8.0 %copy-start.2 = (bf16[240,1024]{1,0:T(8,128)(2,1)}, bf16[240,1024]{1,0:T(8,128)(2,1)S(1)}, u32[]{:S(2)}) copy-start(bf16[240,1024]{1,0:T(8,128)(2,1)S(1)} %collective-permute-done.5.refs_3_) | copy-start | bytes 1474564
  75.7 10.8 %collective-permute-start.9 = (bf16[240,1024]{1,0:T(8,128)(2,1)S(1)}, bf16[240,1024]{1,0:T(8,128)(2,1)S(1)}, u32[]{:S(2)}, u32[]{:S(2)}) collective-permute-start(bf16[240,1024]{1,0:T(8,128)(2,1)S(1)} %collective-permute-done.5.refs_3_), channel_id=1, source_target_pairs={{0,1},{1,0},{2,3},{3,2},{4,5},{5,4},{6,7},{7,6},{8,9},{9,8},{10,11... | collective-permute-start | bytes 1474568 | tf_op jit(solution)/shard_map/ppermute | solution.py:404
  83.8 23.0 %collective-permute-start.10 = (bf16[224,1024]{1,0:T(8,128)(2,1)}, bf16[224,1024]{1,0:T(8,128)(2,1)S(1)}, u32[]{:S(2)}, u32[]{:S(2)}) collective-permute-start(bf16[224,1024]{1,0:T(8,128)(2,1)} %get-tuple-element.75), channel_id=1, source_target_pairs={{0,2},{2,0},{4,6},{6,4},{8,10},{10,8},{12,14},{14,12},{16,18},{18,... | collective-permute-start | bytes 1376264 | tf_op jit(solution)/shard_map/ppermute | solution.py:396
  84.7 22.1 %collective-permute-start.11 = (bf16[224,1024]{1,0:T(8,128)(2,1)}, bf16[224,1024]{1,0:T(8,128)(2,1)}, u32[]{:S(2)}, u32[]{:S(2)}) collective-permute-start(bf16[224,1024]{1,0:T(8,128)(2,1)} %get-tuple-element.76), channel_id=1, source_target_pairs={{0,4},{2,6},{4,0},{6,2},{8,12},{10,14},{12,8},{14,10},{16,20},{18,... | collective-permute-start | bytes 1376264 | tf_op jit(solution)/shard_map/ppermute | solution.py:396
  85.3 21.4 %collective-permute-start.12 = (bf16[224,1024]{1,0:T(8,128)(2,1)}, bf16[224,1024]{1,0:T(8,128)(2,1)}, u32[]{:S(2)}, u32[]{:S(2)}) collective-permute-start(bf16[224,1024]{1,0:T(8,128)(2,1)} %get-tuple-element.77), channel_id=1, source_target_pairs={{0,6},{2,4},{4,2},{6,0},{8,14},{10,12},{12,10},{14,8},{16,22},{18,... | collective-permute-start | bytes 1376264 | tf_op jit(solution)/shard_map/ppermute | solution.py:396
  86.5 21.7 %copy-start.7 = (bf16[224,1024]{1,0:T(8,128)(2,1)S(1)}, bf16[224,1024]{1,0:T(8,128)(2,1)}, u32[]{:S(2)}) copy-start(bf16[224,1024]{1,0:T(8,128)(2,1)} %get-tuple-element.96.refs_0_.refs_8_) | copy-start | bytes 1376260
  106.8 3.0 %collective-permute-start.18 = (bf16[224,1024]{1,0:T(8,128)(2,1)}, bf16[224,1024]{1,0:T(8,128)(2,1)S(1)}, u32[]{:S(2)}, u32[]{:S(2)}) collective-permute-start(bf16[224,1024]{1,0:T(8,128)(2,1)} %get-tuple-element.94), channel_id=1, source_target_pairs={{0,1},{1,0},{2,3},{3,2},{4,5},{5,4},{6,7},{7,6},{8,9},{9,8},{10,11... | collective-permute-start | bytes 1376264 | tf_op jit(solution)/shard_map/ppermute | solution.py:404
  108.1 3.2 %collective-permute-start.16 = (bf16[224,1024]{1,0:T(8,128)(2,1)}, bf16[224,1024]{1,0:T(8,128)(2,1)S(1)}, u32[]{:S(2)}, u32[]{:S(2)}) collective-permute-start(bf16[224,1024]{1,0:T(8,128)(2,1)} %get-tuple-element.90), channel_id=1, source_target_pairs={{0,1},{1,0},{2,3},{3,2},{4,5},{5,4},{6,7},{7,6},{8,9},{9,8},{10,11... | collective-permute-start | bytes 1376264 | tf_op jit(solution)/shard_map/ppermute | solution.py:404
  108.2 6.2 %collective-permute-start.20 = (bf16[224,1024]{1,0:T(8,128)(2,1)S(1)}, bf16[224,1024]{1,0:T(8,128)(2,1)S(1)}, u32[]{:S(2)}, u32[]{:S(2)}) collective-permute-start(bf16[224,1024]{1,0:T(8,128)(2,1)S(1)} %copy-done.7), channel_id=1, source_target_pairs={{0,1},{1,0},{2,3},{3,2},{4,5},{5,4},{6,7},{7,6},{8,9},{9,8},{10,11... | collective-permute-start | bytes 1376264 | tf_op jit(solution)/shard_map/ppermute | solution.py:404
  108.6 7.0 %collective-permute-start.21 = (bf16[224,1024]{1,0:T(8,128)(2,1)S(1)}, bf16[224,1024]{1,0:T(8,128)(2,1)S(1)}, u32[]{:S(2)}, u32[]{:S(2)}) collective-permute-start(bf16[224,1024]{1,0:T(8,128)(2,1)S(1)} %collective-permute-done.10.refs_1_.refs_9_), channel_id=1, source_target_pairs={{0,1},{1,0},{2,3},{3,2},{4,5},{5,4},{6,7},{7,6},{8,9},{9,8},{10,11... | collective-permute-start | bytes 1376264 | tf_op jit(solution)/shard_map/ppermute | solution.py:404
  108.7 9.3 %collective-permute-start.22 = (bf16[224,1024]{1,0:T(8,128)(2,1)}, bf16[224,1024]{1,0:T(8,128)(2,1)S(1)}, u32[]{:S(2)}, u32[]{:S(2)}) collective-permute-start(bf16[224,1024]{1,0:T(8,128)(2,1)} %collective-permute-done.11.refs_2_.refs_10_), channel_id=1, source_target_pairs={{0,1},{1,0},{2,3},{3,2},{4,5},{5,4},{6,7},{7,6},{8,9},{9,8},{10,11... | collective-permute-start | bytes 1376264 | tf_op jit(solution)/shard_map/ppermute | solution.py:404
  109.8 3.3 %collective-permute-start.14 = (bf16[224,1024]{1,0:T(8,128)(2,1)}, bf16[224,1024]{1,0:T(8,128)(2,1)S(1)}, u32[]{:S(2)}, u32[]{:S(2)}) collective-permute-start(bf16[224,1024]{1,0:T(8,128)(2,1)} %get-tuple-element.86), channel_id=1, source_target_pairs={{0,1},{1,0},{2,3},{3,2},{4,5},{5,4},{6,7},{7,6},{8,9},{9,8},{10,11... | collective-permute-start | bytes 1376264 | tf_op jit(solution)/shard_map/ppermute | solution.py:404
  111.3 4.7 %collective-permute-start.13 = (bf16[224,1024]{1,0:T(8,128)(2,1)S(1)}, bf16[224,1024]{1,0:T(8,128)(2,1)S(1)}, u32[]{:S(2)}, u32[]{:S(2)}) collective-permute-start(bf16[224,1024]{1,0:T(8,128)(2,1)S(1)} %copy-done.34), channel_id=1, source_target_pairs={{0,1},{1,0},{2,3},{3,2},{4,5},{5,4},{6,7},{7,6},{8,9},{9,8},{10,11... | collective-permute-start | bytes 1376264 | tf_op jit(solution)/shard_map/ppermute | solution.py:404
  113.0 4.9 %collective-permute-start.23 = (bf16[224,1024]{1,0:T(8,128)(2,1)}, bf16[224,1024]{1,0:T(8,128)(2,1)S(1)}, u32[]{:S(2)}, u32[]{:S(2)}) collective-permute-start(bf16[224,1024]{1,0:T(8,128)(2,1)} %collective-permute-done.12.refs_3_.refs_11_), channel_id=1, source_target_pairs={{0,1},{1,0},{2,3},{3,2},{4,5},{5,4},{6,7},{7,6},{8,9},{9,8},{10,11... | collective-permute-start | bytes 1376264 | tf_op jit(solution)/shard_map/ppermute | solution.py:404
  114.4 23.9 %collective-permute-start.19 = (bf16[224,1024]{1,0:T(8,128)(2,1)S(1)}, bf16[224,1024]{1,0:T(8,128)(2,1)S(1)}, u32[]{:S(2)}, u32[]{:S(2)}) collective-permute-start(bf16[224,1024]{1,0:T(8,128)(2,1)S(1)} %add_convert_fusion.4), channel_id=1, source_target_pairs={{0,6},{2,4},{4,2},{6,0},{8,14},{10,12},{12,10},{14,8},{16,22},{18,... | collective-permute-start | bytes 1376264 | tf_op jit(solution)/shard_map/ppermute | solution.py:396
  115.6 22.6 %collective-permute-start.17 = (bf16[224,1024]{1,0:T(8,128)(2,1)}, bf16[224,1024]{1,0:T(8,128)(2,1)S(1)}, u32[]{:S(2)}, u32[]{:S(2)}) collective-permute-start(bf16[224,1024]{1,0:T(8,128)(2,1)} %add_convert_fusion.5), channel_id=1, source_target_pairs={{0,4},{2,6},{4,0},{6,2},{8,12},{10,14},{12,8},{14,10},{16,20},{18,... | collective-permute-start | bytes 1376264 | tf_op jit(solution)/shard_map/ppermute | solution.py:396
  116.0 22.2 %collective-permute-start.15 = (bf16[224,1024]{1,0:T(8,128)(2,1)}, bf16[224,1024]{1,0:T(8,128)(2,1)S(1)}, u32[]{:S(2)}, u32[]{:S(2)}) collective-permute-start(bf16[224,1024]{1,0:T(8,128)(2,1)} %add_convert_fusion.6), channel_id=1, source_target_pairs={{0,2},{2,0},{4,6},{6,4},{8,10},{10,8},{12,14},{14,12},{16,18},{18,... | collective-permute-start | bytes 1376264 | tf_op jit(solution)/shard_map/ppermute | solution.py:396
  138.3 7.7 %collective-permute-start.29 = (bf16[240,1024]{1,0:T(8,128)(2,1)}, bf16[240,1024]{1,0:T(8,128)(2,1)S(1)}, u32[]{:S(2)}, u32[]{:S(2)}) collective-permute-start(bf16[240,1024]{1,0:T(8,128)(2,1)} %get-tuple-element.118), channel_id=1, source_target_pairs={{0,1},{1,0},{2,3},{3,2},{4,5},{5,4},{6,7},{7,6},{8,9},{9,8},{10,11... | collective-permute-start | bytes 1474568 | tf_op jit(solution)/shard_map/ppermute | solution.py:404
  139.4 8.2 %collective-permute-start.27 = (bf16[240,1024]{1,0:T(8,128)(2,1)}, bf16[240,1024]{1,0:T(8,128)(2,1)S(1)}, u32[]{:S(2)}, u32[]{:S(2)}) collective-permute-start(bf16[240,1024]{1,0:T(8,128)(2,1)} %get-tuple-element.114), channel_id=1, source_target_pairs={{0,1},{1,0},{2,3},{3,2},{4,5},{5,4},{6,7},{7,6},{8,9},{9,8},{10,11... | collective-permute-start | bytes 1474568 | tf_op jit(solution)/shard_map/ppermute | solution.py:404
  145.0 3.2 %collective-permute-start.25 = (bf16[240,1024]{1,0:T(8,128)(2,1)}, bf16[240,1024]{1,0:T(8,128)(2,1)S(1)}, u32[]{:S(2)}, u32[]{:S(2)}) collective-permute-start(bf16[240,1024]{1,0:T(8,128)(2,1)} %get-tuple-element.110), channel_id=1, source_target_pairs={{0,1},{1,0},{2,3},{3,2},{4,5},{5,4},{6,7},{7,6},{8,9},{9,8},{10,11... | collective-permute-start | bytes 1474568 | tf_op jit(solution)/shard_map/ppermute | solution.py:404
  145.9 3.5 %collective-permute-start.24 = (bf16[240,1024]{1,0:T(8,128)(2,1)S(1)}, bf16[240,1024]{1,0:T(8,128)(2,1)S(1)}, u32[]{:S(2)}, u32[]{:S(2)}) collective-permute-start(bf16[240,1024]{1,0:T(8,128)(2,1)S(1)} %copy-done.33), channel_id=1, source_target_pairs={{0,1},{1,0},{2,3},{3,2},{4,5},{5,4},{6,7},{7,6},{8,9},{9,8},{10,11... | collective-permute-start | bytes 1474568 | tf_op jit(solution)/shard_map/ppermute | solution.py:404
  146.2 12.9 %collective-permute-start.30 = (bf16[240,1024]{1,0:T(8,128)(2,1)S(1)}, bf16[240,1024]{1,0:T(8,128)(2,1)S(1)}, u32[]{:S(2)}, u32[]{:S(2)}) collective-permute-start(bf16[240,1024]{1,0:T(8,128)(2,1)S(1)} %add_convert_fusion), channel_id=1, source_target_pairs={{0,6},{2,4},{4,2},{6,0},{8,14},{10,12},{12,10},{14,8},{16,22},{18,... | collective-permute-start | bytes 1474568 | tf_op jit(solution)/shard_map/ppermute | solution.py:396
  147.7 23.1 %collective-permute-start.28 = (bf16[240,1024]{1,0:T(8,128)(2,1)S(1)}, bf16[240,1024]{1,0:T(8,128)(2,1)S(1)}, u32[]{:S(2)}, u32[]{:S(2)}) collective-permute-start(bf16[240,1024]{1,0:T(8,128)(2,1)S(1)} %add_convert_fusion.1), channel_id=1, source_target_pairs={{0,4},{2,6},{4,0},{6,2},{8,12},{10,14},{12,8},{14,10},{16,20},{18,... | collective-permute-start | bytes 1474568 | tf_op jit(solution)/shard_map/ppermute | solution.py:396
  148.4 22.5 %collective-permute-start.26 = (bf16[240,1024]{1,0:T(8,128)(2,1)S(1)}, bf16[240,1024]{1,0:T(8,128)(2,1)S(1)}, u32[]{:S(2)}, u32[]{:S(2)}) collective-permute-start(bf16[240,1024]{1,0:T(8,128)(2,1)S(1)} %add_convert_fusion.2), channel_id=1, source_target_pairs={{0,2},{2,0},{4,6},{6,4},{8,10},{10,8},{12,14},{14,12},{16,18},{18,... | collective-permute-start | bytes 1474568 | tf_op jit(solution)/shard_map/ppermute | solution.py:396
  159.1 11.7 %copy-start.18 = (bf16[240,1024]{1,0:T(8,128)(2,1)}, bf16[240,1024]{1,0:T(8,128)(2,1)S(1)}, u32[]{:S(2)}) copy-start(bf16[240,1024]{1,0:T(8,128)(2,1)S(1)} %collective-permute-done.30.refs_5_) | copy-start | bytes 1474564
  177.6 16.7 %collective-permute-start.31 = (bf16[144,1024]{1,0:T(8,128)(2,1)}, bf16[144,1024]{1,0:T(8,128)(2,1)S(1)}, u32[]{:S(2)}, u32[]{:S(2)}) collective-permute-start(bf16[144,1024]{1,0:T(8,128)(2,1)} %get-tuple-element.120), channel_id=1, source_target_pairs={{0,24},{2,26},{4,28},{6,30},{8,0},{10,2},{12,4},{14,6},{16,8},{18,... | collective-permute-start | bytes 884744 | tf_op jit(solution)/shard_map/ppermute | solution.py:389
  178.7 20.0 %collective-permute-start.32 = (bf16[144,1024]{1,0:T(8,128)(2,1)}, bf16[144,1024]{1,0:T(8,128)(2,1)S(1)}, u32[]{:S(2)}, u32[]{:S(2)}) collective-permute-start(bf16[144,1024]{1,0:T(8,128)(2,1)} %get-tuple-element.121), channel_id=1, source_target_pairs={{0,16},{2,18},{4,20},{6,22},{8,24},{10,26},{12,28},{14,30},{16,0},... | collective-permute-start | bytes 884744 | tf_op jit(solution)/shard_map/ppermute | solution.py:389
  179.2 25.8 %collective-permute-start.33 = (bf16[144,1024]{1,0:T(8,128)(2,1)}, bf16[144,1024]{1,0:T(8,128)(2,1)S(1)}, u32[]{:S(2)}, u32[]{:S(2)}) collective-permute-start(bf16[144,1024]{1,0:T(8,128)(2,1)} %get-tuple-element.122), channel_id=1, source_target_pairs={{0,8},{2,10},{4,12},{6,14},{8,16},{10,18},{12,20},{14,22},{16,24},... | collective-permute-start | bytes 884744 | tf_op jit(solution)/shard_map/ppermute | solution.py:389
  180.5 24.6 %copy-start.32 = (bf16[144,1024]{1,0:T(8,128)(2,1)S(1)}, bf16[144,1024]{1,0:T(8,128)(2,1)}, u32[]{:S(2)}) copy-start(bf16[144,1024]{1,0:T(8,128)(2,1)} %get-tuple-element.119) | copy-start | bytes 884740
  180.5 25.2 %copy-start.31 = (bf16[128,1024]{1,0:T(8,128)(2,1)S(1)}, bf16[128,1024]{1,0:T(8,128)(2,1)}, u32[]{:S(2)}) copy-start(bf16[128,1024]{1,0:T(8,128)(2,1)} %param.10) | copy-start | bytes 786436
  194.3 12.2 %copy-start.27 = (bf16[128,1024]{1,0:T(8,128)(2,1)S(1)}, bf16[128,1024]{1,0:T(8,128)(2,1)}, u32[]{:S(2)}) copy-start(bf16[128,1024]{1,0:T(8,128)(2,1)} %param.9) | copy-start | bytes 786436
  (24 other events, 60.2 us)
Sparse Core Ops, SparseCore 0:
  32.8 28.4 all-gather.2
  145.1 23.5 reduce-scatter.1

commit v6 on v5

--- a/solution.py
+++ b/solution.py
@@ -192,11 +192,8 @@
     loads.finish()
     for s in range(zn):
         here = slice(s * tokens, (s + 1) * tokens)
-        part = dot_nn(chosen[here, :], whole[...]).astype(BF16)
-        if not gates:
-            outs[0][lax.rem(info[3] - s + zn, zn)] = part
-        else:
-            outs[s][0:tokens, :] = part
+        outs[s][0:tokens, :] = dot_nn(chosen[here, :], whole[...]).astype(BF16)
+        if gates:
             outs[s][tokens : tokens + TAIL, :] = jnp.zeros((TAIL, cols), BF16)
             outs[s][tokens : tokens + TAIL, 0:tokens] = totals[s]
 
@@ -454,17 +451,13 @@
     def combine(backs, gates):
         parts = call(
             functools.partial(combine_kernel, **fixed, rows=rows, gates=gates),
-            [shape(tokens + TAIL, cols)] * zn if gates else [shape(zn, tokens, cols)],
+            [shape(tokens + TAIL if gates else tokens, cols)] * zn,
             [info, meta, *sels, chosen, *backs],
             [SMEM] + [VMEM] * (2 + CHUNKS) + [HBM] * pn,
             scratch=[pltpu.VMEM((slots, cols), BF16), pltpu.VMEM((pn, TAIL, cols), BF16)]
             + [dma((2 * pn,))],
             name="combine_gates" if gates else "combine",
         )
-        if not gates:
-            return lax.psum_scatter(
-                parts[0], "expert", scatter_dimension=0, axis_index_groups=columns, tiled=False
-            )
         return [outer_send(part, -s) for s, part in enumerate(parts)]
 
     def swapped(chunks):
@@ -479,7 +472,7 @@
             sums.append(total.astype(BF16))
         return sums
 
-    x_parts = [outer_send(first_half, s) for s in range(zn)]
+    x_parts = [outer_send(first_half if s < 2 else after(first_half, meta), s) for s in range(zn)]
     x_packed = pack_gates(x_parts)
     x_here = inner_exchange(x_packed)
     gathered = lax.all_gather(
@@ -531,7 +524,7 @@
     grads, (gg, ug) = backward[: nt * pn], backward[nt * pn :]
     dx_here = core_sum([after(part, *out_back) for part in grads])
     dx_back = inner_exchange(dx_here)
-    branch = combine(out_back, False).astype(F32)
+    out_parts = combine([after(piece, *dx_here) for piece in out_back], False)
     grad_parts = combine(dx_back, True)
 
     grad_in, grad_out = call(
@@ -550,6 +543,7 @@
         name="expert_weights",
     )
 
+    branch = sum(part.astype(F32) for part in out_parts)
     input_sum = sum(part[:tokens].astype(F32) for part in grad_parts)
     gate_sum = sum(part[tokens : tokens + picks, :tokens].astype(F32) for part in grad_parts)
     restored = (second_half.astype(F32) - branch).astype(BF16)

time: 219 us -> 207 us (0.945); the launches traced: 215 us -> 206 us
  waiting for transfers between devices: 62.5 us -> 46.3 us
  starting transfers between devices: 44.8 us -> 53.5 us
    ppermute x12, waiting for transfers between devices: 26.2 us -> 12.3 us  [inner_send(): return lax.ppermute(value, 'expert', [(e, e ^ q) for e in range(groups)])]
    ppermute x6 -> x9, starting transfers between devices: 6.67 us -> 11.7 us  [outer_send(): lax.ppermute(value, 'expert', [(e, (e // pn + s) % zn * pn + e % pn) for...]
    ppermute x16, starting transfers between devices: 22.7 us -> 26.1 us  [tensor_send(): return lax.ppermute(value, 'tensor', [(c, (c + j) % nt) for c in range(nt)])]
    ppermute x6 -> x9, waiting for transfers between devices: 32.3 us -> 29.9 us  [outer_send(): lax.ppermute(value, 'expert', [(e, (e // pn + s) % zn * pn + e % pn) for...]
    unnamed x70 -> x66, local copies, waits for them, and re-layouts: 4.78 us -> 3.31 us
  transfers between devices with their start and end apart: 37 -> 39, of which waited for: 10 -> 11; matrix products, arithmetic and copies ran while one was open for 5% -> 4% of each run, Pallas kernels for 36% -> 37%
where the time goes in v6:
time: 207 us; the launch traced here: 206 us
  Pallas kernels  76.6 us (37%)
  starting transfers between devices  53.5 us (26%)
  waiting for transfers between devices  46.3 us (22%)
  between operations  14.4 us (7%)
  other arithmetic  11.8 us (6%)
  local copies, waits for them, and re-layouts  3.93 us (2%)
    pallas_call x9, Pallas kernels, call(): pl.pallas_call(kernel, out_shape=outs, in_specs=specs, out_specs=out_spec...  76.6 us
    ppermute x9, waiting for transfers between devices, outer_send(): lax.ppermute(value, 'expert', [(e, (e // pn + s) % zn * pn + e % pn) for...  29.9 us
    ppermute x16, starting transfers between devices, tensor_send(): return lax.ppermute(value, 'tensor', [(c, (c + j) % nt) for c in range(nt)])  26.1 us
    ppermute x12, waiting for transfers between devices, inner_send(): return lax.ppermute(value, 'expert', [(e, e ^ q) for e in range(groups)])  12.3 us
    ppermute x9, starting transfers between devices, outer_send(): lax.ppermute(value, 'expert', [(e, (e // pn + s) % zn * pn + e % pn) for...  11.7 us
    ppermute x12, starting transfers between devices, inner_send(): return lax.ppermute(value, 'expert', [(e, e ^ q) for e in range(groups)])  10.9 us
    convert_element_type x8, other arithmetic, core_sum(): sums.append(total.astype(BF16))  7.33 us
    all_to_all x1, starting transfers between devices, body(): lax.all_to_all(jnp.broadcast_to(own[None], (zn,) + own.shape), 'expert',...  4.76 us
  transfers between devices with their start and end apart: 39, of which 11 were waited for; matrix products, arithmetic and copies ran while one was open for 4% of the time, Pallas kernels for 37%

profile of v6, /device:TPU:9, one launch (start us, length us, event | category | flops | bytes accessed | tf_op | source)
XLA Modules:
  0.0 206.4 jit_solution(7194260354466030330)
XLA Ops:
  9.2 4.8 %all-to-all-start = ((f32[4,16,128]{2,1,0:T(8,128)}), f32[4,16,128]{2,1,0:T(8,128)S(1)}, u32[]{:S(2)}, u32[]{:S(2)}) async-start(f32[4,16,128]{2,1,0:T(8,128)} %broadcast_in_dim.2), calls=%async_computation | async-start | bytes 65536 | tf_op jit(solution)/shard_map/all_to_all | solution.py:413
  13.9 1.2 collective-permute-start
  15.1 2.3 %all-to-all-done.meta = f32[4,16,128]{2,1,0:T(8,128)S(1)} async-done(((f32[4,16,128]{2,1,0:T(8,128)}), f32[4,16,128]{2,1,0:T(8,128)S(1)}, u32[]{:S(2)}, u32[]{:S(2)}) %all-to-all-start) | async-done | bytes 32800 | tf_op jit(solution)/shard_map/all_to_all | solution.py:413
  17.6 1.5 collective-permute-start.2
  19.1 1.6 collective-permute-done.refs_2_
  20.7 16.3 %collective-permute-done.1.refs_3_ = bf16[128,1024]{1,0:T(8,128)(2,1)S(1)} collective-permute-done((bf16[128,1024]{1,0:T(8,128)(2,1)}, bf16[128,1024]{1,0:T(8,128)(2,1)S(1)}, u32[]{:S(2)}, u32[]{:S(2)}) %collective-permute-start.1) | collective-permute-done | bytes 262176 | tf_op jit(solution)/shard_map/ppermute | solution.py:386
  37.7 2.0 select.11.refs_0_.sel
  39.7 4.6 %pack_gates.1 = (bf16[240,1024]{1,0:T(8,128)(2,1)}, bf16[240,1024]{1,0:T(8,128)(2,1)}, bf16[240,1024]{1,0:T(8,128)(2,1)}, bf16[240,1024]{1,0:T(8,128)(2,1)}) custom-call(s32[4]{0:T(128)} %pad_add_fusion.info, f32[4,16,128]{2,1,0:T(8,128)} %copy-done.13, bf16[896,512]{1,0:T(8,128)(2,1)} %select.11.refs_0_.sel, bf16[128,1024]{1,0:T(8,128)(2,1)} %refs_1_.1, ...), custom_call_target="tpu_custom_call" | custom-call | flops 1024 | bytes 1024 | tf_op jit(solution)/shard_map/pack_gates/pallas_call | solution.py:40
  44.3 1.3 collective-permute-start.3
  45.6 1.2 collective-permute-start.4
  47.0 4.7 %collective-permute-start.6 = (bf16[240,1024]{1,0:T(8,128)(2,1)}, bf16[240,1024]{1,0:T(8,128)(2,1)S(1)}, u32[]{:S(2)}, u32[]{:S(2)}) collective-permute-start(bf16[240,1024]{1,0:T(8,128)(2,1)} %get-tuple-element.77.refs_0_), channel_id=1, source_target_pairs={{0,1},{1,0},{2,3},{3,2},{4,5},{5,4},{6,7},{7,6},{8,9},{9,8},{10,11... | collective-permute-start | bytes 1474568 | tf_op jit(solution)/shard_map/ppermute | solution.py:401
  51.8 1.7 collective-permute-done.3.refs_1_
  53.5 9.1 %collective-permute-start.7 = (bf16[240,1024]{1,0:T(8,128)(2,1)S(1)}, bf16[240,1024]{1,0:T(8,128)(2,1)S(1)}, u32[]{:S(2)}, u32[]{:S(2)}) collective-permute-start(bf16[240,1024]{1,0:T(8,128)(2,1)S(1)} %collective-permute-done.3.refs_1_), channel_id=1, source_target_pairs={{0,1},{1,0},{2,3},{3,2},{4,5},{5,4},{6,7},{7,6},{8,9},{9,8},{10,11... | collective-permute-start | bytes 1474568 | tf_op jit(solution)/shard_map/ppermute | solution.py:401
  62.6 7.3 %collective-permute-start.8 = (bf16[240,1024]{1,0:T(8,128)(2,1)S(1)}, bf16[240,1024]{1,0:T(8,128)(2,1)S(1)}, u32[]{:S(2)}, u32[]{:S(2)}) collective-permute-start(bf16[240,1024]{1,0:T(8,128)(2,1)S(1)} %collective-permute-done.4.refs_2_), channel_id=1, source_target_pairs={{0,1},{1,0},{2,3},{3,2},{4,5},{5,4},{6,7},{7,6},{8,9},{9,8},{10,11... | collective-permute-start | bytes 1474568 | tf_op jit(solution)/shard_map/ppermute | solution.py:401
  70.0 3.6 %route.1.refs_1_ = bf16[512,896]{1,0:T(8,128)(2,1)} custom-call(s32[4]{0:T(128)} %pad_add_fusion.info, f32[4,16,128]{2,1,0:T(8,128)} %copy-done.13), custom_call_target="tpu_custom_call" | custom-call | flops 1024 | bytes 1024 | tf_op jit(solution)/shard_map/route/pallas_call | solution.py:40
  73.7 4.3 %pack.1 = (bf16[224,1024]{1,0:T(8,128)(2,1)}, bf16[224,1024]{1,0:T(8,128)(2,1)}, bf16[224,1024]{1,0:T(8,128)(2,1)}, bf16[224,1024]{1,0:T(8,128)(2,1)}) custom-call(s32[4]{0:T(128)} %pad_add_fusion.info, bf16[896,512]{1,0:T(8,128)(2,1)} %select.11.refs_0_.sel, bf16[4,128,1024]{2,1,0:T(8,128)(2,1)} %bitcast.10), custom_call_target="tpu_custom_call" | custom-call | flops 1024 | bytes 1024 | tf_op jit(solution)/shard_map/pack/pallas_call | solution.py:40
  78.0 0.9 collective-permute-start.10
  79.6 1.2 collective-permute-start.12
  80.8 0.7 copy-done.5
  81.5 0.8 copy-done.6
  82.3 18.6 %expert_forward.1 = (bf16[224,1024]{1,0:T(8,128)(2,1)}, bf16[224,1024]{1,0:T(8,128)(2,1)}, bf16[224,1024]{1,0:T(8,128)(2,1)}, bf16[224,1024]{1,0:T(8,128)(2,1)},...) custom-call(s32[4]{0:T(128)} %pad_add_fusion.info, ...), custom_call_target="tpu_custom_call" | custom-call | flops 1024 | bytes 1024 | tf_op jit(solution)/shard_map/expert_forward/pallas_call | solution.py:40
  101.0 1.3 collective-permute-start.18
  104.3 2.0 add_convert_fusion.6
  106.4 0.9 add_convert_fusion.5
  107.8 1.0 add_convert_fusion.4
  109.2 1.1 collective-permute-start.22
  110.3 1.1 collective-permute-start.23
  111.4 1.0 add_convert_fusion.7.refs_2_
  113.3 19.3 %expert_backward.1 = (bf16[240,1024]{1,0:T(8,128)(2,1)}, bf16[240,1024]{1,0:T(8,128)(2,1)}, bf16[240,1024]{1,0:T(8,128)(2,1)}, bf16[240,1024]{1,0:T(8,128)(2,1)}...) custom-call(s32[4]{0:T(128)} %pad_add_fusion.info, ...), custom_call_target="tpu_custom_call" | custom-call | flops 1024 | bytes 1024 | tf_op jit(solution)/shard_map/expert_backward/pallas_call | solution.py:40
  132.7 1.1 collective-permute-start.25
  134.3 1.1 collective-permute-done.25
  135.4 1.2 add_convert_fusion.2
  137.4 1.2 collective-permute-start.32
  138.8 1.1 collective-permute-start.33
  139.9 1.0 add_convert_fusion.3.refs_2_
  140.9 5.0 %combine.1 = (bf16[128,1024]{1,0:T(8,128)(2,1)}, bf16[128,1024]{1,0:T(8,128)(2,1)}, bf16[128,1024]{1,0:T(8,128)(2,1)}, bf16[128,1024]{1,0:T(8,128)(2,1)}) custom-call(s32[4]{0:T(128)} %pad_add_fusion.info, f32[4,16,128]{2,1,0:T(8,128)} %copy-done.13, bf16[896,512]{1,0:T(8,128)(2,1)} %select.11.refs_0_.sel, bf16[512,896]{1,0:T(8,128)(2,1)} %route.1.refs_1_, ...), custom_call_target="tpu_custom_call" | custom-call | flops 1024 | bytes 1024 | tf_op jit(solution)/shard_map/combine/pallas_call | solution.py:40
  145.9 3.1 %collective-permute-start.29 = (bf16[128,1024]{1,0:T(8,128)(2,1)}, bf16[128,1024]{1,0:T(8,128)(2,1)S(1)}, u32[]{:S(2)}, u32[]{:S(2)}) collective-permute-start(bf16[128,1024]{1,0:T(8,128)(2,1)} %get-tuple-element.135), channel_id=1, source_target_pairs={{0,16},{2,18},{4,20},{6,22},{8,24},{10,26},{12,28},{14,30},{16,0},... | collective-permute-start | bytes 786440 | tf_op jit(solution)/shard_map/ppermute | solution.py:386
  149.2 1.2 collective-permute-start.28
  150.4 10.3 %collective-permute-done.33.refs_5_ = bf16[240,1024]{1,0:T(8,128)(2,1)S(1)} collective-permute-done((bf16[240,1024]{1,0:T(8,128)(2,1)S(1)}, bf16[240,1024]{1,0:T(8,128)(2,1)S(1)}, u32[]{:S(2)}, u32[]{:S(2)}) %collective-permute-start.33) | collective-permute-done | bytes 491552 | tf_op jit(solution)/shard_map/ppermute | solution.py:393
  160.7 0.8 copy-done.19
  161.4 5.2 %combine_gates.1 = (bf16[144,1024]{1,0:T(8,128)(2,1)}, bf16[144,1024]{1,0:T(8,128)(2,1)}, bf16[144,1024]{1,0:T(8,128)(2,1)}, bf16[144,1024]{1,0:T(8,128)(2,1)}) custom-call(s32[4]{0:T(128)} %pad_add_fusion.info, f32[4,16,128]{2,1,0:T(8,128)} %copy-done.13, bf16[896,512]{1,0:T(8,128)(2,1)} %select.11.refs_0_.sel, bf16[512,896]{1,0:T(8,128)(2,1)} %route.1.refs_1_, ...), custom_call_target="tpu_custom_call" | custom-call | flops 1024 | bytes 1024 | tf_op jit(solution)/shard_map/combine_gates/pallas_call | solution.py:40
  166.8 3.1 %collective-permute-start.35 = (bf16[144,1024]{1,0:T(8,128)(2,1)}, bf16[144,1024]{1,0:T(8,128)(2,1)S(1)}, u32[]{:S(2)}, u32[]{:S(2)}) collective-permute-start(bf16[144,1024]{1,0:T(8,128)(2,1)} %get-tuple-element.139), channel_id=1, source_target_pairs={{0,16},{2,18},{4,20},{6,22},{8,24},{10,26},{12,28},{14,30},{16,0},... | collective-permute-start | bytes 884744 | tf_op jit(solution)/shard_map/ppermute | solution.py:386
  169.8 1.4 collective-permute-start.34
  171.2 13.9 %expert_weights.1 = (bf16[1,2,704,2048]{3,2,1,0:T(8,128)(2,1)}, bf16[1,704,2048]{2,1,0:T(8,128)(2,1)}) custom-call(s32[4]{0:T(128)} %pad_add_fusion.info, bf16[240,1024]{1,0:T(8,128)(2,1)} %get-tuple-element.77.refs_0_, bf16[240,1024]{1,0:T(8,128)(2,1)} %copy-done, bf16[240,1024]{1,0:T(8,128)(2,1)} %copy-done.1, bf16[240,1024]{1,0:T(8,128)(2,1)} %copy-done.2, ...), custom_call_target="tpu_custom_call" | custom-call | flops 1024 | bytes 1024 | tf_op jit(solution)/shard_map/expert_weights/pallas_call | solution.py:40
  185.4 0.9 subtract_convert_fusion
  186.3 6.7 %collective-permute-done.35 = bf16[144,1024]{1,0:T(8,128)(2,1)S(1)} collective-permute-done((bf16[144,1024]{1,0:T(8,128)(2,1)}, bf16[144,1024]{1,0:T(8,128)(2,1)S(1)}, u32[]{:S(2)}, u32[]{:S(2)}) %collective-permute-start.35) | collective-permute-done | bytes 294944 | tf_op jit(solution)/shard_map/ppermute | solution.py:386
  193.0 5.0 %collective-permute-done.34 = bf16[144,1024]{1,0:T(8,128)(2,1)S(1)} collective-permute-done((bf16[144,1024]{1,0:T(8,128)(2,1)}, bf16[144,1024]{1,0:T(8,128)(2,1)S(1)}, u32[]{:S(2)}, u32[]{:S(2)}) %collective-permute-start.34) | collective-permute-done | bytes 294944 | tf_op jit(solution)/shard_map/ppermute | solution.py:386
  198.6 0.9 add_convert_fusion.8
  (122 shorter events, 10.5 us)
Async XLA Ops:
  9.2 8.3 %all-to-all-start = ((f32[4,16,128]{2,1,0:T(8,128)}), f32[4,16,128]{2,1,0:T(8,128)S(1)}, u32[]{:S(2)}, u32[]{:S(2)}) async-start(f32[4,16,128]{2,1,0:T(8,128)} %broadcast_in_dim.2), calls=%async_computation | async-start | bytes 65536 | tf_op jit(solution)/shard_map/all_to_all | solution.py:413
  13.9 59.7 %all-gather.3.cloned.1.call-start = ((), (), s32[]{:S(2)}) async-start(), calls=%async_computation.1 | async-start | bytes 1310720 | tf_op jit(solution)/shard_map/all_gather | solution.py:478
  13.9 6.8 %collective-permute-start = (bf16[128,1024]{1,0:T(8,128)(2,1)}, bf16[128,1024]{1,0:T(8,128)(2,1)S(1)}, u32[]{:S(2)}, u32[]{:S(2)}) collective-permute-start(bf16[128,1024]{1,0:T(8,128)(2,1)} %refs_1_.1), channel_id=1, source_target_pairs={{0,8},{2,10},{4,12},{6,14},{8,16},{10,18},{12,20},{14,22},{16,24},... | collective-permute-start | bytes 786440 | tf_op jit(solution)/shard_map/ppermute | solution.py:386
  17.4 20.3 %copy-start.13 = (f32[4,16,128]{2,1,0:T(8,128)}, f32[4,16,128]{2,1,0:T(8,128)S(1)}, u32[]{:S(2)}) copy-start(f32[4,16,128]{2,1,0:T(8,128)S(1)} %all-to-all-done.meta) | copy-start | bytes 98308
  17.4 19.6 %collective-permute-start.1 = (bf16[128,1024]{1,0:T(8,128)(2,1)}, bf16[128,1024]{1,0:T(8,128)(2,1)S(1)}, u32[]{:S(2)}, u32[]{:S(2)}) collective-permute-start(bf16[128,1024]{1,0:T(8,128)(2,1)} %refs_1_.1), channel_id=1, source_target_pairs={{0,16},{2,18},{4,20},{6,22},{8,24},{10,26},{12,28},{14,30},{16,0},... | collective-permute-start | bytes 786440 | tf_op jit(solution)/shard_map/ppermute | solution.py:386
  17.6 19.4 %collective-permute-start.2 = (bf16[128,1024]{1,0:T(8,128)(2,1)}, bf16[128,1024]{1,0:T(8,128)(2,1)S(1)}, u32[]{:S(2)}, u32[]{:S(2)}) collective-permute-start(bf16[128,1024]{1,0:T(8,128)(2,1)} %refs_1_.1), channel_id=1, source_target_pairs={{0,24},{2,26},{4,28},{6,30},{8,0},{10,2},{12,4},{14,6},{16,8},{18,... | collective-permute-start | bytes 786440 | tf_op jit(solution)/shard_map/ppermute | solution.py:386
  20.7 19.0 %copy-start.26 = (bf16[128,1024]{1,0:T(8,128)(2,1)}, bf16[128,1024]{1,0:T(8,128)(2,1)S(1)}, u32[]{:S(2)}) copy-start(bf16[128,1024]{1,0:T(8,128)(2,1)S(1)} %collective-permute-done.refs_2_) | copy-start | bytes 786436
  44.3 9.2 %collective-permute-start.3 = (bf16[240,1024]{1,0:T(8,128)(2,1)}, bf16[240,1024]{1,0:T(8,128)(2,1)S(1)}, u32[]{:S(2)}, u32[]{:S(2)}) collective-permute-start(bf16[240,1024]{1,0:T(8,128)(2,1)} %get-tuple-element.78), channel_id=1, source_target_pairs={{0,2},{2,0},{4,6},{6,4},{8,10},{10,8},{12,14},{14,12},{16,18},{18,... | collective-permute-start | bytes 1474568 | tf_op jit(solution)/shard_map/ppermute | solution.py:393
  45.6 17.1 %collective-permute-start.4 = (bf16[240,1024]{1,0:T(8,128)(2,1)}, bf16[240,1024]{1,0:T(8,128)(2,1)S(1)}, u32[]{:S(2)}, u32[]{:S(2)}) collective-permute-start(bf16[240,1024]{1,0:T(8,128)(2,1)} %get-tuple-element.79), channel_id=1, source_target_pairs={{0,4},{2,6},{4,0},{6,2},{8,12},{10,14},{12,8},{14,10},{16,20},{18,... | collective-permute-start | bytes 1474568 | tf_op jit(solution)/shard_map/ppermute | solution.py:393
  46.8 23.1 %collective-permute-start.5 = (bf16[240,1024]{1,0:T(8,128)(2,1)}, bf16[240,1024]{1,0:T(8,128)(2,1)S(1)}, u32[]{:S(2)}, u32[]{:S(2)}) collective-permute-start(bf16[240,1024]{1,0:T(8,128)(2,1)} %get-tuple-element.80), channel_id=1, source_target_pairs={{0,6},{2,4},{4,2},{6,0},{8,14},{10,12},{12,10},{14,8},{16,22},{18,... | collective-permute-start | bytes 1474568 | tf_op jit(solution)/shard_map/ppermute | solution.py:393
  47.0 31.9 %collective-permute-start.6 = (bf16[240,1024]{1,0:T(8,128)(2,1)}, bf16[240,1024]{1,0:T(8,128)(2,1)S(1)}, u32[]{:S(2)}, u32[]{:S(2)}) collective-permute-start(bf16[240,1024]{1,0:T(8,128)(2,1)} %get-tuple-element.77.refs_0_), channel_id=1, source_target_pairs={{0,1},{1,0},{2,3},{3,2},{4,5},{5,4},{6,7},{7,6},{8,9},{9,8},{10,11... | collective-permute-start | bytes 1474568 | tf_op jit(solution)/shard_map/ppermute | solution.py:401
  53.5 24.5 %copy-start = (bf16[240,1024]{1,0:T(8,128)(2,1)}, bf16[240,1024]{1,0:T(8,128)(2,1)S(1)}, u32[]{:S(2)}) copy-start(bf16[240,1024]{1,0:T(8,128)(2,1)S(1)} %collective-permute-done.3.refs_1_) | copy-start | bytes 1474564
  53.5 26.1 %collective-permute-start.7 = (bf16[240,1024]{1,0:T(8,128)(2,1)S(1)}, bf16[240,1024]{1,0:T(8,128)(2,1)S(1)}, u32[]{:S(2)}, u32[]{:S(2)}) collective-permute-start(bf16[240,1024]{1,0:T(8,128)(2,1)S(1)} %collective-permute-done.3.refs_1_), channel_id=1, source_target_pairs={{0,1},{1,0},{2,3},{3,2},{4,5},{5,4},{6,7},{7,6},{8,9},{9,8},{10,11... | collective-permute-start | bytes 1474568 | tf_op jit(solution)/shard_map/ppermute | solution.py:401
  62.6 15.4 %copy-start.1 = (bf16[240,1024]{1,0:T(8,128)(2,1)}, bf16[240,1024]{1,0:T(8,128)(2,1)S(1)}, u32[]{:S(2)}) copy-start(bf16[240,1024]{1,0:T(8,128)(2,1)S(1)} %collective-permute-done.4.refs_2_) | copy-start | bytes 1474564
  62.6 18.1 %collective-permute-start.8 = (bf16[240,1024]{1,0:T(8,128)(2,1)S(1)}, bf16[240,1024]{1,0:T(8,128)(2,1)S(1)}, u32[]{:S(2)}, u32[]{:S(2)}) collective-permute-start(bf16[240,1024]{1,0:T(8,128)(2,1)S(1)} %collective-permute-done.4.refs_2_), channel_id=1, source_target_pairs={{0,1},{1,0},{2,3},{3,2},{4,5},{5,4},{6,7},{7,6},{8,9},{9,8},{10,11... | collective-permute-start | bytes 1474568 | tf_op jit(solution)/shard_map/ppermute | solution.py:401
  70.0 10.8 %collective-permute-start.9 = (bf16[240,1024]{1,0:T(8,128)(2,1)S(1)}, bf16[240,1024]{1,0:T(8,128)(2,1)S(1)}, u32[]{:S(2)}, u32[]{:S(2)}) collective-permute-start(bf16[240,1024]{1,0:T(8,128)(2,1)S(1)} %collective-permute-done.5.refs_3_), channel_id=1, source_target_pairs={{0,1},{1,0},{2,3},{3,2},{4,5},{5,4},{6,7},{7,6},{8,9},{9,8},{10,11... | collective-permute-start | bytes 1474568 | tf_op jit(solution)/shard_map/ppermute | solution.py:401
  78.0 23.0 %collective-permute-start.10 = (bf16[224,1024]{1,0:T(8,128)(2,1)}, bf16[224,1024]{1,0:T(8,128)(2,1)}, u32[]{:S(2)}, u32[]{:S(2)}) collective-permute-start(bf16[224,1024]{1,0:T(8,128)(2,1)} %get-tuple-element.85), channel_id=1, source_target_pairs={{0,2},{2,0},{4,6},{6,4},{8,10},{10,8},{12,14},{14,12},{16,18},{18,... | collective-permute-start | bytes 1376264 | tf_op jit(solution)/shard_map/ppermute | solution.py:393
  78.9 22.0 %collective-permute-start.11 = (bf16[224,1024]{1,0:T(8,128)(2,1)}, bf16[224,1024]{1,0:T(8,128)(2,1)}, u32[]{:S(2)}, u32[]{:S(2)}) collective-permute-start(bf16[224,1024]{1,0:T(8,128)(2,1)} %get-tuple-element.86), channel_id=1, source_target_pairs={{0,4},{2,6},{4,0},{6,2},{8,12},{10,14},{12,8},{14,10},{16,20},{18,... | collective-permute-start | bytes 1376264 | tf_op jit(solution)/shard_map/ppermute | solution.py:393
  79.6 21.4 %collective-permute-start.12 = (bf16[224,1024]{1,0:T(8,128)(2,1)}, bf16[224,1024]{1,0:T(8,128)(2,1)S(1)}, u32[]{:S(2)}, u32[]{:S(2)}) collective-permute-start(bf16[224,1024]{1,0:T(8,128)(2,1)} %get-tuple-element.87), channel_id=1, source_target_pairs={{0,6},{2,4},{4,2},{6,0},{8,14},{10,12},{12,10},{14,8},{16,22},{18,... | collective-permute-start | bytes 1376264 | tf_op jit(solution)/shard_map/ppermute | solution.py:393
  80.7 21.7 %copy-start.7 = (bf16[224,1024]{1,0:T(8,128)(2,1)S(1)}, bf16[224,1024]{1,0:T(8,128)(2,1)}, u32[]{:S(2)}) copy-start(bf16[224,1024]{1,0:T(8,128)(2,1)} %get-tuple-element.94.refs_0_.refs_8_) | copy-start | bytes 1376260
  101.0 3.0 %collective-permute-start.18 = (bf16[224,1024]{1,0:T(8,128)(2,1)}, bf16[224,1024]{1,0:T(8,128)(2,1)S(1)}, u32[]{:S(2)}, u32[]{:S(2)}) collective-permute-start(bf16[224,1024]{1,0:T(8,128)(2,1)} %get-tuple-element.101), channel_id=1, source_target_pairs={{0,1},{1,0},{2,3},{3,2},{4,5},{5,4},{6,7},{7,6},{8,9},{9,8},{10,11... | collective-permute-start | bytes 1376264 | tf_op jit(solution)/shard_map/ppermute | solution.py:401
  102.3 4.0 %collective-permute-start.19 = (bf16[224,1024]{1,0:T(8,128)(2,1)}, bf16[224,1024]{1,0:T(8,128)(2,1)S(1)}, u32[]{:S(2)}, u32[]{:S(2)}) collective-permute-start(bf16[224,1024]{1,0:T(8,128)(2,1)} %get-tuple-element.105), channel_id=1, source_target_pairs={{0,1},{1,0},{2,3},{3,2},{4,5},{5,4},{6,7},{7,6},{8,9},{9,8},{10,11... | collective-permute-start | bytes 1376264 | tf_op jit(solution)/shard_map/ppermute | solution.py:401
  102.4 6.3 %collective-permute-start.14 = (bf16[224,1024]{1,0:T(8,128)(2,1)S(1)}, bf16[224,1024]{1,0:T(8,128)(2,1)S(1)}, u32[]{:S(2)}, u32[]{:S(2)}) collective-permute-start(bf16[224,1024]{1,0:T(8,128)(2,1)S(1)} %copy-done.7), channel_id=1, source_target_pairs={{0,1},{1,0},{2,3},{3,2},{4,5},{5,4},{6,7},{7,6},{8,9},{9,8},{10,11... | collective-permute-start | bytes 1376264 | tf_op jit(solution)/shard_map/ppermute | solution.py:401
  102.8 6.4 %collective-permute-start.13 = (bf16[224,1024]{1,0:T(8,128)(2,1)}, bf16[224,1024]{1,0:T(8,128)(2,1)S(1)}, u32[]{:S(2)}, u32[]{:S(2)}) collective-permute-start(bf16[224,1024]{1,0:T(8,128)(2,1)} %get-tuple-element.92), channel_id=1, source_target_pairs={{0,1},{1,0},{2,3},{3,2},{4,5},{5,4},{6,7},{7,6},{8,9},{9,8},{10,11... | collective-permute-start | bytes 1376264 | tf_op jit(solution)/shard_map/ppermute | solution.py:401
  102.9 7.4 %collective-permute-start.15 = (bf16[224,1024]{1,0:T(8,128)(2,1)}, bf16[224,1024]{1,0:T(8,128)(2,1)S(1)}, u32[]{:S(2)}, u32[]{:S(2)}) collective-permute-start(bf16[224,1024]{1,0:T(8,128)(2,1)} %collective-permute-done.10.refs_1_.refs_9_), channel_id=1, source_target_pairs={{0,1},{1,0},{2,3},{3,2},{4,5},{5,4},{6,7},{7,6},{8,9},{9,8},{10,11... | collective-permute-start | bytes 1376264 | tf_op jit(solution)/shard_map/ppermute | solution.py:401
  104.0 3.4 %collective-permute-start.20 = (bf16[224,1024]{1,0:T(8,128)(2,1)}, bf16[224,1024]{1,0:T(8,128)(2,1)S(1)}, u32[]{:S(2)}, u32[]{:S(2)}) collective-permute-start(bf16[224,1024]{1,0:T(8,128)(2,1)} %get-tuple-element.109), channel_id=1, source_target_pairs={{0,1},{1,0},{2,3},{3,2},{4,5},{5,4},{6,7},{7,6},{8,9},{9,8},{10,11... | collective-permute-start | bytes 1376264 | tf_op jit(solution)/shard_map/ppermute | solution.py:401
  106.3 6.1 %collective-permute-start.16 = (bf16[224,1024]{1,0:T(8,128)(2,1)}, bf16[224,1024]{1,0:T(8,128)(2,1)S(1)}, u32[]{:S(2)}, u32[]{:S(2)}) collective-permute-start(bf16[224,1024]{1,0:T(8,128)(2,1)} %collective-permute-done.11.refs_2_.refs_10_), channel_id=1, source_target_pairs={{0,1},{1,0},{2,3},{3,2},{4,5},{5,4},{6,7},{7,6},{8,9},{9,8},{10,11... | collective-permute-start | bytes 1376264 | tf_op jit(solution)/shard_map/ppermute | solution.py:401
  107.4 5.0 %collective-permute-start.17 = (bf16[224,1024]{1,0:T(8,128)(2,1)S(1)}, bf16[224,1024]{1,0:T(8,128)(2,1)S(1)}, u32[]{:S(2)}, u32[]{:S(2)}) collective-permute-start(bf16[224,1024]{1,0:T(8,128)(2,1)S(1)} %collective-permute-done.12.refs_3_.refs_11_), channel_id=1, source_target_pairs={{0,1},{1,0},{2,3},{3,2},{4,5},{5,4},{6,7},{7,6},{8,9},{9,8},{10,11... | collective-permute-start | bytes 1376264 | tf_op jit(solution)/shard_map/ppermute | solution.py:401
  108.7 23.9 %collective-permute-start.21 = (bf16[224,1024]{1,0:T(8,128)(2,1)}, bf16[224,1024]{1,0:T(8,128)(2,1)S(1)}, u32[]{:S(2)}, u32[]{:S(2)}) collective-permute-start(bf16[224,1024]{1,0:T(8,128)(2,1)} %add_convert_fusion.6), channel_id=1, source_target_pairs={{0,2},{2,0},{4,6},{6,4},{8,10},{10,8},{12,14},{14,12},{16,18},{18,... | collective-permute-start | bytes 1376264 | tf_op jit(solution)/shard_map/ppermute | solution.py:393
  109.2 23.5 %collective-permute-start.22 = (bf16[224,1024]{1,0:T(8,128)(2,1)}, bf16[224,1024]{1,0:T(8,128)(2,1)S(1)}, u32[]{:S(2)}, u32[]{:S(2)}) collective-permute-start(bf16[224,1024]{1,0:T(8,128)(2,1)} %add_convert_fusion.5), channel_id=1, source_target_pairs={{0,4},{2,6},{4,0},{6,2},{8,12},{10,14},{12,8},{14,10},{16,20},{18,... | collective-permute-start | bytes 1376264 | tf_op jit(solution)/shard_map/ppermute | solution.py:393
  110.3 22.4 %collective-permute-start.23 = (bf16[224,1024]{1,0:T(8,128)(2,1)}, bf16[224,1024]{1,0:T(8,128)(2,1)S(1)}, u32[]{:S(2)}, u32[]{:S(2)}) collective-permute-start(bf16[224,1024]{1,0:T(8,128)(2,1)} %add_convert_fusion.4), channel_id=1, source_target_pairs={{0,6},{2,4},{4,2},{6,0},{8,14},{10,12},{12,10},{14,8},{16,22},{18,... | collective-permute-start | bytes 1376264 | tf_op jit(solution)/shard_map/ppermute | solution.py:393
  132.7 2.8 %collective-permute-start.25 = (bf16[240,1024]{1,0:T(8,128)(2,1)}, bf16[240,1024]{1,0:T(8,128)(2,1)S(1)}, u32[]{:S(2)}, u32[]{:S(2)}) collective-permute-start(bf16[240,1024]{1,0:T(8,128)(2,1)} %get-tuple-element.120), channel_id=1, source_target_pairs={{0,1},{1,0},{2,3},{3,2},{4,5},{5,4},{6,7},{7,6},{8,9},{9,8},{10,11... | collective-permute-start | bytes 1474568 | tf_op jit(solution)/shard_map/ppermute | solution.py:401
  133.7 3.5 %collective-permute-start.26 = (bf16[240,1024]{1,0:T(8,128)(2,1)}, bf16[240,1024]{1,0:T(8,128)(2,1)S(1)}, u32[]{:S(2)}, u32[]{:S(2)}) collective-permute-start(bf16[240,1024]{1,0:T(8,128)(2,1)} %get-tuple-element.124), channel_id=1, source_target_pairs={{0,1},{1,0},{2,3},{3,2},{4,5},{5,4},{6,7},{7,6},{8,9},{9,8},{10,11... | collective-permute-start | bytes 1474568 | tf_op jit(solution)/shard_map/ppermute | solution.py:401
  133.8 6.1 %collective-permute-start.24 = (bf16[240,1024]{1,0:T(8,128)(2,1)}, bf16[240,1024]{1,0:T(8,128)(2,1)S(1)}, u32[]{:S(2)}, u32[]{:S(2)}) collective-permute-start(bf16[240,1024]{1,0:T(8,128)(2,1)} %get-tuple-element.116), channel_id=1, source_target_pairs={{0,1},{1,0},{2,3},{3,2},{4,5},{5,4},{6,7},{7,6},{8,9},{9,8},{10,11... | collective-permute-start | bytes 1474568 | tf_op jit(solution)/shard_map/ppermute | solution.py:401
  134.3 4.3 %collective-permute-start.27 = (bf16[240,1024]{1,0:T(8,128)(2,1)}, bf16[240,1024]{1,0:T(8,128)(2,1)S(1)}, u32[]{:S(2)}, u32[]{:S(2)}) collective-permute-start(bf16[240,1024]{1,0:T(8,128)(2,1)} %get-tuple-element.128), channel_id=1, source_target_pairs={{0,1},{1,0},{2,3},{3,2},{4,5},{5,4},{6,7},{7,6},{8,9},{9,8},{10,11... | collective-permute-start | bytes 1474568 | tf_op jit(solution)/shard_map/ppermute | solution.py:401
  136.7 12.5 %collective-permute-start.31 = (bf16[240,1024]{1,0:T(8,128)(2,1)S(1)}, bf16[240,1024]{1,0:T(8,128)(2,1)S(1)}, u32[]{:S(2)}, u32[]{:S(2)}) collective-permute-start(bf16[240,1024]{1,0:T(8,128)(2,1)S(1)} %add_convert_fusion.2), channel_id=1, source_target_pairs={{0,2},{2,0},{4,6},{6,4},{8,10},{10,8},{12,14},{14,12},{16,18},{18,... | collective-permute-start | bytes 1474568 | tf_op jit(solution)/shard_map/ppermute | solution.py:393
  137.4 13.0 %collective-permute-start.32 = (bf16[240,1024]{1,0:T(8,128)(2,1)S(1)}, bf16[240,1024]{1,0:T(8,128)(2,1)S(1)}, u32[]{:S(2)}, u32[]{:S(2)}) collective-permute-start(bf16[240,1024]{1,0:T(8,128)(2,1)S(1)} %add_convert_fusion.1), channel_id=1, source_target_pairs={{0,4},{2,6},{4,0},{6,2},{8,12},{10,14},{12,8},{14,10},{16,20},{18,... | collective-permute-start | bytes 1474568 | tf_op jit(solution)/shard_map/ppermute | solution.py:393
  138.8 21.9 %collective-permute-start.33 = (bf16[240,1024]{1,0:T(8,128)(2,1)S(1)}, bf16[240,1024]{1,0:T(8,128)(2,1)S(1)}, u32[]{:S(2)}, u32[]{:S(2)}) collective-permute-start(bf16[240,1024]{1,0:T(8,128)(2,1)S(1)} %add_convert_fusion), channel_id=1, source_target_pairs={{0,6},{2,4},{4,2},{6,0},{8,14},{10,12},{12,10},{14,8},{16,22},{18,... | collective-permute-start | bytes 1474568 | tf_op jit(solution)/shard_map/ppermute | solution.py:393
  145.8 24.0 %collective-permute-start.30 = (bf16[128,1024]{1,0:T(8,128)(2,1)}, bf16[128,1024]{1,0:T(8,128)(2,1)S(1)}, u32[]{:S(2)}, u32[]{:S(2)}) collective-permute-start(bf16[128,1024]{1,0:T(8,128)(2,1)} %get-tuple-element.136), channel_id=1, source_target_pairs={{0,8},{2,10},{4,12},{6,14},{8,16},{10,18},{12,20},{14,22},{16,24},... | collective-permute-start | bytes 786440 | tf_op jit(solution)/shard_map/ppermute | solution.py:386
  145.9 39.2 %collective-permute-start.29 = (bf16[128,1024]{1,0:T(8,128)(2,1)}, bf16[128,1024]{1,0:T(8,128)(2,1)S(1)}, u32[]{:S(2)}, u32[]{:S(2)}) collective-permute-start(bf16[128,1024]{1,0:T(8,128)(2,1)} %get-tuple-element.135), channel_id=1, source_target_pairs={{0,16},{2,18},{4,20},{6,22},{8,24},{10,26},{12,28},{14,30},{16,0},... | collective-permute-start | bytes 786440 | tf_op jit(solution)/shard_map/ppermute | solution.py:386
  149.2 36.2 %collective-permute-start.28 = (bf16[128,1024]{1,0:T(8,128)(2,1)}, bf16[128,1024]{1,0:T(8,128)(2,1)S(1)}, u32[]{:S(2)}, u32[]{:S(2)}) collective-permute-start(bf16[128,1024]{1,0:T(8,128)(2,1)} %get-tuple-element.134), channel_id=1, source_target_pairs={{0,24},{2,26},{4,28},{6,30},{8,0},{10,2},{12,4},{14,6},{16,8},{18,... | collective-permute-start | bytes 786440 | tf_op jit(solution)/shard_map/ppermute | solution.py:386
  166.7 19.6 %collective-permute-start.36 = (bf16[144,1024]{1,0:T(8,128)(2,1)}, bf16[144,1024]{1,0:T(8,128)(2,1)S(1)}, u32[]{:S(2)}, u32[]{:S(2)}) collective-permute-start(bf16[144,1024]{1,0:T(8,128)(2,1)} %get-tuple-element.140), channel_id=1, source_target_pairs={{0,8},{2,10},{4,12},{6,14},{8,16},{10,18},{12,20},{14,22},{16,24},... | collective-permute-start | bytes 884744 | tf_op jit(solution)/shard_map/ppermute | solution.py:386
  166.8 26.3 %collective-permute-start.35 = (bf16[144,1024]{1,0:T(8,128)(2,1)}, bf16[144,1024]{1,0:T(8,128)(2,1)S(1)}, u32[]{:S(2)}, u32[]{:S(2)}) collective-permute-start(bf16[144,1024]{1,0:T(8,128)(2,1)} %get-tuple-element.139), channel_id=1, source_target_pairs={{0,16},{2,18},{4,20},{6,22},{8,24},{10,26},{12,28},{14,30},{16,0},... | collective-permute-start | bytes 884744 | tf_op jit(solution)/shard_map/ppermute | solution.py:386
  169.8 28.2 %collective-permute-start.34 = (bf16[144,1024]{1,0:T(8,128)(2,1)}, bf16[144,1024]{1,0:T(8,128)(2,1)S(1)}, u32[]{:S(2)}, u32[]{:S(2)}) collective-permute-start(bf16[144,1024]{1,0:T(8,128)(2,1)} %get-tuple-element.138), channel_id=1, source_target_pairs={{0,24},{2,26},{4,28},{6,30},{8,0},{10,2},{12,4},{14,6},{16,8},{18,... | collective-permute-start | bytes 884744 | tf_op jit(solution)/shard_map/ppermute | solution.py:386
  171.2 14.2 %copy-start.29 = (bf16[128,1024]{1,0:T(8,128)(2,1)S(1)}, bf16[128,1024]{1,0:T(8,128)(2,1)}, u32[]{:S(2)}) copy-start(bf16[128,1024]{1,0:T(8,128)(2,1)} %param.9) | copy-start | bytes 786436
  171.2 14.2 %copy-start.31 = (bf16[128,1024]{1,0:T(8,128)(2,1)S(1)}, bf16[128,1024]{1,0:T(8,128)(2,1)}, u32[]{:S(2)}) copy-start(bf16[128,1024]{1,0:T(8,128)(2,1)} %get-tuple-element.133) | copy-start | bytes 786436
  185.1 13.0 %copy-start.32 = (bf16[144,1024]{1,0:T(8,128)(2,1)S(1)}, bf16[144,1024]{1,0:T(8,128)(2,1)}, u32[]{:S(2)}) copy-start(bf16[144,1024]{1,0:T(8,128)(2,1)} %get-tuple-element.137) | copy-start | bytes 884740
  185.1 13.6 %copy-start.30 = (bf16[128,1024]{1,0:T(8,128)(2,1)S(1)}, bf16[128,1024]{1,0:T(8,128)(2,1)}, u32[]{:S(2)}) copy-start(bf16[128,1024]{1,0:T(8,128)(2,1)} %param.10) | copy-start | bytes 786436
  (24 other events, 93.8 us)
Sparse Core Ops, SparseCore 0:
  37.1 30.8 all-gather.2

commit v7 on v6

--- a/solution.py
+++ b/solution.py
@@ -9,8 +9,9 @@
 
 PLANE = 4
 CHUNKS = 1
+RETURNS = 2
 TAIL = 16
-VMEM_LIMIT = 60 * 1024 * 1024
+VMEM_LIMIT = 62 * 1024 * 1024
 F32 = jnp.float32
 BF16 = jnp.bfloat16
 
@@ -78,25 +79,26 @@
             )
 
 
-def route_kernel(info, meta, ones, *, zn, pn, tokens, picks, cap):
-    rows = zn * cap
+def route_kernel(info, meta, *chosen, zn, pn, tokens, picks, cap):
+    zr = zn // RETURNS
+    rows = zr * cap
     partner = iota((1, 8), 1)
     experts = jnp.where(partner < pn, info[0] + (partner ^ info[1]), -2).astype(F32)
     after = (iota((tokens, tokens), 1) < iota((tokens, tokens), 0)).astype(F32).astype(BF16)
     eye = (iota((16, 16), 0) == iota((16, 16), 1)).astype(F32).astype(BF16)
     lane = iota((tokens, pn * rows), 1).astype(F32)
     for s in range(zn):
-        here = slice(s * tokens, (s + 1) * tokens)
+        g, local = divmod(s, zr)
         columned = dot_tn(outer_meta(info, meta, s, zn).astype(BF16), eye)
         named = jnp.zeros((tokens, 8), F32)
         for k in range(picks):
             named += (columned[:, k : k + 1] == experts).astype(F32)
-        dest = dot_nn(after, named.astype(BF16)) + s * cap
+        dest = dot_nn(after, named.astype(BF16)) + local * cap
         dest = jnp.where(named > 0, dest + rows * partner.astype(F32), -1.0)
         picked = jnp.zeros((tokens, pn * rows), F32)
         for q in range(pn):
             picked += (lane == dest[:, q : q + 1]).astype(F32)
-        ones[here, :] = picked.astype(BF16)
+        chosen[g][local * tokens : (local + 1) * tokens, :] = picked.astype(BF16)
 
 
 def tail_lanes(rows):
@@ -160,42 +162,62 @@
         outs[q][0:rows, :] = dot_nn(chosen, whole[...]).astype(BF16)
 
 
-def combine_kernel(info, meta, *refs, zn, pn, tokens, rows, gates):
-    zc, part_rows = zn // CHUNKS, rows // CHUNKS
-    sels, chosen, backs = refs[:CHUNKS], refs[CHUNKS], refs[CHUNKS + 1 : CHUNKS + 1 + pn]
-    outs, (whole, tails, sems) = refs[CHUNKS + 1 + pn : -3], refs[-3:]
-    cols = whole.shape[1]
+def combine_kernel(info, *refs, zn, pn, tokens, rows):
+    zr = zn // RETURNS
+    chosen, backs = refs[:RETURNS], refs[RETURNS : RETURNS + pn]
+    out, whole, sems = refs[RETURNS + pn :]
+    loads = Loads(sems)
+    for g in range(RETURNS):
+        for q in range(pn):
+            to = whole.at[g, pl.ds(q * rows, rows)]
+            loads.add((g, q), backs[q].at[pl.ds(g * rows, rows)], to)
+    for g in range(RETURNS):
+        loads.need(*((g, q) for q in range(pn)))
+        part = dot_nn(chosen[g][...], whole[g]).astype(BF16)
+        for local in range(zr):
+            place = lax.rem(info[3] - (g * zr + local) + zn, zn)
+            out[place] = part[local * tokens : (local + 1) * tokens, :]
+
+
+def combine_far_kernel(info, meta, sel, chosen, *refs, zn, pn, tokens, rows):
+    zr, slots = zn // RETURNS, RETURNS * rows
+    backs, outs, (gates, whole, tails, sems) = refs[:pn], refs[pn:-4], refs[-4:]
     loads = Loads(sems)
     for q in range(pn):
-        if gates:
-            loads.add(("t", q), backs[q].at[pl.ds(rows, TAIL)], tails.at[q])
+        loads.add(("t", q), backs[q].at[pl.ds(rows, TAIL)], tails.at[q])
         loads.add(q, backs[q].at[pl.ds(0, rows)], whole.at[pl.ds(q * rows, rows)])
-    totals = {}
-    if gates:
-        loads.need(*(("t", q) for q in range(pn)))
-        for g in range(CHUNKS):
-            spreads = []
-            for q in range(pn):
-                at = g * tail_lanes(part_rows)
-                row = tails[q, :, at : at + part_rows]
-                spreads.append(dot_nn(row, sels[g][q * part_rows : (q + 1) * part_rows, :])[0:8, :])
-            for local in range(zc):
-                ids = outer_meta(info, meta, g * zc + local, zn)[0:8, :]
-                total = jnp.zeros((8, tokens), F32)
-                for q in range(pn):
-                    expert = (info[0] + (info[1] ^ q)).astype(F32)
-                    spread = spreads[q][:, local * tokens : (local + 1) * tokens]
-                    total += jnp.where(ids == expert, spread, 0.0)
-                totals[g * zc + local] = jnp.concatenate(
-                    [total, jnp.zeros((TAIL - 8, tokens), F32)], axis=0
-                ).astype(BF16)
+    spreads = []
+    for q in range(pn):
+        loads.need(("t", q))
+        spreads.append(dot_nn(tails[q, :, 0:slots], sel[q * slots : (q + 1) * slots, :])[0:8, :])
+    for s in range(zn):
+        ids = outer_meta(info, meta, s, zn)[0:8, :]
+        total = jnp.zeros((8, tokens), F32)
+        for q in range(pn):
+            expert = (info[0] + (info[1] ^ q)).astype(F32)
+            total += jnp.where(ids == expert, spreads[q][:, s * tokens : (s + 1) * tokens], 0.0)
+        total = jnp.concatenate([total, jnp.zeros((TAIL - 8, tokens), F32)], axis=0)
+        gates[:, s * tokens : (s + 1) * tokens] = total.astype(BF16)
     loads.finish()
-    for s in range(zn):
-        here = slice(s * tokens, (s + 1) * tokens)
-        outs[s][0:tokens, :] = dot_nn(chosen[here, :], whole[...]).astype(BF16)
-        if gates:
-            outs[s][tokens : tokens + TAIL, :] = jnp.zeros((TAIL, cols), BF16)
-            outs[s][tokens : tokens + TAIL, 0:tokens] = totals[s]
+    finish_combine(chosen, whole, gates, outs, zn - zr, tokens)
+
+
+def combine_near_kernel(gates, chosen, *refs, pn, tokens, rows):
+    backs, outs, (whole, sems) = refs[:pn], refs[pn:-2], refs[-2:]
+    loads = Loads(sems)
+    for q in range(pn):
+        loads.add(q, backs[q], whole.at[pl.ds(q * rows, rows)])
+    loads.finish()
+    finish_combine(chosen, whole, gates, outs, 0, tokens)
+
+
+def finish_combine(chosen, whole, gates, outs, first, tokens):
+    part = dot_nn(chosen[...], whole[...]).astype(BF16)
+    for local, out in enumerate(outs):
+        at = first + local
+        out[0:tokens, :] = part[local * tokens : (local + 1) * tokens, :]
+        out[tokens : tokens + TAIL, :] = jnp.zeros((TAIL, part.shape[1]), BF16)
+        out[tokens : tokens + TAIL, 0:tokens] = gates[:, at * tokens : (at + 1) * tokens]
 
 
 def column_block(info, j, nt, cols):
@@ -410,14 +432,21 @@
         axis=0,
     )
     columns = [[z * pn + q for z in range(zn)] for q in range(pn)]
-    meta = lax.all_to_all(
-        jnp.broadcast_to(own[None], (zn,) + own.shape),
-        "expert",
-        split_axis=0,
-        concat_axis=0,
-        axis_index_groups=columns,
-        tiled=True,
-    )
+
+    def outer_exchange(value):
+        return lax.all_to_all(
+            value,
+            "expert",
+            split_axis=0,
+            concat_axis=0,
+            axis_index_groups=columns,
+            tiled=True,
+        )
+
+    def outer_gather(value):
+        return outer_exchange(jnp.broadcast_to(value[None], (zn,) + value.shape))
+
+    meta = outer_gather(own)
     sels = call(
         functools.partial(select_kernel, **fixed, picks=picks, cap=cap),
         [shape(pn * part_rows, zc * tokens)] * CHUNKS,
@@ -448,47 +477,73 @@
             name="pack_gates",
         )
 
-    def combine(backs, gates):
+    zr = zn // RETURNS
+    half = zr * cap
+
+    def send_back(parts, first):
+        return [outer_send(part, -(first + local)) for local, part in enumerate(parts)]
+
+    def combine(backs):
         parts = call(
-            functools.partial(combine_kernel, **fixed, rows=rows, gates=gates),
-            [shape(tokens + TAIL if gates else tokens, cols)] * zn,
-            [info, meta, *sels, chosen, *backs],
-            [SMEM] + [VMEM] * (2 + CHUNKS) + [HBM] * pn,
-            scratch=[pltpu.VMEM((slots, cols), BF16), pltpu.VMEM((pn, TAIL, cols), BF16)]
+            functools.partial(combine_kernel, **fixed, rows=half),
+            [shape(zn, tokens, cols)],
+            [info, *chosen, *backs],
+            [SMEM] + [VMEM] * RETURNS + [HBM] * pn,
+            scratch=[pltpu.VMEM((RETURNS, pn * half, cols), BF16), dma((RETURNS * pn,))],
+            name="combine",
+        )
+        return outer_exchange(parts[0])
+
+    def combine_far(backs):
+        *parts, gates = call(
+            functools.partial(combine_far_kernel, **fixed, rows=half),
+            [shape(tokens + TAIL, cols)] * zr + [shape(TAIL, zn * tokens)],
+            [info, meta, sels[0], chosen[RETURNS - 1], *backs],
+            [SMEM] + [VMEM] * 3 + [HBM] * pn,
+            scratch=[pltpu.VMEM((pn * half, cols), BF16), pltpu.VMEM((pn, TAIL, cols), BF16)]
             + [dma((2 * pn,))],
-            name="combine_gates" if gates else "combine",
+            name="combine_far",
         )
-        return [outer_send(part, -s) for s, part in enumerate(parts)]
+        return send_back(parts, zn - zr), gates
+
+    def combine_near(gates, backs):
+        parts = call(
+            functools.partial(combine_near_kernel, pn=pn, tokens=tokens, rows=half),
+            [shape(tokens + TAIL, cols)] * zr,
+            [gates, chosen[0], *backs],
+            [VMEM] * 2 + [HBM] * pn,
+            scratch=[pltpu.VMEM((pn * half, cols), BF16), dma((pn,))],
+            name="combine_near",
+        )
+        return send_back(parts, 0)
 
     def swapped(chunks):
         return [tensor_send(piece, j) for j in range(nt) for pieces in chunks for piece in pieces]
 
-    def core_sum(arrays):
-        sums = []
+    def core_sum(arrays, spans=(slice(None),)):
+        sums = [[] for _ in spans]
         for q in range(pn):
-            total = arrays[q].astype(F32)
-            for j in range(1, nt):
-                total += tensor_send(arrays[j * pn + q], j).astype(F32)
-            sums.append(total.astype(BF16))
+            parts = [tensor_send(arrays[j * pn + q], j) for j in range(nt)]
+            for at, span in enumerate(spans):
+                total = sum(part[span].astype(F32) for part in parts)
+                sums[at].append(total.astype(BF16))
         return sums
 
-    x_parts = [outer_send(first_half if s < 2 else after(first_half, meta), s) for s in range(zn)]
+    x_parts = [outer_send(first_half, s) for s in range(zn)]
     x_packed = pack_gates(x_parts)
     x_here = inner_exchange(x_packed)
-    gathered = lax.all_gather(
-        after(second_grad, *x_parts[1:]), "expert", axis_index_groups=columns, tiled=False
-    )
+    gathered = outer_gather(after(second_grad, *x_parts[1:]))
     chosen = call(
         functools.partial(route_kernel, **fixed, picks=picks, cap=cap),
-        [shape(zn * tokens, slots)],
+        [shape(zr * tokens, pn * half)] * RETURNS,
         [info, after(meta, *x_packed)],
         [SMEM, VMEM],
         name="route",
-    )[0]
-    c_packed = pack(after(gathered, chosen))
+    )
+    c_packed = pack(after(gathered, *chosen))
     c_here = inner_exchange(c_packed)
 
-    xs = swapped((x_here,))
+    xs = swapped(([after(piece, gathered) for piece in x_here],))
     pieces = nt * CHUNKS * pn
     forward = call(
         functools.partial(forward_kernel, **sizes),
@@ -503,9 +558,8 @@
         name="expert_forward",
     )
     outs, (hs, hid, a1, a2) = forward[: nt * pn], forward[nt * pn :]
-    outs = [after(part, *c_here) for part in outs]
     cs = swapped(([after(piece, hid) for piece in c_here],))
-    out_here = core_sum(outs)
+    out_here = core_sum(outs)[0]
     out_back = inner_exchange(out_here)
 
     backward = call(
@@ -522,15 +576,16 @@
         name="expert_backward",
     )
     grads, (gg, ug) = backward[: nt * pn], backward[nt * pn :]
-    dx_here = core_sum([after(part, *out_back) for part in grads])
-    dx_back = inner_exchange(dx_here)
-    out_parts = combine([after(piece, *dx_here) for piece in out_back], False)
-    grad_parts = combine(dx_back, True)
+    spans = (slice(half, rows + TAIL), slice(0, half))
+    far_here, near_here = core_sum([after(part, *out_back) for part in grads], spans)
+    far_back = inner_exchange(far_here)
+    near_back = inner_exchange(near_here)
+    out_parts = combine([after(piece, *near_here) for piece in out_back])
 
     grad_in, grad_out = call(
         functools.partial(weights_kernel, **sizes),
         [shape(*expert_in.shape), shape(*expert_out.shape)],
-        [info, *xs, *cs, gg, ug, after(hs, *dx_here)],
+        [after(info, *near_here), *xs, *cs, gg, ug, hs],
         [SMEM] + [HBM] * (2 * pieces + 3),
         out_specs=[HBM, HBM],
         scratch=[
@@ -543,7 +598,9 @@
         name="expert_weights",
     )
 
-    branch = sum(part.astype(F32) for part in out_parts)
+    far_parts, gate_parts = combine_far([after(piece, grad_in) for piece in far_back])
+    grad_parts = combine_near(gate_parts, near_back) + far_parts
+    branch = jnp.sum(out_parts.astype(F32), axis=0)
     input_sum = sum(part[:tokens].astype(F32) for part in grad_parts)
     gate_sum = sum(part[tokens : tokens + picks, :tokens].astype(F32) for part in grad_parts)
     restored = (second_half.astype(F32) - branch).astype(BF16)

time: 207 us -> 208 us (level)
  waiting for transfers between devices: 46.3 us -> 60.6 us
  between operations: 14.4 us -> 0.93 us
  starting transfers between devices: 53.5 us -> 42.4 us
  other arithmetic: 11.8 us -> 22.1 us
    ppermute x16, starting transfers between devices: 26.1 us -> 7.92 us  [tensor_send(): return lax.ppermute(value, 'tensor', [(c, (c + j) % nt) for c in range(nt)])]
    all_to_all x1 -> x3, waiting for transfers between devices: 2.32 us -> 12.3 us  [outer_exchange(): lax.all_to_all(value, 'expert', split_axis=0, concat_axis=0, axis_index_g...]
    all_to_all x1 -> x3, starting transfers between devices: 4.76 us -> 13.5 us  [outer_exchange(): lax.all_to_all(value, 'expert', split_axis=0, concat_axis=0, axis_index_g...]
    convert_element_type x8 -> x12, other arithmetic: 7.33 us -> 16 us  [core_sum(): sums[at].append(total.astype(BF16))]
    ppermute x9 -> x6, waiting for transfers between devices: 29.9 us -> 38.1 us  [outer_send(): lax.ppermute(value, 'expert', [(e, (e // pn + s) % zn * pn + e % pn) for...]
    ppermute x9 -> x6, starting transfers between devices: 11.7 us -> 7.49 us  [outer_send(): lax.ppermute(value, 'expert', [(e, (e // pn + s) % zn * pn + e % pn) for...]
    ppermute x12 -> x15, waiting for transfers between devices: 12.3 us -> 8.75 us  [inner_send(): return lax.ppermute(value, 'expert', [(e, e ^ q) for e in range(groups)])]
    ppermute x12 -> x15, starting transfers between devices: 10.9 us -> 13.4 us  [inner_send(): return lax.ppermute(value, 'expert', [(e, e ^ q) for e in range(groups)])]
  transfers between devices with their start and end apart: 39 -> 40, of which waited for: 11 -> 9; matrix products, arithmetic and copies ran while one was open for 4% -> 10% of each run, Pallas kernels for 37% -> 35%
where the time goes in v7:
time: 208 us; the launch traced here: 207 us
  Pallas kernels  77.7 us (37%)
  waiting for transfers between devices  60.6 us (29%)
  starting transfers between devices  42.4 us (20%)
  other arithmetic  22.1 us (11%)
  local copies, waits for them, and re-layouts  3.54 us (2%)
    pallas_call x10, Pallas kernels, call(): pl.pallas_call(kernel, out_shape=outs, in_specs=specs, out_specs=out_spec...  77.7 us
    ppermute x6, waiting for transfers between devices, outer_send(): lax.ppermute(value, 'expert', [(e, (e // pn + s) % zn * pn + e % pn) for...  38.1 us
    convert_element_type x12, other arithmetic, core_sum(): sums[at].append(total.astype(BF16))  16 us
    all_to_all x3, starting transfers between devices, outer_exchange(): lax.all_to_all(value, 'expert', split_axis=0, concat_axis=0, axis_index_g...  13.5 us
    ppermute x15, starting transfers between devices, inner_send(): return lax.ppermute(value, 'expert', [(e, e ^ q) for e in range(groups)])  13.4 us
    all_to_all x3, waiting for transfers between devices, outer_exchange(): lax.all_to_all(value, 'expert', split_axis=0, concat_axis=0, axis_index_g...  12.3 us
    ppermute x15, waiting for transfers between devices, inner_send(): return lax.ppermute(value, 'expert', [(e, e ^ q) for e in range(groups)])  8.75 us
    ppermute x16, starting transfers between devices, tensor_send(): return lax.ppermute(value, 'tensor', [(c, (c + j) % nt) for c in range(nt)])  7.92 us
  transfers between devices with their start and end apart: 40, of which 9 were waited for; matrix products, arithmetic and copies ran while one was open for 10% of the time, Pallas kernels for 35%

profile of v7, /device:TPU:9, one launch (start us, length us, event | category | flops | bytes accessed | tf_op | source)
XLA Modules:
  0.0 207.2 jit_solution(17284442789922666486)
XLA Ops:
  0.6 1.3 collective-permute-start
  2.0 1.1 collective-permute-start.1
  3.1 1.4 collective-permute-start.2
  6.5 4.3 %all-to-all-start = ((f32[4,16,128]{2,1,0:T(8,128)}), f32[4,16,128]{2,1,0:T(8,128)S(1)}, u32[]{:S(2)}, u32[]{:S(2)}) async-start(f32[4,16,128]{2,1,0:T(8,128)} %broadcast_in_dim.4), calls=%async_computation | async-start | bytes 65536 | tf_op jit(solution)/shard_map/all_to_all | solution.py:437
  10.8 13.7 %collective-permute-done.1.refs_3_ = bf16[128,1024]{1,0:T(8,128)(2,1)S(1)} collective-permute-done((bf16[128,1024]{1,0:T(8,128)(2,1)}, bf16[128,1024]{1,0:T(8,128)(2,1)S(1)}, u32[]{:S(2)}, u32[]{:S(2)}) %collective-permute-start.1) | collective-permute-done | bytes 262176 | tf_op jit(solution)/shard_map/ppermute | solution.py:408
  24.5 2.8 %collective-permute-done.2.refs_4_ = bf16[128,1024]{1,0:T(8,128)(2,1)S(1)} collective-permute-done((bf16[128,1024]{1,0:T(8,128)(2,1)}, bf16[128,1024]{1,0:T(8,128)(2,1)S(1)}, u32[]{:S(2)}, u32[]{:S(2)}) %collective-permute-start.2) | collective-permute-done | bytes 262176 | tf_op jit(solution)/shard_map/ppermute | solution.py:408
  27.4 2.1 broadcast_in_dim.5
  29.5 4.6 %all-to-all-start.1 = ((bf16[4,128,1024]{2,1,0:T(8,128)(2,1)}), bf16[4,128,1024]{2,1,0:T(8,128)(2,1)S(1)}, u32[]{:S(2)}, u32[]{:S(2)}) async-start(bf16[4,128,1024]{2,1,0:T(8,128)(2,1)} %broadcast_in_dim.5), calls=%async_computation.1 | async-start | bytes 2097152 | tf_op jit(solution)/shard_map/all_to_all | solution.py:437
  34.6 2.0 select.11.refs_0_.sel
  36.7 4.6 %pack_gates.1 = (bf16[240,1024]{1,0:T(8,128)(2,1)}, bf16[240,1024]{1,0:T(8,128)(2,1)}, bf16[240,1024]{1,0:T(8,128)(2,1)}, bf16[240,1024]{1,0:T(8,128)(2,1)}) custom-call(s32[4]{0:T(128)} %pad_add_fusion.info, f32[4,16,128]{2,1,0:T(8,128)} %copy-done.7, bf16[896,512]{1,0:T(8,128)(2,1)} %select.11.refs_0_.sel, bf16[128,1024]{1,0:T(8,128)(2,1)} %refs_1_.1, ...), custom_call_target="tpu_custom_call" | custom-call | flops 1024 | bytes 1024 | tf_op jit(solution)/shard_map/pack_gates/pallas_call | solution.py:41
  41.3 1.3 collective-permute-start.3
  42.5 1.2 collective-permute-start.4
  44.0 12.1 %all-to-all-done.1.source = bf16[4,128,1024]{2,1,0:T(8,128)(2,1)S(1)} async-done(((bf16[4,128,1024]{2,1,0:T(8,128)(2,1)}), bf16[4,128,1024]{2,1,0:T(8,128)(2,1)S(1)}, u32[]{:S(2)}, u32[]{:S(2)}) %all-to-all-start.1) | async-done | bytes 1048608 | tf_op jit(solution)/shard_map/all_to_all | solution.py:437
  56.1 8.7 %collective-permute-done.5.refs_3_ = bf16[240,1024]{1,0:T(8,128)(2,1)} collective-permute-done((bf16[240,1024]{1,0:T(8,128)(2,1)}, bf16[240,1024]{1,0:T(8,128)(2,1)}, u32[]{:S(2)}, u32[]{:S(2)}) %collective-permute-start.5) | collective-permute-done | bytes 491552 | tf_op jit(solution)/shard_map/ppermute | solution.py:415
  64.8 2.1 %collective-permute-start.6 = (bf16[240,1024]{1,0:T(8,128)(2,1)}, bf16[240,1024]{1,0:T(8,128)(2,1)}, u32[]{:S(2)}, u32[]{:S(2)}) collective-permute-start(bf16[240,1024]{1,0:T(8,128)(2,1)} %get-tuple-element.88.refs_0_), channel_id=1, source_target_pairs={{0,1},{1,0},{2,3},{3,2},{4,5},{5,4},{6,7},{7,6},{8,9},{9,8},{10,11... | collective-permute-start | bytes 1474568 | tf_op jit(solution)/shard_map/ppermute | solution.py:423
  67.5 3.1 %route.1 = (bf16[256,448]{1,0:T(8,128)(2,1)}, bf16[256,448]{1,0:T(8,128)(2,1)}) custom-call(s32[4]{0:T(128)} %pad_add_fusion.info, f32[4,16,128]{2,1,0:T(8,128)} %copy-done.7), custom_call_target="tpu_custom_call" | custom-call | flops 1024 | bytes 1024 | tf_op jit(solution)/shard_map/route/pallas_call | solution.py:41
  70.6 4.3 %pack.1 = (bf16[224,1024]{1,0:T(8,128)(2,1)}, bf16[224,1024]{1,0:T(8,128)(2,1)}, bf16[224,1024]{1,0:T(8,128)(2,1)}, bf16[224,1024]{1,0:T(8,128)(2,1)}) custom-call(s32[4]{0:T(128)} %pad_add_fusion.info, bf16[896,512]{1,0:T(8,128)(2,1)} %select.11.refs_0_.sel, bf16[4,128,1024]{2,1,0:T(8,128)(2,1)} %copy-done), custom_call_target="tpu_custom_call" | custom-call | flops 1024 | bytes 1024 | tf_op jit(solution)/shard_map/pack/pallas_call | solution.py:41
  74.9 1.1 collective-permute-start.11
  76.5 1.2 collective-permute-start.13
  77.7 18.7 %expert_forward.1 = (bf16[224,1024]{1,0:T(8,128)(2,1)}, bf16[224,1024]{1,0:T(8,128)(2,1)}, bf16[224,1024]{1,0:T(8,128)(2,1)}, bf16[224,1024]{1,0:T(8,128)(2,1)},...) custom-call(s32[4]{0:T(128)} %pad_add_fusion.info, ...), custom_call_target="tpu_custom_call" | custom-call | flops 1024 | bytes 1024 | tf_op jit(solution)/shard_map/expert_forward/pallas_call | solution.py:41
  96.4 1.3 collective-permute-start.18
  99.7 2.0 add_convert_fusion.2
  104.2 1.1 collective-permute-start.21
  105.8 1.1 collective-permute-start.23
  107.8 19.4 %expert_backward.1 = (bf16[240,1024]{1,0:T(8,128)(2,1)}, bf16[240,1024]{1,0:T(8,128)(2,1)}, bf16[240,1024]{1,0:T(8,128)(2,1)}, bf16[240,1024]{1,0:T(8,128)(2,1)}...) custom-call(s32[4]{0:T(128)} %pad_add_fusion.info, ...), custom_call_target="tpu_custom_call" | custom-call | flops 1024 | bytes 1024 | tf_op jit(solution)/shard_map/expert_backward/pallas_call | solution.py:41
  127.2 1.1 collective-permute-start.24
  128.9 1.1 collective-permute-done.24
  130.0 1.7 add_convert_fusion.12.refs_0_
  131.7 1.9 add_convert_fusion.11
  133.6 1.9 add_convert_fusion.10
  137.0 4.3 %combine.1 = bf16[4,128,1024]{2,1,0:T(8,128)(2,1)} custom-call(s32[4]{0:T(128)} %pad_add_fusion.info, bf16[256,448]{1,0:T(8,128)(2,1)} %get-tuple-element.79.refs_0_.chosen, bf16[256,448]{1,0:T(8,128)(2,1)} %get-tuple-element.80.refs_1_.chosen, bf16[224,1024]{1,0:T(8,128)(2,1)} %add_convert_fusion.3.refs_2_, ...), custom_call_target="tpu_custom_call" | custom-call | flops 1024 | bytes 1024 | tf_op jit(solution)/shard_map/combine/pallas_call | solution.py:41
  141.3 4.7 %all-to-all-start.2 = ((bf16[4,128,1024]{2,1,0:T(8,128)(2,1)}), bf16[4,128,1024]{2,1,0:T(8,128)(2,1)S(1)}, u32[]{:S(2)}, u32[]{:S(2)}) async-start(bf16[4,128,1024]{2,1,0:T(8,128)(2,1)} %combine.1), calls=%async_computation.2 | async-start | bytes 2097152 | tf_op jit(solution)/shard_map/all_to_all | solution.py:437
  146.0 1.7 add_convert_fusion.7
  147.7 1.1 collective-permute-start.28
  148.8 1.7 add_convert_fusion.6
  151.8 1.0 collective-permute-start.30
  152.9 1.1 collective-permute-start.31
  154.5 13.9 %expert_weights.1 = (bf16[1,2,704,2048]{3,2,1,0:T(8,128)(2,1)}, bf16[1,704,2048]{2,1,0:T(8,128)(2,1)}) custom-call(s32[4]{0:T(128)} %pad_add_fusion.info, bf16[240,1024]{1,0:T(8,128)(2,1)} %get-tuple-element.88.refs_0_, bf16[240,1024]{1,0:T(8,128)(2,1)} %copy-done.1, bf16[240,1024]{1,0:T(8,128)(2,1)} %copy-done.2, ...), custom_call_target="tpu_custom_call" | custom-call | flops 1024 | bytes 1024 | tf_op jit(solution)/shard_map/expert_weights/pallas_call | solution.py:41
  168.4 1.1 collective-permute-start.33
  170.3 4.0 %combine_far.1 = (bf16[144,1024]{1,0:T(8,128)(2,1)}, bf16[144,1024]{1,0:T(8,128)(2,1)}, bf16[16,512]{1,0:T(8,128)(2,1)}) custom-call(s32[4]{0:T(128)} %pad_add_fusion.info, f32[4,16,128]{2,1,0:T(8,128)} %copy-done.7, bf16[896,512]{1,0:T(8,128)(2,1)} %select.11.refs_0_.sel, bf16[256,448]{1,0:T(8,128)(2,1)} %get-tuple-element.80.refs_1_.chosen, ...), custom_call_target="tpu_custom_call" | custom-call | flops 1024 | bytes 1024 | tf_op jit(solution)/shard_map/combine_far/pallas_call | solution.py:41
  174.2 1.2 collective-permute-start.36
  175.5 1.0 collective-permute-start.35
  176.5 3.5 %combine_near.1 = (bf16[144,1024]{1,0:T(8,128)(2,1)}, bf16[144,1024]{1,0:T(8,128)(2,1)}) custom-call(bf16[16,512]{1,0:T(8,128)(2,1)} %get-tuple-element.137.gates, bf16[256,448]{1,0:T(8,128)(2,1)} %get-tuple-element.79.refs_0_.chosen, bf16[112,1024]{1,0:T(8,128)(2,1)} %add_convert_fusion.12.refs_0_, bf16[112,1024]{1,0:T(8,128)(2,1)} %collective-permute-done.31.refs_1_, ...), custom_call_target="tpu_custom_call" | custom-call | flops 1024 | bytes 1024 | tf_op jit(solution)/shard_map/combine_near/pallas_call | solution.py:41
  180.0 1.4 collective-permute-start.34
  181.4 17.0 %collective-permute-done.35 = bf16[144,1024]{1,0:T(8,128)(2,1)S(1)} collective-permute-done((bf16[144,1024]{1,0:T(8,128)(2,1)}, bf16[144,1024]{1,0:T(8,128)(2,1)S(1)}, u32[]{:S(2)}, u32[]{:S(2)}) %collective-permute-start.35) | collective-permute-done | bytes 294944 | tf_op jit(solution)/shard_map/ppermute | solution.py:408
  198.4 4.6 %collective-permute-done.34 = bf16[144,1024]{1,0:T(8,128)(2,1)S(1)} collective-permute-done((bf16[144,1024]{1,0:T(8,128)(2,1)}, bf16[144,1024]{1,0:T(8,128)(2,1)S(1)}, u32[]{:S(2)}, u32[]{:S(2)}) %collective-permute-start.34) | collective-permute-done | bytes 294944 | tf_op jit(solution)/shard_map/ppermute | solution.py:408
  203.1 1.2 add_bitcast_fusion
  204.3 1.9 add_convert_fusion.4
  (116 shorter events, 15.8 us)
Async XLA Ops:
  0.6 10.1 %collective-permute-start = (bf16[128,1024]{1,0:T(8,128)(2,1)}, bf16[128,1024]{1,0:T(8,128)(2,1)S(1)}, u32[]{:S(2)}, u32[]{:S(2)}) collective-permute-start(bf16[128,1024]{1,0:T(8,128)(2,1)} %refs_1_.1), channel_id=1, source_target_pairs={{0,8},{2,10},{4,12},{6,14},{8,16},{10,18},{12,20},{14,22},{16,24},... | collective-permute-start | bytes 786440 | tf_op jit(solution)/shard_map/ppermute | solution.py:408
  2.0 22.5 %collective-permute-start.1 = (bf16[128,1024]{1,0:T(8,128)(2,1)}, bf16[128,1024]{1,0:T(8,128)(2,1)S(1)}, u32[]{:S(2)}, u32[]{:S(2)}) collective-permute-start(bf16[128,1024]{1,0:T(8,128)(2,1)} %refs_1_.1), channel_id=1, source_target_pairs={{0,16},{2,18},{4,20},{6,22},{8,24},{10,26},{12,28},{14,30},{16,0},... | collective-permute-start | bytes 786440 | tf_op jit(solution)/shard_map/ppermute | solution.py:408
  3.1 24.2 %collective-permute-start.2 = (bf16[128,1024]{1,0:T(8,128)(2,1)}, bf16[128,1024]{1,0:T(8,128)(2,1)S(1)}, u32[]{:S(2)}, u32[]{:S(2)}) collective-permute-start(bf16[128,1024]{1,0:T(8,128)(2,1)} %refs_1_.1), channel_id=1, source_target_pairs={{0,24},{2,26},{4,28},{6,30},{8,0},{10,2},{12,4},{14,6},{16,8},{18,... | collective-permute-start | bytes 786440 | tf_op jit(solution)/shard_map/ppermute | solution.py:408
  6.5 21.0 %all-to-all-start = ((f32[4,16,128]{2,1,0:T(8,128)}), f32[4,16,128]{2,1,0:T(8,128)S(1)}, u32[]{:S(2)}, u32[]{:S(2)}) async-start(f32[4,16,128]{2,1,0:T(8,128)} %broadcast_in_dim.4), calls=%async_computation | async-start | bytes 65536 | tf_op jit(solution)/shard_map/all_to_all | solution.py:437
  10.8 18.7 %copy-start.21 = (bf16[128,1024]{1,0:T(8,128)(2,1)}, bf16[128,1024]{1,0:T(8,128)(2,1)S(1)}, u32[]{:S(2)}) copy-start(bf16[128,1024]{1,0:T(8,128)(2,1)S(1)} %collective-permute-done.refs_2_) | copy-start | bytes 786436
  29.5 26.6 %all-to-all-start.1 = ((bf16[4,128,1024]{2,1,0:T(8,128)(2,1)}), bf16[4,128,1024]{2,1,0:T(8,128)(2,1)S(1)}, u32[]{:S(2)}, u32[]{:S(2)}) async-start(bf16[4,128,1024]{2,1,0:T(8,128)(2,1)} %broadcast_in_dim.5), calls=%async_computation.1 | async-start | bytes 2097152 | tf_op jit(solution)/shard_map/all_to_all | solution.py:437
  41.3 14.8 %collective-permute-start.3 = (bf16[240,1024]{1,0:T(8,128)(2,1)}, bf16[240,1024]{1,0:T(8,128)(2,1)S(1)}, u32[]{:S(2)}, u32[]{:S(2)}) collective-permute-start(bf16[240,1024]{1,0:T(8,128)(2,1)} %get-tuple-element.75), channel_id=1, source_target_pairs={{0,2},{2,0},{4,6},{6,4},{8,10},{10,8},{12,14},{14,12},{16,18},{18,... | collective-permute-start | bytes 1474568 | tf_op jit(solution)/shard_map/ppermute | solution.py:415
  42.5 13.6 %collective-permute-start.4 = (bf16[240,1024]{1,0:T(8,128)(2,1)}, bf16[240,1024]{1,0:T(8,128)(2,1)S(1)}, u32[]{:S(2)}, u32[]{:S(2)}) collective-permute-start(bf16[240,1024]{1,0:T(8,128)(2,1)} %get-tuple-element.76), channel_id=1, source_target_pairs={{0,4},{2,6},{4,0},{6,2},{8,12},{10,14},{12,8},{14,10},{16,20},{18,... | collective-permute-start | bytes 1474568 | tf_op jit(solution)/shard_map/ppermute | solution.py:415
  43.8 21.0 %collective-permute-start.5 = (bf16[240,1024]{1,0:T(8,128)(2,1)}, bf16[240,1024]{1,0:T(8,128)(2,1)}, u32[]{:S(2)}, u32[]{:S(2)}) collective-permute-start(bf16[240,1024]{1,0:T(8,128)(2,1)} %get-tuple-element.77), channel_id=1, source_target_pairs={{0,6},{2,4},{4,2},{6,0},{8,14},{10,12},{12,10},{14,8},{16,22},{18,... | collective-permute-start | bytes 1474568 | tf_op jit(solution)/shard_map/ppermute | solution.py:415
  56.1 14.5 %copy-start = (bf16[4,128,1024]{2,1,0:T(8,128)(2,1)}, bf16[4,128,1024]{2,1,0:T(8,128)(2,1)S(1)}, u32[]{:S(2)}) copy-start(bf16[4,128,1024]{2,1,0:T(8,128)(2,1)S(1)} %all-to-all-done.1.source) | copy-start | bytes 3145732
  56.1 21.6 %copy-start.1 = (bf16[240,1024]{1,0:T(8,128)(2,1)}, bf16[240,1024]{1,0:T(8,128)(2,1)S(1)}, u32[]{:S(2)}) copy-start(bf16[240,1024]{1,0:T(8,128)(2,1)S(1)} %collective-permute-done.3.refs_1_) | copy-start | bytes 1474564
  56.1 21.6 %copy-start.2 = (bf16[240,1024]{1,0:T(8,128)(2,1)}, bf16[240,1024]{1,0:T(8,128)(2,1)S(1)}, u32[]{:S(2)}) copy-start(bf16[240,1024]{1,0:T(8,128)(2,1)S(1)} %collective-permute-done.4.refs_2_) | copy-start | bytes 1474564
  64.8 11.2 %collective-permute-start.6 = (bf16[240,1024]{1,0:T(8,128)(2,1)}, bf16[240,1024]{1,0:T(8,128)(2,1)}, u32[]{:S(2)}, u32[]{:S(2)}) collective-permute-start(bf16[240,1024]{1,0:T(8,128)(2,1)} %get-tuple-element.88.refs_0_), channel_id=1, source_target_pairs={{0,1},{1,0},{2,3},{3,2},{4,5},{5,4},{6,7},{7,6},{8,9},{9,8},{10,11... | collective-permute-start | bytes 1474568 | tf_op jit(solution)/shard_map/ppermute | solution.py:423
  66.9 9.6 %collective-permute-start.7 = (bf16[240,1024]{1,0:T(8,128)(2,1)S(1)}, bf16[240,1024]{1,0:T(8,128)(2,1)}, u32[]{:S(2)}, u32[]{:S(2)}) collective-permute-start(bf16[240,1024]{1,0:T(8,128)(2,1)S(1)} %collective-permute-done.3.refs_1_), channel_id=1, source_target_pairs={{0,1},{1,0},{2,3},{3,2},{4,5},{5,4},{6,7},{7,6},{8,9},{9,8},{10,11... | collective-permute-start | bytes 1474568 | tf_op jit(solution)/shard_map/ppermute | solution.py:423
  67.0 10.7 %collective-permute-start.8 = (bf16[240,1024]{1,0:T(8,128)(2,1)S(1)}, bf16[240,1024]{1,0:T(8,128)(2,1)}, u32[]{:S(2)}, u32[]{:S(2)}) collective-permute-start(bf16[240,1024]{1,0:T(8,128)(2,1)S(1)} %collective-permute-done.4.refs_2_), channel_id=1, source_target_pairs={{0,1},{1,0},{2,3},{3,2},{4,5},{5,4},{6,7},{7,6},{8,9},{9,8},{10,11... | collective-permute-start | bytes 1474568 | tf_op jit(solution)/shard_map/ppermute | solution.py:423
  67.4 10.2 %collective-permute-start.9 = (bf16[240,1024]{1,0:T(8,128)(2,1)}, bf16[240,1024]{1,0:T(8,128)(2,1)}, u32[]{:S(2)}, u32[]{:S(2)}) collective-permute-start(bf16[240,1024]{1,0:T(8,128)(2,1)} %collective-permute-done.5.refs_3_), channel_id=1, source_target_pairs={{0,1},{1,0},{2,3},{3,2},{4,5},{5,4},{6,7},{7,6},{8,9},{9,8},{10,11... | collective-permute-start | bytes 1474568 | tf_op jit(solution)/shard_map/ppermute | solution.py:423
  74.9 22.9 %collective-permute-start.11 = (bf16[224,1024]{1,0:T(8,128)(2,1)}, bf16[224,1024]{1,0:T(8,128)(2,1)S(1)}, u32[]{:S(2)}, u32[]{:S(2)}) collective-permute-start(bf16[224,1024]{1,0:T(8,128)(2,1)} %get-tuple-element.84), channel_id=1, source_target_pairs={{0,2},{2,0},{4,6},{6,4},{8,10},{10,8},{12,14},{14,12},{16,18},{18,... | collective-permute-start | bytes 1376264 | tf_op jit(solution)/shard_map/ppermute | solution.py:415
  76.0 22.2 %copy-start.3 = (bf16[224,1024]{1,0:T(8,128)(2,1)S(1)}, bf16[224,1024]{1,0:T(8,128)(2,1)}, u32[]{:S(2)}) copy-start(bf16[224,1024]{1,0:T(8,128)(2,1)} %get-tuple-element.95.refs_0_.refs_8_) | copy-start | bytes 1376260
  76.0 22.2 %collective-permute-start.12 = (bf16[224,1024]{1,0:T(8,128)(2,1)}, bf16[224,1024]{1,0:T(8,128)(2,1)}, u32[]{:S(2)}, u32[]{:S(2)}) collective-permute-start(bf16[224,1024]{1,0:T(8,128)(2,1)} %get-tuple-element.85), channel_id=1, source_target_pairs={{0,4},{2,6},{4,0},{6,2},{8,12},{10,14},{12,8},{14,10},{16,20},{18,... | collective-permute-start | bytes 1376264 | tf_op jit(solution)/shard_map/ppermute | solution.py:415
  76.5 21.7 %collective-permute-start.13 = (bf16[224,1024]{1,0:T(8,128)(2,1)}, bf16[224,1024]{1,0:T(8,128)(2,1)}, u32[]{:S(2)}, u32[]{:S(2)}) collective-permute-start(bf16[224,1024]{1,0:T(8,128)(2,1)} %get-tuple-element.86), channel_id=1, source_target_pairs={{0,6},{2,4},{4,2},{6,0},{8,14},{10,12},{12,10},{14,8},{16,22},{18,... | collective-permute-start | bytes 1376264 | tf_op jit(solution)/shard_map/ppermute | solution.py:415
  96.4 3.0 %collective-permute-start.18 = (bf16[224,1024]{1,0:T(8,128)(2,1)}, bf16[224,1024]{1,0:T(8,128)(2,1)S(1)}, u32[]{:S(2)}, u32[]{:S(2)}) collective-permute-start(bf16[224,1024]{1,0:T(8,128)(2,1)} %get-tuple-element.100), channel_id=1, source_target_pairs={{0,1},{1,0},{2,3},{3,2},{4,5},{5,4},{6,7},{7,6},{8,9},{9,8},{10,11... | collective-permute-start | bytes 1376264 | tf_op jit(solution)/shard_map/ppermute | solution.py:423
  97.7 4.0 %collective-permute-start.19 = (bf16[224,1024]{1,0:T(8,128)(2,1)}, bf16[224,1024]{1,0:T(8,128)(2,1)S(1)}, u32[]{:S(2)}, u32[]{:S(2)}) collective-permute-start(bf16[224,1024]{1,0:T(8,128)(2,1)} %get-tuple-element.102), channel_id=1, source_target_pairs={{0,1},{1,0},{2,3},{3,2},{4,5},{5,4},{6,7},{7,6},{8,9},{9,8},{10,11... | collective-permute-start | bytes 1376264 | tf_op jit(solution)/shard_map/ppermute | solution.py:423
  97.8 6.4 %collective-permute-start.10 = (bf16[224,1024]{1,0:T(8,128)(2,1)}, bf16[224,1024]{1,0:T(8,128)(2,1)S(1)}, u32[]{:S(2)}, u32[]{:S(2)}) collective-permute-start(bf16[224,1024]{1,0:T(8,128)(2,1)} %get-tuple-element.93), channel_id=1, source_target_pairs={{0,1},{1,0},{2,3},{3,2},{4,5},{5,4},{6,7},{7,6},{8,9},{9,8},{10,11... | collective-permute-start | bytes 1376264 | tf_op jit(solution)/shard_map/ppermute | solution.py:423
  98.2 7.0 %collective-permute-start.14 = (bf16[224,1024]{1,0:T(8,128)(2,1)S(1)}, bf16[224,1024]{1,0:T(8,128)(2,1)S(1)}, u32[]{:S(2)}, u32[]{:S(2)}) collective-permute-start(bf16[224,1024]{1,0:T(8,128)(2,1)S(1)} %copy-done.3), channel_id=1, source_target_pairs={{0,1},{1,0},{2,3},{3,2},{4,5},{5,4},{6,7},{7,6},{8,9},{9,8},{10,11... | collective-permute-start | bytes 1376264 | tf_op jit(solution)/shard_map/ppermute | solution.py:423
  99.1 6.7 %collective-permute-start.15 = (bf16[224,1024]{1,0:T(8,128)(2,1)S(1)}, bf16[224,1024]{1,0:T(8,128)(2,1)S(1)}, u32[]{:S(2)}, u32[]{:S(2)}) collective-permute-start(bf16[224,1024]{1,0:T(8,128)(2,1)S(1)} %collective-permute-done.11.refs_1_.refs_9_), channel_id=1, source_target_pairs={{0,1},{1,0},{2,3},{3,2},{4,5},{5,4},{6,7},{7,6},{8,9},{9,8},{10,11... | collective-permute-start | bytes 1376264 | tf_op jit(solution)/shard_map/ppermute | solution.py:423
  99.4 3.5 %collective-permute-start.20 = (bf16[224,1024]{1,0:T(8,128)(2,1)}, bf16[224,1024]{1,0:T(8,128)(2,1)S(1)}, u32[]{:S(2)}, u32[]{:S(2)}) collective-permute-start(bf16[224,1024]{1,0:T(8,128)(2,1)} %get-tuple-element.104), channel_id=1, source_target_pairs={{0,1},{1,0},{2,3},{3,2},{4,5},{5,4},{6,7},{7,6},{8,9},{9,8},{10,11... | collective-permute-start | bytes 1376264 | tf_op jit(solution)/shard_map/ppermute | solution.py:423
  101.7 6.0 %collective-permute-start.16 = (bf16[224,1024]{1,0:T(8,128)(2,1)}, bf16[224,1024]{1,0:T(8,128)(2,1)}, u32[]{:S(2)}, u32[]{:S(2)}) collective-permute-start(bf16[224,1024]{1,0:T(8,128)(2,1)} %collective-permute-done.12.refs_2_.refs_10_), channel_id=1, source_target_pairs={{0,1},{1,0},{2,3},{3,2},{4,5},{5,4},{6,7},{7,6},{8,9},{9,8},{10,11... | collective-permute-start | bytes 1376264 | tf_op jit(solution)/shard_map/ppermute | solution.py:423
  102.8 4.9 %collective-permute-start.17 = (bf16[224,1024]{1,0:T(8,128)(2,1)}, bf16[224,1024]{1,0:T(8,128)(2,1)}, u32[]{:S(2)}, u32[]{:S(2)}) collective-permute-start(bf16[224,1024]{1,0:T(8,128)(2,1)} %collective-permute-done.13.refs_3_.refs_11_), channel_id=1, source_target_pairs={{0,1},{1,0},{2,3},{3,2},{4,5},{5,4},{6,7},{7,6},{8,9},{9,8},{10,11... | collective-permute-start | bytes 1376264 | tf_op jit(solution)/shard_map/ppermute | solution.py:423
  104.2 23.0 %collective-permute-start.21 = (bf16[224,1024]{1,0:T(8,128)(2,1)}, bf16[224,1024]{1,0:T(8,128)(2,1)}, u32[]{:S(2)}, u32[]{:S(2)}) collective-permute-start(bf16[224,1024]{1,0:T(8,128)(2,1)} %add_convert_fusion.2), channel_id=1, source_target_pairs={{0,2},{2,0},{4,6},{6,4},{8,10},{10,8},{12,14},{14,12},{16,18},{18,... | collective-permute-start | bytes 1376264 | tf_op jit(solution)/shard_map/ppermute | solution.py:415
  105.2 22.0 %collective-permute-start.22 = (bf16[224,1024]{1,0:T(8,128)(2,1)}, bf16[224,1024]{1,0:T(8,128)(2,1)S(1)}, u32[]{:S(2)}, u32[]{:S(2)}) collective-permute-start(bf16[224,1024]{1,0:T(8,128)(2,1)} %add_convert_fusion.1), channel_id=1, source_target_pairs={{0,4},{2,6},{4,0},{6,2},{8,12},{10,14},{12,8},{14,10},{16,20},{18,... | collective-permute-start | bytes 1376264 | tf_op jit(solution)/shard_map/ppermute | solution.py:415
  105.8 21.5 %collective-permute-start.23 = (bf16[224,1024]{1,0:T(8,128)(2,1)}, bf16[224,1024]{1,0:T(8,128)(2,1)S(1)}, u32[]{:S(2)}, u32[]{:S(2)}) collective-permute-start(bf16[224,1024]{1,0:T(8,128)(2,1)} %add_convert_fusion), channel_id=1, source_target_pairs={{0,6},{2,4},{4,2},{6,0},{8,14},{10,12},{12,10},{14,8},{16,22},{18,... | collective-permute-start | bytes 1376264 | tf_op jit(solution)/shard_map/ppermute | solution.py:415
  127.2 9.8 %copy-start.17 = (bf16[224,1024]{1,0:T(8,128)(2,1)}, bf16[224,1024]{1,0:T(8,128)(2,1)S(1)}, u32[]{:S(2)}) copy-start(bf16[224,1024]{1,0:T(8,128)(2,1)S(1)} %collective-permute-done.22.refs_4_) | copy-start | bytes 1376260
  127.2 2.8 %collective-permute-start.24 = (bf16[240,1024]{1,0:T(8,128)(2,1)}, bf16[240,1024]{1,0:T(8,128)(2,1)S(1)}, u32[]{:S(2)}, u32[]{:S(2)}) collective-permute-start(bf16[240,1024]{1,0:T(8,128)(2,1)} %get-tuple-element.111), channel_id=1, source_target_pairs={{0,1},{1,0},{2,3},{3,2},{4,5},{5,4},{6,7},{7,6},{8,9},{9,8},{10,11... | collective-permute-start | bytes 1474568 | tf_op jit(solution)/shard_map/ppermute | solution.py:423
  128.3 3.4 %collective-permute-start.25 = (bf16[240,1024]{1,0:T(8,128)(2,1)}, bf16[240,1024]{1,0:T(8,128)(2,1)S(1)}, u32[]{:S(2)}, u32[]{:S(2)}) collective-permute-start(bf16[240,1024]{1,0:T(8,128)(2,1)} %get-tuple-element.115), channel_id=1, source_target_pairs={{0,1},{1,0},{2,3},{3,2},{4,5},{5,4},{6,7},{7,6},{8,9},{9,8},{10,11... | collective-permute-start | bytes 1474568 | tf_op jit(solution)/shard_map/ppermute | solution.py:423
  128.4 5.2 %collective-permute-start.26 = (bf16[240,1024]{1,0:T(8,128)(2,1)}, bf16[240,1024]{1,0:T(8,128)(2,1)S(1)}, u32[]{:S(2)}, u32[]{:S(2)}) collective-permute-start(bf16[240,1024]{1,0:T(8,128)(2,1)} %get-tuple-element.119), channel_id=1, source_target_pairs={{0,1},{1,0},{2,3},{3,2},{4,5},{5,4},{6,7},{7,6},{8,9},{9,8},{10,11... | collective-permute-start | bytes 1474568 | tf_op jit(solution)/shard_map/ppermute | solution.py:423
  128.8 6.7 %collective-permute-start.27 = (bf16[240,1024]{1,0:T(8,128)(2,1)}, bf16[240,1024]{1,0:T(8,128)(2,1)S(1)}, u32[]{:S(2)}, u32[]{:S(2)}) collective-permute-start(bf16[240,1024]{1,0:T(8,128)(2,1)} %get-tuple-element.123), channel_id=1, source_target_pairs={{0,1},{1,0},{2,3},{3,2},{4,5},{5,4},{6,7},{7,6},{8,9},{9,8},{10,11... | collective-permute-start | bytes 1474568 | tf_op jit(solution)/shard_map/ppermute | solution.py:423
  141.3 64.9 %all-to-all-start.2 = ((bf16[4,128,1024]{2,1,0:T(8,128)(2,1)}), bf16[4,128,1024]{2,1,0:T(8,128)(2,1)S(1)}, u32[]{:S(2)}, u32[]{:S(2)}) async-start(bf16[4,128,1024]{2,1,0:T(8,128)(2,1)} %combine.1), calls=%async_computation.2 | async-start | bytes 2097152 | tf_op jit(solution)/shard_map/all_to_all | solution.py:437
  147.7 20.6 %collective-permute-start.28 = (bf16[128,1024]{1,0:T(8,128)(2,1)}, bf16[128,1024]{1,0:T(8,128)(2,1)}, u32[]{:S(2)}, u32[]{:S(2)}) collective-permute-start(bf16[128,1024]{1,0:T(8,128)(2,1)} %add_convert_fusion.7), channel_id=1, source_target_pairs={{0,2},{2,0},{4,6},{6,4},{8,10},{10,8},{12,14},{14,12},{16,18},{18,... | collective-permute-start | bytes 786440 | tf_op jit(solution)/shard_map/ppermute | solution.py:415
  150.5 19.8 %collective-permute-start.29 = (bf16[128,1024]{1,0:T(8,128)(2,1)}, bf16[128,1024]{1,0:T(8,128)(2,1)}, u32[]{:S(2)}, u32[]{:S(2)}) collective-permute-start(bf16[128,1024]{1,0:T(8,128)(2,1)} %add_convert_fusion.6), channel_id=1, source_target_pairs={{0,4},{2,6},{4,0},{6,2},{8,12},{10,14},{12,8},{14,10},{16,20},{18,... | collective-permute-start | bytes 786440 | tf_op jit(solution)/shard_map/ppermute | solution.py:415
  151.8 18.4 %collective-permute-start.30 = (bf16[128,1024]{1,0:T(8,128)(2,1)}, bf16[128,1024]{1,0:T(8,128)(2,1)}, u32[]{:S(2)}, u32[]{:S(2)}) collective-permute-start(bf16[128,1024]{1,0:T(8,128)(2,1)} %add_convert_fusion.5), channel_id=1, source_target_pairs={{0,6},{2,4},{4,2},{6,0},{8,14},{10,12},{12,10},{14,8},{16,22},{18,... | collective-permute-start | bytes 786440 | tf_op jit(solution)/shard_map/ppermute | solution.py:415
  152.9 23.6 %collective-permute-start.31 = (bf16[112,1024]{1,0:T(8,128)(2,1)}, bf16[112,1024]{1,0:T(8,128)(2,1)}, u32[]{:S(2)}, u32[]{:S(2)}) collective-permute-start(bf16[112,1024]{1,0:T(8,128)(2,1)} %add_convert_fusion.11), channel_id=1, source_target_pairs={{0,2},{2,0},{4,6},{6,4},{8,10},{10,8},{12,14},{14,12},{16,18},{18,... | collective-permute-start | bytes 688136 | tf_op jit(solution)/shard_map/ppermute | solution.py:415
  153.9 22.5 %collective-permute-start.32 = (bf16[112,1024]{1,0:T(8,128)(2,1)}, bf16[112,1024]{1,0:T(8,128)(2,1)}, u32[]{:S(2)}, u32[]{:S(2)}) collective-permute-start(bf16[112,1024]{1,0:T(8,128)(2,1)} %add_convert_fusion.10), channel_id=1, source_target_pairs={{0,4},{2,6},{4,0},{6,2},{8,12},{10,14},{12,8},{14,10},{16,20},{18,... | collective-permute-start | bytes 688136 | tf_op jit(solution)/shard_map/ppermute | solution.py:415
  154.5 15.0 %copy-start.8 = (bf16[240,1024]{1,0:T(8,128)(2,1)S(1)}, bf16[240,1024]{1,0:T(8,128)(2,1)}, u32[]{:S(2)}) copy-start(bf16[240,1024]{1,0:T(8,128)(2,1)} %get-tuple-element.109) | copy-start | bytes 1474564
  168.4 8.1 %collective-permute-start.33 = (bf16[112,1024]{1,0:T(8,128)(2,1)}, bf16[112,1024]{1,0:T(8,128)(2,1)}, u32[]{:S(2)}, u32[]{:S(2)}) collective-permute-start(bf16[112,1024]{1,0:T(8,128)(2,1)} %add_convert_fusion.9), channel_id=1, source_target_pairs={{0,6},{2,4},{4,2},{6,0},{8,14},{10,12},{12,10},{14,8},{16,22},{18,... | collective-permute-start | bytes 688136 | tf_op jit(solution)/shard_map/ppermute | solution.py:415
  170.3 34.0 %copy-start.24 = (bf16[128,1024]{1,0:T(8,128)(2,1)S(1)}, bf16[128,1024]{1,0:T(8,128)(2,1)}, u32[]{:S(2)}) copy-start(bf16[128,1024]{1,0:T(8,128)(2,1)} %param.10) | copy-start | bytes 786436
  174.2 7.2 %collective-permute-start.36 = (bf16[144,1024]{1,0:T(8,128)(2,1)}, bf16[144,1024]{1,0:T(8,128)(2,1)S(1)}, u32[]{:S(2)}, u32[]{:S(2)}) collective-permute-start(bf16[144,1024]{1,0:T(8,128)(2,1)} %get-tuple-element.141), channel_id=1, source_target_pairs={{0,8},{2,10},{4,12},{6,14},{8,16},{10,18},{12,20},{14,22},{16,24},... | collective-permute-start | bytes 884744 | tf_op jit(solution)/shard_map/ppermute | solution.py:408
  175.5 23.0 %collective-permute-start.35 = (bf16[144,1024]{1,0:T(8,128)(2,1)}, bf16[144,1024]{1,0:T(8,128)(2,1)S(1)}, u32[]{:S(2)}, u32[]{:S(2)}) collective-permute-start(bf16[144,1024]{1,0:T(8,128)(2,1)} %get-tuple-element.140), channel_id=1, source_target_pairs={{0,16},{2,18},{4,20},{6,22},{8,24},{10,26},{12,28},{14,30},{16,0},... | collective-permute-start | bytes 884744 | tf_op jit(solution)/shard_map/ppermute | solution.py:408
  180.0 23.1 %collective-permute-start.34 = (bf16[144,1024]{1,0:T(8,128)(2,1)}, bf16[144,1024]{1,0:T(8,128)(2,1)S(1)}, u32[]{:S(2)}, u32[]{:S(2)}) collective-permute-start(bf16[144,1024]{1,0:T(8,128)(2,1)} %get-tuple-element.139), channel_id=1, source_target_pairs={{0,24},{2,26},{4,28},{6,30},{8,0},{10,2},{12,4},{14,6},{16,8},{18,... | collective-permute-start | bytes 884744 | tf_op jit(solution)/shard_map/ppermute | solution.py:408
  (18 other events, 82.2 us)
